TPU v7x, 32 devices: a whole 2x2x4 slice. The times are simulated.
32 devices in a mesh: pipe: 4 (over z), zero: 8 (over y, x, core).
Axes of the slice: x: 2, y: 2, z: 4, core: 2. Of those that a mesh axis runs over, the one named last changes fastest.
Arguments:
- down_out: bfloat16 [4, 64, 2048], P('pipe', 'zero'), may hold values from -6 to 6
- up_out: bfloat16 [4, 64, 2048], P('pipe', 'zero'), may hold values from -6 to 6
- feeds: bfloat16 [2, 64, 2048], P(None, 'zero'), may hold values from -6 to 6
- order: int32 [2], replicated, may hold values from 0 to 1, each once
- gains: float32 [4, 2, 2048], P('pipe'), may hold values from 0.1 to 1.9
- gate_w: bfloat16 [4, 2, 2048, 4096], P('pipe', None, None, 'zero'), may hold values from -0.125 to 0.125
- up_w: bfloat16 [4, 2, 2048, 4096], P('pipe', None, None, 'zero'), may hold values from -0.125 to 0.125
- down_w: bfloat16 [4, 2, 4096, 2048], P('pipe', None, 'zero'), may hold values from -0.09375 to 0.09375
Outputs:
- down_next: bfloat16 [4, 64, 2048], P('pipe', 'zero')
- up_next: bfloat16 [4, 64, 2048], P('pipe', 'zero')
Inputs may be any that keep to these rules, and one draw needn't show every extreme that they name: `order`: every micro-batch index enters exactly once.
All inputs are finite; a program needn't handle non-finite values.
Results may differ from a plain program's by a relative error of at most 0.02.
Values may be sent and summed in bfloat16 or wider, within the bound.
No kernel may reach another device: no remote copies, remote signals or barrier semaphores. Data moves between devices by JAX's collectives and lax.ppermute only.
A program may use at most 64 MiB of HBM per device.

v0:
```python
import jax
import jax.numpy as jnp
from jax import lax
from jax.sharding import PartitionSpec as P

TICKS = 2


def shifted(value, axis, steps):
    count = lax.axis_size(axis)
    first, last = (max(0, -steps), min(count, count - steps))
    return lax.ppermute(value, axis, [(source, source + steps) for source in range(first, last)])


def normalize(x, gain):
    xf = x.astype(jnp.float32)
    return (xf * lax.rsqrt(jnp.mean(xf * xf, axis=-1, keepdims=True) + 1e-05) * gain).astype(
        jnp.bfloat16
    )


def hidden_rows(piece, w_gate, w_up):
    gate = jnp.dot(piece, w_gate, preferred_element_type=jnp.float32)
    up = jnp.dot(piece, w_up, preferred_element_type=jnp.float32)
    return (jax.nn.silu(gate) * up).astype(jnp.bfloat16)


def on_device(down_out, up_out, feeds, order, gains, gate_w, up_w, down_w):
    section = lax.axis_index("pipe")
    first_section = section == 0
    last_section = section == lax.axis_size("pipe") - 1
    down_state = down_out[0]
    up_state = up_out[0]
    for tick in range(TICKS):
        arriving = shifted(down_state, "pipe", 1)
        returning = shifted(up_state, "pipe", -1)
        down_in = jnp.where(first_section, feeds[order[tick]], arriving)
        up_in = jnp.where(last_section, down_state, returning)
        normed_down = normalize(down_in, gains[0, 0])
        normed_up = normalize(up_in, gains[0, 1])
        pieces = lax.all_gather((normed_down, normed_up), "zero", axis=0, tiled=True)
        hidden_down = hidden_rows(pieces[0], gate_w[0, 0], up_w[0, 0])
        hidden_up = hidden_rows(pieces[1], gate_w[0, 1], up_w[0, 1])
        summed = lax.psum_scatter(
            jnp.concatenate(
                [
                    jnp.dot(hidden_down, down_w[0, 0], preferred_element_type=jnp.float32),
                    jnp.dot(hidden_up, down_w[0, 1], preferred_element_type=jnp.float32),
                ],
                axis=1,
            ).astype(jnp.bfloat16),
            "zero",
            scatter_dimension=0,
            tiled=True,
        ).astype(jnp.float32)
        width = down_in.shape[1]
        new_down = (down_in.astype(jnp.float32) + summed[:, :width]).astype(jnp.bfloat16)
        new_up = (up_in.astype(jnp.float32) + summed[:, width:]).astype(jnp.bfloat16)
        down_state = new_down
        up_state = new_up
    return (down_state[None], up_state[None])


def solution(mesh):
    return jax.shard_map(
        on_device,
        mesh=mesh,
        in_specs=(
            P("pipe", "zero", None),
            P("pipe", "zero", None),
            P(None, "zero", None),
            P(),
            P("pipe", None, None),
            P("pipe", None, None, "zero"),
            P("pipe", None, None, "zero"),
            P("pipe", None, "zero", None),
        ),
        out_specs=(P("pipe", "zero", None), P("pipe", "zero", None)),
        check_vma=False,
    )
```

profile of v0, /device:TPU:0, one launch (start us, length us, event | category | flops | bytes accessed | tf_op | source)
XLA Modules:
  0.0 164.2 jit_solution(11527066585380563291)
XLA Ops:
  7.2 1.3 collective-permute-start.1
  8.5 5.6 %collective-permute-start = (bf16[8,2048]{1,0:T(8,128)(2,1)}, bf16[8,2048]{1,0:T(8,128)(2,1)S(1)}, u32[]{:S(2)}, u32[]{:S(2)}) collective-permute-start(bf16[8,2048]{1,0:T(8,128)(2,1)} %bitcast.84), channel_id=1, source_target_pairs={{0,8},{8,16},{16,24},{1,9},{9,17},{17,25},{2,10},{10,18},{18,26},{... | collective-permute-start | bytes 98312 | tf_op jit(solution)/shard_map/ppermute | solution.py:12
  14.1 0.8 fusion.111
  14.9 1.3 fusion.112
  18.2 0.9 fusion.88
  19.1 0.9 fusion.84
  20.0 0.1 fusion.86
  20.1 9.7 %all_gather.12 = bf16[64,2048]{1,0:T(8,128)(2,1)S(1)} all-gather(bf16[8,2048]{1,0:T(8,128)(2,1)S(1)} %fusion.86), channel_id=1, replica_groups=mesh['pipe'=4,'zero'=8] {'zero'}, dimensions={0}, use_global_device_ids=true | all-gather | bytes 294912 | tf_op jit(solution)/shard_map/all_gather | solution.py:41
  29.9 9.3 %all_gather.13 = bf16[64,2048]{1,0:T(8,128)(2,1)S(1)} all-gather(bf16[8,2048]{1,0:T(8,128)(2,1)S(1)} %fusion.90), channel_id=1, replica_groups=mesh['pipe'=4,'zero'=8] {'zero'}, dimensions={0}, use_global_device_ids=true | all-gather | bytes 294912 | tf_op jit(solution)/shard_map/all_gather | solution.py:41
  39.2 2.1 %fusion.18 = f32[64,512]{1,0:T(8,128)S(1)} fusion(bf16[64,2048]{1,0:T(8,128)(2,1)S(1)} %all_gather.12, bf16[1,2,2048,512]{3,2,1,0:T(8,128)(2,1)} %param.13), kind=kOutput, calls=%fused_computation.22 | convolution fusion | flops 134217728 | bytes 2490368 | tf_op jit(solution)/shard_map/dot_general | solution.py:23
  41.2 2.1 %fusion.8 = f32[64,512]{1,0:T(8,128)S(1)} fusion(bf16[64,2048]{1,0:T(8,128)(2,1)S(1)} %all_gather.13, bf16[1,2,2048,512]{3,2,1,0:T(8,128)(2,1)} %param.13), kind=kOutput, calls=%fused_computation.12 | convolution fusion | flops 134217728 | bytes 2490368 | tf_op jit(solution)/shard_map/dot_general | solution.py:23
  43.3 3.1 %convolution_convert_fusion.3 = bf16[64,2048]{1,0:T(8,128)(2,1)S(1)} fusion(bf16[1,2,512,2048]{3,2,1,0:T(8,128)(2,1)} %param.15, bf16[64,2048]{1,0:T(8,128)(2,1)S(1)} %all_gather.12, bf16[1,2,2048,512]{3,2,1,0:T(8,128)(2,1)} %param.14, f32[64,512]{1,0:T(8,128)S(1)} %fusion.18), kind=kOutput, calls=%fused_computation.3 | convolution fusion | flops 268763136 | bytes 4849664 | tf_op jit(solution)/shard_map/dot_general | solution.py:47
  46.4 3.1 %convolution_convert_fusion.2 = bf16[64,2048]{1,0:T(8,128)(2,1)S(1)} fusion(bf16[1,2,512,2048]{3,2,1,0:T(8,128)(2,1)} %param.15, bf16[64,2048]{1,0:T(8,128)(2,1)S(1)} %all_gather.13, bf16[1,2,2048,512]{3,2,1,0:T(8,128)(2,1)} %param.14, f32[64,512]{1,0:T(8,128)S(1)} %fusion.8), kind=kOutput, calls=%fused_computation.2 | convolution fusion | flops 268763136 | bytes 4849664 | tf_op jit(solution)/shard_map/dot_general | solution.py:48
  49.6 0.8 pad_maximum_fusion
  50.5 33.5 %reduce-scatter.3.cloned.1.call-done = bf16[8,4096]{1,0:T(8,128)(2,1)} async-done(((bf16[64,4096]{1,0:T(8,128)(2,1)}), bf16[8,4096]{1,0:T(8,128)(2,1)}) %reduce-scatter.3.cloned.1.call-update) | async-done | bytes 65552 | tf_op jit(solution)/shard_map/reduce_scatter | solution.py:44
  84.0 0.8 convert_element_type.66
  84.8 1.3 collective-permute-start.3
  88.1 2.6 %collective-permute-done.3 = bf16[8,2048]{1,0:T(8,128)(2,1)S(1)} collective-permute-done((bf16[8,2048]{1,0:T(8,128)(2,1)S(1)}, bf16[8,2048]{1,0:T(8,128)(2,1)S(1)}, u32[]{:S(2)}, u32[]{:S(2)}) %collective-permute-start.3) | collective-permute-done | bytes 32800 | tf_op jit(solution)/shard_map/ppermute | solution.py:12
  90.6 0.1 fusion.96
  90.8 3.4 %collective-permute-start.2 = (bf16[8,2048]{1,0:T(8,128)(2,1)S(1)}, bf16[8,2048]{1,0:T(8,128)(2,1)S(1)}, u32[]{:S(2)}, u32[]{:S(2)}) collective-permute-start(bf16[8,2048]{1,0:T(8,128)(2,1)S(1)} %get-tuple-element.6), channel_id=1, source_target_pairs={{0,8},{8,16},{16,24},{1,9},{9,17},{17,25},{2,10},{10,18},{18,26},{... | collective-permute-start | bytes 98312 | tf_op jit(solution)/shard_map/ppermute | solution.py:12
  94.3 9.2 %all_gather.15 = bf16[64,2048]{1,0:T(8,128)(2,1)S(1)} all-gather(bf16[8,2048]{1,0:T(8,128)(2,1)S(1)} %fusion.98), channel_id=1, replica_groups=mesh['pipe'=4,'zero'=8] {'zero'}, dimensions={0}, use_global_device_ids=true | all-gather | bytes 294912 | tf_op jit(solution)/shard_map/all_gather | solution.py:41
  103.5 2.1 %fusion.6 = f32[64,512]{1,0:T(8,128)S(1)} fusion(bf16[64,2048]{1,0:T(8,128)(2,1)S(1)} %all_gather.15, bf16[1,2,2048,512]{3,2,1,0:T(8,128)(2,1)} %param.13), kind=kOutput, calls=%fused_computation.10 | convolution fusion | flops 134217728 | bytes 2490368 | tf_op jit(solution)/shard_map/dot_general | solution.py:23
  105.6 3.1 %convolution_convert_fusion = bf16[64,2048]{1,0:T(8,128)(2,1)S(1)} fusion(bf16[1,2,512,2048]{3,2,1,0:T(8,128)(2,1)} %param.15, bf16[64,2048]{1,0:T(8,128)(2,1)S(1)} %all_gather.15, bf16[1,2,2048,512]{3,2,1,0:T(8,128)(2,1)} %param.14, f32[64,512]{1,0:T(8,128)S(1)} %fusion.6), kind=kOutput, calls=%fused_computation | convolution fusion | flops 268763136 | bytes 4849664 | tf_op jit(solution)/shard_map/dot_general | solution.py:48
  108.8 0.1 fusion.92
  108.9 0.1 fusion.94
  109.0 8.4 %all_gather.14 = bf16[64,2048]{1,0:T(8,128)(2,1)S(1)} all-gather(bf16[8,2048]{1,0:T(8,128)(2,1)S(1)} %fusion.94), channel_id=1, replica_groups=mesh['pipe'=4,'zero'=8] {'zero'}, dimensions={0}, use_global_device_ids=true | all-gather | bytes 294912 | tf_op jit(solution)/shard_map/all_gather | solution.py:41
  117.4 2.1 %fusion.16 = f32[64,512]{1,0:T(8,128)S(1)} fusion(bf16[64,2048]{1,0:T(8,128)(2,1)S(1)} %all_gather.14, bf16[1,2,2048,512]{3,2,1,0:T(8,128)(2,1)} %param.13), kind=kOutput, calls=%fused_computation.20 | convolution fusion | flops 134217728 | bytes 2490368 | tf_op jit(solution)/shard_map/dot_general | solution.py:23
  119.4 3.1 %convolution_convert_fusion.1 = bf16[64,2048]{1,0:T(8,128)(2,1)S(1)} fusion(bf16[1,2,512,2048]{3,2,1,0:T(8,128)(2,1)} %param.15, bf16[64,2048]{1,0:T(8,128)(2,1)S(1)} %all_gather.14, bf16[1,2,2048,512]{3,2,1,0:T(8,128)(2,1)} %param.14, f32[64,512]{1,0:T(8,128)S(1)} %fusion.16), kind=kOutput, calls=%fused_computation.1 | convolution fusion | flops 268763136 | bytes 4849664 | tf_op jit(solution)/shard_map/dot_general | solution.py:47
  122.6 0.8 pad_maximum_fusion.1
  123.4 32.5 %reduce-scatter.5.cloned.1.call-done = bf16[8,4096]{1,0:T(8,128)(2,1)} async-done(((bf16[64,4096]{1,0:T(8,128)(2,1)}), bf16[8,4096]{1,0:T(8,128)(2,1)}) %reduce-scatter.5.cloned.1.call-update) | async-done | bytes 65552 | tf_op jit(solution)/shard_map/reduce_scatter | solution.py:44
  155.9 0.8 convert_element_type.75
  156.8 0.6 fusion.104
  (16 shorter events, 0.3 us)
Async XLA Ops:
  7.2 76.8 %reduce-scatter.3.cloned.1.call-start = ((), (), s32[]{:S(2)}) async-start(), calls=%async_computation.2 | async-start | bytes 589824 | tf_op jit(solution)/shard_map/reduce_scatter | solution.py:44
  7.2 10.9 %collective-permute-start.1 = (bf16[8,2048]{1,0:T(8,128)(2,1)}, bf16[8,2048]{1,0:T(8,128)(2,1)S(1)}, u32[]{:S(2)}, u32[]{:S(2)}) collective-permute-start(bf16[8,2048]{1,0:T(8,128)(2,1)} %bitcast.85), channel_id=1, source_target_pairs={{8,0},{16,8},{24,16},{9,1},{17,9},{25,17},{10,2},{18,10},{26,18},{... | collective-permute-start | bytes 98312 | tf_op jit(solution)/shard_map/ppermute | solution.py:12
  8.5 10.6 %collective-permute-start = (bf16[8,2048]{1,0:T(8,128)(2,1)}, bf16[8,2048]{1,0:T(8,128)(2,1)S(1)}, u32[]{:S(2)}, u32[]{:S(2)}) collective-permute-start(bf16[8,2048]{1,0:T(8,128)(2,1)} %bitcast.84), channel_id=1, source_target_pairs={{0,8},{8,16},{16,24},{1,9},{9,17},{17,25},{2,10},{10,18},{18,26},{... | collective-permute-start | bytes 98312 | tf_op jit(solution)/shard_map/ppermute | solution.py:12
  50.4 105.5 %reduce-scatter.5.cloned.1.call-start = ((), (), s32[]{:S(2)}) async-start(), calls=%async_computation.3 | async-start | bytes 589824 | tf_op jit(solution)/shard_map/reduce_scatter | solution.py:44
  84.8 5.8 %collective-permute-start.3 = (bf16[8,2048]{1,0:T(8,128)(2,1)S(1)}, bf16[8,2048]{1,0:T(8,128)(2,1)S(1)}, u32[]{:S(2)}, u32[]{:S(2)}) collective-permute-start(bf16[8,2048]{1,0:T(8,128)(2,1)S(1)} %fusion.91), channel_id=1, source_target_pairs={{8,0},{16,8},{24,16},{9,1},{17,9},{25,17},{10,2},{18,10},{26,18},{... | collective-permute-start | bytes 98312 | tf_op jit(solution)/shard_map/ppermute | solution.py:12
  90.8 18.0 %collective-permute-start.2 = (bf16[8,2048]{1,0:T(8,128)(2,1)S(1)}, bf16[8,2048]{1,0:T(8,128)(2,1)S(1)}, u32[]{:S(2)}, u32[]{:S(2)}) collective-permute-start(bf16[8,2048]{1,0:T(8,128)(2,1)S(1)} %get-tuple-element.6), channel_id=1, source_target_pairs={{0,8},{8,16},{16,24},{1,9},{9,17},{17,25},{2,10},{10,18},{18,26},{... | collective-permute-start | bytes 98312 | tf_op jit(solution)/shard_map/ppermute | solution.py:12
  103.5 5.3 %copy-start = (bf16[2,8,2048]{2,1,0:T(8,128)(2,1)S(1)}, bf16[2,8,2048]{2,1,0:T(8,128)(2,1)}, u32[]{:S(2)}) copy-start(bf16[2,8,2048]{2,1,0:T(8,128)(2,1)} %param.10) | copy-start | bytes 196612
Sparse Core Ops, SparseCore 0:
  50.5 33.3 reduce-scatter.2
  123.6 32.3 reduce-scatter.4
where the time goes:
time: 165 us; the launch traced here: 164 us
  waiting for transfers between devices  68.6 us (42%)
  blocking collectives  36.6 us (22%)
  matrix products  20.8 us (13%)
  between operations  18.1 us (11%)
  starting transfers between devices  11.6 us (7%)
  other arithmetic  6.4 us (4%)
  local copies, waits for them, and re-layouts  2.13 us (1%)
    reduce_scatter x2, waiting for transfers between devices, on_device(): lax.psum_scatter(jnp.concatenate([jnp.dot(hidden_down, down_w[0, 0], pref...  66 us
    all_gather x4, blocking collectives, on_device(): lax.all_gather((normed_down, normed_up), 'zero', axis=0, tiled=True)  36.6 us
    ppermute x4, starting transfers between devices, shifted(): lax.ppermute(value, axis, [(source, source + steps) for source in range(f...  11.5 us
    dot_general x4, matrix products, hidden_rows(): gate = jnp.dot(piece, w_gate, preferred_element_type=jnp.float32)  8.27 us
    dot_general x2, matrix products, on_device(): jnp.dot(hidden_up, down_w[0, 1], preferred_element_type=jnp.float32)  6.28 us
    dot_general x2, matrix products, on_device(): jnp.dot(hidden_down, down_w[0, 0], preferred_element_type=jnp.float32)  6.28 us
  transfers between devices with their start and end apart: 6, of which 3 were waited for; matrix products, arithmetic and copies ran while one was open for 5% of the time, Pallas kernels for 0%

commit v1 on v0

v1 whole, which is shorter than its diff:
```python
import functools

import jax
import jax.numpy as jnp
from jax import lax
from jax.experimental import pallas as pl
from jax.experimental.pallas import tpu as pltpu
from jax.sharding import PartitionSpec as P

CORES = 2
EPS = 1e-05


def normalize(x, gain):
    xf = x.astype(jnp.float32)
    return (xf * lax.rsqrt(jnp.mean(xf * xf, axis=-1, keepdims=True) + EPS) * gain).astype(jnp.bfloat16)


def group_kernel(role_ref, mine_ref, sibling_ref, gains_ref, gate_ref, up_ref, down_ref, own_out, sibling_out):
    role = role_ref[0]
    for group, x_ref, out in ((1 - role, sibling_ref, sibling_out), (role, mine_ref, own_out)):
        normed = normalize(x_ref[...], gains_ref[pl.ds(group, 1), :])
        gate = jnp.dot(normed, gate_ref[group], preferred_element_type=jnp.float32)
        up = jnp.dot(normed, up_ref[group], preferred_element_type=jnp.float32)
        hidden = (gate / (1.0 + jnp.exp(-gate)) * up).astype(jnp.bfloat16)
        out[...] = jnp.dot(hidden, down_ref[group], preferred_element_type=jnp.float32).astype(out.dtype)


def groups(role, mine, sibling, gains, gate_w, up_w, down_w):
    vmem = pl.BlockSpec(memory_space=pltpu.VMEM)
    weights = gate_w.size + up_w.size + down_w.size
    return pl.pallas_call(
        group_kernel,
        out_shape=(
            jax.ShapeDtypeStruct(mine.shape, jnp.float32),
            jax.ShapeDtypeStruct(mine.shape, jnp.bfloat16),
        ),
        in_specs=[pl.BlockSpec(memory_space=pltpu.SMEM)] + [vmem] * 6,
        out_specs=(vmem, vmem),
        compiler_params=pltpu.CompilerParams(vmem_limit_bytes=20 * 2**20),
        cost_estimate=pl.CostEstimate(
            flops=2 * mine.shape[0] * weights, bytes_accessed=2 * weights, transcendentals=0
        ),
    )(role, mine, sibling, gains, gate_w, up_w, down_w)


def chip_pairs(chips, step):
    if chips & (chips - 1) == 0:
        return [(chip, chip ^ step) for chip in range(chips)]
    return [(chip, (chip + step) % chips) for chip in range(chips)]


def on_device(down_out, up_out, feeds, order, gains, gate_w, up_w, down_w):
    sections, zero = lax.axis_size("pipe"), lax.axis_size("zero")
    chips = zero // CORES
    section, place = lax.axis_index("pipe"), lax.axis_index("zero")
    core = place % CORES
    ticks = feeds.shape[0]
    both = ("pipe", "zero")

    def to_sibling(value):
        return lax.ppermute(value, "zero", [(k, k ^ 1) for k in range(zero)])

    def to_chip(value, step):
        pairs = [(a * CORES + r, b * CORES + r) for a, b in chip_pairs(chips, step) for r in range(CORES)]
        return lax.ppermute(value, "zero", pairs)

    def to_section(value, tick):
        pairs = []
        for s in range(sections):
            for k in range(zero):
                other = s - 1 if (s + k % CORES + tick) % 2 == 0 else s + 1
                other = other if 0 <= other < sections else s
                pairs.append((s * zero + k, other * zero + k))
        return lax.ppermute(value, both, pairs)

    def joined(own, other):
        first = jnp.where(core == 0, own, other)
        second = jnp.where(core == 0, other, own)
        return jnp.concatenate([first, second], axis=0)

    def role_at(tick):
        return (section + core + tick) % 2

    ascended = jnp.where(section == 0, feeds[order[0]], up_out[0])
    descended = down_out[0]
    rows = descended.shape[0]
    was_down = role_at(-1) == 0
    given = jnp.where(was_down, ascended, descended)
    later = [feeds[order[tick]] for tick in range(1, ticks)]
    taken = to_sibling(jnp.concatenate([given] + later, axis=0))
    state = joined(jnp.where(was_down, descended, ascended), taken[:rows])
    entering = [joined(own, taken[rows * (n + 1) : rows * (n + 2)]) for n, own in enumerate(later)]

    for tick in range(ticks):
        role = role_at(tick)
        if tick > 0:
            state = jnp.where((section == 0) & (role == 0), entering[tick - 1], state)
        x = to_section(state, tick)
        mine = jnp.concatenate([x] + [to_chip(x, step) for step in range(1, chips)], axis=0)
        sibling = to_sibling(mine)
        own_part, sibling_part = groups(
            role.reshape(1).astype(jnp.int32), mine, sibling, gains[0], gate_w[0], up_w[0], down_w[0]
        )
        part = own_part + to_sibling(sibling_part).astype(jnp.float32)
        height = x.shape[0]
        back = chips if chips & (chips - 1) == 0 else 0
        total = x.astype(jnp.float32) + part[:height]
        for step in range(1, chips):
            source = step if back else chips - step
            piece = part[source * height : (source + 1) * height].astype(jnp.bfloat16)
            total = total + to_chip(piece, step).astype(jnp.float32)
        state = total.astype(jnp.bfloat16)

    role = role_at(ticks - 1)
    kept = jnp.where(core == 0, state[:rows], state[rows:])
    received = to_sibling(jnp.where(core == 0, state[rows:], state[:rows]))
    down_state = jnp.where(role == 0, kept, received)
    up_state = jnp.where(role == 0, received, kept)
    return (down_state[None], up_state[None])


def solution(mesh):
    return jax.shard_map(
        on_device,
        mesh=mesh,
        in_specs=(
            P("pipe", "zero", None),
            P("pipe", "zero", None),
            P(None, "zero", None),
            P(),
            P("pipe", None, None),
            P("pipe", None, None, "zero"),
            P("pipe", None, None, "zero"),
            P("pipe", None, "zero", None),
        ),
        out_specs=(P("pipe", "zero", None), P("pipe", "zero", None)),
        check_vma=False,
    )
```

time: 165 us -> 79.2 us (0.48)
  waiting for transfers between devices: 68.6 us -> 24.8 us
  blocking collectives: 36.6 us -> 0 us
  matrix products: 20.8 us -> 0 us
  starting transfers between devices: 11.6 us -> 27 us
  between operations: 18.1 us -> 4.7 us
  local copies, waits for them, and re-layouts: 2.13 us -> 15.2 us
  Pallas kernels: 0 us -> 5.14 us
  other arithmetic: 6.4 us -> 1.7 us
    reduce_scatter x2 -> x0, waiting for transfers between devices: 66 us -> none  [on_device(): lax.psum_scatter(jnp.concatenate([jnp.dot(hidden_down, down_w[0, 0], pref...]
    all_gather x4 -> x0, blocking collectives: 36.6 us -> none  [on_device(): lax.all_gather((normed_down, normed_up), 'zero', axis=0, tiled=True)]
    ppermute x4 -> x20, waiting for transfers between devices: 2.58 us -> 24.8 us  [the longest x12 15.2 us: to_chip(): return lax.ppermute(value, 'zero', pairs)]
    dot_general x8 -> x0, matrix products: 20.8 us -> none  [the longest x4 8.27 us: hidden_rows(): gate = jnp.dot(piece, w_gate, preferred_element_type=jnp.float32)]
    ppermute x4 -> x20, starting transfers between devices: 11.5 us -> 27 us  [the longest x12 15.1 us: to_chip(): return lax.ppermute(value, 'zero', pairs)]
    unnamed x2 -> x22, local copies, waits for them, and re-layouts: 0.01 us -> 13.9 us
    pallas_call x0 -> x2, Pallas kernels: none -> 5.14 us  [groups(): pl.pallas_call(group_kernel, out_shape=(jax.ShapeDtypeStruct(mine.shape,...]
    reduce_sum x4 -> x0, other arithmetic: 2.05 us -> none  [normalize(): jnp.mean(xf * xf, axis=-1, keepdims=True) + 1e-05]
  transfers between devices with their start and end apart: 6 -> 20, of which waited for: 3 -> 18; matrix products, arithmetic and copies ran while one was open for 5% -> 0% of each run, Pallas kernels for 0% -> 0%
where the time goes in v1:
time: 79.2 us; the launch traced here: 78.6 us
  starting transfers between devices  27 us (34%)
  waiting for transfers between devices  24.8 us (31%)
  local copies, waits for them, and re-layouts  15.2 us (19%)
  Pallas kernels  5.14 us (6%)
  between operations  4.7 us (6%)
  other arithmetic  1.7 us (2%)
    ppermute x12, waiting for transfers between devices, to_chip(): return lax.ppermute(value, 'zero', pairs)  15.2 us
    ppermute x12, starting transfers between devices, to_chip(): return lax.ppermute(value, 'zero', pairs)  15.1 us
    unnamed x22, local copies, waits for them, and re-layouts  13.9 us
    ppermute x6, waiting for transfers between devices, to_sibling(): return lax.ppermute(value, 'zero', [(k, k ^ 1) for k in range(zero)])  7.35 us
    ppermute x2, starting transfers between devices, to_section(): return lax.ppermute(value, both, pairs)  6.91 us
    pallas_call x2, Pallas kernels, groups(): pl.pallas_call(group_kernel, out_shape=(jax.ShapeDtypeStruct(mine.shape,...  5.14 us
    ppermute x6, starting transfers between devices, to_sibling(): return lax.ppermute(value, 'zero', [(k, k ^ 1) for k in range(zero)])  4.98 us
    ppermute x2, waiting for transfers between devices, to_section(): return lax.ppermute(value, both, pairs)  2.23 us
  transfers between devices with their start and end apart: 20, of which 18 were waited for; matrix products, arithmetic and copies ran while one was open for 0% of the time, Pallas kernels for 0%

profile of v1, /device:TPU:0, one launch (start us, length us, event | category | flops | bytes accessed | tf_op | source)
XLA Modules:
  0.0 78.6 jit_solution(11783137037422438619)
XLA Ops:
  0.7 1.3 %fusion.13 = (s32[1]{0:T(128)}, s32[1]{0:T(128)}) fusion(s32[2]{0:T(128)} %param.11), kind=kLoop, calls=%fused_computation.39 | loop fusion | bytes 16 | tf_op jit(solution)/shard_map/slice | solution.py:85
  7.2 0.9 %collective-permute-done = bf16[16,2048]{1,0:T(8,128)(2,1)S(1)} collective-permute-done((bf16[16,2048]{1,0:T(8,128)(2,1)S(1)}, bf16[16,2048]{1,0:T(8,128)(2,1)S(1)}, u32[]{:S(2)}, u32[]{:S(2)}) %collective-permute-start) | collective-permute-done | bytes 65568 | tf_op jit(solution)/shard_map/ppermute | solution.py:62
  8.8 2.9 %collective-permute-start.2 = (bf16[16,2048]{1,0:T(8,128)(2,1)S(1)}, bf16[16,2048]{1,0:T(8,128)(2,1)S(1)}, u32[]{:S(2)}, u32[]{:S(2)}) collective-permute-start(bf16[16,2048]{1,0:T(8,128)(2,1)S(1)} %collective-permute-done.1), channel_id=1, source_target_pairs={{0,2},{1,3},{2,0},{3,1},{4,6},{5,7},{6,4},{7,5},{8,10},{9,11},{10,... | collective-permute-start | bytes 196616 | tf_op jit(solution)/shard_map/ppermute | solution.py:66
  11.8 1.5 %collective-permute-start.3 = (bf16[16,2048]{1,0:T(8,128)(2,1)S(1)}, bf16[16,2048]{1,0:T(8,128)(2,1)S(1)}, u32[]{:S(2)}, u32[]{:S(2)}) collective-permute-start(bf16[16,2048]{1,0:T(8,128)(2,1)S(1)} %collective-permute-done.1), channel_id=1, source_target_pairs={{0,4},{1,5},{2,6},{3,7},{4,0},{5,1},{6,2},{7,3},{8,12},{9,13},{10,... | collective-permute-start | bytes 196616 | tf_op jit(solution)/shard_map/ppermute | solution.py:66
  14.0 2.0 %collective-permute-done.3 = bf16[16,2048]{1,0:T(8,128)(2,1)S(1)} collective-permute-done((bf16[16,2048]{1,0:T(8,128)(2,1)S(1)}, bf16[16,2048]{1,0:T(8,128)(2,1)S(1)}, u32[]{:S(2)}, u32[]{:S(2)}) %collective-permute-start.3) | collective-permute-done | bytes 65568 | tf_op jit(solution)/shard_map/ppermute | solution.py:66
  16.0 2.4 %collective-permute-done.4 = bf16[16,2048]{1,0:T(8,128)(2,1)S(1)} collective-permute-done((bf16[16,2048]{1,0:T(8,128)(2,1)S(1)}, bf16[16,2048]{1,0:T(8,128)(2,1)S(1)}, u32[]{:S(2)}, u32[]{:S(2)}) %collective-permute-start.4) | collective-permute-done | bytes 65568 | tf_op jit(solution)/shard_map/ppermute | solution.py:66
  18.4 3.8 %collective-permute-start.5 = (bf16[64,2048]{1,0:T(8,128)(2,1)S(1)}, bf16[64,2048]{1,0:T(8,128)(2,1)S(1)}, u32[]{:S(2)}, u32[]{:S(2)}) collective-permute-start(bf16[64,2048]{1,0:T(8,128)(2,1)S(1)} %constant_dynamic-update-slice_fusion.mine_ref), channel_id=1, source_target_pairs={{0,1},{1,0},{2,3},{3,2},{4,5},{5,4},{6,7},{7,6},{8,9},{9,8},{10,11... | collective-permute-start | bytes 786440 | tf_op jit(solution)/shard_map/ppermute | solution.py:62
  22.2 1.2 %collective-permute-done.5.sibling_ref = bf16[64,2048]{1,0:T(8,128)(2,1)S(1)} collective-permute-done((bf16[64,2048]{1,0:T(8,128)(2,1)S(1)}, bf16[64,2048]{1,0:T(8,128)(2,1)S(1)}, u32[]{:S(2)}, u32[]{:S(2)}) %collective-permute-start.5) | collective-permute-done | bytes 262176 | tf_op jit(solution)/shard_map/ppermute | solution.py:62
  23.4 2.2 %copy-done = bf16[1,2,2048,512]{3,2,1,0:T(8,128)(2,1)S(1)} copy-done((bf16[1,2,2048,512]{3,2,1,0:T(8,128)(2,1)S(1)}, bf16[1,2,2048,512]{3,2,1,0:T(8,128)(2,1)}, u32[]{:S(2)}) %copy-start) | copy-done | bytes 4194328
  25.6 2.2 %copy-done.2 = bf16[1,2,2048,512]{3,2,1,0:T(8,128)(2,1)S(1)} copy-done((bf16[1,2,2048,512]{3,2,1,0:T(8,128)(2,1)S(1)}, bf16[1,2,2048,512]{3,2,1,0:T(8,128)(2,1)}, u32[]{:S(2)}) %copy-start.2) | copy-done | bytes 4194328
  27.7 2.2 %copy-done.4 = bf16[1,2,512,2048]{3,2,1,0:T(8,128)(2,1)S(1)} copy-done((bf16[1,2,512,2048]{3,2,1,0:T(8,128)(2,1)S(1)}, bf16[1,2,512,2048]{3,2,1,0:T(8,128)(2,1)}, u32[]{:S(2)}) %copy-start.4) | copy-done | bytes 4194328
  30.7 2.6 %shard_map.95 = (f32[64,2048]{1,0:T(8,128)S(1)}, bf16[64,2048]{1,0:T(8,128)(2,1)S(1)}) custom-call(s32[1]{0:T(128)} %bitcast.5.role_ref, bf16[64,2048]{1,0:T(8,128)(2,1)S(1)} %constant_dynamic-update-slice_fusion.mine_ref, bf16[64,2048]{1,0:T(8,128)(2,1)S(1)} %collective-permute-done.5.sibling_ref, f32[2,2048]{1,0:T(2,128)S(1)} %bitcast.25, ...), custom_call_target="tpu_custom_call" | custom-call | flops 805306368 | bytes 12582912 | tf_op jit(solution)/shard_map/pallas_call | solution.py:32
  33.7 1.2 %collective-permute-done.6 = bf16[64,2048]{1,0:T(8,128)(2,1)S(1)} collective-permute-done((bf16[64,2048]{1,0:T(8,128)(2,1)S(1)}, bf16[64,2048]{1,0:T(8,128)(2,1)S(1)}, u32[]{:S(2)}, u32[]{:S(2)}) %collective-permute-start.6) | collective-permute-done | bytes 262176 | tf_op jit(solution)/shard_map/ppermute | solution.py:62
  35.9 2.6 %collective-permute-start.9 = (bf16[16,2048]{1,0:T(8,128)(2,1)S(1)}, bf16[16,2048]{1,0:T(8,128)(2,1)S(1)}, u32[]{:S(2)}, u32[]{:S(2)}) collective-permute-start(bf16[16,2048]{1,0:T(8,128)(2,1)S(1)} %get-tuple-element.20), channel_id=1, source_target_pairs={{0,6},{1,7},{2,4},{3,5},{4,2},{5,3},{6,0},{7,1},{8,14},{9,15},{10,... | collective-permute-start | bytes 196616 | tf_op jit(solution)/shard_map/ppermute | solution.py:66
  38.5 0.9 %collective-permute-done.7 = bf16[16,2048]{1,0:T(8,128)(2,1)S(1)} collective-permute-done((bf16[16,2048]{1,0:T(8,128)(2,1)S(1)}, bf16[16,2048]{1,0:T(8,128)(2,1)S(1)}, u32[]{:S(2)}, u32[]{:S(2)}) %collective-permute-start.7) | collective-permute-done | bytes 65568 | tf_op jit(solution)/shard_map/ppermute | solution.py:66
  39.4 1.8 %collective-permute-done.8 = bf16[16,2048]{1,0:T(8,128)(2,1)S(1)} collective-permute-done((bf16[16,2048]{1,0:T(8,128)(2,1)S(1)}, bf16[16,2048]{1,0:T(8,128)(2,1)S(1)}, u32[]{:S(2)}, u32[]{:S(2)}) %collective-permute-start.8) | collective-permute-done | bytes 65568 | tf_op jit(solution)/shard_map/ppermute | solution.py:66
  41.3 6.2 %collective-permute-start.10 = (bf16[16,2048]{1,0:T(8,128)(2,1)S(1)}, bf16[16,2048]{1,0:T(8,128)(2,1)S(1)}, u32[]{:S(2)}, u32[]{:S(2)}) collective-permute-start(bf16[16,2048]{1,0:T(8,128)(2,1)S(1)} %fusion.8), channel_id=1, source_target_pairs={{0,8},{1,1},{2,10},{3,3},{4,12},{5,5},{6,14},{7,7},{8,0},{9,17},{1... | collective-permute-start | bytes 196616 | tf_op jit(solution)/shard_map/ppermute | solution.py:75
  47.5 2.2 %collective-permute-done.10 = bf16[16,2048]{1,0:T(8,128)(2,1)S(1)} collective-permute-done((bf16[16,2048]{1,0:T(8,128)(2,1)S(1)}, bf16[16,2048]{1,0:T(8,128)(2,1)S(1)}, u32[]{:S(2)}, u32[]{:S(2)}) %collective-permute-start.10) | collective-permute-done | bytes 65568 | tf_op jit(solution)/shard_map/ppermute | solution.py:75
  49.8 1.5 %collective-permute-start.11 = (bf16[16,2048]{1,0:T(8,128)(2,1)S(1)}, bf16[16,2048]{1,0:T(8,128)(2,1)S(1)}, u32[]{:S(2)}, u32[]{:S(2)}) collective-permute-start(bf16[16,2048]{1,0:T(8,128)(2,1)S(1)} %collective-permute-done.10), channel_id=1, source_target_pairs={{0,2},{1,3},{2,0},{3,1},{4,6},{5,7},{6,4},{7,5},{8,10},{9,11},{10,... | collective-permute-start | bytes 196616 | tf_op jit(solution)/shard_map/ppermute | solution.py:66
  51.3 1.5 %collective-permute-start.12 = (bf16[16,2048]{1,0:T(8,128)(2,1)S(1)}, bf16[16,2048]{1,0:T(8,128)(2,1)S(1)}, u32[]{:S(2)}, u32[]{:S(2)}) collective-permute-start(bf16[16,2048]{1,0:T(8,128)(2,1)S(1)} %collective-permute-done.10), channel_id=1, source_target_pairs={{0,4},{1,5},{2,6},{3,7},{4,0},{5,1},{6,2},{7,3},{8,12},{9,13},{10,... | collective-permute-start | bytes 196616 | tf_op jit(solution)/shard_map/ppermute | solution.py:66
  54.0 1.5 %collective-permute-done.12 = bf16[16,2048]{1,0:T(8,128)(2,1)S(1)} collective-permute-done((bf16[16,2048]{1,0:T(8,128)(2,1)S(1)}, bf16[16,2048]{1,0:T(8,128)(2,1)S(1)}, u32[]{:S(2)}, u32[]{:S(2)}) %collective-permute-start.12) | collective-permute-done | bytes 65568 | tf_op jit(solution)/shard_map/ppermute | solution.py:66
  55.5 2.4 %collective-permute-done.13 = bf16[16,2048]{1,0:T(8,128)(2,1)S(1)} collective-permute-done((bf16[16,2048]{1,0:T(8,128)(2,1)S(1)}, bf16[16,2048]{1,0:T(8,128)(2,1)S(1)}, u32[]{:S(2)}, u32[]{:S(2)}) %collective-permute-start.13) | collective-permute-done | bytes 65568 | tf_op jit(solution)/shard_map/ppermute | solution.py:66
  58.0 1.5 %collective-permute-done.14.sibling_ref = bf16[64,2048]{1,0:T(8,128)(2,1)S(1)} collective-permute-done((bf16[64,2048]{1,0:T(8,128)(2,1)S(1)}, bf16[64,2048]{1,0:T(8,128)(2,1)S(1)}, u32[]{:S(2)}, u32[]{:S(2)}) %collective-permute-start.14) | collective-permute-done | bytes 262176 | tf_op jit(solution)/shard_map/ppermute | solution.py:62
  59.5 2.2 %copy-done.1 = bf16[1,2,2048,512]{3,2,1,0:T(8,128)(2,1)S(1)} copy-done((bf16[1,2,2048,512]{3,2,1,0:T(8,128)(2,1)S(1)}, bf16[1,2,2048,512]{3,2,1,0:T(8,128)(2,1)}, u32[]{:S(2)}) %copy-start.1) | copy-done | bytes 4194328
  61.7 2.2 %copy-done.3 = bf16[1,2,2048,512]{3,2,1,0:T(8,128)(2,1)S(1)} copy-done((bf16[1,2,2048,512]{3,2,1,0:T(8,128)(2,1)S(1)}, bf16[1,2,2048,512]{3,2,1,0:T(8,128)(2,1)}, u32[]{:S(2)}) %copy-start.3) | copy-done | bytes 4194328
  63.9 2.2 %copy-done.5 = bf16[1,2,512,2048]{3,2,1,0:T(8,128)(2,1)S(1)} copy-done((bf16[1,2,512,2048]{3,2,1,0:T(8,128)(2,1)S(1)}, bf16[1,2,512,2048]{3,2,1,0:T(8,128)(2,1)}, u32[]{:S(2)}) %copy-start.5) | copy-done | bytes 4194328
  66.1 2.6 %shard_map.96 = (f32[64,2048]{1,0:T(8,128)S(1)}, bf16[64,2048]{1,0:T(8,128)(2,1)S(1)}) custom-call(s32[1]{0:T(128)} %bitcast.10.role_ref, bf16[64,2048]{1,0:T(8,128)(2,1)S(1)} %constant_dynamic-update-slice_fusion.4.mine_ref, bf16[64,2048]{1,0:T(8,128)(2,1)S(1)} %collective-permute-done.14.sibling_ref, f32[2,2048]{1,0:T(2,128)S(1)} %bitcast.26, ...), custom_call_target="tpu_custom_call" | custom-call | flops 805306368 | bytes 12582912 | tf_op jit(solution)/shard_map/pallas_call | solution.py:32
  68.8 1.4 %collective-permute-done.15 = bf16[64,2048]{1,0:T(8,128)(2,1)S(1)} collective-permute-done((bf16[64,2048]{1,0:T(8,128)(2,1)S(1)}, bf16[64,2048]{1,0:T(8,128)(2,1)S(1)}, u32[]{:S(2)}, u32[]{:S(2)}) %collective-permute-start.15) | collective-permute-done | bytes 262176 | tf_op jit(solution)/shard_map/ppermute | solution.py:62
  71.4 2.4 %collective-permute-start.18 = (bf16[16,2048]{1,0:T(8,128)(2,1)S(1)}, bf16[16,2048]{1,0:T(8,128)(2,1)S(1)}, u32[]{:S(2)}, u32[]{:S(2)}) collective-permute-start(bf16[16,2048]{1,0:T(8,128)(2,1)S(1)} %get-tuple-element.17), channel_id=1, source_target_pairs={{0,6},{1,7},{2,4},{3,5},{4,2},{5,3},{6,0},{7,1},{8,14},{9,15},{10,... | collective-permute-start | bytes 196616 | tf_op jit(solution)/shard_map/ppermute | solution.py:66
  73.9 0.9 %collective-permute-done.16 = bf16[16,2048]{1,0:T(8,128)(2,1)S(1)} collective-permute-done((bf16[16,2048]{1,0:T(8,128)(2,1)S(1)}, bf16[16,2048]{1,0:T(8,128)(2,1)S(1)}, u32[]{:S(2)}, u32[]{:S(2)}) %collective-permute-start.16) | collective-permute-done | bytes 65568 | tf_op jit(solution)/shard_map/ppermute | solution.py:66
  74.8 1.1 %collective-permute-done.17 = bf16[16,2048]{1,0:T(8,128)(2,1)S(1)} collective-permute-done((bf16[16,2048]{1,0:T(8,128)(2,1)S(1)}, bf16[16,2048]{1,0:T(8,128)(2,1)S(1)}, u32[]{:S(2)}, u32[]{:S(2)}) %collective-permute-start.17) | collective-permute-done | bytes 65568 | tf_op jit(solution)/shard_map/ppermute | solution.py:66
  76.7 1.2 %collective-permute-done.19 = bf16[8,2048]{1,0:T(8,128)(2,1)S(1)} collective-permute-done((bf16[8,2048]{1,0:T(8,128)(2,1)S(1)}, bf16[8,2048]{1,0:T(8,128)(2,1)S(1)}, u32[]{:S(2)}, u32[]{:S(2)}) %collective-permute-start.19) | collective-permute-done | bytes 32800 | tf_op jit(solution)/shard_map/ppermute | solution.py:62
  (47 shorter events, 9.1 us)
Async XLA Ops:
  6.7 1.4 %collective-permute-start = (bf16[16,2048]{1,0:T(8,128)(2,1)S(1)}, bf16[16,2048]{1,0:T(8,128)(2,1)S(1)}, u32[]{:S(2)}, u32[]{:S(2)}) collective-permute-start(bf16[16,2048]{1,0:T(8,128)(2,1)S(1)} %pad_maximum_fusion), channel_id=1, source_target_pairs={{0,1},{1,0},{2,3},{3,2},{4,5},{5,4},{6,7},{7,6},{8,9},{9,8},{10,11... | collective-permute-start | bytes 196616 | tf_op jit(solution)/shard_map/ppermute | solution.py:62
  8.1 0.7 collective-permute-start.1
  8.8 5.2 %collective-permute-start.2 = (bf16[16,2048]{1,0:T(8,128)(2,1)S(1)}, bf16[16,2048]{1,0:T(8,128)(2,1)S(1)}, u32[]{:S(2)}, u32[]{:S(2)}) collective-permute-start(bf16[16,2048]{1,0:T(8,128)(2,1)S(1)} %collective-permute-done.1), channel_id=1, source_target_pairs={{0,2},{1,3},{2,0},{3,1},{4,6},{5,7},{6,4},{7,5},{8,10},{9,11},{10,... | collective-permute-start | bytes 196616 | tf_op jit(solution)/shard_map/ppermute | solution.py:66
  11.8 4.3 %collective-permute-start.3 = (bf16[16,2048]{1,0:T(8,128)(2,1)S(1)}, bf16[16,2048]{1,0:T(8,128)(2,1)S(1)}, u32[]{:S(2)}, u32[]{:S(2)}) collective-permute-start(bf16[16,2048]{1,0:T(8,128)(2,1)S(1)} %collective-permute-done.1), channel_id=1, source_target_pairs={{0,4},{1,5},{2,6},{3,7},{4,0},{5,1},{6,2},{7,3},{8,12},{9,13},{10,... | collective-permute-start | bytes 196616 | tf_op jit(solution)/shard_map/ppermute | solution.py:66
  13.3 5.2 %collective-permute-start.4 = (bf16[16,2048]{1,0:T(8,128)(2,1)S(1)}, bf16[16,2048]{1,0:T(8,128)(2,1)S(1)}, u32[]{:S(2)}, u32[]{:S(2)}) collective-permute-start(bf16[16,2048]{1,0:T(8,128)(2,1)S(1)} %collective-permute-done.1), channel_id=1, source_target_pairs={{0,6},{1,7},{2,4},{3,5},{4,2},{5,3},{6,0},{7,1},{8,14},{9,15},{10,... | collective-permute-start | bytes 196616 | tf_op jit(solution)/shard_map/ppermute | solution.py:66
  18.4 4.9 %collective-permute-start.5 = (bf16[64,2048]{1,0:T(8,128)(2,1)S(1)}, bf16[64,2048]{1,0:T(8,128)(2,1)S(1)}, u32[]{:S(2)}, u32[]{:S(2)}) collective-permute-start(bf16[64,2048]{1,0:T(8,128)(2,1)S(1)} %constant_dynamic-update-slice_fusion.mine_ref), channel_id=1, source_target_pairs={{0,1},{1,0},{2,3},{3,2},{4,5},{5,4},{6,7},{7,6},{8,9},{9,8},{10,11... | collective-permute-start | bytes 786440 | tf_op jit(solution)/shard_map/ppermute | solution.py:62
  23.4 2.2 %copy-start = (bf16[1,2,2048,512]{3,2,1,0:T(8,128)(2,1)S(1)}, bf16[1,2,2048,512]{3,2,1,0:T(8,128)(2,1)}, u32[]{:S(2)}) copy-start(bf16[1,2,2048,512]{3,2,1,0:T(8,128)(2,1)} %param.13) | copy-start | bytes 12582916
  25.6 2.2 %copy-start.2 = (bf16[1,2,2048,512]{3,2,1,0:T(8,128)(2,1)S(1)}, bf16[1,2,2048,512]{3,2,1,0:T(8,128)(2,1)}, u32[]{:S(2)}) copy-start(bf16[1,2,2048,512]{3,2,1,0:T(8,128)(2,1)} %param.14) | copy-start | bytes 12582916
  27.7 2.2 %copy-start.4 = (bf16[1,2,512,2048]{3,2,1,0:T(8,128)(2,1)S(1)}, bf16[1,2,512,2048]{3,2,1,0:T(8,128)(2,1)}, u32[]{:S(2)}) copy-start(bf16[1,2,512,2048]{3,2,1,0:T(8,128)(2,1)} %param.15) | copy-start | bytes 12582916
  29.9 0.7 copy-start.6
  30.6 28.8 %copy-start.7 = (f32[1,2,2048]{2,1,0:T(2,128)S(1)}, f32[1,2,2048]{2,1,0:T(2,128)}, u32[]{:S(2)}) copy-start(f32[1,2,2048]{2,1,0:T(2,128)} %param.12) | copy-start | bytes 49156
  33.2 1.6 %collective-permute-start.6 = (bf16[64,2048]{1,0:T(8,128)(2,1)S(1)}, bf16[64,2048]{1,0:T(8,128)(2,1)S(1)}, u32[]{:S(2)}, u32[]{:S(2)}) collective-permute-start(bf16[64,2048]{1,0:T(8,128)(2,1)S(1)} %get-tuple-element.7), channel_id=1, source_target_pairs={{0,1},{1,0},{2,3},{3,2},{4,5},{5,4},{6,7},{7,6},{8,9},{9,8},{10,11... | collective-permute-start | bytes 786440 | tf_op jit(solution)/shard_map/ppermute | solution.py:62
  34.9 4.4 %collective-permute-start.7 = (bf16[16,2048]{1,0:T(8,128)(2,1)S(1)}, bf16[16,2048]{1,0:T(8,128)(2,1)S(1)}, u32[]{:S(2)}, u32[]{:S(2)}) collective-permute-start(bf16[16,2048]{1,0:T(8,128)(2,1)S(1)} %get-tuple-element.19), channel_id=1, source_target_pairs={{0,2},{1,3},{2,0},{3,1},{4,6},{5,7},{6,4},{7,5},{8,10},{9,11},{10,... | collective-permute-start | bytes 196616 | tf_op jit(solution)/shard_map/ppermute | solution.py:66
  35.5 5.7 %collective-permute-start.8 = (bf16[16,2048]{1,0:T(8,128)(2,1)S(1)}, bf16[16,2048]{1,0:T(8,128)(2,1)S(1)}, u32[]{:S(2)}, u32[]{:S(2)}) collective-permute-start(bf16[16,2048]{1,0:T(8,128)(2,1)S(1)} %get-tuple-element.21), channel_id=1, source_target_pairs={{0,4},{1,5},{2,6},{3,7},{4,0},{5,1},{6,2},{7,3},{8,12},{9,13},{10,... | collective-permute-start | bytes 196616 | tf_op jit(solution)/shard_map/ppermute | solution.py:66
  35.9 5.3 %collective-permute-start.9 = (bf16[16,2048]{1,0:T(8,128)(2,1)S(1)}, bf16[16,2048]{1,0:T(8,128)(2,1)S(1)}, u32[]{:S(2)}, u32[]{:S(2)}) collective-permute-start(bf16[16,2048]{1,0:T(8,128)(2,1)S(1)} %get-tuple-element.20), channel_id=1, source_target_pairs={{0,6},{1,7},{2,4},{3,5},{4,2},{5,3},{6,0},{7,1},{8,14},{9,15},{10,... | collective-permute-start | bytes 196616 | tf_op jit(solution)/shard_map/ppermute | solution.py:66
  41.3 8.5 %collective-permute-start.10 = (bf16[16,2048]{1,0:T(8,128)(2,1)S(1)}, bf16[16,2048]{1,0:T(8,128)(2,1)S(1)}, u32[]{:S(2)}, u32[]{:S(2)}) collective-permute-start(bf16[16,2048]{1,0:T(8,128)(2,1)S(1)} %fusion.8), channel_id=1, source_target_pairs={{0,8},{1,1},{2,10},{3,3},{4,12},{5,5},{6,14},{7,7},{8,0},{9,17},{1... | collective-permute-start | bytes 196616 | tf_op jit(solution)/shard_map/ppermute | solution.py:75
  49.8 4.3 %collective-permute-start.11 = (bf16[16,2048]{1,0:T(8,128)(2,1)S(1)}, bf16[16,2048]{1,0:T(8,128)(2,1)S(1)}, u32[]{:S(2)}, u32[]{:S(2)}) collective-permute-start(bf16[16,2048]{1,0:T(8,128)(2,1)S(1)} %collective-permute-done.10), channel_id=1, source_target_pairs={{0,2},{1,3},{2,0},{3,1},{4,6},{5,7},{6,4},{7,5},{8,10},{9,11},{10,... | collective-permute-start | bytes 196616 | tf_op jit(solution)/shard_map/ppermute | solution.py:66
  51.3 4.3 %collective-permute-start.12 = (bf16[16,2048]{1,0:T(8,128)(2,1)S(1)}, bf16[16,2048]{1,0:T(8,128)(2,1)S(1)}, u32[]{:S(2)}, u32[]{:S(2)}) collective-permute-start(bf16[16,2048]{1,0:T(8,128)(2,1)S(1)} %collective-permute-done.10), channel_id=1, source_target_pairs={{0,4},{1,5},{2,6},{3,7},{4,0},{5,1},{6,2},{7,3},{8,12},{9,13},{10,... | collective-permute-start | bytes 196616 | tf_op jit(solution)/shard_map/ppermute | solution.py:66
  52.8 5.2 %collective-permute-start.13 = (bf16[16,2048]{1,0:T(8,128)(2,1)S(1)}, bf16[16,2048]{1,0:T(8,128)(2,1)S(1)}, u32[]{:S(2)}, u32[]{:S(2)}) collective-permute-start(bf16[16,2048]{1,0:T(8,128)(2,1)S(1)} %collective-permute-done.10), channel_id=1, source_target_pairs={{0,6},{1,7},{2,4},{3,5},{4,2},{5,3},{6,0},{7,1},{8,14},{9,15},{10,... | collective-permute-start | bytes 196616 | tf_op jit(solution)/shard_map/ppermute | solution.py:66
  57.9 1.5 %collective-permute-start.14 = (bf16[64,2048]{1,0:T(8,128)(2,1)S(1)}, bf16[64,2048]{1,0:T(8,128)(2,1)S(1)}, u32[]{:S(2)}, u32[]{:S(2)}) collective-permute-start(bf16[64,2048]{1,0:T(8,128)(2,1)S(1)} %constant_dynamic-update-slice_fusion.4.mine_ref), channel_id=1, source_target_pairs={{0,1},{1,0},{2,3},{3,2},{4,5},{5,4},{6,7},{7,6},{8,9},{9,8},{10,11... | collective-permute-start | bytes 786440 | tf_op jit(solution)/shard_map/ppermute | solution.py:62
  59.5 2.2 %copy-start.1 = (bf16[1,2,2048,512]{3,2,1,0:T(8,128)(2,1)S(1)}, bf16[1,2,2048,512]{3,2,1,0:T(8,128)(2,1)}, u32[]{:S(2)}) copy-start(bf16[1,2,2048,512]{3,2,1,0:T(8,128)(2,1)} %param.13) | copy-start | bytes 12582916
  61.7 2.2 %copy-start.3 = (bf16[1,2,2048,512]{3,2,1,0:T(8,128)(2,1)S(1)}, bf16[1,2,2048,512]{3,2,1,0:T(8,128)(2,1)}, u32[]{:S(2)}) copy-start(bf16[1,2,2048,512]{3,2,1,0:T(8,128)(2,1)} %param.14) | copy-start | bytes 12582916
  63.9 2.2 %copy-start.5 = (bf16[1,2,512,2048]{3,2,1,0:T(8,128)(2,1)S(1)}, bf16[1,2,512,2048]{3,2,1,0:T(8,128)(2,1)}, u32[]{:S(2)}) copy-start(bf16[1,2,512,2048]{3,2,1,0:T(8,128)(2,1)} %param.15) | copy-start | bytes 12582916
  68.6 1.6 %collective-permute-start.15 = (bf16[64,2048]{1,0:T(8,128)(2,1)S(1)}, bf16[64,2048]{1,0:T(8,128)(2,1)S(1)}, u32[]{:S(2)}, u32[]{:S(2)}) collective-permute-start(bf16[64,2048]{1,0:T(8,128)(2,1)S(1)} %get-tuple-element.9), channel_id=1, source_target_pairs={{0,1},{1,0},{2,3},{3,2},{4,5},{5,4},{6,7},{7,6},{8,9},{9,8},{10,11... | collective-permute-start | bytes 786440 | tf_op jit(solution)/shard_map/ppermute | solution.py:62
  70.3 4.5 %collective-permute-start.16 = (bf16[16,2048]{1,0:T(8,128)(2,1)S(1)}, bf16[16,2048]{1,0:T(8,128)(2,1)S(1)}, u32[]{:S(2)}, u32[]{:S(2)}) collective-permute-start(bf16[16,2048]{1,0:T(8,128)(2,1)S(1)} %get-tuple-element.16), channel_id=1, source_target_pairs={{0,2},{1,3},{2,0},{3,1},{4,6},{5,7},{6,4},{7,5},{8,10},{9,11},{10,... | collective-permute-start | bytes 196616 | tf_op jit(solution)/shard_map/ppermute | solution.py:66
  70.9 5.0 %collective-permute-start.17 = (bf16[16,2048]{1,0:T(8,128)(2,1)S(1)}, bf16[16,2048]{1,0:T(8,128)(2,1)S(1)}, u32[]{:S(2)}, u32[]{:S(2)}) collective-permute-start(bf16[16,2048]{1,0:T(8,128)(2,1)S(1)} %get-tuple-element.18), channel_id=1, source_target_pairs={{0,4},{1,5},{2,6},{3,7},{4,0},{5,1},{6,2},{7,3},{8,12},{9,13},{10,... | collective-permute-start | bytes 196616 | tf_op jit(solution)/shard_map/ppermute | solution.py:66
  71.4 5.2 %collective-permute-start.18 = (bf16[16,2048]{1,0:T(8,128)(2,1)S(1)}, bf16[16,2048]{1,0:T(8,128)(2,1)S(1)}, u32[]{:S(2)}, u32[]{:S(2)}) collective-permute-start(bf16[16,2048]{1,0:T(8,128)(2,1)S(1)} %get-tuple-element.17), channel_id=1, source_target_pairs={{0,6},{1,7},{2,4},{3,5},{4,2},{5,3},{6,0},{7,1},{8,14},{9,15},{10,... | collective-permute-start | bytes 196616 | tf_op jit(solution)/shard_map/ppermute | solution.py:66
  76.6 1.3 %collective-permute-start.19 = (bf16[8,2048]{1,0:T(8,128)(2,1)S(1)}, bf16[8,2048]{1,0:T(8,128)(2,1)S(1)}, u32[]{:S(2)}, u32[]{:S(2)}) collective-permute-start(bf16[8,2048]{1,0:T(8,128)(2,1)S(1)} %broadcast_select_fusion.1), channel_id=1, source_target_pairs={{0,1},{1,0},{2,3},{3,2},{4,5},{5,4},{6,7},{7,6},{8,9},{9,8},{10,11... | collective-permute-start | bytes 98312 | tf_op jit(solution)/shard_map/ppermute | solution.py:62

commit v2 on v1

v2 whole, which is shorter than its diff:
```python
import functools

import jax
import jax.numpy as jnp
from jax import lax
from jax.experimental import pallas as pl
from jax.experimental.pallas import tpu as pltpu
from jax.sharding import PartitionSpec as P

CORES = 2
EPS = 1e-05
LIMIT = 8 * 2**20
HOLD = (48 * 2**20, 44 * 2**20)
FLOPS = 2 * 10**10


def normalize(x, gain):
    xf = x.astype(jnp.float32)
    return (xf * lax.rsqrt(jnp.mean(xf * xf, axis=-1, keepdims=True) + EPS) * gain).astype(jnp.bfloat16)


def role_at(tick):
    return (lax.axis_index("pipe") + lax.axis_index("zero") % CORES + tick) % 2


def first_kernel(order_ref, down_hbm, up_hbm, feeds_hbm, own_out, given_out, down, up, feeds, sems):
    copies = [
        pltpu.make_async_copy(source, target, sems.at[n])
        for n, (source, target) in enumerate(((down_hbm, down), (up_hbm, up), (feeds_hbm, feeds)))
    ]
    for copy in copies:
        copy.start()
    for copy in copies:
        copy.wait()
    ticks = feeds.shape[0]

    def feed(tick):
        chosen = feeds[0].astype(jnp.float32)
        for n in range(1, ticks):
            chosen = jnp.where(order_ref[tick] == n, feeds[n].astype(jnp.float32), chosen)
        return chosen

    descended = down[0].astype(jnp.float32)
    ascended = jnp.where(lax.axis_index("pipe") == 0, feed(0), up[0].astype(jnp.float32))
    was_down = role_at(1) == 0
    own = jnp.where(was_down, descended, ascended)
    given = jnp.where(was_down, ascended, descended)
    later = [feed(tick) for tick in range(1, ticks)]
    own_out[...] = jnp.concatenate([own] + later, axis=0).astype(own_out.dtype)
    given_out[...] = jnp.concatenate([given] + later, axis=0).astype(given_out.dtype)


def first_rows(order, down_out, up_out, feeds):
    vmem, hbm = pl.BlockSpec(memory_space=pltpu.VMEM), pl.BlockSpec(memory_space=pltpu.HBM)
    ticks, rows, width = feeds.shape
    shape = jax.ShapeDtypeStruct((ticks * rows, width), feeds.dtype)
    return pl.pallas_call(
        first_kernel,
        out_shape=(shape, shape),
        in_specs=[pl.BlockSpec(memory_space=pltpu.SMEM), hbm, hbm, hbm],
        out_specs=(vmem, vmem),
        scratch_shapes=[pltpu.VMEM(a.shape, a.dtype) for a in (down_out, up_out, feeds)]
        + [pltpu.SemaphoreType.DMA((3,))],
        compiler_params=pltpu.CompilerParams(vmem_limit_bytes=4 * 2**20),
        cost_estimate=pl.CostEstimate(flops=FLOPS, bytes_accessed=8 * shape.size, transcendentals=0),
    )(order, down_out, up_out, feeds)


def group_kernel(tick, other, x_ref, gains_ref, gate_ref, up_ref, down_ref, out):
    group = (role_at(tick) + other) % 2
    normed = normalize(x_ref[...], gains_ref[pl.ds(group, 1), :])
    gate = jnp.dot(normed, gate_ref[group], preferred_element_type=jnp.float32)
    up = jnp.dot(normed, up_ref[group], preferred_element_type=jnp.float32)
    hidden = (gate / (1.0 + jnp.exp(-gate)) * up).astype(jnp.bfloat16)
    out[...] = jnp.dot(hidden, down_ref[group], preferred_element_type=jnp.float32).astype(out.dtype)


def held_kernel(count, x_ref, *refs):
    sources, x_out, outs, sems = refs[-2 * count - 2 : -count - 2], refs[-count - 2], refs[-count - 1 : -1], refs[-1]
    copies = [
        pltpu.make_async_copy(source.at[group], out.at[group], sems.at[n, group])
        for n, (source, out) in enumerate(zip(sources, outs))
        for group in range(source.shape[0])
    ]
    for copy in copies:
        copy.start()
    x_out[...] = x_ref[...]
    for copy in copies:
        copy.wait()


def held(x, weights, after=()):
    vmem = pl.BlockSpec(memory_space=pltpu.VMEM)
    results = (x,) + tuple(weights)
    return pl.pallas_call(
        functools.partial(held_kernel, len(weights)),
        out_shape=tuple(jax.ShapeDtypeStruct(a.shape, a.dtype) for a in results),
        in_specs=[vmem] * (1 + len(after)) + [pl.BlockSpec(memory_space=pl.ANY)] * len(weights),
        out_specs=(vmem,) * len(results),
        scratch_shapes=[pltpu.SemaphoreType.DMA((len(weights), weights[0].shape[0]))],
        compiler_params=pltpu.CompilerParams(vmem_limit_bytes=HOLD[len(weights) - 1]),
        cost_estimate=pl.CostEstimate(flops=FLOPS // 8, bytes_accessed=0, transcendentals=0),
    )(x, *after, *weights)


def stack_kernel(*refs):
    height = refs[0].shape[0]
    for slot, ref in enumerate(refs[:-1]):
        refs[-1][slot * height : (slot + 1) * height] = ref[...]


def stacked(pieces):
    vmem = pl.BlockSpec(memory_space=pltpu.VMEM)
    rows, width = pieces[0].shape
    return pl.pallas_call(
        stack_kernel,
        out_shape=jax.ShapeDtypeStruct((len(pieces) * rows, width), pieces[0].dtype),
        in_specs=[vmem] * len(pieces),
        out_specs=vmem,
        compiler_params=pltpu.CompilerParams(vmem_limit_bytes=LIMIT),
    )(*pieces)


def partial(tick, other, x, gains, weights):
    vmem = pl.BlockSpec(memory_space=pltpu.VMEM)
    size = sum(w.size // w.shape[0] for w in weights)
    return pl.pallas_call(
        functools.partial(group_kernel, tick, other),
        out_shape=jax.ShapeDtypeStruct(x.shape, jnp.bfloat16 if other else jnp.float32),
        in_specs=[vmem] * (2 + len(weights)),
        out_specs=vmem,
        compiler_params=pltpu.CompilerParams(vmem_limit_bytes=LIMIT),
        cost_estimate=pl.CostEstimate(flops=2 * x.shape[0] * size, bytes_accessed=2 * size, transcendentals=0),
    )(x, gains, *weights)


def chip_pairs(chips, step):
    if chips & (chips - 1) == 0:
        return [(chip, chip ^ step) for chip in range(chips)]
    return [(chip, (chip + step) % chips) for chip in range(chips)]


def on_device(down_out, up_out, feeds, order, gains, gate_w, up_w, down_w):
    sections, zero = lax.axis_size("pipe"), lax.axis_size("zero")
    chips = zero // CORES
    section, place = lax.axis_index("pipe"), lax.axis_index("zero")
    core = place % CORES
    ticks = feeds.shape[0]
    both = ("pipe", "zero")

    def to_sibling(value):
        return lax.ppermute(value, "zero", [(k, k ^ 1) for k in range(zero)])

    def to_chip(value, step):
        pairs = [(a * CORES + r, b * CORES + r) for a, b in chip_pairs(chips, step) for r in range(CORES)]
        return lax.ppermute(value, "zero", pairs)

    def to_section(value, tick):
        pairs = []
        for s in range(sections):
            for k in range(zero):
                other = s - 1 if (s + k % CORES + tick) % 2 == 0 else s + 1
                other = other if 0 <= other < sections else s
                pairs.append((s * zero + k, other * zero + k))
        return lax.ppermute(value, both, pairs)

    def joined(own, other):
        first = jnp.where(core == 0, own, other)
        second = jnp.where(core == 0, other, own)
        return jnp.concatenate([first, second], axis=0)

    own, given = first_rows(order, down_out, up_out, feeds)
    rows = down_out.shape[1]
    taken = to_sibling(given)
    state, *entering = [
        joined(own[n * rows : (n + 1) * rows], taken[n * rows : (n + 1) * rows]) for n in range(ticks)
    ]

    for tick in range(ticks):
        if tick > 0:
            state = jnp.where((section == 0) & (role_at(tick) == 0), entering[tick - 1], state)
        mark, gate = held(state, [gate_w[0]])
        x = to_section(state, tick)
        own, up, down = held(x, [up_w[0], down_w[0]], [mark])
        weights = (gate, up, down)
        pieces = [own] + [to_chip(x, step) for step in range(1, chips)]
        mine = stacked(pieces)
        sibling = to_sibling(mine)
        part = partial(tick, 0, mine, gains[0], weights)
        given = partial(tick, 1, sibling, gains[0], weights)
        part = part + to_sibling(given).astype(jnp.float32)
        height = x.shape[0]
        total = x.astype(jnp.float32) + part[:height]
        for step in range(1, chips):
            slot = step if chips & (chips - 1) == 0 else chips - step
            piece = part[slot * height : (slot + 1) * height].astype(jnp.bfloat16)
            total = total + to_chip(piece, step).astype(jnp.float32)
        state = total.astype(jnp.bfloat16)

    role = role_at(ticks - 1)
    kept = jnp.where(core == 0, state[:rows], state[rows:])
    received = to_sibling(jnp.where(core == 0, state[rows:], state[:rows]))
    down_state = jnp.where(role == 0, kept, received)
    up_state = jnp.where(role == 0, received, kept)
    return (down_state[None], up_state[None])


def solution(mesh):
    return jax.shard_map(
        on_device,
        mesh=mesh,
        in_specs=(
            P("pipe", "zero", None),
            P("pipe", "zero", None),
            P(None, "zero", None),
            P(),
            P("pipe", None, None),
            P("pipe", None, None, "zero"),
            P("pipe", None, None, "zero"),
            P("pipe", None, "zero", None),
        ),
        out_specs=(P("pipe", "zero", None), P("pipe", "zero", None)),
        check_vma=False,
    )
```

time: 79.2 us -> 60.7 us (0.77)
  Pallas kernels: 5.14 us -> 17.7 us
  local copies, waits for them, and re-layouts: 15.2 us -> 3.04 us
  waiting for transfers between devices: 24.8 us -> 14.1 us
  between operations: 4.7 us -> 0.88 us
  starting transfers between devices: 27 us -> 23.7 us
  other arithmetic: 1.7 us -> 0.9 us
    pallas_call x2 -> x11, Pallas kernels: 5.14 us -> 17.7 us  [the longest x4 11.5 us: held(): pl.pallas_call(functools.partial(held_kernel, len(weights)), out_shape=tu...]
    unnamed x22 -> x10, local copies, waits for them, and re-layouts: 13.9 us -> 3.01 us
    ppermute x12, waiting for transfers between devices: 15.2 us -> 9.29 us  [to_chip(): return lax.ppermute(value, 'zero', pairs)]
    ppermute x6, waiting for transfers between devices: 7.35 us -> 4.82 us  [to_sibling(): return lax.ppermute(value, 'zero', [(k, k ^ 1) for k in range(zero)])]
    ppermute x6, starting transfers between devices: 4.98 us -> 2.62 us  [to_sibling(): return lax.ppermute(value, 'zero', [(k, k ^ 1) for k in range(zero)])]
    ppermute x2, waiting for transfers between devices: 2.23 us -> 0.01 us  [to_section(): return lax.ppermute(value, both, pairs)]
    slice x3 -> x2, local copies, waits for them, and re-layouts: 1.34 us -> 0.03 us  [on_device(): piece = part[slot * height:(slot + 1) * height].astype(jnp.bfloat16)]
    ppermute x2, starting transfers between devices: 6.91 us -> 5.89 us  [to_section(): return lax.ppermute(value, both, pairs)]
  transfers between devices with their start and end apart: 20 -> 20, of which waited for: 18 -> 12; matrix products, arithmetic and copies ran while one was open for 0% -> 0% of each run, Pallas kernels for 0% -> 24%
where the time goes in v2:
time: 60.7 us; the launch traced here: 60.3 us
  starting transfers between devices  23.7 us (39%)
  Pallas kernels  17.7 us (29%)
  waiting for transfers between devices  14.1 us (23%)
  local copies, waits for them, and re-layouts  3.04 us (5%)
  other arithmetic  0.9 us (1%)
  between operations  0.88 us (1%)
    ppermute x12, starting transfers between devices, to_chip(): return lax.ppermute(value, 'zero', pairs)  15.2 us
    pallas_call x4, Pallas kernels, held(): pl.pallas_call(functools.partial(held_kernel, len(weights)), out_shape=tu...  11.5 us
    ppermute x12, waiting for transfers between devices, to_chip(): return lax.ppermute(value, 'zero', pairs)  9.29 us
    ppermute x2, starting transfers between devices, to_section(): return lax.ppermute(value, both, pairs)  5.89 us
    pallas_call x4, Pallas kernels, partial(): pl.pallas_call(functools.partial(group_kernel, tick, other), out_shape=ja...  5.44 us
    ppermute x6, waiting for transfers between devices, to_sibling(): return lax.ppermute(value, 'zero', [(k, k ^ 1) for k in range(zero)])  4.82 us
    unnamed x10, local copies, waits for them, and re-layouts  3.01 us
    ppermute x6, starting transfers between devices, to_sibling(): return lax.ppermute(value, 'zero', [(k, k ^ 1) for k in range(zero)])  2.62 us
  transfers between devices with their start and end apart: 20, of which 12 were waited for; matrix products, arithmetic and copies ran while one was open for 0% of the time, Pallas kernels for 24%

profile of v2, /device:TPU:0, one launch (start us, length us, event | category | flops | bytes accessed | tf_op | source)
XLA Modules:
  0.0 60.3 jit_solution(402566029947981613)
XLA Ops:
  0.6 0.8 %copy-done.1 = bf16[2,8,2048]{2,1,0:T(8,128)(2,1)S(1)} copy-done((bf16[2,8,2048]{2,1,0:T(8,128)(2,1)S(1)}, bf16[2,8,2048]{2,1,0:T(8,128)(2,1)}, u32[]{:S(2)}) %copy-start.1) | copy-done | bytes 65560
  3.6 0.8 %shard_map.95 = (bf16[16,2048]{1,0:T(8,128)(2,1)S(1)}, bf16[16,2048]{1,0:T(8,128)(2,1)S(1)}) custom-call(s32[2]{0:T(128)S(1)} %copy-done.4, bf16[1,8,2048]{2,1,0:T(8,128)(2,1)S(1)} %copy-done.2, bf16[1,8,2048]{2,1,0:T(8,128)(2,1)S(1)} %copy-done.3, bf16[2,8,2048]{2,1,0:T(8,128)(2,1)S(1)} %copy-done.1), custom_call_target="tpu_custom_call" | custom-call | flops 20000000000 | bytes 262144 | tf_op jit(solution)/shard_map/pallas_call | solution.py:57
  4.9 0.9 %collective-permute-done = bf16[16,2048]{1,0:T(8,128)(2,1)S(1)} collective-permute-done((bf16[16,2048]{1,0:T(8,128)(2,1)S(1)}, bf16[16,2048]{1,0:T(8,128)(2,1)S(1)}, u32[]{:S(2)}, u32[]{:S(2)}) %collective-permute-start) | collective-permute-done | bytes 65568 | tf_op jit(solution)/shard_map/ppermute | solution.py:152
  6.5 2.2 %shard_map.96 = (bf16[16,2048]{1,0:T(8,128)(2,1)S(1)}, bf16[2,2048,512]{2,1,0:T(8,128)(2,1)S(1)}) custom-call(bf16[16,2048]{1,0:T(8,128)(2,1)S(1)} %pad_maximum_fusion.x_ref, bf16[2,2048,512]{2,1,0:T(8,128)(2,1)} %bitcast.12), custom_call_target="tpu_custom_call" | custom-call | flops 2500000000 | tf_op jit(solution)/shard_map/pallas_call | solution.py:95
  8.8 3.9 %collective-permute-start.4 = (bf16[16,2048]{1,0:T(8,128)(2,1)S(1)}, bf16[16,2048]{1,0:T(8,128)(2,1)S(1)}, u32[]{:S(2)}, u32[]{:S(2)}) collective-permute-start(bf16[16,2048]{1,0:T(8,128)(2,1)S(1)} %collective-permute-done.1.x_ref), channel_id=1, source_target_pairs={{0,6},{1,7},{2,4},{3,5},{4,2},{5,3},{6,0},{7,1},{8,14},{9,15},{10,... | collective-permute-start | bytes 196616 | tf_op jit(solution)/shard_map/ppermute | solution.py:156
  13.3 3.5 %shard_map.97 = (bf16[16,2048]{1,0:T(8,128)(2,1)S(1)}, bf16[2,2048,512]{2,1,0:T(8,128)(2,1)S(1)}, bf16[2,512,2048]{2,1,0:T(8,128)(2,1)S(1)}) custom-call(bf16[16,2048]{1,0:T(8,128)(2,1)S(1)} %collective-permute-done.1.x_ref, bf16[16,2048]{1,0:T(8,128)(2,1)S(1)} %get-tuple-element.16.refs_0_, bf16[2,2048,512]{2,1,0:T(8,128)(2,1)} %bitcast.14, ...), custom_call_target="tpu_custom_call" | custom-call | flops 2500000000 | tf_op jit(solution)/shard_map/pallas_call | solution.py:95
  16.8 0.8 %collective-permute-done.3.refs_2_ = bf16[16,2048]{1,0:T(8,128)(2,1)S(1)} collective-permute-done((bf16[16,2048]{1,0:T(8,128)(2,1)S(1)}, bf16[16,2048]{1,0:T(8,128)(2,1)S(1)}, u32[]{:S(2)}, u32[]{:S(2)}) %collective-permute-start.3) | collective-permute-done | bytes 65568 | tf_op jit(solution)/shard_map/ppermute | solution.py:156
  17.9 1.3 %collective-permute-start.5 = (bf16[64,2048]{1,0:T(8,128)(2,1)S(1)}, bf16[64,2048]{1,0:T(8,128)(2,1)S(1)}, u32[]{:S(2)}, u32[]{:S(2)}) collective-permute-start(bf16[64,2048]{1,0:T(8,128)(2,1)S(1)} %shard_map.98.x_ref), channel_id=1, source_target_pairs={{0,1},{1,0},{2,3},{3,2},{4,5},{5,4},{6,7},{7,6},{8,9},{9,8},{10,11... | collective-permute-start | bytes 786440 | tf_op jit(solution)/shard_map/ppermute | solution.py:152
  19.2 1.2 %collective-permute-done.5.x_ref = bf16[64,2048]{1,0:T(8,128)(2,1)S(1)} collective-permute-done((bf16[64,2048]{1,0:T(8,128)(2,1)S(1)}, bf16[64,2048]{1,0:T(8,128)(2,1)S(1)}, u32[]{:S(2)}, u32[]{:S(2)}) %collective-permute-start.5) | collective-permute-done | bytes 262176 | tf_op jit(solution)/shard_map/ppermute | solution.py:152
  20.4 1.4 %shard_map.100 = bf16[64,2048]{1,0:T(8,128)(2,1)S(1)} custom-call(bf16[64,2048]{1,0:T(8,128)(2,1)S(1)} %collective-permute-done.5.x_ref, f32[2,2048]{1,0:T(2,128)S(1)} %bitcast.8, bf16[2,2048,512]{2,1,0:T(8,128)(2,1)S(1)} %get-tuple-element.18.gate_ref, bf16[2,2048,512]{2,1,0:T(8,128)(2,1)S(1)} %get-tuple-element.19.up_ref, ...), custom_call_target="tpu_custom_call" | custom-call | flops 402653184 | bytes 6291456 | tf_op jit(solution)/shard_map/pallas_call | solution.py:127
  22.2 1.4 %shard_map.99 = f32[64,2048]{1,0:T(8,128)S(1)} custom-call(bf16[64,2048]{1,0:T(8,128)(2,1)S(1)} %shard_map.98.x_ref, f32[2,2048]{1,0:T(2,128)S(1)} %bitcast.9, bf16[2,2048,512]{2,1,0:T(8,128)(2,1)S(1)} %get-tuple-element.18.gate_ref, bf16[2,2048,512]{2,1,0:T(8,128)(2,1)S(1)} %get-tuple-element.19.up_ref, bf16[2,512,2048]{2,1,0:T(8,128)(2,1)S(1)} %get-tuple-element.20.down_ref), custom_call_target="tpu_custom_call" | custom-call | flops 402653184 | bytes 6291456 | tf_op jit(solution)/shard_map/pallas_call | solution.py:127
  23.7 1.6 %collective-permute-start.7 = (bf16[16,2048]{1,0:T(8,128)(2,1)S(1)}, bf16[16,2048]{1,0:T(8,128)(2,1)S(1)}, u32[]{:S(2)}, u32[]{:S(2)}) collective-permute-start(bf16[16,2048]{1,0:T(8,128)(2,1)S(1)} %get-tuple-element.33), channel_id=1, source_target_pairs={{0,2},{1,3},{2,0},{3,1},{4,6},{5,7},{6,4},{7,5},{8,10},{9,11},{10,... | collective-permute-start | bytes 196616 | tf_op jit(solution)/shard_map/ppermute | solution.py:156
  25.2 1.5 %collective-permute-start.9 = (bf16[16,2048]{1,0:T(8,128)(2,1)S(1)}, bf16[16,2048]{1,0:T(8,128)(2,1)S(1)}, u32[]{:S(2)}, u32[]{:S(2)}) collective-permute-start(bf16[16,2048]{1,0:T(8,128)(2,1)S(1)} %get-tuple-element.34), channel_id=1, source_target_pairs={{0,6},{1,7},{2,4},{3,5},{4,2},{5,3},{6,0},{7,1},{8,14},{9,15},{10,... | collective-permute-start | bytes 196616 | tf_op jit(solution)/shard_map/ppermute | solution.py:156
  27.2 0.8 %collective-permute-done.7 = bf16[16,2048]{1,0:T(8,128)(2,1)S(1)} collective-permute-done((bf16[16,2048]{1,0:T(8,128)(2,1)S(1)}, bf16[16,2048]{1,0:T(8,128)(2,1)S(1)}, u32[]{:S(2)}, u32[]{:S(2)}) %collective-permute-start.7) | collective-permute-done | bytes 65568 | tf_op jit(solution)/shard_map/ppermute | solution.py:156
  28.0 2.5 %collective-permute-done.9 = bf16[16,2048]{1,0:T(8,128)(2,1)S(1)} collective-permute-done((bf16[16,2048]{1,0:T(8,128)(2,1)S(1)}, bf16[16,2048]{1,0:T(8,128)(2,1)S(1)}, u32[]{:S(2)}, u32[]{:S(2)}) %collective-permute-start.9) | collective-permute-done | bytes 65568 | tf_op jit(solution)/shard_map/ppermute | solution.py:156
  30.5 1.1 %collective-permute-done.8 = bf16[16,2048]{1,0:T(8,128)(2,1)S(1)} collective-permute-done((bf16[16,2048]{1,0:T(8,128)(2,1)S(1)}, bf16[16,2048]{1,0:T(8,128)(2,1)S(1)}, u32[]{:S(2)}, u32[]{:S(2)}) %collective-permute-start.8) | collective-permute-done | bytes 65568 | tf_op jit(solution)/shard_map/ppermute | solution.py:156
  31.6 5.2 %collective-permute-start.10 = (bf16[16,2048]{1,0:T(8,128)(2,1)S(1)}, bf16[16,2048]{1,0:T(8,128)(2,1)S(1)}, u32[]{:S(2)}, u32[]{:S(2)}) collective-permute-start(bf16[16,2048]{1,0:T(8,128)(2,1)S(1)} %fusion.8.x_ref), channel_id=1, source_target_pairs={{0,8},{1,1},{2,10},{3,3},{4,12},{5,5},{6,14},{7,7},{8,0},{9,17},{1... | collective-permute-start | bytes 196616 | tf_op jit(solution)/shard_map/ppermute | solution.py:165
  36.8 2.2 %shard_map.101 = (bf16[16,2048]{1,0:T(8,128)(2,1)S(1)}, bf16[2,2048,512]{2,1,0:T(8,128)(2,1)S(1)}) custom-call(bf16[16,2048]{1,0:T(8,128)(2,1)S(1)} %fusion.8.x_ref, bf16[2,2048,512]{2,1,0:T(8,128)(2,1)} %bitcast.13), custom_call_target="tpu_custom_call" | custom-call | flops 2500000000 | tf_op jit(solution)/shard_map/pallas_call | solution.py:95
  39.1 1.5 %collective-permute-start.13 = (bf16[16,2048]{1,0:T(8,128)(2,1)S(1)}, bf16[16,2048]{1,0:T(8,128)(2,1)S(1)}, u32[]{:S(2)}, u32[]{:S(2)}) collective-permute-start(bf16[16,2048]{1,0:T(8,128)(2,1)S(1)} %collective-permute-done.10.x_ref), channel_id=1, source_target_pairs={{0,6},{1,7},{2,4},{3,5},{4,2},{5,3},{6,0},{7,1},{8,14},{9,15},{10,... | collective-permute-start | bytes 196616 | tf_op jit(solution)/shard_map/ppermute | solution.py:156
  40.6 1.3 %collective-permute-start.12 = (bf16[16,2048]{1,0:T(8,128)(2,1)S(1)}, bf16[16,2048]{1,0:T(8,128)(2,1)S(1)}, u32[]{:S(2)}, u32[]{:S(2)}) collective-permute-start(bf16[16,2048]{1,0:T(8,128)(2,1)S(1)} %collective-permute-done.10.x_ref), channel_id=1, source_target_pairs={{0,4},{1,5},{2,6},{3,7},{4,0},{5,1},{6,2},{7,3},{8,12},{9,13},{10,... | collective-permute-start | bytes 196616 | tf_op jit(solution)/shard_map/ppermute | solution.py:156
  41.9 0.8 %collective-permute-start.11 = (bf16[16,2048]{1,0:T(8,128)(2,1)S(1)}, bf16[16,2048]{1,0:T(8,128)(2,1)S(1)}, u32[]{:S(2)}, u32[]{:S(2)}) collective-permute-start(bf16[16,2048]{1,0:T(8,128)(2,1)S(1)} %collective-permute-done.10.x_ref), channel_id=1, source_target_pairs={{0,2},{1,3},{2,0},{3,1},{4,6},{5,7},{6,4},{7,5},{8,10},{9,11},{10,... | collective-permute-start | bytes 196616 | tf_op jit(solution)/shard_map/ppermute | solution.py:156
  42.7 3.5 %shard_map.102 = (bf16[16,2048]{1,0:T(8,128)(2,1)S(1)}, bf16[2,2048,512]{2,1,0:T(8,128)(2,1)S(1)}, bf16[2,512,2048]{2,1,0:T(8,128)(2,1)S(1)}) custom-call(bf16[16,2048]{1,0:T(8,128)(2,1)S(1)} %collective-permute-done.10.x_ref, bf16[16,2048]{1,0:T(8,128)(2,1)S(1)} %get-tuple-element.21.refs_0_, bf16[2,2048,512]{2,1,0:T(8,128)(2,1)} %bitcast.15, ...), custom_call_target="tpu_custom_call" | custom-call | flops 2500000000 | tf_op jit(solution)/shard_map/pallas_call | solution.py:95
  46.3 1.5 %collective-permute-done.14.x_ref = bf16[64,2048]{1,0:T(8,128)(2,1)S(1)} collective-permute-done((bf16[64,2048]{1,0:T(8,128)(2,1)S(1)}, bf16[64,2048]{1,0:T(8,128)(2,1)S(1)}, u32[]{:S(2)}, u32[]{:S(2)}) %collective-permute-start.14) | collective-permute-done | bytes 262176 | tf_op jit(solution)/shard_map/ppermute | solution.py:152
  47.8 1.4 %shard_map.105 = bf16[64,2048]{1,0:T(8,128)(2,1)S(1)} custom-call(bf16[64,2048]{1,0:T(8,128)(2,1)S(1)} %collective-permute-done.14.x_ref, f32[2,2048]{1,0:T(2,128)S(1)} %bitcast.10, bf16[2,2048,512]{2,1,0:T(8,128)(2,1)S(1)} %get-tuple-element.23.gate_ref, bf16[2,2048,512]{2,1,0:T(8,128)(2,1)S(1)} %get-tuple-element.24.up_ref, ...), custom_call_target="tpu_custom_call" | custom-call | flops 402653184 | bytes 6291456 | tf_op jit(solution)/shard_map/pallas_call | solution.py:127
  49.4 1.4 %shard_map.104 = f32[64,2048]{1,0:T(8,128)S(1)} custom-call(bf16[64,2048]{1,0:T(8,128)(2,1)S(1)} %shard_map.103.x_ref, f32[2,2048]{1,0:T(2,128)S(1)} %bitcast.11, bf16[2,2048,512]{2,1,0:T(8,128)(2,1)S(1)} %get-tuple-element.23.gate_ref, bf16[2,2048,512]{2,1,0:T(8,128)(2,1)S(1)} %get-tuple-element.24.up_ref, bf16[2,512,2048]{2,1,0:T(8,128)(2,1)S(1)} %get-tuple-element.25.down_ref), custom_call_target="tpu_custom_call" | custom-call | flops 402653184 | bytes 6291456 | tf_op jit(solution)/shard_map/pallas_call | solution.py:127
  50.9 1.3 %collective-permute-start.16 = (bf16[16,2048]{1,0:T(8,128)(2,1)S(1)}, bf16[16,2048]{1,0:T(8,128)(2,1)S(1)}, u32[]{:S(2)}, u32[]{:S(2)}) collective-permute-start(bf16[16,2048]{1,0:T(8,128)(2,1)S(1)} %get-tuple-element.30), channel_id=1, source_target_pairs={{0,2},{1,3},{2,0},{3,1},{4,6},{5,7},{6,4},{7,5},{8,10},{9,11},{10,... | collective-permute-start | bytes 196616 | tf_op jit(solution)/shard_map/ppermute | solution.py:156
  52.2 1.0 %collective-permute-start.18 = (bf16[16,2048]{1,0:T(8,128)(2,1)S(1)}, bf16[16,2048]{1,0:T(8,128)(2,1)S(1)}, u32[]{:S(2)}, u32[]{:S(2)}) collective-permute-start(bf16[16,2048]{1,0:T(8,128)(2,1)S(1)} %get-tuple-element.31), channel_id=1, source_target_pairs={{0,6},{1,7},{2,4},{3,5},{4,2},{5,3},{6,0},{7,1},{8,14},{9,15},{10,... | collective-permute-start | bytes 196616 | tf_op jit(solution)/shard_map/ppermute | solution.py:156
  53.2 1.3 %collective-permute-start.17 = (bf16[16,2048]{1,0:T(8,128)(2,1)S(1)}, bf16[16,2048]{1,0:T(8,128)(2,1)S(1)}, u32[]{:S(2)}, u32[]{:S(2)}) collective-permute-start(bf16[16,2048]{1,0:T(8,128)(2,1)S(1)} %get-tuple-element.32), channel_id=1, source_target_pairs={{0,4},{1,5},{2,6},{3,7},{4,0},{5,1},{6,2},{7,3},{8,12},{9,13},{10,... | collective-permute-start | bytes 196616 | tf_op jit(solution)/shard_map/ppermute | solution.py:156
  54.4 1.2 %collective-permute-done.16 = bf16[16,2048]{1,0:T(8,128)(2,1)S(1)} collective-permute-done((bf16[16,2048]{1,0:T(8,128)(2,1)S(1)}, bf16[16,2048]{1,0:T(8,128)(2,1)S(1)}, u32[]{:S(2)}, u32[]{:S(2)}) %collective-permute-start.16) | collective-permute-done | bytes 65568 | tf_op jit(solution)/shard_map/ppermute | solution.py:156
  55.6 1.8 %collective-permute-done.18 = bf16[16,2048]{1,0:T(8,128)(2,1)S(1)} collective-permute-done((bf16[16,2048]{1,0:T(8,128)(2,1)S(1)}, bf16[16,2048]{1,0:T(8,128)(2,1)S(1)}, u32[]{:S(2)}, u32[]{:S(2)}) %collective-permute-start.18) | collective-permute-done | bytes 65568 | tf_op jit(solution)/shard_map/ppermute | solution.py:156
  57.4 0.9 %collective-permute-done.17 = bf16[16,2048]{1,0:T(8,128)(2,1)S(1)} collective-permute-done((bf16[16,2048]{1,0:T(8,128)(2,1)S(1)}, bf16[16,2048]{1,0:T(8,128)(2,1)S(1)}, u32[]{:S(2)}, u32[]{:S(2)}) %collective-permute-start.17) | collective-permute-done | bytes 65568 | tf_op jit(solution)/shard_map/ppermute | solution.py:156
  58.5 1.2 %collective-permute-done.19 = bf16[8,2048]{1,0:T(8,128)(2,1)S(1)} collective-permute-done((bf16[8,2048]{1,0:T(8,128)(2,1)S(1)}, bf16[8,2048]{1,0:T(8,128)(2,1)S(1)}, u32[]{:S(2)}, u32[]{:S(2)}) %collective-permute-start.19) | collective-permute-done | bytes 32800 | tf_op jit(solution)/shard_map/ppermute | solution.py:152
  (39 shorter events, 6.5 us)
Async XLA Ops:
  0.6 0.8 %copy-start.1 = (bf16[2,8,2048]{2,1,0:T(8,128)(2,1)S(1)}, bf16[2,8,2048]{2,1,0:T(8,128)(2,1)}, u32[]{:S(2)}) copy-start(bf16[2,8,2048]{2,1,0:T(8,128)(2,1)} %feeds_hbm.1) | copy-start | bytes 196612
  1.5 0.8 %copy-start.2 = (bf16[1,8,2048]{2,1,0:T(8,128)(2,1)S(1)}, bf16[1,8,2048]{2,1,0:T(8,128)(2,1)}, u32[]{:S(2)}) copy-start(bf16[1,8,2048]{2,1,0:T(8,128)(2,1)} %down_hbm.1) | copy-start | bytes 98308
  2.2 0.8 %copy-start.3 = (bf16[1,8,2048]{2,1,0:T(8,128)(2,1)S(1)}, bf16[1,8,2048]{2,1,0:T(8,128)(2,1)}, u32[]{:S(2)}) copy-start(bf16[1,8,2048]{2,1,0:T(8,128)(2,1)} %up_hbm.1) | copy-start | bytes 98308
  3.0 0.7 %copy-start.4 = (s32[2]{0:T(128)S(1)}, s32[2]{0:T(128)}, u32[]{:S(2)}) copy-start(s32[2]{0:T(128)} %order_ref.1) | copy-start | bytes 28
  4.4 1.4 %collective-permute-start = (bf16[16,2048]{1,0:T(8,128)(2,1)S(1)}, bf16[16,2048]{1,0:T(8,128)(2,1)S(1)}, u32[]{:S(2)}, u32[]{:S(2)}) collective-permute-start(bf16[16,2048]{1,0:T(8,128)(2,1)S(1)} %get-tuple-element.15), channel_id=1, source_target_pairs={{0,1},{1,0},{2,3},{3,2},{4,5},{5,4},{6,7},{7,6},{8,9},{9,8},{10,11... | collective-permute-start | bytes 196616 | tf_op jit(solution)/shard_map/ppermute | solution.py:152
  5.9 2.9 %collective-permute-start.1 = (bf16[16,2048]{1,0:T(8,128)(2,1)S(1)}, bf16[16,2048]{1,0:T(8,128)(2,1)S(1)}, u32[]{:S(2)}, u32[]{:S(2)}) collective-permute-start(bf16[16,2048]{1,0:T(8,128)(2,1)S(1)} %pad_maximum_fusion.x_ref), channel_id=1, source_target_pairs={{0,0},{1,9},{2,2},{3,11},{4,4},{5,13},{6,6},{7,15},{8,16},{9,1},{1... | collective-permute-start | bytes 196616 | tf_op jit(solution)/shard_map/ppermute | solution.py:165
  8.8 8.0 %collective-permute-start.4 = (bf16[16,2048]{1,0:T(8,128)(2,1)S(1)}, bf16[16,2048]{1,0:T(8,128)(2,1)S(1)}, u32[]{:S(2)}, u32[]{:S(2)}) collective-permute-start(bf16[16,2048]{1,0:T(8,128)(2,1)S(1)} %collective-permute-done.1.x_ref), channel_id=1, source_target_pairs={{0,6},{1,7},{2,4},{3,5},{4,2},{5,3},{6,0},{7,1},{8,14},{9,15},{10,... | collective-permute-start | bytes 196616 | tf_op jit(solution)/shard_map/ppermute | solution.py:156
  12.7 5.0 %collective-permute-start.3 = (bf16[16,2048]{1,0:T(8,128)(2,1)S(1)}, bf16[16,2048]{1,0:T(8,128)(2,1)S(1)}, u32[]{:S(2)}, u32[]{:S(2)}) collective-permute-start(bf16[16,2048]{1,0:T(8,128)(2,1)S(1)} %collective-permute-done.1.x_ref), channel_id=1, source_target_pairs={{0,4},{1,5},{2,6},{3,7},{4,0},{5,1},{6,2},{7,3},{8,12},{9,13},{10,... | collective-permute-start | bytes 196616 | tf_op jit(solution)/shard_map/ppermute | solution.py:156
  13.2 4.7 %collective-permute-start.2 = (bf16[16,2048]{1,0:T(8,128)(2,1)S(1)}, bf16[16,2048]{1,0:T(8,128)(2,1)S(1)}, u32[]{:S(2)}, u32[]{:S(2)}) collective-permute-start(bf16[16,2048]{1,0:T(8,128)(2,1)S(1)} %collective-permute-done.1.x_ref), channel_id=1, source_target_pairs={{0,2},{1,3},{2,0},{3,1},{4,6},{5,7},{6,4},{7,5},{8,10},{9,11},{10,... | collective-permute-start | bytes 196616 | tf_op jit(solution)/shard_map/ppermute | solution.py:156
  13.3 7.1 %copy-start = (f32[1,2,2048]{2,1,0:T(2,128)S(1)}, f32[1,2,2048]{2,1,0:T(2,128)}, u32[]{:S(2)}) copy-start(f32[1,2,2048]{2,1,0:T(2,128)} %param.12) | copy-start | bytes 49156
  17.9 2.5 %collective-permute-start.5 = (bf16[64,2048]{1,0:T(8,128)(2,1)S(1)}, bf16[64,2048]{1,0:T(8,128)(2,1)S(1)}, u32[]{:S(2)}, u32[]{:S(2)}) collective-permute-start(bf16[64,2048]{1,0:T(8,128)(2,1)S(1)} %shard_map.98.x_ref), channel_id=1, source_target_pairs={{0,1},{1,0},{2,3},{3,2},{4,5},{5,4},{6,7},{7,6},{8,9},{9,8},{10,11... | collective-permute-start | bytes 786440 | tf_op jit(solution)/shard_map/ppermute | solution.py:152
  21.7 1.8 %collective-permute-start.6 = (bf16[64,2048]{1,0:T(8,128)(2,1)S(1)}, bf16[64,2048]{1,0:T(8,128)(2,1)S(1)}, u32[]{:S(2)}, u32[]{:S(2)}) collective-permute-start(bf16[64,2048]{1,0:T(8,128)(2,1)S(1)} %shard_map.100), channel_id=1, source_target_pairs={{0,1},{1,0},{2,3},{3,2},{4,5},{5,4},{6,7},{7,6},{8,9},{9,8},{10,11... | collective-permute-start | bytes 786440 | tf_op jit(solution)/shard_map/ppermute | solution.py:152
  23.7 4.3 %collective-permute-start.7 = (bf16[16,2048]{1,0:T(8,128)(2,1)S(1)}, bf16[16,2048]{1,0:T(8,128)(2,1)S(1)}, u32[]{:S(2)}, u32[]{:S(2)}) collective-permute-start(bf16[16,2048]{1,0:T(8,128)(2,1)S(1)} %get-tuple-element.33), channel_id=1, source_target_pairs={{0,2},{1,3},{2,0},{3,1},{4,6},{5,7},{6,4},{7,5},{8,10},{9,11},{10,... | collective-permute-start | bytes 196616 | tf_op jit(solution)/shard_map/ppermute | solution.py:156
  25.2 5.2 %collective-permute-start.9 = (bf16[16,2048]{1,0:T(8,128)(2,1)S(1)}, bf16[16,2048]{1,0:T(8,128)(2,1)S(1)}, u32[]{:S(2)}, u32[]{:S(2)}) collective-permute-start(bf16[16,2048]{1,0:T(8,128)(2,1)S(1)} %get-tuple-element.34), channel_id=1, source_target_pairs={{0,6},{1,7},{2,4},{3,5},{4,2},{5,3},{6,0},{7,1},{8,14},{9,15},{10,... | collective-permute-start | bytes 196616 | tf_op jit(solution)/shard_map/ppermute | solution.py:156
  26.7 4.8 %collective-permute-start.8 = (bf16[16,2048]{1,0:T(8,128)(2,1)S(1)}, bf16[16,2048]{1,0:T(8,128)(2,1)S(1)}, u32[]{:S(2)}, u32[]{:S(2)}) collective-permute-start(bf16[16,2048]{1,0:T(8,128)(2,1)S(1)} %get-tuple-element.35), channel_id=1, source_target_pairs={{0,4},{1,5},{2,6},{3,7},{4,0},{5,1},{6,2},{7,3},{8,12},{9,13},{10,... | collective-permute-start | bytes 196616 | tf_op jit(solution)/shard_map/ppermute | solution.py:156
  31.6 7.5 %collective-permute-start.10 = (bf16[16,2048]{1,0:T(8,128)(2,1)S(1)}, bf16[16,2048]{1,0:T(8,128)(2,1)S(1)}, u32[]{:S(2)}, u32[]{:S(2)}) collective-permute-start(bf16[16,2048]{1,0:T(8,128)(2,1)S(1)} %fusion.8.x_ref), channel_id=1, source_target_pairs={{0,8},{1,1},{2,10},{3,3},{4,12},{5,5},{6,14},{7,7},{8,0},{9,17},{1... | collective-permute-start | bytes 196616 | tf_op jit(solution)/shard_map/ppermute | solution.py:165
  39.1 7.1 %collective-permute-start.13 = (bf16[16,2048]{1,0:T(8,128)(2,1)S(1)}, bf16[16,2048]{1,0:T(8,128)(2,1)S(1)}, u32[]{:S(2)}, u32[]{:S(2)}) collective-permute-start(bf16[16,2048]{1,0:T(8,128)(2,1)S(1)} %collective-permute-done.10.x_ref), channel_id=1, source_target_pairs={{0,6},{1,7},{2,4},{3,5},{4,2},{5,3},{6,0},{7,1},{8,14},{9,15},{10,... | collective-permute-start | bytes 196616 | tf_op jit(solution)/shard_map/ppermute | solution.py:156
  40.6 5.6 %collective-permute-start.12 = (bf16[16,2048]{1,0:T(8,128)(2,1)S(1)}, bf16[16,2048]{1,0:T(8,128)(2,1)S(1)}, u32[]{:S(2)}, u32[]{:S(2)}) collective-permute-start(bf16[16,2048]{1,0:T(8,128)(2,1)S(1)} %collective-permute-done.10.x_ref), channel_id=1, source_target_pairs={{0,4},{1,5},{2,6},{3,7},{4,0},{5,1},{6,2},{7,3},{8,12},{9,13},{10,... | collective-permute-start | bytes 196616 | tf_op jit(solution)/shard_map/ppermute | solution.py:156
  41.9 4.3 %collective-permute-start.11 = (bf16[16,2048]{1,0:T(8,128)(2,1)S(1)}, bf16[16,2048]{1,0:T(8,128)(2,1)S(1)}, u32[]{:S(2)}, u32[]{:S(2)}) collective-permute-start(bf16[16,2048]{1,0:T(8,128)(2,1)S(1)} %collective-permute-done.10.x_ref), channel_id=1, source_target_pairs={{0,2},{1,3},{2,0},{3,1},{4,6},{5,7},{6,4},{7,5},{8,10},{9,11},{10,... | collective-permute-start | bytes 196616 | tf_op jit(solution)/shard_map/ppermute | solution.py:156
  46.2 1.6 %collective-permute-start.14 = (bf16[64,2048]{1,0:T(8,128)(2,1)S(1)}, bf16[64,2048]{1,0:T(8,128)(2,1)S(1)}, u32[]{:S(2)}, u32[]{:S(2)}) collective-permute-start(bf16[64,2048]{1,0:T(8,128)(2,1)S(1)} %shard_map.103.x_ref), channel_id=1, source_target_pairs={{0,1},{1,0},{2,3},{3,2},{4,5},{5,4},{6,7},{7,6},{8,9},{9,8},{10,11... | collective-permute-start | bytes 786440 | tf_op jit(solution)/shard_map/ppermute | solution.py:152
  49.2 1.6 %collective-permute-start.15 = (bf16[64,2048]{1,0:T(8,128)(2,1)S(1)}, bf16[64,2048]{1,0:T(8,128)(2,1)S(1)}, u32[]{:S(2)}, u32[]{:S(2)}) collective-permute-start(bf16[64,2048]{1,0:T(8,128)(2,1)S(1)} %shard_map.105), channel_id=1, source_target_pairs={{0,1},{1,0},{2,3},{3,2},{4,5},{5,4},{6,7},{7,6},{8,9},{9,8},{10,11... | collective-permute-start | bytes 786440 | tf_op jit(solution)/shard_map/ppermute | solution.py:152
  50.9 4.7 %collective-permute-start.16 = (bf16[16,2048]{1,0:T(8,128)(2,1)S(1)}, bf16[16,2048]{1,0:T(8,128)(2,1)S(1)}, u32[]{:S(2)}, u32[]{:S(2)}) collective-permute-start(bf16[16,2048]{1,0:T(8,128)(2,1)S(1)} %get-tuple-element.30), channel_id=1, source_target_pairs={{0,2},{1,3},{2,0},{3,1},{4,6},{5,7},{6,4},{7,5},{8,10},{9,11},{10,... | collective-permute-start | bytes 196616 | tf_op jit(solution)/shard_map/ppermute | solution.py:156
  52.2 5.2 %collective-permute-start.18 = (bf16[16,2048]{1,0:T(8,128)(2,1)S(1)}, bf16[16,2048]{1,0:T(8,128)(2,1)S(1)}, u32[]{:S(2)}, u32[]{:S(2)}) collective-permute-start(bf16[16,2048]{1,0:T(8,128)(2,1)S(1)} %get-tuple-element.31), channel_id=1, source_target_pairs={{0,6},{1,7},{2,4},{3,5},{4,2},{5,3},{6,0},{7,1},{8,14},{9,15},{10,... | collective-permute-start | bytes 196616 | tf_op jit(solution)/shard_map/ppermute | solution.py:156
  53.2 5.2 %collective-permute-start.17 = (bf16[16,2048]{1,0:T(8,128)(2,1)S(1)}, bf16[16,2048]{1,0:T(8,128)(2,1)S(1)}, u32[]{:S(2)}, u32[]{:S(2)}) collective-permute-start(bf16[16,2048]{1,0:T(8,128)(2,1)S(1)} %get-tuple-element.32), channel_id=1, source_target_pairs={{0,4},{1,5},{2,6},{3,7},{4,0},{5,1},{6,2},{7,3},{8,12},{9,13},{10,... | collective-permute-start | bytes 196616 | tf_op jit(solution)/shard_map/ppermute | solution.py:156
  58.4 1.3 %collective-permute-start.19 = (bf16[8,2048]{1,0:T(8,128)(2,1)S(1)}, bf16[8,2048]{1,0:T(8,128)(2,1)S(1)}, u32[]{:S(2)}, u32[]{:S(2)}) collective-permute-start(bf16[8,2048]{1,0:T(8,128)(2,1)S(1)} %broadcast_select_fusion), channel_id=1, source_target_pairs={{0,1},{1,0},{2,3},{3,2},{4,5},{5,4},{6,7},{7,6},{8,9},{9,8},{10,11... | collective-permute-start | bytes 98312 | tf_op jit(solution)/shard_map/ppermute | solution.py:152

commit v3 on v1

v3 whole, which is shorter than its diff:
```python
import functools

import jax
import jax.numpy as jnp
from jax import lax
from jax.experimental import pallas as pl
from jax.experimental.pallas import tpu as pltpu
from jax.sharding import PartitionSpec as P

CORES = 2
EPS = 1e-05
LIMIT = 8 * 2**20
BESIDE = 10**10


def normalize(x, gain):
    xf = x.astype(jnp.float32)
    return (xf * lax.rsqrt(jnp.mean(xf * xf, axis=-1, keepdims=True) + EPS) * gain).astype(jnp.bfloat16)


def role_at(tick):
    return (lax.axis_index("pipe") + lax.axis_index("zero") % CORES + tick) % 2


def group_kernel(tick, other, x_ref, gains_ref, gate_ref, up_ref, down_ref, out):
    group = (role_at(tick) + other) % 2
    normed = normalize(x_ref[...], gains_ref[pl.ds(group, 1), :])
    gate = jnp.dot(normed, gate_ref[group], preferred_element_type=jnp.float32)
    up = jnp.dot(normed, up_ref[group], preferred_element_type=jnp.float32)
    hidden = (gate / (1.0 + jnp.exp(-gate)) * up).astype(jnp.bfloat16)
    out[...] = jnp.dot(hidden, down_ref[group], preferred_element_type=jnp.float32).astype(out.dtype)


def pass_kernel(x_ref, out):
    out[...] = x_ref[...]


def passed(x):
    vmem = pl.BlockSpec(memory_space=pltpu.VMEM)
    return pl.pallas_call(
        pass_kernel,
        out_shape=jax.ShapeDtypeStruct(x.shape, x.dtype),
        in_specs=[vmem],
        out_specs=vmem,
        compiler_params=pltpu.CompilerParams(vmem_limit_bytes=LIMIT),
        cost_estimate=pl.CostEstimate(flops=BESIDE, bytes_accessed=4 * x.size, transcendentals=0),
    )(x)


def stack_kernel(mark_ref, *refs):
    height = refs[0].shape[0]
    for slot, ref in enumerate(refs[:-1]):
        refs[-1][slot * height : (slot + 1) * height] = ref[...]


def stacked(pieces, mark):
    vmem = pl.BlockSpec(memory_space=pltpu.VMEM)
    rows, width = mark.shape
    return pl.pallas_call(
        stack_kernel,
        out_shape=jax.ShapeDtypeStruct((len(pieces) * rows, width), mark.dtype),
        in_specs=[vmem] * (1 + len(pieces)),
        out_specs=vmem,
        compiler_params=pltpu.CompilerParams(vmem_limit_bytes=LIMIT),
    )(mark, *pieces)


def sum_kernel(*refs):
    total = refs[0][...].astype(jnp.float32)
    for ref in refs[1:-1]:
        total += ref[...].astype(jnp.float32)
    refs[-1][...] = total.astype(refs[-1].dtype)


def summed(parts):
    vmem = pl.BlockSpec(memory_space=pltpu.VMEM)
    return pl.pallas_call(
        sum_kernel,
        out_shape=jax.ShapeDtypeStruct(parts[0].shape, jnp.bfloat16),
        in_specs=[vmem] * len(parts),
        out_specs=vmem,
        compiler_params=pltpu.CompilerParams(vmem_limit_bytes=LIMIT),
    )(*parts)


def partial(tick, other, x, gains, weights):
    vmem = pl.BlockSpec(memory_space=pltpu.VMEM)
    size = sum(w.size // w.shape[0] for w in weights)
    return pl.pallas_call(
        functools.partial(group_kernel, tick, other),
        out_shape=jax.ShapeDtypeStruct(x.shape, jnp.bfloat16 if other else jnp.float32),
        in_specs=[vmem] * (2 + len(weights)),
        out_specs=vmem,
        compiler_params=pltpu.CompilerParams(vmem_limit_bytes=LIMIT),
        cost_estimate=pl.CostEstimate(flops=2 * x.shape[0] * size, bytes_accessed=2 * size, transcendentals=0),
    )(x, gains, *weights)


def chip_pairs(chips, step):
    if chips & (chips - 1) == 0:
        return [(chip, chip ^ step) for chip in range(chips)]
    return [(chip, (chip + step) % chips) for chip in range(chips)]


def on_device(down_out, up_out, feeds, order, gains, gate_w, up_w, down_w):
    sections, zero = lax.axis_size("pipe"), lax.axis_size("zero")
    chips = zero // CORES
    section, place = lax.axis_index("pipe"), lax.axis_index("zero")
    core = place % CORES
    ticks = feeds.shape[0]
    both = ("pipe", "zero")

    def to_sibling(value):
        return lax.ppermute(value, "zero", [(k, k ^ 1) for k in range(zero)])

    def to_chip(value, step):
        pairs = [(a * CORES + r, b * CORES + r) for a, b in chip_pairs(chips, step) for r in range(CORES)]
        return lax.ppermute(value, "zero", pairs)

    def to_next(value, tick, step):
        pairs = []
        for s in range(sections):
            for r in range(CORES):
                other = s - 1 if (s + r + tick) % 2 == 0 else s + 1
                other = other if 0 <= other < sections else s
                for a, b in chip_pairs(chips, step):
                    pairs.append((s * zero + a * CORES + r, other * zero + b * CORES + r))
        return lax.ppermute(value, both, pairs)

    def joined(own, other):
        first = jnp.where(core == 0, own, other)
        second = jnp.where(core == 0, other, own)
        return jnp.concatenate([first, second], axis=0)

    weights = (gate_w[0], up_w[0], down_w[0])
    chosen = (order[:, None] == jnp.arange(ticks)[None, :]).astype(feeds.dtype)
    fed = jnp.einsum("tn,nrd->trd", chosen, feeds, preferred_element_type=jnp.float32).astype(feeds.dtype)
    was_down = role_at(1) == 0
    ascended = jnp.where(section == 0, fed[0], up_out[0])
    given = jnp.where(was_down, ascended, down_out[0])
    own = jnp.where(was_down, down_out[0], ascended)
    rows = own.shape[0]
    given = jnp.concatenate([given] + [fed[tick] for tick in range(1, ticks)], axis=0)
    own, given = lax.optimization_barrier((own, given))
    taken = to_sibling(given)
    state = joined(own, taken[:rows])
    entering = [joined(given[rows * tick : rows * (tick + 1)], taken[rows * tick : rows * (tick + 1)]) for tick in range(1, ticks)]

    for tick in range(ticks):
        if tick == 0:
            pieces = [to_next(state, tick, step) for step in range(chips)]
        else:
            pieces = [state] + [to_chip(state, step) for step in range(1, chips)]
        x = pieces[0]
        height = x.shape[0]
        mine = stacked(pieces, passed(state))
        sibling = to_sibling(mine)
        part = partial(tick, 0, mine, gains[0], weights)
        given = partial(tick, 1, sibling, gains[0], weights)
        part = part + to_sibling(given).astype(jnp.float32)
        slots = [step if chips & (chips - 1) == 0 else (chips - step) % chips for step in range(chips)]
        sums = [part[slot * height : (slot + 1) * height] for slot in slots]
        sums[0] = sums[0] + x.astype(jnp.float32)
        if tick + 1 < ticks:
            sums = lax.optimization_barrier([part.astype(jnp.bfloat16) for part in sums])
            sums = [to_next(part, tick + 1, step) for step, part in enumerate(sums)]
        else:
            sums[1:] = [to_chip(part.astype(jnp.bfloat16), step) for step, part in enumerate(sums) if step > 0]
        state = summed(sums[::-1] if tick + 1 < ticks else sums)
        if tick + 1 < ticks:
            state = jnp.where((section == 0) & (role_at(tick + 1) == 0), entering[tick], state)

    role = role_at(ticks - 1)
    kept = jnp.where(core == 0, state[:rows], state[rows:])
    received = to_sibling(jnp.where(core == 0, state[rows:], state[:rows]))
    down_state = jnp.where(role == 0, kept, received)
    up_state = jnp.where(role == 0, received, kept)
    return (down_state[None], up_state[None])


def solution(mesh):
    return jax.shard_map(
        on_device,
        mesh=mesh,
        in_specs=(
            P("pipe", "zero", None),
            P("pipe", "zero", None),
            P(None, "zero", None),
            P(),
            P("pipe", None, None),
            P("pipe", None, None, "zero"),
            P("pipe", None, None, "zero"),
            P("pipe", None, "zero", None),
        ),
        out_specs=(P("pipe", "zero", None), P("pipe", "zero", None)),
        check_vma=False,
    )
```

time: 79.2 us -> 55.2 us (0.70)
  local copies, waits for them, and re-layouts: 15.2 us -> 0.91 us
  waiting for transfers between devices: 24.8 us -> 20 us
  between operations: 4.7 us -> 0.93 us
  starting transfers between devices: 27 us -> 25 us
  matrix products: 0 us -> 0.93 us
    unnamed x22 -> x16, local copies, waits for them, and re-layouts: 13.9 us -> 0.86 us
    ppermute x12 -> x6, waiting for transfers between devices: 15.2 us -> 6.92 us  [to_chip(): return lax.ppermute(value, 'zero', pairs)]
    ppermute x12 -> x6, starting transfers between devices: 15.1 us -> 7.11 us  [to_chip(): return lax.ppermute(value, 'zero', pairs)]
    ppermute x2 -> x8, starting transfers between devices: 6.91 us -> 14.7 us  [to_next(): return lax.ppermute(value, both, pairs)]
    ppermute x2 -> x8, waiting for transfers between devices: 2.23 us -> 8.22 us  [to_next(): return lax.ppermute(value, both, pairs)]
    ppermute x6, waiting for transfers between devices: 7.35 us -> 4.82 us  [to_sibling(): return lax.ppermute(value, 'zero', [(k, k ^ 1) for k in range(zero)])]
    ppermute x6, starting transfers between devices: 4.98 us -> 3.17 us  [to_sibling(): return lax.ppermute(value, 'zero', [(k, k ^ 1) for k in range(zero)])]
    slice x3 -> x2, local copies, waits for them, and re-layouts: 1.34 us -> 0.03 us  [on_device(): sums = [part[slot * height:(slot + 1) * height] for slot in slots]]
  transfers between devices with their start and end apart: 20 -> 20, of which waited for: 18 -> 15; matrix products, arithmetic and copies ran while one was open for 0% -> 0% of each run, Pallas kernels for 0% -> 5%
where the time goes in v3:
time: 55.2 us; the launch traced here: 54.9 us
  starting transfers between devices  25 us (45%)
  waiting for transfers between devices  20 us (36%)
  Pallas kernels  5.56 us (10%)
  other arithmetic  1.63 us (3%)
  matrix products  0.93 us (2%)
  between operations  0.93 us (2%)
  local copies, waits for them, and re-layouts  0.91 us (2%)
    ppermute x8, starting transfers between devices, to_next(): return lax.ppermute(value, both, pairs)  14.7 us
    ppermute x8, waiting for transfers between devices, to_next(): return lax.ppermute(value, both, pairs)  8.22 us
    ppermute x6, starting transfers between devices, to_chip(): return lax.ppermute(value, 'zero', pairs)  7.11 us
    ppermute x6, waiting for transfers between devices, to_chip(): return lax.ppermute(value, 'zero', pairs)  6.92 us
    pallas_call x4, Pallas kernels, partial(): pl.pallas_call(functools.partial(group_kernel, tick, other), out_shape=ja...  5.44 us
    ppermute x6, waiting for transfers between devices, to_sibling(): return lax.ppermute(value, 'zero', [(k, k ^ 1) for k in range(zero)])  4.82 us
    ppermute x6, starting transfers between devices, to_sibling(): return lax.ppermute(value, 'zero', [(k, k ^ 1) for k in range(zero)])  3.17 us
  transfers between devices with their start and end apart: 20, of which 15 were waited for; matrix products, arithmetic and copies ran while one was open for 0% of the time, Pallas kernels for 5%

profile of v3, /device:TPU:0, one launch (start us, length us, event | category | flops | bytes accessed | tf_op | source)
XLA Modules:
  0.0 54.9 jit_solution(10850299072563982834)
XLA Ops:
  0.7 0.8 %copy-done = bf16[2,8,2048]{2,1,0:T(8,128)(2,1)S(1)} copy-done((bf16[2,8,2048]{2,1,0:T(8,128)(2,1)S(1)}, bf16[2,8,2048]{2,1,0:T(8,128)(2,1)}, u32[]{:S(2)}) %copy-start) | copy-done | bytes 65560
  1.5 0.9 %fusion.1 = bf16[2,8,2048]{2,0,1:T(2,128)(2,1)S(1)} fusion(bf16[2,8,2048]{2,1,0:T(8,128)(2,1)S(1)} %copy-done, s32[2]{0:T(128)} %param.11), kind=kOutput, calls=%fused_computation.9 | convolution fusion | flops 131076 | bytes 131080 | tf_op jit(solution)/shard_map/tn,nrd->trd/dot_general | solution.py:137
  2.4 0.8 %select_bitcast_fusion.2 = (bf16[8,2048]{1,0:T(8,128)(2,1)S(1)}, bf16[8,2048]{1,0:T(8,128)(2,1)S(1)}, bf16[8,2048]{1,0:T(8,128)(2,1)S(1)}) fusion(bf16[1,8,2048]{2,1,0:T(8,128)(2,1)} %param.8, pred[]{:T(512)S(6)} %eq.20, bf16[1,8,2048]{2,1,0:T(8,128)(2,1)} %param.9, bf16[2,8,2048]{2,1,0:T(8,128)(2,1)S(1)} %copy.15, pred[]{:T(512)S(6)} %eq.41), kind=kLoop, calls=%fused_computation.15 | loop fusion | flops 49152 | bytes 229378 | tf_op jit(solution)/shard_map/jit(_where)/select_n | solution.py:140
  3.2 0.5 collective-permute-start
  3.8 0.9 %collective-permute-done = bf16[16,2048]{1,0:T(8,128)(2,1)S(1)} collective-permute-done((bf16[16,2048]{1,0:T(8,128)(2,1)S(1)}, bf16[16,2048]{1,0:T(8,128)(2,1)S(1)}, u32[]{:S(2)}, u32[]{:S(2)}) %collective-permute-start) | collective-permute-done | bytes 65568 | tf_op jit(solution)/shard_map/ppermute | solution.py:114
  4.7 3.9 %collective-permute-start.4 = (bf16[16,2048]{1,0:T(8,128)(2,1)S(1)}, bf16[16,2048]{1,0:T(8,128)(2,1)S(1)}, u32[]{:S(2)}, u32[]{:S(2)}) collective-permute-start(bf16[16,2048]{1,0:T(8,128)(2,1)S(1)} %pad_maximum_fusion.1.x_ref), channel_id=1, source_target_pairs={{0,6},{2,4},{4,2},{6,0},{1,15},{3,13},{5,11},{7,9},{8,22},{10,20},... | collective-permute-start | bytes 196616 | tf_op jit(solution)/shard_map/ppermute | solution.py:128
  9.2 0.7 %collective-permute-start.1 = (bf16[16,2048]{1,0:T(8,128)(2,1)S(1)}, bf16[16,2048]{1,0:T(8,128)(2,1)S(1)}, u32[]{:S(2)}, u32[]{:S(2)}) collective-permute-start(bf16[16,2048]{1,0:T(8,128)(2,1)S(1)} %pad_maximum_fusion.1.x_ref), channel_id=1, source_target_pairs={{0,0},{2,2},{4,4},{6,6},{1,9},{3,11},{5,13},{7,15},{8,16},{10,18},... | collective-permute-start | bytes 196616 | tf_op jit(solution)/shard_map/ppermute | solution.py:128
  9.9 1.6 %collective-permute-done.4.refs_3_ = bf16[16,2048]{1,0:T(8,128)(2,1)S(1)} collective-permute-done((bf16[16,2048]{1,0:T(8,128)(2,1)S(1)}, bf16[16,2048]{1,0:T(8,128)(2,1)S(1)}, u32[]{:S(2)}, u32[]{:S(2)}) %collective-permute-start.4) | collective-permute-done | bytes 65568 | tf_op jit(solution)/shard_map/ppermute | solution.py:128
  11.5 1.3 %collective-permute-done.3.refs_2_ = bf16[16,2048]{1,0:T(8,128)(2,1)S(1)} collective-permute-done((bf16[16,2048]{1,0:T(8,128)(2,1)S(1)}, bf16[16,2048]{1,0:T(8,128)(2,1)S(1)}, u32[]{:S(2)}, u32[]{:S(2)}) %collective-permute-start.3) | collective-permute-done | bytes 65568 | tf_op jit(solution)/shard_map/ppermute | solution.py:128
  12.9 1.2 %collective-permute-done.2.refs_1_ = bf16[16,2048]{1,0:T(8,128)(2,1)S(1)} collective-permute-done((bf16[16,2048]{1,0:T(8,128)(2,1)S(1)}, bf16[16,2048]{1,0:T(8,128)(2,1)S(1)}, u32[]{:S(2)}, u32[]{:S(2)}) %collective-permute-start.2) | collective-permute-done | bytes 65568 | tf_op jit(solution)/shard_map/ppermute | solution.py:128
  14.1 1.9 %collective-permute-start.5 = (bf16[64,2048]{1,0:T(8,128)(2,1)S(1)}, bf16[64,2048]{1,0:T(8,128)(2,1)S(1)}, u32[]{:S(2)}, u32[]{:S(2)}) collective-permute-start(bf16[64,2048]{1,0:T(8,128)(2,1)S(1)} %shard_map.96.x_ref), channel_id=1, source_target_pairs={{0,1},{1,0},{2,3},{3,2},{4,5},{5,4},{6,7},{7,6},{8,9},{9,8},{10,11... | collective-permute-start | bytes 786440 | tf_op jit(solution)/shard_map/ppermute | solution.py:114
  16.0 1.2 %collective-permute-done.5.x_ref = bf16[64,2048]{1,0:T(8,128)(2,1)S(1)} collective-permute-done((bf16[64,2048]{1,0:T(8,128)(2,1)S(1)}, bf16[64,2048]{1,0:T(8,128)(2,1)S(1)}, u32[]{:S(2)}, u32[]{:S(2)}) %collective-permute-start.5) | collective-permute-done | bytes 262176 | tf_op jit(solution)/shard_map/ppermute | solution.py:114
  17.1 1.4 %shard_map.98 = bf16[64,2048]{1,0:T(8,128)(2,1)S(1)} custom-call(bf16[64,2048]{1,0:T(8,128)(2,1)S(1)} %collective-permute-done.5.x_ref, f32[2,2048]{1,0:T(2,128)S(1)} %bitcast.29, bf16[2,2048,512]{2,1,0:T(8,128)(2,1)S(1)} %bitcast.17, bf16[2,2048,512]{2,1,0:T(8,128)(2,1)S(1)} %bitcast.21, bf16[2,512,2048]{2,1,0:T(8,128)(2,1)S(1)} %bitcast.25), custom_call_target="tpu_custom_call" | custom-call | flops 402653184 | bytes 6291456 | tf_op jit(solution)/shard_map/pallas_call | solution.py:89
  19.0 1.4 %shard_map.97 = f32[64,2048]{1,0:T(8,128)S(1)} custom-call(bf16[64,2048]{1,0:T(8,128)(2,1)S(1)} %shard_map.96.x_ref, f32[2,2048]{1,0:T(2,128)S(1)} %bitcast.30, bf16[2,2048,512]{2,1,0:T(8,128)(2,1)S(1)} %bitcast.18, bf16[2,2048,512]{2,1,0:T(8,128)(2,1)S(1)} %bitcast.22, bf16[2,512,2048]{2,1,0:T(8,128)(2,1)S(1)} %bitcast.26), custom_call_target="tpu_custom_call" | custom-call | flops 402653184 | bytes 6291456 | tf_op jit(solution)/shard_map/pallas_call | solution.py:89
  20.4 5.5 %collective-permute-start.7 = (bf16[16,2048]{1,0:T(8,128)(2,1)S(1)}, bf16[16,2048]{1,0:T(8,128)(2,1)S(1)}, u32[]{:S(2)}, u32[]{:S(2)}) collective-permute-start(bf16[16,2048]{1,0:T(8,128)(2,1)S(1)} %get-tuple-element.10), channel_id=1, source_target_pairs={{0,14},{2,12},{4,10},{6,8},{1,7},{3,5},{5,3},{7,1},{8,6},{10,4},{1... | collective-permute-start | bytes 196616 | tf_op jit(solution)/shard_map/ppermute | solution.py:128
  26.0 1.9 %collective-permute-start.9 = (bf16[16,2048]{1,0:T(8,128)(2,1)S(1)}, bf16[16,2048]{1,0:T(8,128)(2,1)S(1)}, u32[]{:S(2)}, u32[]{:S(2)}) collective-permute-start(bf16[16,2048]{1,0:T(8,128)(2,1)S(1)} %get-tuple-element.12), channel_id=1, source_target_pairs={{0,10},{2,8},{4,14},{6,12},{1,3},{3,1},{5,7},{7,5},{8,2},{10,0},{1... | collective-permute-start | bytes 196616 | tf_op jit(solution)/shard_map/ppermute | solution.py:128
  27.9 2.1 %collective-permute-start.10 = (bf16[16,2048]{1,0:T(8,128)(2,1)S(1)}, bf16[16,2048]{1,0:T(8,128)(2,1)S(1)}, u32[]{:S(2)}, u32[]{:S(2)}) collective-permute-start(bf16[16,2048]{1,0:T(8,128)(2,1)S(1)} %fusion), channel_id=1, source_target_pairs={{0,8},{2,10},{4,12},{6,14},{1,1},{3,3},{5,5},{7,7},{8,0},{10,2},{1... | collective-permute-start | bytes 196616 | tf_op jit(solution)/shard_map/ppermute | solution.py:128
  30.0 1.4 %collective-permute-done.8.refs_1_ = bf16[16,2048]{1,0:T(8,128)(2,1)S(1)} collective-permute-done((bf16[16,2048]{1,0:T(8,128)(2,1)S(1)}, bf16[16,2048]{1,0:T(8,128)(2,1)S(1)}, u32[]{:S(2)}, u32[]{:S(2)}) %collective-permute-start.8) | collective-permute-done | bytes 65568 | tf_op jit(solution)/shard_map/ppermute | solution.py:128
  31.4 2.7 %collective-permute-done.10.refs_3_ = bf16[16,2048]{1,0:T(8,128)(2,1)S(1)} collective-permute-done((bf16[16,2048]{1,0:T(8,128)(2,1)S(1)}, bf16[16,2048]{1,0:T(8,128)(2,1)S(1)}, u32[]{:S(2)}, u32[]{:S(2)}) %collective-permute-start.10) | collective-permute-done | bytes 65568 | tf_op jit(solution)/shard_map/ppermute | solution.py:128
  34.2 2.5 %collective-permute-start.13 = (bf16[16,2048]{1,0:T(8,128)(2,1)S(1)}, bf16[16,2048]{1,0:T(8,128)(2,1)S(1)}, u32[]{:S(2)}, u32[]{:S(2)}) collective-permute-start(bf16[16,2048]{1,0:T(8,128)(2,1)S(1)} %maximum_select_fusion.x_ref.refs_0_), channel_id=1, source_target_pairs={{0,6},{1,7},{2,4},{3,5},{4,2},{5,3},{6,0},{7,1},{8,14},{9,15},{10,... | collective-permute-start | bytes 196616 | tf_op jit(solution)/shard_map/ppermute | solution.py:118
  37.2 0.5 collective-permute-start.11
  37.7 1.7 %collective-permute-done.13.refs_3_ = bf16[16,2048]{1,0:T(8,128)(2,1)S(1)} collective-permute-done((bf16[16,2048]{1,0:T(8,128)(2,1)S(1)}, bf16[16,2048]{1,0:T(8,128)(2,1)S(1)}, u32[]{:S(2)}, u32[]{:S(2)}) %collective-permute-start.13) | collective-permute-done | bytes 65568 | tf_op jit(solution)/shard_map/ppermute | solution.py:118
  39.4 1.5 %collective-permute-done.12.refs_2_ = bf16[16,2048]{1,0:T(8,128)(2,1)S(1)} collective-permute-done((bf16[16,2048]{1,0:T(8,128)(2,1)S(1)}, bf16[16,2048]{1,0:T(8,128)(2,1)S(1)}, u32[]{:S(2)}, u32[]{:S(2)}) %collective-permute-start.12) | collective-permute-done | bytes 65568 | tf_op jit(solution)/shard_map/ppermute | solution.py:118
  41.5 1.5 %collective-permute-done.14.x_ref = bf16[64,2048]{1,0:T(8,128)(2,1)S(1)} collective-permute-done((bf16[64,2048]{1,0:T(8,128)(2,1)S(1)}, bf16[64,2048]{1,0:T(8,128)(2,1)S(1)}, u32[]{:S(2)}, u32[]{:S(2)}) %collective-permute-start.14) | collective-permute-done | bytes 262176 | tf_op jit(solution)/shard_map/ppermute | solution.py:114
  43.1 1.4 %shard_map.103 = bf16[64,2048]{1,0:T(8,128)(2,1)S(1)} custom-call(bf16[64,2048]{1,0:T(8,128)(2,1)S(1)} %collective-permute-done.14.x_ref, f32[2,2048]{1,0:T(2,128)S(1)} %bitcast.31, bf16[2,2048,512]{2,1,0:T(8,128)(2,1)S(1)} %bitcast.19, bf16[2,2048,512]{2,1,0:T(8,128)(2,1)S(1)} %bitcast.23, bf16[2,512,2048]{2,1,0:T(8,128)(2,1)S(1)} %bitcast.27), custom_call_target="tpu_custom_call" | custom-call | flops 402653184 | bytes 6291456 | tf_op jit(solution)/shard_map/pallas_call | solution.py:89
  44.6 1.4 %shard_map.102 = f32[64,2048]{1,0:T(8,128)S(1)} custom-call(bf16[64,2048]{1,0:T(8,128)(2,1)S(1)} %shard_map.101.x_ref, f32[2,2048]{1,0:T(2,128)S(1)} %bitcast.32, bf16[2,2048,512]{2,1,0:T(8,128)(2,1)S(1)} %bitcast.20, bf16[2,2048,512]{2,1,0:T(8,128)(2,1)S(1)} %bitcast.24, bf16[2,512,2048]{2,1,0:T(8,128)(2,1)S(1)} %bitcast.28), custom_call_target="tpu_custom_call" | custom-call | flops 402653184 | bytes 6291456 | tf_op jit(solution)/shard_map/pallas_call | solution.py:89
  46.1 1.6 %collective-permute-start.18 = (bf16[16,2048]{1,0:T(8,128)(2,1)S(1)}, bf16[16,2048]{1,0:T(8,128)(2,1)S(1)}, u32[]{:S(2)}, u32[]{:S(2)}) collective-permute-start(bf16[16,2048]{1,0:T(8,128)(2,1)S(1)} %get-tuple-element.18), channel_id=1, source_target_pairs={{0,6},{1,7},{2,4},{3,5},{4,2},{5,3},{6,0},{7,1},{8,14},{9,15},{10,... | collective-permute-start | bytes 196616 | tf_op jit(solution)/shard_map/ppermute | solution.py:118
  48.2 1.5 %collective-permute-start.16 = (bf16[16,2048]{1,0:T(8,128)(2,1)S(1)}, bf16[16,2048]{1,0:T(8,128)(2,1)S(1)}, u32[]{:S(2)}, u32[]{:S(2)}) collective-permute-start(bf16[16,2048]{1,0:T(8,128)(2,1)S(1)} %get-tuple-element.20), channel_id=1, source_target_pairs={{0,2},{1,3},{2,0},{3,1},{4,6},{5,7},{6,4},{7,5},{8,10},{9,11},{10,... | collective-permute-start | bytes 196616 | tf_op jit(solution)/shard_map/ppermute | solution.py:118
  49.7 1.8 %collective-permute-done.18.refs_3_ = bf16[16,2048]{1,0:T(8,128)(2,1)S(1)} collective-permute-done((bf16[16,2048]{1,0:T(8,128)(2,1)S(1)}, bf16[16,2048]{1,0:T(8,128)(2,1)S(1)}, u32[]{:S(2)}, u32[]{:S(2)}) %collective-permute-start.18) | collective-permute-done | bytes 65568 | tf_op jit(solution)/shard_map/ppermute | solution.py:118
  51.6 1.3 %collective-permute-done.17.refs_2_ = bf16[16,2048]{1,0:T(8,128)(2,1)S(1)} collective-permute-done((bf16[16,2048]{1,0:T(8,128)(2,1)S(1)}, bf16[16,2048]{1,0:T(8,128)(2,1)S(1)}, u32[]{:S(2)}, u32[]{:S(2)}) %collective-permute-start.17) | collective-permute-done | bytes 65568 | tf_op jit(solution)/shard_map/ppermute | solution.py:118
  53.0 1.2 %collective-permute-done.19 = bf16[8,2048]{1,0:T(8,128)(2,1)S(1)} collective-permute-done((bf16[8,2048]{1,0:T(8,128)(2,1)S(1)}, bf16[8,2048]{1,0:T(8,128)(2,1)S(1)}, u32[]{:S(2)}, u32[]{:S(2)}) %collective-permute-start.19) | collective-permute-done | bytes 32800 | tf_op jit(solution)/shard_map/ppermute | solution.py:114
  54.2 0.6 %select_bitcast_fusion = (bf16[1,8,2048]{2,1,0:T(8,128)(2,1)}, bf16[1,8,2048]{2,1,0:T(8,128)(2,1)}) fusion(bf16[8,2048]{1,0:T(8,128)(2,1)S(1)} %collective-permute-done.19, pred[]{:T(512)S(6)} %eq.20, bf16[16,2048]{1,0:T(8,128)(2,1)S(1)} %shard_map.104, pred[]{:T(512)S(6)} %eq.40), kind=kLoop, calls=%fused_computation.13 | loop fusion | flops 49152 | bytes 163842 | tf_op jit(solution)/shard_map/broadcast_in_dim | solution.py:178
  (49 shorter events, 3.5 us)
Async XLA Ops:
  0.6 0.8 %copy-start = (bf16[2,8,2048]{2,1,0:T(8,128)(2,1)S(1)}, bf16[2,8,2048]{2,1,0:T(8,128)(2,1)}, u32[]{:S(2)}) copy-start(bf16[2,8,2048]{2,1,0:T(8,128)(2,1)} %param.10) | copy-start | bytes 196612
  3.2 1.4 %collective-permute-start = (bf16[16,2048]{1,0:T(8,128)(2,1)S(1)}, bf16[16,2048]{1,0:T(8,128)(2,1)S(1)}, u32[]{:S(2)}, u32[]{:S(2)}) collective-permute-start(bf16[16,2048]{1,0:T(8,128)(2,1)S(1)} %pad_maximum_fusion), channel_id=1, source_target_pairs={{0,1},{1,0},{2,3},{3,2},{4,5},{5,4},{6,7},{7,6},{8,9},{9,8},{10,11... | collective-permute-start | bytes 196616 | tf_op jit(solution)/shard_map/ppermute | solution.py:114
  4.7 12.4 %copy-start.1 = (bf16[1,2,2048,512]{3,2,1,0:T(8,128)(2,1)S(1)}, bf16[1,2,2048,512]{3,2,1,0:T(8,128)(2,1)}, u32[]{:S(2)}) copy-start(bf16[1,2,2048,512]{3,2,1,0:T(8,128)(2,1)} %param.13) | copy-start | bytes 12582916
  4.7 12.4 %copy-start.3 = (bf16[1,2,2048,512]{3,2,1,0:T(8,128)(2,1)S(1)}, bf16[1,2,2048,512]{3,2,1,0:T(8,128)(2,1)}, u32[]{:S(2)}) copy-start(bf16[1,2,2048,512]{3,2,1,0:T(8,128)(2,1)} %param.14) | copy-start | bytes 12582916
  4.7 12.4 %copy-start.5 = (bf16[1,2,512,2048]{3,2,1,0:T(8,128)(2,1)S(1)}, bf16[1,2,512,2048]{3,2,1,0:T(8,128)(2,1)}, u32[]{:S(2)}) copy-start(bf16[1,2,512,2048]{3,2,1,0:T(8,128)(2,1)} %param.15) | copy-start | bytes 12582916
  4.7 12.4 %copy-start.7 = (f32[1,2,2048]{2,1,0:T(2,128)S(1)}, f32[1,2,2048]{2,1,0:T(2,128)}, u32[]{:S(2)}) copy-start(f32[1,2,2048]{2,1,0:T(2,128)} %param.12) | copy-start | bytes 49156
  4.7 6.8 %collective-permute-start.4 = (bf16[16,2048]{1,0:T(8,128)(2,1)S(1)}, bf16[16,2048]{1,0:T(8,128)(2,1)S(1)}, u32[]{:S(2)}, u32[]{:S(2)}) collective-permute-start(bf16[16,2048]{1,0:T(8,128)(2,1)S(1)} %pad_maximum_fusion.1.x_ref), channel_id=1, source_target_pairs={{0,6},{2,4},{4,2},{6,0},{1,15},{3,13},{5,11},{7,9},{8,22},{10,20},... | collective-permute-start | bytes 196616 | tf_op jit(solution)/shard_map/ppermute | solution.py:128
  8.6 4.3 %collective-permute-start.3 = (bf16[16,2048]{1,0:T(8,128)(2,1)S(1)}, bf16[16,2048]{1,0:T(8,128)(2,1)S(1)}, u32[]{:S(2)}, u32[]{:S(2)}) collective-permute-start(bf16[16,2048]{1,0:T(8,128)(2,1)S(1)} %pad_maximum_fusion.1.x_ref), channel_id=1, source_target_pairs={{0,4},{2,6},{4,0},{6,2},{1,13},{3,15},{5,9},{7,11},{8,20},{10,22},... | collective-permute-start | bytes 196616 | tf_op jit(solution)/shard_map/ppermute | solution.py:128
  9.1 5.0 %collective-permute-start.2 = (bf16[16,2048]{1,0:T(8,128)(2,1)S(1)}, bf16[16,2048]{1,0:T(8,128)(2,1)S(1)}, u32[]{:S(2)}, u32[]{:S(2)}) collective-permute-start(bf16[16,2048]{1,0:T(8,128)(2,1)S(1)} %pad_maximum_fusion.1.x_ref), channel_id=1, source_target_pairs={{0,2},{2,0},{4,6},{6,4},{1,11},{3,9},{5,15},{7,13},{8,18},{10,16},... | collective-permute-start | bytes 196616 | tf_op jit(solution)/shard_map/ppermute | solution.py:128
  9.2 4.8 %collective-permute-start.1 = (bf16[16,2048]{1,0:T(8,128)(2,1)S(1)}, bf16[16,2048]{1,0:T(8,128)(2,1)S(1)}, u32[]{:S(2)}, u32[]{:S(2)}) collective-permute-start(bf16[16,2048]{1,0:T(8,128)(2,1)S(1)} %pad_maximum_fusion.1.x_ref), channel_id=1, source_target_pairs={{0,0},{2,2},{4,4},{6,6},{1,9},{3,11},{5,13},{7,15},{8,16},{10,18},... | collective-permute-start | bytes 196616 | tf_op jit(solution)/shard_map/ppermute | solution.py:128
  14.1 3.0 %collective-permute-start.5 = (bf16[64,2048]{1,0:T(8,128)(2,1)S(1)}, bf16[64,2048]{1,0:T(8,128)(2,1)S(1)}, u32[]{:S(2)}, u32[]{:S(2)}) collective-permute-start(bf16[64,2048]{1,0:T(8,128)(2,1)S(1)} %shard_map.96.x_ref), channel_id=1, source_target_pairs={{0,1},{1,0},{2,3},{3,2},{4,5},{5,4},{6,7},{7,6},{8,9},{9,8},{10,11... | collective-permute-start | bytes 786440 | tf_op jit(solution)/shard_map/ppermute | solution.py:114
  18.5 1.8 %collective-permute-start.6 = (bf16[64,2048]{1,0:T(8,128)(2,1)S(1)}, bf16[64,2048]{1,0:T(8,128)(2,1)S(1)}, u32[]{:S(2)}, u32[]{:S(2)}) collective-permute-start(bf16[64,2048]{1,0:T(8,128)(2,1)S(1)} %shard_map.98), channel_id=1, source_target_pairs={{0,1},{1,0},{2,3},{3,2},{4,5},{5,4},{6,7},{7,6},{8,9},{9,8},{10,11... | collective-permute-start | bytes 786440 | tf_op jit(solution)/shard_map/ppermute | solution.py:114
  20.4 9.5 %collective-permute-start.7 = (bf16[16,2048]{1,0:T(8,128)(2,1)S(1)}, bf16[16,2048]{1,0:T(8,128)(2,1)S(1)}, u32[]{:S(2)}, u32[]{:S(2)}) collective-permute-start(bf16[16,2048]{1,0:T(8,128)(2,1)S(1)} %get-tuple-element.10), channel_id=1, source_target_pairs={{0,14},{2,12},{4,10},{6,8},{1,7},{3,5},{5,3},{7,1},{8,6},{10,4},{1... | collective-permute-start | bytes 196616 | tf_op jit(solution)/shard_map/ppermute | solution.py:128
  26.0 5.4 %collective-permute-start.8 = (bf16[16,2048]{1,0:T(8,128)(2,1)S(1)}, bf16[16,2048]{1,0:T(8,128)(2,1)S(1)}, u32[]{:S(2)}, u32[]{:S(2)}) collective-permute-start(bf16[16,2048]{1,0:T(8,128)(2,1)S(1)} %get-tuple-element.11), channel_id=1, source_target_pairs={{0,12},{2,14},{4,8},{6,10},{1,5},{3,7},{5,1},{7,3},{8,4},{10,6},{1... | collective-permute-start | bytes 196616 | tf_op jit(solution)/shard_map/ppermute | solution.py:128
  26.0 5.4 %collective-permute-start.9 = (bf16[16,2048]{1,0:T(8,128)(2,1)S(1)}, bf16[16,2048]{1,0:T(8,128)(2,1)S(1)}, u32[]{:S(2)}, u32[]{:S(2)}) collective-permute-start(bf16[16,2048]{1,0:T(8,128)(2,1)S(1)} %get-tuple-element.12), channel_id=1, source_target_pairs={{0,10},{2,8},{4,14},{6,12},{1,3},{3,1},{5,7},{7,5},{8,2},{10,0},{1... | collective-permute-start | bytes 196616 | tf_op jit(solution)/shard_map/ppermute | solution.py:128
  27.9 6.1 %collective-permute-start.10 = (bf16[16,2048]{1,0:T(8,128)(2,1)S(1)}, bf16[16,2048]{1,0:T(8,128)(2,1)S(1)}, u32[]{:S(2)}, u32[]{:S(2)}) collective-permute-start(bf16[16,2048]{1,0:T(8,128)(2,1)S(1)} %fusion), channel_id=1, source_target_pairs={{0,8},{2,10},{4,12},{6,14},{1,1},{3,3},{5,5},{7,7},{8,0},{10,2},{1... | collective-permute-start | bytes 196616 | tf_op jit(solution)/shard_map/ppermute | solution.py:128
  34.1 8.9 %copy-start.2 = (bf16[1,2,2048,512]{3,2,1,0:T(8,128)(2,1)S(1)}, bf16[1,2,2048,512]{3,2,1,0:T(8,128)(2,1)}, u32[]{:S(2)}) copy-start(bf16[1,2,2048,512]{3,2,1,0:T(8,128)(2,1)} %param.13) | copy-start | bytes 12582916
  34.1 8.9 %copy-start.4 = (bf16[1,2,2048,512]{3,2,1,0:T(8,128)(2,1)S(1)}, bf16[1,2,2048,512]{3,2,1,0:T(8,128)(2,1)}, u32[]{:S(2)}) copy-start(bf16[1,2,2048,512]{3,2,1,0:T(8,128)(2,1)} %param.14) | copy-start | bytes 12582916
  34.1 8.9 %copy-start.6 = (bf16[1,2,512,2048]{3,2,1,0:T(8,128)(2,1)S(1)}, bf16[1,2,512,2048]{3,2,1,0:T(8,128)(2,1)}, u32[]{:S(2)}) copy-start(bf16[1,2,512,2048]{3,2,1,0:T(8,128)(2,1)} %param.15) | copy-start | bytes 12582916
  34.2 5.2 %collective-permute-start.13 = (bf16[16,2048]{1,0:T(8,128)(2,1)S(1)}, bf16[16,2048]{1,0:T(8,128)(2,1)S(1)}, u32[]{:S(2)}, u32[]{:S(2)}) collective-permute-start(bf16[16,2048]{1,0:T(8,128)(2,1)S(1)} %maximum_select_fusion.x_ref.refs_0_), channel_id=1, source_target_pairs={{0,6},{1,7},{2,4},{3,5},{4,2},{5,3},{6,0},{7,1},{8,14},{9,15},{10,... | collective-permute-start | bytes 196616 | tf_op jit(solution)/shard_map/ppermute | solution.py:118
  36.7 4.3 %collective-permute-start.12 = (bf16[16,2048]{1,0:T(8,128)(2,1)S(1)}, bf16[16,2048]{1,0:T(8,128)(2,1)S(1)}, u32[]{:S(2)}, u32[]{:S(2)}) collective-permute-start(bf16[16,2048]{1,0:T(8,128)(2,1)S(1)} %maximum_select_fusion.x_ref.refs_0_), channel_id=1, source_target_pairs={{0,4},{1,5},{2,6},{3,7},{4,0},{5,1},{6,2},{7,3},{8,12},{9,13},{10,... | collective-permute-start | bytes 196616 | tf_op jit(solution)/shard_map/ppermute | solution.py:118
  37.2 4.3 %collective-permute-start.11 = (bf16[16,2048]{1,0:T(8,128)(2,1)S(1)}, bf16[16,2048]{1,0:T(8,128)(2,1)S(1)}, u32[]{:S(2)}, u32[]{:S(2)}) collective-permute-start(bf16[16,2048]{1,0:T(8,128)(2,1)S(1)} %maximum_select_fusion.x_ref.refs_0_), channel_id=1, source_target_pairs={{0,2},{1,3},{2,0},{3,1},{4,6},{5,7},{6,4},{7,5},{8,10},{9,11},{10,... | collective-permute-start | bytes 196616 | tf_op jit(solution)/shard_map/ppermute | solution.py:118
  41.5 1.6 %collective-permute-start.14 = (bf16[64,2048]{1,0:T(8,128)(2,1)S(1)}, bf16[64,2048]{1,0:T(8,128)(2,1)S(1)}, u32[]{:S(2)}, u32[]{:S(2)}) collective-permute-start(bf16[64,2048]{1,0:T(8,128)(2,1)S(1)} %shard_map.101.x_ref), channel_id=1, source_target_pairs={{0,1},{1,0},{2,3},{3,2},{4,5},{5,4},{6,7},{7,6},{8,9},{9,8},{10,11... | collective-permute-start | bytes 786440 | tf_op jit(solution)/shard_map/ppermute | solution.py:114
  44.4 1.6 %collective-permute-start.15 = (bf16[64,2048]{1,0:T(8,128)(2,1)S(1)}, bf16[64,2048]{1,0:T(8,128)(2,1)S(1)}, u32[]{:S(2)}, u32[]{:S(2)}) collective-permute-start(bf16[64,2048]{1,0:T(8,128)(2,1)S(1)} %shard_map.103), channel_id=1, source_target_pairs={{0,1},{1,0},{2,3},{3,2},{4,5},{5,4},{6,7},{7,6},{8,9},{9,8},{10,11... | collective-permute-start | bytes 786440 | tf_op jit(solution)/shard_map/ppermute | solution.py:114
  46.1 5.4 %collective-permute-start.18 = (bf16[16,2048]{1,0:T(8,128)(2,1)S(1)}, bf16[16,2048]{1,0:T(8,128)(2,1)S(1)}, u32[]{:S(2)}, u32[]{:S(2)}) collective-permute-start(bf16[16,2048]{1,0:T(8,128)(2,1)S(1)} %get-tuple-element.18), channel_id=1, source_target_pairs={{0,6},{1,7},{2,4},{3,5},{4,2},{5,3},{6,0},{7,1},{8,14},{9,15},{10,... | collective-permute-start | bytes 196616 | tf_op jit(solution)/shard_map/ppermute | solution.py:118
  47.7 5.2 %collective-permute-start.17 = (bf16[16,2048]{1,0:T(8,128)(2,1)S(1)}, bf16[16,2048]{1,0:T(8,128)(2,1)S(1)}, u32[]{:S(2)}, u32[]{:S(2)}) collective-permute-start(bf16[16,2048]{1,0:T(8,128)(2,1)S(1)} %get-tuple-element.19), channel_id=1, source_target_pairs={{0,4},{1,5},{2,6},{3,7},{4,0},{5,1},{6,2},{7,3},{8,12},{9,13},{10,... | collective-permute-start | bytes 196616 | tf_op jit(solution)/shard_map/ppermute | solution.py:118
  48.2 4.7 %collective-permute-start.16 = (bf16[16,2048]{1,0:T(8,128)(2,1)S(1)}, bf16[16,2048]{1,0:T(8,128)(2,1)S(1)}, u32[]{:S(2)}, u32[]{:S(2)}) collective-permute-start(bf16[16,2048]{1,0:T(8,128)(2,1)S(1)} %get-tuple-element.20), channel_id=1, source_target_pairs={{0,2},{1,3},{2,0},{3,1},{4,6},{5,7},{6,4},{7,5},{8,10},{9,11},{10,... | collective-permute-start | bytes 196616 | tf_op jit(solution)/shard_map/ppermute | solution.py:118
  53.0 1.3 %collective-permute-start.19 = (bf16[8,2048]{1,0:T(8,128)(2,1)S(1)}, bf16[8,2048]{1,0:T(8,128)(2,1)S(1)}, u32[]{:S(2)}, u32[]{:S(2)}) collective-permute-start(bf16[8,2048]{1,0:T(8,128)(2,1)S(1)} %broadcast_select_fusion), channel_id=1, source_target_pairs={{0,1},{1,0},{2,3},{3,2},{4,5},{5,4},{6,7},{7,6},{8,9},{9,8},{10,11... | collective-permute-start | bytes 98312 | tf_op jit(solution)/shard_map/ppermute | solution.py:114

commit v4 on v3

--- a/solution.py
+++ b/solution.py
@@ -22,13 +22,15 @@
     return (lax.axis_index("pipe") + lax.axis_index("zero") % CORES + tick) % 2
 
 
-def group_kernel(tick, other, x_ref, gains_ref, gate_ref, up_ref, down_ref, out):
+def group_kernel(tick, other, ready, mark_ref, gains_ref, gate_ref, up_ref, down_ref, *refs):
     group = (role_at(tick) + other) % 2
-    normed = normalize(x_ref[...], gains_ref[pl.ds(group, 1), :])
+    normed = jnp.concatenate([ref[...] for ref in refs[:-1]], axis=0)
+    if not ready:
+        normed = normalize(normed, gains_ref[pl.ds(group, 1), :])
     gate = jnp.dot(normed, gate_ref[group], preferred_element_type=jnp.float32)
     up = jnp.dot(normed, up_ref[group], preferred_element_type=jnp.float32)
     hidden = (gate / (1.0 + jnp.exp(-gate)) * up).astype(jnp.bfloat16)
-    out[...] = jnp.dot(hidden, down_ref[group], preferred_element_type=jnp.float32).astype(out.dtype)
+    refs[-1][...] = jnp.dot(hidden, down_ref[group], preferred_element_type=jnp.float32).astype(refs[-1].dtype)
 
 
 def pass_kernel(x_ref, out):
@@ -45,24 +47,6 @@
         compiler_params=pltpu.CompilerParams(vmem_limit_bytes=LIMIT),
         cost_estimate=pl.CostEstimate(flops=BESIDE, bytes_accessed=4 * x.size, transcendentals=0),
     )(x)
-
-
-def stack_kernel(mark_ref, *refs):
-    height = refs[0].shape[0]
-    for slot, ref in enumerate(refs[:-1]):
-        refs[-1][slot * height : (slot + 1) * height] = ref[...]
-
-
-def stacked(pieces, mark):
-    vmem = pl.BlockSpec(memory_space=pltpu.VMEM)
-    rows, width = mark.shape
-    return pl.pallas_call(
-        stack_kernel,
-        out_shape=jax.ShapeDtypeStruct((len(pieces) * rows, width), mark.dtype),
-        in_specs=[vmem] * (1 + len(pieces)),
-        out_specs=vmem,
-        compiler_params=pltpu.CompilerParams(vmem_limit_bytes=LIMIT),
-    )(mark, *pieces)
 
 
 def sum_kernel(*refs):
@@ -83,17 +67,42 @@
     )(*parts)
 
 
-def partial(tick, other, x, gains, weights):
-    vmem = pl.BlockSpec(memory_space=pltpu.VMEM)
+def next_kernel(tick, gains_ref, entering_ref, *refs):
+    *parts, x_out, normed_out = refs
+    total = parts[0][...].astype(jnp.float32)
+    for part in parts[1:]:
+        total += part[...].astype(jnp.float32)
+    role = role_at(tick)
+    entry = (lax.axis_index("pipe") == 0) & (role == 0)
+    x = jnp.where(entry, entering_ref[...].astype(jnp.float32), total).astype(x_out.dtype)
+    x_out[...] = x
+    normed_out[...] = normalize(x, gains_ref[pl.ds(role, 1), :])
+
+
+def next_rows(tick, gains, entering, parts):
+    vmem = pl.BlockSpec(memory_space=pltpu.VMEM)
+    shape = jax.ShapeDtypeStruct(entering.shape, entering.dtype)
+    return pl.pallas_call(
+        functools.partial(next_kernel, tick),
+        out_shape=(shape, shape),
+        in_specs=[vmem] * (2 + len(parts)),
+        out_specs=(vmem, vmem),
+        compiler_params=pltpu.CompilerParams(vmem_limit_bytes=LIMIT),
+    )(gains, entering, *parts)
+
+
+def partial(tick, other, ready, pieces, gains, weights, mark):
+    vmem = pl.BlockSpec(memory_space=pltpu.VMEM)
+    rows, width = len(pieces) * mark.shape[0], mark.shape[1]
     size = sum(w.size // w.shape[0] for w in weights)
     return pl.pallas_call(
-        functools.partial(group_kernel, tick, other),
-        out_shape=jax.ShapeDtypeStruct(x.shape, jnp.bfloat16 if other else jnp.float32),
-        in_specs=[vmem] * (2 + len(weights)),
+        functools.partial(group_kernel, tick, other, ready),
+        out_shape=jax.ShapeDtypeStruct((rows, width), jnp.bfloat16 if other else jnp.float32),
+        in_specs=[vmem] * (2 + len(weights) + len(pieces)),
         out_specs=vmem,
         compiler_params=pltpu.CompilerParams(vmem_limit_bytes=LIMIT),
-        cost_estimate=pl.CostEstimate(flops=2 * x.shape[0] * size, bytes_accessed=2 * size, transcendentals=0),
-    )(x, gains, *weights)
+        cost_estimate=pl.CostEstimate(flops=2 * rows * size, bytes_accessed=2 * size, transcendentals=0),
+    )(mark, gains, *weights, *pieces)
 
 
 def chip_pairs(chips, step):
@@ -133,7 +142,9 @@
         return jnp.concatenate([first, second], axis=0)
 
     weights = (gate_w[0], up_w[0], down_w[0])
-    chosen = (order[:, None] == jnp.arange(ticks)[None, :]).astype(feeds.dtype)
+    place_in_pipe = jnp.full((1, ticks), section, jnp.float32)
+    numbers = jnp.arange(ticks) + (passed(place_in_pipe)[0] - place_in_pipe[0]).astype(order.dtype)
+    chosen = (order[:, None] == numbers[None, :]).astype(feeds.dtype)
     fed = jnp.einsum("tn,nrd->trd", chosen, feeds, preferred_element_type=jnp.float32).astype(feeds.dtype)
     was_down = role_at(1) == 0
     ascended = jnp.where(section == 0, fed[0], up_out[0])
@@ -150,25 +161,27 @@
         if tick == 0:
             pieces = [to_next(state, tick, step) for step in range(chips)]
         else:
-            pieces = [state] + [to_chip(state, step) for step in range(1, chips)]
-        x = pieces[0]
+            pieces = [normed] + [to_chip(normed, step) for step in range(1, chips)]
+        x = pieces[0] if tick == 0 else state
         height = x.shape[0]
-        mine = stacked(pieces, passed(state))
-        sibling = to_sibling(mine)
-        part = partial(tick, 0, mine, gains[0], weights)
-        given = partial(tick, 1, sibling, gains[0], weights)
+        mark = passed(state)
+        pieces = pieces[::-1]
+        siblings = [to_sibling(piece) for piece in pieces]
+        part = partial(tick, 0, tick > 0, pieces, gains[0], weights, mark)
+        given = partial(tick, 1, tick > 0, siblings, gains[0], weights, mark)
         part = part + to_sibling(given).astype(jnp.float32)
         slots = [step if chips & (chips - 1) == 0 else (chips - step) % chips for step in range(chips)]
-        sums = [part[slot * height : (slot + 1) * height] for slot in slots]
+        sums = [part[(chips - 1 - slot) * height : (chips - slot) * height] for slot in slots]
         sums[0] = sums[0] + x.astype(jnp.float32)
         if tick + 1 < ticks:
             sums = lax.optimization_barrier([part.astype(jnp.bfloat16) for part in sums])
             sums = [to_next(part, tick + 1, step) for step, part in enumerate(sums)]
         else:
             sums[1:] = [to_chip(part.astype(jnp.bfloat16), step) for step, part in enumerate(sums) if step > 0]
-        state = summed(sums[::-1] if tick + 1 < ticks else sums)
         if tick + 1 < ticks:
-            state = jnp.where((section == 0) & (role_at(tick + 1) == 0), entering[tick], state)
+            state, normed = next_rows(tick + 1, gains[0], entering[tick], sums[::-1])
+        else:
+            state = summed(sums[::-1])
 
     role = role_at(ticks - 1)
     kept = jnp.where(core == 0, state[:rows], state[rows:])

time: 55.2 us -> 52.8 us (0.957)
  waiting for transfers between devices: 20 us -> 17.4 us
  starting transfers between devices: 25 us -> 26.8 us
  other arithmetic: 1.63 us -> 0.88 us
  matrix products: 0.93 us -> 0.28 us
    ppermute x8, waiting for transfers between devices: 8.22 us -> 6.27 us  [to_next(): return lax.ppermute(value, both, pairs)]
    ppermute x6 -> x12, starting transfers between devices: 3.17 us -> 5 us  [to_sibling(): return lax.ppermute(value, 'zero', [(k, k ^ 1) for k in range(zero)])]
    select_n x1, other arithmetic: 0.78 us -> 0.02 us  [on_device(): given = jnp.where(was_down, ascended, down_out[0])]
    dot_general x1, matrix products: 0.93 us -> 0.28 us  [on_device(): jnp.einsum('tn,nrd->trd', chosen, feeds, preferred_element_type=jnp.float32)]
    ppermute x6 -> x12, waiting for transfers between devices: 4.82 us -> 4.29 us  [to_sibling(): return lax.ppermute(value, 'zero', [(k, k ^ 1) for k in range(zero)])]
    pallas_call x6 -> x5, Pallas kernels: 5.48 us -> 5.42 us  [the longest x4 5.27 us: partial(): pl.pallas_call(functools.partial(group_kernel, tick, other, ready), out_s...]
  transfers between devices with their start and end apart: 20 -> 26, of which waited for: 15 -> 16; matrix products, arithmetic and copies ran while one was open for 0% -> 0% of each run, Pallas kernels for 5% -> 5%
where the time goes in v4:
time: 52.8 us; the launch traced here: 52.6 us
  starting transfers between devices  26.8 us (51%)
  waiting for transfers between devices  17.4 us (33%)
  Pallas kernels  5.46 us (10%)
  between operations  0.98 us (2%)
  other arithmetic  0.88 us (2%)
  local copies, waits for them, and re-layouts  0.84 us (2%)
    ppermute x8, starting transfers between devices, to_next(): return lax.ppermute(value, both, pairs)  14.7 us
    ppermute x6, starting transfers between devices, to_chip(): return lax.ppermute(value, 'zero', pairs)  7.11 us
    ppermute x6, waiting for transfers between devices, to_chip(): return lax.ppermute(value, 'zero', pairs)  6.84 us
    ppermute x8, waiting for transfers between devices, to_next(): return lax.ppermute(value, both, pairs)  6.27 us
    pallas_call x4, Pallas kernels, partial(): pl.pallas_call(functools.partial(group_kernel, tick, other, ready), out_s...  5.27 us
    ppermute x12, starting transfers between devices, to_sibling(): return lax.ppermute(value, 'zero', [(k, k ^ 1) for k in range(zero)])  5 us
    ppermute x12, waiting for transfers between devices, to_sibling(): return lax.ppermute(value, 'zero', [(k, k ^ 1) for k in range(zero)])  4.29 us
  transfers between devices with their start and end apart: 26, of which 16 were waited for; matrix products, arithmetic and copies ran while one was open for 0% of the time, Pallas kernels for 5%

profile of v4, /device:TPU:0, one launch (start us, length us, event | category | flops | bytes accessed | tf_op | source)
XLA Modules:
  0.0 52.6 jit_solution(14442832275402758127)
XLA Ops:
  0.7 0.7 %copy-done = bf16[2,8,2048]{2,1,0:T(8,128)(2,1)S(1)} copy-done((bf16[2,8,2048]{2,1,0:T(8,128)(2,1)S(1)}, bf16[2,8,2048]{2,1,0:T(8,128)(2,1)}, u32[]{:S(2)}) %copy-start) | copy-done | bytes 65560
  1.8 0.5 collective-permute-start
  2.4 0.9 %collective-permute-done = bf16[16,2048]{1,0:T(8,128)(2,1)S(1)} collective-permute-done((bf16[16,2048]{1,0:T(8,128)(2,1)S(1)}, bf16[16,2048]{1,0:T(8,128)(2,1)S(1)}, u32[]{:S(2)}, u32[]{:S(2)}) %collective-permute-start) | collective-permute-done | bytes 65568 | tf_op jit(solution)/shard_map/ppermute | solution.py:123
  3.3 3.9 %collective-permute-start.1 = (bf16[16,2048]{1,0:T(8,128)(2,1)S(1)}, bf16[16,2048]{1,0:T(8,128)(2,1)S(1)}, u32[]{:S(2)}, u32[]{:S(2)}) collective-permute-start(bf16[16,2048]{1,0:T(8,128)(2,1)S(1)} %pad_maximum_fusion.2.x_ref), channel_id=1, source_target_pairs={{0,6},{2,4},{4,2},{6,0},{1,15},{3,13},{5,11},{7,9},{8,22},{10,20},... | collective-permute-start | bytes 196616 | tf_op jit(solution)/shard_map/ppermute | solution.py:137
  7.2 0.5 collective-permute-start.2
  7.8 0.7 %collective-permute-start.4 = (bf16[16,2048]{1,0:T(8,128)(2,1)S(1)}, bf16[16,2048]{1,0:T(8,128)(2,1)S(1)}, u32[]{:S(2)}, u32[]{:S(2)}) collective-permute-start(bf16[16,2048]{1,0:T(8,128)(2,1)S(1)} %pad_maximum_fusion.2.x_ref), channel_id=1, source_target_pairs={{0,0},{2,2},{4,4},{6,6},{1,9},{3,11},{5,13},{7,15},{8,16},{10,18},... | collective-permute-start | bytes 196616 | tf_op jit(solution)/shard_map/ppermute | solution.py:137
  8.5 1.6 %collective-permute-done.1.refs_0_ = bf16[16,2048]{1,0:T(8,128)(2,1)S(1)} collective-permute-done((bf16[16,2048]{1,0:T(8,128)(2,1)S(1)}, bf16[16,2048]{1,0:T(8,128)(2,1)S(1)}, u32[]{:S(2)}, u32[]{:S(2)}) %collective-permute-start.1) | collective-permute-done | bytes 65568 | tf_op jit(solution)/shard_map/ppermute | solution.py:137
  10.2 1.6 %collective-permute-start.5 = (bf16[16,2048]{1,0:T(8,128)(2,1)S(1)}, bf16[16,2048]{1,0:T(8,128)(2,1)S(1)}, u32[]{:S(2)}, u32[]{:S(2)}) collective-permute-start(bf16[16,2048]{1,0:T(8,128)(2,1)S(1)} %collective-permute-done.1.refs_0_), channel_id=1, source_target_pairs={{0,1},{1,0},{2,3},{3,2},{4,5},{5,4},{6,7},{7,6},{8,9},{9,8},{10,11... | collective-permute-start | bytes 196616 | tf_op jit(solution)/shard_map/ppermute | solution.py:123
  12.1 0.6 %collective-permute-done.3.refs_2_ = bf16[16,2048]{1,0:T(8,128)(2,1)S(1)} collective-permute-done((bf16[16,2048]{1,0:T(8,128)(2,1)S(1)}, bf16[16,2048]{1,0:T(8,128)(2,1)S(1)}, u32[]{:S(2)}, u32[]{:S(2)}) %collective-permute-start.3) | collective-permute-done | bytes 65568 | tf_op jit(solution)/shard_map/ppermute | solution.py:137
  12.7 1.8 %collective-permute-start.8 = (bf16[16,2048]{1,0:T(8,128)(2,1)S(1)}, bf16[16,2048]{1,0:T(8,128)(2,1)S(1)}, u32[]{:S(2)}, u32[]{:S(2)}) collective-permute-start(bf16[16,2048]{1,0:T(8,128)(2,1)S(1)} %collective-permute-done.4.refs_3_), channel_id=1, source_target_pairs={{0,1},{1,0},{2,3},{3,2},{4,5},{5,4},{6,7},{7,6},{8,9},{9,8},{10,11... | collective-permute-start | bytes 196616 | tf_op jit(solution)/shard_map/ppermute | solution.py:123
  14.5 0.9 %collective-permute-done.8.refs_3_ = bf16[16,2048]{1,0:T(8,128)(2,1)S(1)} collective-permute-done((bf16[16,2048]{1,0:T(8,128)(2,1)S(1)}, bf16[16,2048]{1,0:T(8,128)(2,1)S(1)}, u32[]{:S(2)}, u32[]{:S(2)}) %collective-permute-start.8) | collective-permute-done | bytes 65568 | tf_op jit(solution)/shard_map/ppermute | solution.py:123
  15.4 1.4 %shard_map.98 = bf16[64,2048]{1,0:T(8,128)(2,1)S(1)} custom-call(bf16[16,2048]{1,0:T(8,128)(2,1)S(1)} %shard_map.96.mark_ref, f32[2,2048]{1,0:T(2,128)S(1)} %bitcast.31, bf16[2,2048,512]{2,1,0:T(8,128)(2,1)S(1)} %bitcast.19, bf16[2,2048,512]{2,1,0:T(8,128)(2,1)S(1)} %bitcast.23, bf16[2,512,2048]{2,1,0:T(8,128)(2,1)S(1)} %bitcast.27, ...), custom_call_target="tpu_custom_call" | custom-call | flops 402653184 | bytes 6291456 | tf_op jit(solution)/shard_map/pallas_call | solution.py:98
  17.2 1.4 %shard_map.97 = f32[64,2048]{1,0:T(8,128)S(1)} custom-call(bf16[16,2048]{1,0:T(8,128)(2,1)S(1)} %shard_map.96.mark_ref, f32[2,2048]{1,0:T(2,128)S(1)} %bitcast.32, bf16[2,2048,512]{2,1,0:T(8,128)(2,1)S(1)} %bitcast.20, bf16[2,2048,512]{2,1,0:T(8,128)(2,1)S(1)} %bitcast.24, bf16[2,512,2048]{2,1,0:T(8,128)(2,1)S(1)} %bitcast.28, ...), custom_call_target="tpu_custom_call" | custom-call | flops 402653184 | bytes 6291456 | tf_op jit(solution)/shard_map/pallas_call | solution.py:98
  18.7 5.5 %collective-permute-start.10 = (bf16[16,2048]{1,0:T(8,128)(2,1)S(1)}, bf16[16,2048]{1,0:T(8,128)(2,1)S(1)}, u32[]{:S(2)}, u32[]{:S(2)}) collective-permute-start(bf16[16,2048]{1,0:T(8,128)(2,1)S(1)} %get-tuple-element.12), channel_id=1, source_target_pairs={{0,14},{2,12},{4,10},{6,8},{1,7},{3,5},{5,3},{7,1},{8,6},{10,4},{1... | collective-permute-start | bytes 196616 | tf_op jit(solution)/shard_map/ppermute | solution.py:137
  24.2 1.9 %collective-permute-start.12 = (bf16[16,2048]{1,0:T(8,128)(2,1)S(1)}, bf16[16,2048]{1,0:T(8,128)(2,1)S(1)}, u32[]{:S(2)}, u32[]{:S(2)}) collective-permute-start(bf16[16,2048]{1,0:T(8,128)(2,1)S(1)} %get-tuple-element.14), channel_id=1, source_target_pairs={{0,10},{2,8},{4,14},{6,12},{1,3},{3,1},{5,7},{7,5},{8,2},{10,0},{1... | collective-permute-start | bytes 196616 | tf_op jit(solution)/shard_map/ppermute | solution.py:137
  26.1 2.1 %collective-permute-start.13 = (bf16[16,2048]{1,0:T(8,128)(2,1)S(1)}, bf16[16,2048]{1,0:T(8,128)(2,1)S(1)}, u32[]{:S(2)}, u32[]{:S(2)}) collective-permute-start(bf16[16,2048]{1,0:T(8,128)(2,1)S(1)} %fusion), channel_id=1, source_target_pairs={{0,8},{2,10},{4,12},{6,14},{1,1},{3,3},{5,5},{7,7},{8,0},{10,2},{1... | collective-permute-start | bytes 196616 | tf_op jit(solution)/shard_map/ppermute | solution.py:137
  28.2 1.4 %collective-permute-done.11.refs_1_ = bf16[16,2048]{1,0:T(8,128)(2,1)S(1)} collective-permute-done((bf16[16,2048]{1,0:T(8,128)(2,1)S(1)}, bf16[16,2048]{1,0:T(8,128)(2,1)S(1)}, u32[]{:S(2)}, u32[]{:S(2)}) %collective-permute-start.11) | collective-permute-done | bytes 65568 | tf_op jit(solution)/shard_map/ppermute | solution.py:137
  29.6 2.6 %collective-permute-done.13.refs_3_ = bf16[16,2048]{1,0:T(8,128)(2,1)S(1)} collective-permute-done((bf16[16,2048]{1,0:T(8,128)(2,1)S(1)}, bf16[16,2048]{1,0:T(8,128)(2,1)S(1)}, u32[]{:S(2)}, u32[]{:S(2)}) %collective-permute-start.13) | collective-permute-done | bytes 65568 | tf_op jit(solution)/shard_map/ppermute | solution.py:137
  32.4 2.5 %collective-permute-start.14 = (bf16[16,2048]{1,0:T(8,128)(2,1)S(1)}, bf16[16,2048]{1,0:T(8,128)(2,1)S(1)}, u32[]{:S(2)}, u32[]{:S(2)}) collective-permute-start(bf16[16,2048]{1,0:T(8,128)(2,1)S(1)} %get-tuple-element.17.refs_3_), channel_id=1, source_target_pairs={{0,6},{1,7},{2,4},{3,5},{4,2},{5,3},{6,0},{7,1},{8,14},{9,15},{10,... | collective-permute-start | bytes 196616 | tf_op jit(solution)/shard_map/ppermute | solution.py:127
  35.5 0.5 %collective-permute-start.16 = (bf16[16,2048]{1,0:T(8,128)(2,1)S(1)}, bf16[16,2048]{1,0:T(8,128)(2,1)S(1)}, u32[]{:S(2)}, u32[]{:S(2)}) collective-permute-start(bf16[16,2048]{1,0:T(8,128)(2,1)S(1)} %get-tuple-element.17.refs_3_), channel_id=1, source_target_pairs={{0,2},{1,3},{2,0},{3,1},{4,6},{5,7},{6,4},{7,5},{8,10},{9,11},{10,... | collective-permute-start | bytes 196616 | tf_op jit(solution)/shard_map/ppermute | solution.py:127
  36.0 1.7 %collective-permute-done.14.refs_0_ = bf16[16,2048]{1,0:T(8,128)(2,1)S(1)} collective-permute-done((bf16[16,2048]{1,0:T(8,128)(2,1)S(1)}, bf16[16,2048]{1,0:T(8,128)(2,1)S(1)}, u32[]{:S(2)}, u32[]{:S(2)}) %collective-permute-start.14) | collective-permute-done | bytes 65568 | tf_op jit(solution)/shard_map/ppermute | solution.py:127
  37.7 1.5 %collective-permute-done.15.refs_1_ = bf16[16,2048]{1,0:T(8,128)(2,1)S(1)} collective-permute-done((bf16[16,2048]{1,0:T(8,128)(2,1)S(1)}, bf16[16,2048]{1,0:T(8,128)(2,1)S(1)}, u32[]{:S(2)}, u32[]{:S(2)}) %collective-permute-start.15) | collective-permute-done | bytes 65568 | tf_op jit(solution)/shard_map/ppermute | solution.py:127
  39.8 0.7 %collective-permute-done.18.refs_1_ = bf16[16,2048]{1,0:T(8,128)(2,1)S(1)} collective-permute-done((bf16[16,2048]{1,0:T(8,128)(2,1)S(1)}, bf16[16,2048]{1,0:T(8,128)(2,1)S(1)}, u32[]{:S(2)}, u32[]{:S(2)}) %collective-permute-start.18) | collective-permute-done | bytes 65568 | tf_op jit(solution)/shard_map/ppermute | solution.py:123
  41.0 1.3 %shard_map.102 = bf16[64,2048]{1,0:T(8,128)(2,1)S(1)} custom-call(bf16[16,2048]{1,0:T(8,128)(2,1)S(1)} %shard_map.100.mark_ref, f32[2,2048]{1,0:T(2,128)S(1)} %bitcast.34, bf16[2,2048,512]{2,1,0:T(8,128)(2,1)S(1)} %bitcast.21, bf16[2,2048,512]{2,1,0:T(8,128)(2,1)S(1)} %bitcast.25, bf16[2,512,2048]{2,1,0:T(8,128)(2,1)S(1)} %bitcast.29, ...), custom_call_target="tpu_custom_call" | custom-call | flops 402653184 | bytes 6291456 | tf_op jit(solution)/shard_map/pallas_call | solution.py:98
  42.5 1.3 %shard_map.101 = f32[64,2048]{1,0:T(8,128)S(1)} custom-call(bf16[16,2048]{1,0:T(8,128)(2,1)S(1)} %shard_map.100.mark_ref, f32[2,2048]{1,0:T(2,128)S(1)} %bitcast.35, bf16[2,2048,512]{2,1,0:T(8,128)(2,1)S(1)} %bitcast.22, bf16[2,2048,512]{2,1,0:T(8,128)(2,1)S(1)} %bitcast.26, bf16[2,512,2048]{2,1,0:T(8,128)(2,1)S(1)} %bitcast.30, ...), custom_call_target="tpu_custom_call" | custom-call | flops 402653184 | bytes 6291456 | tf_op jit(solution)/shard_map/pallas_call | solution.py:98
  44.0 1.6 %collective-permute-start.22 = (bf16[16,2048]{1,0:T(8,128)(2,1)S(1)}, bf16[16,2048]{1,0:T(8,128)(2,1)S(1)}, u32[]{:S(2)}, u32[]{:S(2)}) collective-permute-start(bf16[16,2048]{1,0:T(8,128)(2,1)S(1)} %get-tuple-element.24), channel_id=1, source_target_pairs={{0,6},{1,7},{2,4},{3,5},{4,2},{5,3},{6,0},{7,1},{8,14},{9,15},{10,... | collective-permute-start | bytes 196616 | tf_op jit(solution)/shard_map/ppermute | solution.py:127
  45.5 0.5 collective-permute-start.23
  46.0 1.5 %collective-permute-start.24 = (bf16[16,2048]{1,0:T(8,128)(2,1)S(1)}, bf16[16,2048]{1,0:T(8,128)(2,1)S(1)}, u32[]{:S(2)}, u32[]{:S(2)}) collective-permute-start(bf16[16,2048]{1,0:T(8,128)(2,1)S(1)} %get-tuple-element.22), channel_id=1, source_target_pairs={{0,2},{1,3},{2,0},{3,1},{4,6},{5,7},{6,4},{7,5},{8,10},{9,11},{10,... | collective-permute-start | bytes 196616 | tf_op jit(solution)/shard_map/ppermute | solution.py:127
  47.5 1.8 %collective-permute-done.22.refs_0_ = bf16[16,2048]{1,0:T(8,128)(2,1)S(1)} collective-permute-done((bf16[16,2048]{1,0:T(8,128)(2,1)S(1)}, bf16[16,2048]{1,0:T(8,128)(2,1)S(1)}, u32[]{:S(2)}, u32[]{:S(2)}) %collective-permute-start.22) | collective-permute-done | bytes 65568 | tf_op jit(solution)/shard_map/ppermute | solution.py:127
  49.3 1.3 %collective-permute-done.23.refs_1_ = bf16[16,2048]{1,0:T(8,128)(2,1)S(1)} collective-permute-done((bf16[16,2048]{1,0:T(8,128)(2,1)S(1)}, bf16[16,2048]{1,0:T(8,128)(2,1)S(1)}, u32[]{:S(2)}, u32[]{:S(2)}) %collective-permute-start.23) | collective-permute-done | bytes 65568 | tf_op jit(solution)/shard_map/ppermute | solution.py:127
  50.8 1.2 %collective-permute-done.25 = bf16[8,2048]{1,0:T(8,128)(2,1)S(1)} collective-permute-done((bf16[8,2048]{1,0:T(8,128)(2,1)S(1)}, bf16[8,2048]{1,0:T(8,128)(2,1)S(1)}, u32[]{:S(2)}, u32[]{:S(2)}) %collective-permute-start.25) | collective-permute-done | bytes 32800 | tf_op jit(solution)/shard_map/ppermute | solution.py:123
  52.0 0.6 %select_bitcast_fusion = (bf16[1,8,2048]{2,1,0:T(8,128)(2,1)}, bf16[1,8,2048]{2,1,0:T(8,128)(2,1)}) fusion(bf16[8,2048]{1,0:T(8,128)(2,1)S(1)} %collective-permute-done.25, pred[]{:T(512)S(6)} %eq.37, bf16[16,2048]{1,0:T(8,128)(2,1)S(1)} %shard_map.103, pred[]{:T(512)S(6)} %eq.38), kind=kLoop, calls=%fused_computation.13 | loop fusion | flops 49152 | bytes 163842 | tf_op jit(solution)/shard_map/broadcast_in_dim | solution.py:191
  (62 shorter events, 3.7 us)
Async XLA Ops:
  0.7 1.1 %copy-start.5 = (bf16[1,8,2048]{2,1,0:T(8,128)(2,1)S(1)}, bf16[1,8,2048]{2,1,0:T(8,128)(2,1)}, u32[]{:S(2)}) copy-start(bf16[1,8,2048]{2,1,0:T(8,128)(2,1)} %param.8) | copy-start | bytes 98308
  0.7 1.1 %copy-start.6 = (bf16[1,8,2048]{2,1,0:T(8,128)(2,1)S(1)}, bf16[1,8,2048]{2,1,0:T(8,128)(2,1)}, u32[]{:S(2)}) copy-start(bf16[1,8,2048]{2,1,0:T(8,128)(2,1)} %param.9) | copy-start | bytes 98308
  1.8 1.4 %collective-permute-start = (bf16[16,2048]{1,0:T(8,128)(2,1)S(1)}, bf16[16,2048]{1,0:T(8,128)(2,1)S(1)}, u32[]{:S(2)}, u32[]{:S(2)}) collective-permute-start(bf16[16,2048]{1,0:T(8,128)(2,1)S(1)} %pad_maximum_fusion), channel_id=1, source_target_pairs={{0,1},{1,0},{2,3},{3,2},{4,5},{5,4},{6,7},{7,6},{8,9},{9,8},{10,11... | collective-permute-start | bytes 196616 | tf_op jit(solution)/shard_map/ppermute | solution.py:123
  3.3 12.1 %copy-start.1 = (bf16[1,2,2048,512]{3,2,1,0:T(8,128)(2,1)S(1)}, bf16[1,2,2048,512]{3,2,1,0:T(8,128)(2,1)}, u32[]{:S(2)}) copy-start(bf16[1,2,2048,512]{3,2,1,0:T(8,128)(2,1)} %param.13) | copy-start | bytes 12582916
  3.3 12.1 %copy-start.2 = (bf16[1,2,2048,512]{3,2,1,0:T(8,128)(2,1)S(1)}, bf16[1,2,2048,512]{3,2,1,0:T(8,128)(2,1)}, u32[]{:S(2)}) copy-start(bf16[1,2,2048,512]{3,2,1,0:T(8,128)(2,1)} %param.14) | copy-start | bytes 12582916
  3.3 12.1 %copy-start.3 = (bf16[1,2,512,2048]{3,2,1,0:T(8,128)(2,1)S(1)}, bf16[1,2,512,2048]{3,2,1,0:T(8,128)(2,1)}, u32[]{:S(2)}) copy-start(bf16[1,2,512,2048]{3,2,1,0:T(8,128)(2,1)} %param.15) | copy-start | bytes 12582916
  3.3 12.1 %copy-start.4 = (f32[1,2,2048]{2,1,0:T(2,128)S(1)}, f32[1,2,2048]{2,1,0:T(2,128)}, u32[]{:S(2)}) copy-start(f32[1,2,2048]{2,1,0:T(2,128)} %param.12) | copy-start | bytes 49156
  3.3 6.8 %collective-permute-start.1 = (bf16[16,2048]{1,0:T(8,128)(2,1)S(1)}, bf16[16,2048]{1,0:T(8,128)(2,1)S(1)}, u32[]{:S(2)}, u32[]{:S(2)}) collective-permute-start(bf16[16,2048]{1,0:T(8,128)(2,1)S(1)} %pad_maximum_fusion.2.x_ref), channel_id=1, source_target_pairs={{0,6},{2,4},{4,2},{6,0},{1,15},{3,13},{5,11},{7,9},{8,22},{10,20},... | collective-permute-start | bytes 196616 | tf_op jit(solution)/shard_map/ppermute | solution.py:137
  7.2 4.5 %collective-permute-start.2 = (bf16[16,2048]{1,0:T(8,128)(2,1)S(1)}, bf16[16,2048]{1,0:T(8,128)(2,1)S(1)}, u32[]{:S(2)}, u32[]{:S(2)}) collective-permute-start(bf16[16,2048]{1,0:T(8,128)(2,1)S(1)} %pad_maximum_fusion.2.x_ref), channel_id=1, source_target_pairs={{0,4},{2,6},{4,0},{6,2},{1,13},{3,15},{5,9},{7,11},{8,20},{10,22},... | collective-permute-start | bytes 196616 | tf_op jit(solution)/shard_map/ppermute | solution.py:137
  7.7 5.0 %collective-permute-start.3 = (bf16[16,2048]{1,0:T(8,128)(2,1)S(1)}, bf16[16,2048]{1,0:T(8,128)(2,1)S(1)}, u32[]{:S(2)}, u32[]{:S(2)}) collective-permute-start(bf16[16,2048]{1,0:T(8,128)(2,1)S(1)} %pad_maximum_fusion.2.x_ref), channel_id=1, source_target_pairs={{0,2},{2,0},{4,6},{6,4},{1,11},{3,9},{5,15},{7,13},{8,18},{10,16},... | collective-permute-start | bytes 196616 | tf_op jit(solution)/shard_map/ppermute | solution.py:137
  7.8 4.8 %collective-permute-start.4 = (bf16[16,2048]{1,0:T(8,128)(2,1)S(1)}, bf16[16,2048]{1,0:T(8,128)(2,1)S(1)}, u32[]{:S(2)}, u32[]{:S(2)}) collective-permute-start(bf16[16,2048]{1,0:T(8,128)(2,1)S(1)} %pad_maximum_fusion.2.x_ref), channel_id=1, source_target_pairs={{0,0},{2,2},{4,4},{6,6},{1,9},{3,11},{5,13},{7,15},{8,16},{10,18},... | collective-permute-start | bytes 196616 | tf_op jit(solution)/shard_map/ppermute | solution.py:137
  10.2 4.3 %collective-permute-start.5 = (bf16[16,2048]{1,0:T(8,128)(2,1)S(1)}, bf16[16,2048]{1,0:T(8,128)(2,1)S(1)}, u32[]{:S(2)}, u32[]{:S(2)}) collective-permute-start(bf16[16,2048]{1,0:T(8,128)(2,1)S(1)} %collective-permute-done.1.refs_0_), channel_id=1, source_target_pairs={{0,1},{1,0},{2,3},{3,2},{4,5},{5,4},{6,7},{7,6},{8,9},{9,8},{10,11... | collective-permute-start | bytes 196616 | tf_op jit(solution)/shard_map/ppermute | solution.py:123
  11.8 2.7 %collective-permute-start.6 = (bf16[16,2048]{1,0:T(8,128)(2,1)S(1)}, bf16[16,2048]{1,0:T(8,128)(2,1)S(1)}, u32[]{:S(2)}, u32[]{:S(2)}) collective-permute-start(bf16[16,2048]{1,0:T(8,128)(2,1)S(1)} %collective-permute-done.2.refs_1_), channel_id=1, source_target_pairs={{0,1},{1,0},{2,3},{3,2},{4,5},{5,4},{6,7},{7,6},{8,9},{9,8},{10,11... | collective-permute-start | bytes 196616 | tf_op jit(solution)/shard_map/ppermute | solution.py:123
  12.7 1.8 %collective-permute-start.7 = (bf16[16,2048]{1,0:T(8,128)(2,1)S(1)}, bf16[16,2048]{1,0:T(8,128)(2,1)S(1)}, u32[]{:S(2)}, u32[]{:S(2)}) collective-permute-start(bf16[16,2048]{1,0:T(8,128)(2,1)S(1)} %collective-permute-done.3.refs_2_), channel_id=1, source_target_pairs={{0,1},{1,0},{2,3},{3,2},{4,5},{5,4},{6,7},{7,6},{8,9},{9,8},{10,11... | collective-permute-start | bytes 196616 | tf_op jit(solution)/shard_map/ppermute | solution.py:123
  12.7 2.7 %collective-permute-start.8 = (bf16[16,2048]{1,0:T(8,128)(2,1)S(1)}, bf16[16,2048]{1,0:T(8,128)(2,1)S(1)}, u32[]{:S(2)}, u32[]{:S(2)}) collective-permute-start(bf16[16,2048]{1,0:T(8,128)(2,1)S(1)} %collective-permute-done.4.refs_3_), channel_id=1, source_target_pairs={{0,1},{1,0},{2,3},{3,2},{4,5},{5,4},{6,7},{7,6},{8,9},{9,8},{10,11... | collective-permute-start | bytes 196616 | tf_op jit(solution)/shard_map/ppermute | solution.py:123
  16.8 1.8 %collective-permute-start.9 = (bf16[64,2048]{1,0:T(8,128)(2,1)S(1)}, bf16[64,2048]{1,0:T(8,128)(2,1)S(1)}, u32[]{:S(2)}, u32[]{:S(2)}) collective-permute-start(bf16[64,2048]{1,0:T(8,128)(2,1)S(1)} %shard_map.98), channel_id=1, source_target_pairs={{0,1},{1,0},{2,3},{3,2},{4,5},{5,4},{6,7},{7,6},{8,9},{9,8},{10,11... | collective-permute-start | bytes 786440 | tf_op jit(solution)/shard_map/ppermute | solution.py:123
  18.7 9.5 %collective-permute-start.10 = (bf16[16,2048]{1,0:T(8,128)(2,1)S(1)}, bf16[16,2048]{1,0:T(8,128)(2,1)S(1)}, u32[]{:S(2)}, u32[]{:S(2)}) collective-permute-start(bf16[16,2048]{1,0:T(8,128)(2,1)S(1)} %get-tuple-element.12), channel_id=1, source_target_pairs={{0,14},{2,12},{4,10},{6,8},{1,7},{3,5},{5,3},{7,1},{8,6},{10,4},{1... | collective-permute-start | bytes 196616 | tf_op jit(solution)/shard_map/ppermute | solution.py:137
  24.2 5.4 %collective-permute-start.11 = (bf16[16,2048]{1,0:T(8,128)(2,1)S(1)}, bf16[16,2048]{1,0:T(8,128)(2,1)S(1)}, u32[]{:S(2)}, u32[]{:S(2)}) collective-permute-start(bf16[16,2048]{1,0:T(8,128)(2,1)S(1)} %get-tuple-element.13), channel_id=1, source_target_pairs={{0,12},{2,14},{4,8},{6,10},{1,5},{3,7},{5,1},{7,3},{8,4},{10,6},{1... | collective-permute-start | bytes 196616 | tf_op jit(solution)/shard_map/ppermute | solution.py:137
  24.2 5.4 %collective-permute-start.12 = (bf16[16,2048]{1,0:T(8,128)(2,1)S(1)}, bf16[16,2048]{1,0:T(8,128)(2,1)S(1)}, u32[]{:S(2)}, u32[]{:S(2)}) collective-permute-start(bf16[16,2048]{1,0:T(8,128)(2,1)S(1)} %get-tuple-element.14), channel_id=1, source_target_pairs={{0,10},{2,8},{4,14},{6,12},{1,3},{3,1},{5,7},{7,5},{8,2},{10,0},{1... | collective-permute-start | bytes 196616 | tf_op jit(solution)/shard_map/ppermute | solution.py:137
  26.1 6.1 %collective-permute-start.13 = (bf16[16,2048]{1,0:T(8,128)(2,1)S(1)}, bf16[16,2048]{1,0:T(8,128)(2,1)S(1)}, u32[]{:S(2)}, u32[]{:S(2)}) collective-permute-start(bf16[16,2048]{1,0:T(8,128)(2,1)S(1)} %fusion), channel_id=1, source_target_pairs={{0,8},{2,10},{4,12},{6,14},{1,1},{3,3},{5,5},{7,7},{8,0},{10,2},{1... | collective-permute-start | bytes 196616 | tf_op jit(solution)/shard_map/ppermute | solution.py:137
  32.4 5.2 %collective-permute-start.14 = (bf16[16,2048]{1,0:T(8,128)(2,1)S(1)}, bf16[16,2048]{1,0:T(8,128)(2,1)S(1)}, u32[]{:S(2)}, u32[]{:S(2)}) collective-permute-start(bf16[16,2048]{1,0:T(8,128)(2,1)S(1)} %get-tuple-element.17.refs_3_), channel_id=1, source_target_pairs={{0,6},{1,7},{2,4},{3,5},{4,2},{5,3},{6,0},{7,1},{8,14},{9,15},{10,... | collective-permute-start | bytes 196616 | tf_op jit(solution)/shard_map/ppermute | solution.py:127
  35.0 4.3 %collective-permute-start.15 = (bf16[16,2048]{1,0:T(8,128)(2,1)S(1)}, bf16[16,2048]{1,0:T(8,128)(2,1)S(1)}, u32[]{:S(2)}, u32[]{:S(2)}) collective-permute-start(bf16[16,2048]{1,0:T(8,128)(2,1)S(1)} %get-tuple-element.17.refs_3_), channel_id=1, source_target_pairs={{0,4},{1,5},{2,6},{3,7},{4,0},{5,1},{6,2},{7,3},{8,12},{9,13},{10,... | collective-permute-start | bytes 196616 | tf_op jit(solution)/shard_map/ppermute | solution.py:127
  35.5 4.3 %collective-permute-start.16 = (bf16[16,2048]{1,0:T(8,128)(2,1)S(1)}, bf16[16,2048]{1,0:T(8,128)(2,1)S(1)}, u32[]{:S(2)}, u32[]{:S(2)}) collective-permute-start(bf16[16,2048]{1,0:T(8,128)(2,1)S(1)} %get-tuple-element.17.refs_3_), channel_id=1, source_target_pairs={{0,2},{1,3},{2,0},{3,1},{4,6},{5,7},{6,4},{7,5},{8,10},{9,11},{10,... | collective-permute-start | bytes 196616 | tf_op jit(solution)/shard_map/ppermute | solution.py:127
  36.0 3.7 %collective-permute-start.20 = (bf16[16,2048]{1,0:T(8,128)(2,1)S(1)}, bf16[16,2048]{1,0:T(8,128)(2,1)S(1)}, u32[]{:S(2)}, u32[]{:S(2)}) collective-permute-start(bf16[16,2048]{1,0:T(8,128)(2,1)S(1)} %get-tuple-element.17.refs_3_), channel_id=1, source_target_pairs={{0,1},{1,0},{2,3},{3,2},{4,5},{5,4},{6,7},{7,6},{8,9},{9,8},{10,11... | collective-permute-start | bytes 196616 | tf_op jit(solution)/shard_map/ppermute | solution.py:123
  37.7 2.1 %collective-permute-start.17 = (bf16[16,2048]{1,0:T(8,128)(2,1)S(1)}, bf16[16,2048]{1,0:T(8,128)(2,1)S(1)}, u32[]{:S(2)}, u32[]{:S(2)}) collective-permute-start(bf16[16,2048]{1,0:T(8,128)(2,1)S(1)} %collective-permute-done.14.refs_0_), channel_id=1, source_target_pairs={{0,1},{1,0},{2,3},{3,2},{4,5},{5,4},{6,7},{7,6},{8,9},{9,8},{10,11... | collective-permute-start | bytes 196616 | tf_op jit(solution)/shard_map/ppermute | solution.py:123
  39.2 1.3 %collective-permute-start.18 = (bf16[16,2048]{1,0:T(8,128)(2,1)S(1)}, bf16[16,2048]{1,0:T(8,128)(2,1)S(1)}, u32[]{:S(2)}, u32[]{:S(2)}) collective-permute-start(bf16[16,2048]{1,0:T(8,128)(2,1)S(1)} %collective-permute-done.15.refs_1_), channel_id=1, source_target_pairs={{0,1},{1,0},{2,3},{3,2},{4,5},{5,4},{6,7},{7,6},{8,9},{9,8},{10,11... | collective-permute-start | bytes 196616 | tf_op jit(solution)/shard_map/ppermute | solution.py:123
  39.7 1.3 %collective-permute-start.19 = (bf16[16,2048]{1,0:T(8,128)(2,1)S(1)}, bf16[16,2048]{1,0:T(8,128)(2,1)S(1)}, u32[]{:S(2)}, u32[]{:S(2)}) collective-permute-start(bf16[16,2048]{1,0:T(8,128)(2,1)S(1)} %collective-permute-done.16.refs_2_), channel_id=1, source_target_pairs={{0,1},{1,0},{2,3},{3,2},{4,5},{5,4},{6,7},{7,6},{8,9},{9,8},{10,11... | collective-permute-start | bytes 196616 | tf_op jit(solution)/shard_map/ppermute | solution.py:123
  42.3 1.6 %collective-permute-start.21 = (bf16[64,2048]{1,0:T(8,128)(2,1)S(1)}, bf16[64,2048]{1,0:T(8,128)(2,1)S(1)}, u32[]{:S(2)}, u32[]{:S(2)}) collective-permute-start(bf16[64,2048]{1,0:T(8,128)(2,1)S(1)} %shard_map.102), channel_id=1, source_target_pairs={{0,1},{1,0},{2,3},{3,2},{4,5},{5,4},{6,7},{7,6},{8,9},{9,8},{10,11... | collective-permute-start | bytes 786440 | tf_op jit(solution)/shard_map/ppermute | solution.py:123
  44.0 5.3 %collective-permute-start.22 = (bf16[16,2048]{1,0:T(8,128)(2,1)S(1)}, bf16[16,2048]{1,0:T(8,128)(2,1)S(1)}, u32[]{:S(2)}, u32[]{:S(2)}) collective-permute-start(bf16[16,2048]{1,0:T(8,128)(2,1)S(1)} %get-tuple-element.24), channel_id=1, source_target_pairs={{0,6},{1,7},{2,4},{3,5},{4,2},{5,3},{6,0},{7,1},{8,14},{9,15},{10,... | collective-permute-start | bytes 196616 | tf_op jit(solution)/shard_map/ppermute | solution.py:127
  45.5 5.1 %collective-permute-start.23 = (bf16[16,2048]{1,0:T(8,128)(2,1)S(1)}, bf16[16,2048]{1,0:T(8,128)(2,1)S(1)}, u32[]{:S(2)}, u32[]{:S(2)}) collective-permute-start(bf16[16,2048]{1,0:T(8,128)(2,1)S(1)} %get-tuple-element.23), channel_id=1, source_target_pairs={{0,4},{1,5},{2,6},{3,7},{4,0},{5,1},{6,2},{7,3},{8,12},{9,13},{10,... | collective-permute-start | bytes 196616 | tf_op jit(solution)/shard_map/ppermute | solution.py:127
  46.0 4.6 %collective-permute-start.24 = (bf16[16,2048]{1,0:T(8,128)(2,1)S(1)}, bf16[16,2048]{1,0:T(8,128)(2,1)S(1)}, u32[]{:S(2)}, u32[]{:S(2)}) collective-permute-start(bf16[16,2048]{1,0:T(8,128)(2,1)S(1)} %get-tuple-element.22), channel_id=1, source_target_pairs={{0,2},{1,3},{2,0},{3,1},{4,6},{5,7},{6,4},{7,5},{8,10},{9,11},{10,... | collective-permute-start | bytes 196616 | tf_op jit(solution)/shard_map/ppermute | solution.py:127
  50.7 1.3 %collective-permute-start.25 = (bf16[8,2048]{1,0:T(8,128)(2,1)S(1)}, bf16[8,2048]{1,0:T(8,128)(2,1)S(1)}, u32[]{:S(2)}, u32[]{:S(2)}) collective-permute-start(bf16[8,2048]{1,0:T(8,128)(2,1)S(1)} %broadcast_select_fusion), channel_id=1, source_target_pairs={{0,1},{1,0},{2,3},{3,2},{4,5},{5,4},{6,7},{7,6},{8,9},{9,8},{10,11... | collective-permute-start | bytes 98312 | tf_op jit(solution)/shard_map/ppermute | solution.py:123
  (2 other events, 1.6 us)

commit v5 on v4

--- a/solution.py
+++ b/solution.py
@@ -22,15 +22,26 @@
     return (lax.axis_index("pipe") + lax.axis_index("zero") % CORES + tick) % 2
 
 
-def group_kernel(tick, other, ready, mark_ref, gains_ref, gate_ref, up_ref, down_ref, *refs):
+def group_kernel(tick, other, ready, count, chips, mark_ref, gains_ref, gate_ref, up_ref, down_ref, *refs):
     group = (role_at(tick) + other) % 2
-    normed = jnp.concatenate([ref[...] for ref in refs[:-1]], axis=0)
+    pieces, outs = refs[:count], refs[count:]
+    normed = jnp.concatenate([ref[...] for ref in pieces], axis=0)
     if not ready:
         normed = normalize(normed, gains_ref[pl.ds(group, 1), :])
     gate = jnp.dot(normed, gate_ref[group], preferred_element_type=jnp.float32)
     up = jnp.dot(normed, up_ref[group], preferred_element_type=jnp.float32)
     hidden = (gate / (1.0 + jnp.exp(-gate)) * up).astype(jnp.bfloat16)
-    refs[-1][...] = jnp.dot(hidden, down_ref[group], preferred_element_type=jnp.float32).astype(refs[-1].dtype)
+    part = jnp.dot(hidden, down_ref[group], preferred_element_type=jnp.float32)
+    if len(outs) == 1:
+        outs[0][...] = part.astype(outs[0].dtype)
+        return
+    first_core = lax.axis_index("zero") % CORES == 0
+    rows = part.shape[0] // (CORES * chips)
+    halves = [part[n * rows : (n + 1) * rows] for n in range(CORES * chips)]
+    keep = [jnp.where(first_core, a, b) for a, b in zip(halves[::2], halves[1::2])]
+    give = [jnp.where(first_core, b, a) for a, b in zip(halves[::2], halves[1::2])]
+    outs[0][...] = jnp.concatenate(keep, axis=0).astype(outs[0].dtype)
+    outs[1][...] = jnp.concatenate(give, axis=0).astype(outs[1].dtype)
 
 
 def pass_kernel(x_ref, out):
@@ -47,6 +58,24 @@
         compiler_params=pltpu.CompilerParams(vmem_limit_bytes=LIMIT),
         cost_estimate=pl.CostEstimate(flops=BESIDE, bytes_accessed=4 * x.size, transcendentals=0),
     )(x)
+
+
+def stack_kernel(mark_ref, *refs):
+    height = refs[0].shape[0]
+    for slot, ref in enumerate(refs[:-1]):
+        refs[-1][slot * height : (slot + 1) * height] = ref[...]
+
+
+def stacked(pieces, mark):
+    vmem = pl.BlockSpec(memory_space=pltpu.VMEM)
+    rows, width = mark.shape
+    return pl.pallas_call(
+        stack_kernel,
+        out_shape=jax.ShapeDtypeStruct((len(pieces) * rows, width), mark.dtype),
+        in_specs=[vmem] * (1 + len(pieces)),
+        out_specs=vmem,
+        compiler_params=pltpu.CompilerParams(vmem_limit_bytes=LIMIT),
+    )(mark, *pieces)
 
 
 def sum_kernel(*refs):
@@ -91,15 +120,18 @@
     )(gains, entering, *parts)
 
 
-def partial(tick, other, ready, pieces, gains, weights, mark):
-    vmem = pl.BlockSpec(memory_space=pltpu.VMEM)
-    rows, width = len(pieces) * mark.shape[0], mark.shape[1]
+def partial(tick, other, ready, split, chips, pieces, gains, weights, mark):
+    vmem = pl.BlockSpec(memory_space=pltpu.VMEM)
+    rows, width = chips * mark.shape[0], mark.shape[1]
     size = sum(w.size // w.shape[0] for w in weights)
-    return pl.pallas_call(
-        functools.partial(group_kernel, tick, other, ready),
-        out_shape=jax.ShapeDtypeStruct((rows, width), jnp.bfloat16 if other else jnp.float32),
+    out = jax.ShapeDtypeStruct((rows, width), jnp.bfloat16 if other else jnp.float32)
+    if split:
+        out = tuple(jax.ShapeDtypeStruct((rows // CORES, width), dtype) for dtype in (jnp.float32, jnp.bfloat16))
+    return pl.pallas_call(
+        functools.partial(group_kernel, tick, other, ready, len(pieces), chips),
+        out_shape=out,
         in_specs=[vmem] * (2 + len(weights) + len(pieces)),
-        out_specs=vmem,
+        out_specs=(vmem, vmem) if split else vmem,
         compiler_params=pltpu.CompilerParams(vmem_limit_bytes=LIMIT),
         cost_estimate=pl.CostEstimate(flops=2 * rows * size, bytes_accessed=2 * size, transcendentals=0),
     )(mark, gains, *weights, *pieces)
@@ -165,29 +197,36 @@
         x = pieces[0] if tick == 0 else state
         height = x.shape[0]
         mark = passed(state)
-        pieces = pieces[::-1]
+        slots = [step if chips & (chips - 1) == 0 else (chips - step) % chips for step in range(chips)]
+        if tick + 1 == ticks:
+            break
         siblings = [to_sibling(piece) for piece in pieces]
-        part = partial(tick, 0, tick > 0, pieces, gains[0], weights, mark)
-        given = partial(tick, 1, tick > 0, siblings, gains[0], weights, mark)
+        part = partial(tick, 0, tick > 0, False, chips, pieces, gains[0], weights, mark)
+        given = partial(tick, 1, tick > 0, False, chips, siblings, gains[0], weights, mark)
         part = part + to_sibling(given).astype(jnp.float32)
-        slots = [step if chips & (chips - 1) == 0 else (chips - step) % chips for step in range(chips)]
-        sums = [part[(chips - 1 - slot) * height : (chips - slot) * height] for slot in slots]
+        sums = [part[slot * height : (slot + 1) * height] for slot in slots]
         sums[0] = sums[0] + x.astype(jnp.float32)
-        if tick + 1 < ticks:
-            sums = lax.optimization_barrier([part.astype(jnp.bfloat16) for part in sums])
-            sums = [to_next(part, tick + 1, step) for step, part in enumerate(sums)]
-        else:
-            sums[1:] = [to_chip(part.astype(jnp.bfloat16), step) for step, part in enumerate(sums) if step > 0]
-        if tick + 1 < ticks:
-            state, normed = next_rows(tick + 1, gains[0], entering[tick], sums[::-1])
-        else:
-            state = summed(sums[::-1])
-
+        sums = lax.optimization_barrier([part.astype(jnp.bfloat16) for part in sums])
+        sums = [to_next(part, tick + 1, step) for step, part in enumerate(sums)]
+        state, normed = next_rows(tick + 1, gains[0], entering[tick], sums[::-1])
+
+    rows_here = jnp.where(core == 0, x[:rows], x[rows:])
+    rows_there = to_sibling(jnp.where(core == 0, x[rows:], x[:rows]))
+    stack = stacked(pieces, mark)
+    mine, given = partial(tick, 0, tick > 0, True, chips, [stack], gains[0], weights, mark)
+    theirs, back = partial(tick, 1, tick > 0, True, chips, [to_sibling(stack)], gains[0], weights, mark)
+    theirs = theirs + to_sibling(given).astype(jnp.float32)
+    mine = mine + to_sibling(back).astype(jnp.float32)
+    sums = [
+        jnp.concatenate([part[slot * rows : (slot + 1) * rows] for part in (mine, theirs)], axis=0) for slot in slots
+    ]
+    sums[0] = sums[0] + jnp.concatenate([rows_here, rows_there], axis=0).astype(jnp.float32)
+    sums[1:] = lax.optimization_barrier([part.astype(jnp.bfloat16) for part in sums[1:]])
+    sums[1:] = [to_chip(part, step) for step, part in enumerate(sums) if step > 0]
+    state = summed(sums[::-1])
     role = role_at(ticks - 1)
-    kept = jnp.where(core == 0, state[:rows], state[rows:])
-    received = to_sibling(jnp.where(core == 0, state[rows:], state[:rows]))
-    down_state = jnp.where(role == 0, kept, received)
-    up_state = jnp.where(role == 0, received, kept)
+    down_state = jnp.where(role == 0, state[:rows], state[rows:])
+    up_state = jnp.where(role == 0, state[rows:], state[:rows])
     return (down_state[None], up_state[None])
 
 

time: 52.8 us -> 52.4 us (level)
  waiting for transfers between devices: 17.4 us -> 15.9 us
  starting transfers between devices: 26.8 us -> 27.7 us
    ppermute x12 -> x10, waiting for transfers between devices: 4.29 us -> 2.71 us  [to_sibling(): return lax.ppermute(value, 'zero', [(k, k ^ 1) for k in range(zero)])]
    ppermute x12 -> x10, starting transfers between devices: 5 us -> 5.93 us  [to_sibling(): return lax.ppermute(value, 'zero', [(k, k ^ 1) for k in range(zero)])]
    pallas_call x4 -> x5, Pallas kernels: 5.27 us -> 5.32 us  [the longest x4 5.31 us: partial(): pl.pallas_call(functools.partial(group_kernel, tick, other, ready, len(pi...]
  transfers between devices with their start and end apart: 26 -> 24, of which waited for: 16 -> 13; matrix products, arithmetic and copies ran while one was open for 0% -> 0% of each run, Pallas kernels for 5% -> 8%
where the time goes in v5:
time: 52.4 us; the launch traced here: 52.2 us
  starting transfers between devices  27.7 us (53%)
  waiting for transfers between devices  15.9 us (30%)
  Pallas kernels  5.51 us (11%)
  between operations  1.01 us (2%)
  other arithmetic  0.89 us (2%)
  local copies, waits for them, and re-layouts  0.86 us (2%)
    ppermute x8, starting transfers between devices, to_next(): return lax.ppermute(value, both, pairs)  14.7 us
    ppermute x6, starting transfers between devices, to_chip(): return lax.ppermute(value, 'zero', pairs)  7.12 us
    ppermute x6, waiting for transfers between devices, to_chip(): return lax.ppermute(value, 'zero', pairs)  6.92 us
    ppermute x8, waiting for transfers between devices, to_next(): return lax.ppermute(value, both, pairs)  6.27 us
    ppermute x10, starting transfers between devices, to_sibling(): return lax.ppermute(value, 'zero', [(k, k ^ 1) for k in range(zero)])  5.93 us
    pallas_call x4, Pallas kernels, partial(): pl.pallas_call(functools.partial(group_kernel, tick, other, ready, len(pi...  5.31 us
    ppermute x10, waiting for transfers between devices, to_sibling(): return lax.ppermute(value, 'zero', [(k, k ^ 1) for k in range(zero)])  2.71 us
  transfers between devices with their start and end apart: 24, of which 13 were waited for; matrix products, arithmetic and copies ran while one was open for 0% of the time, Pallas kernels for 8%

profile of v5, /device:TPU:0, one launch (start us, length us, event | category | flops | bytes accessed | tf_op | source)
XLA Modules:
  0.0 52.2 jit_solution(12361267172913799825)
XLA Ops:
  0.7 0.7 %copy-done = bf16[2,8,2048]{2,1,0:T(8,128)(2,1)S(1)} copy-done((bf16[2,8,2048]{2,1,0:T(8,128)(2,1)S(1)}, bf16[2,8,2048]{2,1,0:T(8,128)(2,1)}, u32[]{:S(2)}) %copy-start) | copy-done | bytes 65560
  1.8 0.5 collective-permute-start
  2.4 0.9 %collective-permute-done = bf16[16,2048]{1,0:T(8,128)(2,1)S(1)} collective-permute-done((bf16[16,2048]{1,0:T(8,128)(2,1)S(1)}, bf16[16,2048]{1,0:T(8,128)(2,1)S(1)}, u32[]{:S(2)}, u32[]{:S(2)}) %collective-permute-start) | collective-permute-done | bytes 65568 | tf_op jit(solution)/shard_map/ppermute | solution.py:155
  3.3 3.9 %collective-permute-start.4 = (bf16[16,2048]{1,0:T(8,128)(2,1)S(1)}, bf16[16,2048]{1,0:T(8,128)(2,1)S(1)}, u32[]{:S(2)}, u32[]{:S(2)}) collective-permute-start(bf16[16,2048]{1,0:T(8,128)(2,1)S(1)} %pad_maximum_fusion.2.x_ref), channel_id=1, source_target_pairs={{0,6},{2,4},{4,2},{6,0},{1,15},{3,13},{5,11},{7,9},{8,22},{10,20},... | collective-permute-start | bytes 196616 | tf_op jit(solution)/shard_map/ppermute | solution.py:169
  7.8 0.7 %collective-permute-start.1 = (bf16[16,2048]{1,0:T(8,128)(2,1)S(1)}, bf16[16,2048]{1,0:T(8,128)(2,1)S(1)}, u32[]{:S(2)}, u32[]{:S(2)}) collective-permute-start(bf16[16,2048]{1,0:T(8,128)(2,1)S(1)} %pad_maximum_fusion.2.x_ref), channel_id=1, source_target_pairs={{0,0},{2,2},{4,4},{6,6},{1,9},{3,11},{5,13},{7,15},{8,16},{10,18},... | collective-permute-start | bytes 196616 | tf_op jit(solution)/shard_map/ppermute | solution.py:169
  8.5 1.6 %collective-permute-done.4.refs_3_ = bf16[16,2048]{1,0:T(8,128)(2,1)S(1)} collective-permute-done((bf16[16,2048]{1,0:T(8,128)(2,1)S(1)}, bf16[16,2048]{1,0:T(8,128)(2,1)S(1)}, u32[]{:S(2)}, u32[]{:S(2)}) %collective-permute-start.4) | collective-permute-done | bytes 65568 | tf_op jit(solution)/shard_map/ppermute | solution.py:169
  10.2 1.6 %collective-permute-start.8 = (bf16[16,2048]{1,0:T(8,128)(2,1)S(1)}, bf16[16,2048]{1,0:T(8,128)(2,1)S(1)}, u32[]{:S(2)}, u32[]{:S(2)}) collective-permute-start(bf16[16,2048]{1,0:T(8,128)(2,1)S(1)} %collective-permute-done.4.refs_3_), channel_id=1, source_target_pairs={{0,1},{1,0},{2,3},{3,2},{4,5},{5,4},{6,7},{7,6},{8,9},{9,8},{10,11... | collective-permute-start | bytes 196616 | tf_op jit(solution)/shard_map/ppermute | solution.py:155
  12.1 0.6 %collective-permute-done.2.refs_1_ = bf16[16,2048]{1,0:T(8,128)(2,1)S(1)} collective-permute-done((bf16[16,2048]{1,0:T(8,128)(2,1)S(1)}, bf16[16,2048]{1,0:T(8,128)(2,1)S(1)}, u32[]{:S(2)}, u32[]{:S(2)}) %collective-permute-start.2) | collective-permute-done | bytes 65568 | tf_op jit(solution)/shard_map/ppermute | solution.py:169
  12.7 1.8 %collective-permute-start.5 = (bf16[16,2048]{1,0:T(8,128)(2,1)S(1)}, bf16[16,2048]{1,0:T(8,128)(2,1)S(1)}, u32[]{:S(2)}, u32[]{:S(2)}) collective-permute-start(bf16[16,2048]{1,0:T(8,128)(2,1)S(1)} %collective-permute-done.1.refs_0_), channel_id=1, source_target_pairs={{0,1},{1,0},{2,3},{3,2},{4,5},{5,4},{6,7},{7,6},{8,9},{9,8},{10,11... | collective-permute-start | bytes 196616 | tf_op jit(solution)/shard_map/ppermute | solution.py:155
  14.5 0.9 %collective-permute-done.5.refs_0_ = bf16[16,2048]{1,0:T(8,128)(2,1)S(1)} collective-permute-done((bf16[16,2048]{1,0:T(8,128)(2,1)S(1)}, bf16[16,2048]{1,0:T(8,128)(2,1)S(1)}, u32[]{:S(2)}, u32[]{:S(2)}) %collective-permute-start.5) | collective-permute-done | bytes 65568 | tf_op jit(solution)/shard_map/ppermute | solution.py:155
  15.4 1.4 %shard_map.98 = bf16[64,2048]{1,0:T(8,128)(2,1)S(1)} custom-call(bf16[16,2048]{1,0:T(8,128)(2,1)S(1)} %shard_map.96.mark_ref, f32[2,2048]{1,0:T(2,128)S(1)} %bitcast.31, bf16[2,2048,512]{2,1,0:T(8,128)(2,1)S(1)} %bitcast.19, bf16[2,2048,512]{2,1,0:T(8,128)(2,1)S(1)} %bitcast.23, bf16[2,512,2048]{2,1,0:T(8,128)(2,1)S(1)} %bitcast.27, ...), custom_call_target="tpu_custom_call" | custom-call | flops 402653184 | bytes 6291456 | tf_op jit(solution)/shard_map/pallas_call | solution.py:130
  17.2 1.4 %shard_map.97 = f32[64,2048]{1,0:T(8,128)S(1)} custom-call(bf16[16,2048]{1,0:T(8,128)(2,1)S(1)} %shard_map.96.mark_ref, f32[2,2048]{1,0:T(2,128)S(1)} %bitcast.32, bf16[2,2048,512]{2,1,0:T(8,128)(2,1)S(1)} %bitcast.20, bf16[2,2048,512]{2,1,0:T(8,128)(2,1)S(1)} %bitcast.24, bf16[2,512,2048]{2,1,0:T(8,128)(2,1)S(1)} %bitcast.28, ...), custom_call_target="tpu_custom_call" | custom-call | flops 402653184 | bytes 6291456 | tf_op jit(solution)/shard_map/pallas_call | solution.py:130
  18.7 5.5 %collective-permute-start.10 = (bf16[16,2048]{1,0:T(8,128)(2,1)S(1)}, bf16[16,2048]{1,0:T(8,128)(2,1)S(1)}, u32[]{:S(2)}, u32[]{:S(2)}) collective-permute-start(bf16[16,2048]{1,0:T(8,128)(2,1)S(1)} %get-tuple-element.19), channel_id=1, source_target_pairs={{0,14},{2,12},{4,10},{6,8},{1,7},{3,5},{5,3},{7,1},{8,6},{10,4},{1... | collective-permute-start | bytes 196616 | tf_op jit(solution)/shard_map/ppermute | solution.py:169
  24.2 1.9 %collective-permute-start.12 = (bf16[16,2048]{1,0:T(8,128)(2,1)S(1)}, bf16[16,2048]{1,0:T(8,128)(2,1)S(1)}, u32[]{:S(2)}, u32[]{:S(2)}) collective-permute-start(bf16[16,2048]{1,0:T(8,128)(2,1)S(1)} %get-tuple-element.21), channel_id=1, source_target_pairs={{0,10},{2,8},{4,14},{6,12},{1,3},{3,1},{5,7},{7,5},{8,2},{10,0},{1... | collective-permute-start | bytes 196616 | tf_op jit(solution)/shard_map/ppermute | solution.py:169
  26.1 2.1 %collective-permute-start.13 = (bf16[16,2048]{1,0:T(8,128)(2,1)S(1)}, bf16[16,2048]{1,0:T(8,128)(2,1)S(1)}, u32[]{:S(2)}, u32[]{:S(2)}) collective-permute-start(bf16[16,2048]{1,0:T(8,128)(2,1)S(1)} %fusion), channel_id=1, source_target_pairs={{0,8},{2,10},{4,12},{6,14},{1,1},{3,3},{5,5},{7,7},{8,0},{10,2},{1... | collective-permute-start | bytes 196616 | tf_op jit(solution)/shard_map/ppermute | solution.py:169
  28.2 1.4 %collective-permute-done.11.refs_1_ = bf16[16,2048]{1,0:T(8,128)(2,1)S(1)} collective-permute-done((bf16[16,2048]{1,0:T(8,128)(2,1)S(1)}, bf16[16,2048]{1,0:T(8,128)(2,1)S(1)}, u32[]{:S(2)}, u32[]{:S(2)}) %collective-permute-start.11) | collective-permute-done | bytes 65568 | tf_op jit(solution)/shard_map/ppermute | solution.py:169
  29.6 2.6 %collective-permute-done.13.refs_3_ = bf16[16,2048]{1,0:T(8,128)(2,1)S(1)} collective-permute-done((bf16[16,2048]{1,0:T(8,128)(2,1)S(1)}, bf16[16,2048]{1,0:T(8,128)(2,1)S(1)}, u32[]{:S(2)}, u32[]{:S(2)}) %collective-permute-start.13) | collective-permute-done | bytes 65568 | tf_op jit(solution)/shard_map/ppermute | solution.py:169
  32.4 2.5 %collective-permute-start.16 = (bf16[16,2048]{1,0:T(8,128)(2,1)S(1)}, bf16[16,2048]{1,0:T(8,128)(2,1)S(1)}, u32[]{:S(2)}, u32[]{:S(2)}) collective-permute-start(bf16[16,2048]{1,0:T(8,128)(2,1)S(1)} %get-tuple-element.24.refs_0_), channel_id=1, source_target_pairs={{0,6},{1,7},{2,4},{3,5},{4,2},{5,3},{6,0},{7,1},{8,14},{9,15},{10,... | collective-permute-start | bytes 196616 | tf_op jit(solution)/shard_map/ppermute | solution.py:159
  35.5 0.5 %collective-permute-start.14 = (bf16[16,2048]{1,0:T(8,128)(2,1)S(1)}, bf16[16,2048]{1,0:T(8,128)(2,1)S(1)}, u32[]{:S(2)}, u32[]{:S(2)}) collective-permute-start(bf16[16,2048]{1,0:T(8,128)(2,1)S(1)} %get-tuple-element.24.refs_0_), channel_id=1, source_target_pairs={{0,2},{1,3},{2,0},{3,1},{4,6},{5,7},{6,4},{7,5},{8,10},{9,11},{10,... | collective-permute-start | bytes 196616 | tf_op jit(solution)/shard_map/ppermute | solution.py:159
  36.0 1.7 %collective-permute-done.16.refs_3_ = bf16[16,2048]{1,0:T(8,128)(2,1)S(1)} collective-permute-done((bf16[16,2048]{1,0:T(8,128)(2,1)S(1)}, bf16[16,2048]{1,0:T(8,128)(2,1)S(1)}, u32[]{:S(2)}, u32[]{:S(2)}) %collective-permute-start.16) | collective-permute-done | bytes 65568 | tf_op jit(solution)/shard_map/ppermute | solution.py:159
  37.7 1.5 %collective-permute-done.15.refs_2_ = bf16[16,2048]{1,0:T(8,128)(2,1)S(1)} collective-permute-done((bf16[16,2048]{1,0:T(8,128)(2,1)S(1)}, bf16[16,2048]{1,0:T(8,128)(2,1)S(1)}, u32[]{:S(2)}, u32[]{:S(2)}) %collective-permute-start.15) | collective-permute-done | bytes 65568 | tf_op jit(solution)/shard_map/ppermute | solution.py:159
  39.8 1.3 %shard_map.102 = (f32[32,2048]{1,0:T(8,128)S(1)}, bf16[32,2048]{1,0:T(8,128)(2,1)S(1)}) custom-call(bf16[16,2048]{1,0:T(8,128)(2,1)S(1)} %shard_map.100.mark_ref, f32[2,2048]{1,0:T(2,128)S(1)} %bitcast.34, bf16[2,2048,512]{2,1,0:T(8,128)(2,1)S(1)} %bitcast.21, bf16[2,2048,512]{2,1,0:T(8,128)(2,1)S(1)} %bitcast.25, bf16[2,512,2048]{2,1,0:T(8,128)(2,1)S(1)} %bitcast.29, ...), custom_call_target="tpu_custom_call" | custom-call | flops 402653184 | bytes 6291456 | tf_op jit(solution)/shard_map/pallas_call | solution.py:130
  41.1 0.5 %collective-permute-start.19 = (bf16[32,2048]{1,0:T(8,128)(2,1)S(1)}, bf16[32,2048]{1,0:T(8,128)(2,1)S(1)}, u32[]{:S(2)}, u32[]{:S(2)}) collective-permute-start(bf16[32,2048]{1,0:T(8,128)(2,1)S(1)} %get-tuple-element.28), channel_id=1, source_target_pairs={{0,1},{1,0},{2,3},{3,2},{4,5},{5,4},{6,7},{7,6},{8,9},{9,8},{10,11... | collective-permute-start | bytes 393224 | tf_op jit(solution)/shard_map/ppermute | solution.py:155
  41.8 1.3 %shard_map.103 = (f32[32,2048]{1,0:T(8,128)S(1)}, bf16[32,2048]{1,0:T(8,128)(2,1)S(1)}) custom-call(bf16[16,2048]{1,0:T(8,128)(2,1)S(1)} %shard_map.100.mark_ref, f32[2,2048]{1,0:T(2,128)S(1)} %bitcast.35, bf16[2,2048,512]{2,1,0:T(8,128)(2,1)S(1)} %bitcast.22, bf16[2,2048,512]{2,1,0:T(8,128)(2,1)S(1)} %bitcast.26, bf16[2,512,2048]{2,1,0:T(8,128)(2,1)S(1)} %bitcast.30, ...), custom_call_target="tpu_custom_call" | custom-call | flops 402653184 | bytes 6291456 | tf_op jit(solution)/shard_map/pallas_call | solution.py:130
  43.1 0.5 %collective-permute-start.18 = (bf16[32,2048]{1,0:T(8,128)(2,1)S(1)}, bf16[32,2048]{1,0:T(8,128)(2,1)S(1)}, u32[]{:S(2)}, u32[]{:S(2)}) collective-permute-start(bf16[32,2048]{1,0:T(8,128)(2,1)S(1)} %get-tuple-element.26), channel_id=1, source_target_pairs={{0,1},{1,0},{2,3},{3,2},{4,5},{5,4},{6,7},{7,6},{8,9},{9,8},{10,11... | collective-permute-start | bytes 393224 | tf_op jit(solution)/shard_map/ppermute | solution.py:155
  43.7 0.9 %collective-permute-done.18 = bf16[32,2048]{1,0:T(8,128)(2,1)S(1)} collective-permute-done((bf16[32,2048]{1,0:T(8,128)(2,1)S(1)}, bf16[32,2048]{1,0:T(8,128)(2,1)S(1)}, u32[]{:S(2)}, u32[]{:S(2)}) %collective-permute-start.18) | collective-permute-done | bytes 131104 | tf_op jit(solution)/shard_map/ppermute | solution.py:155
  44.7 1.6 %collective-permute-start.20 = (bf16[16,2048]{1,0:T(8,128)(2,1)S(1)}, bf16[16,2048]{1,0:T(8,128)(2,1)S(1)}, u32[]{:S(2)}, u32[]{:S(2)}) collective-permute-start(bf16[16,2048]{1,0:T(8,128)(2,1)S(1)} %pad_maximum_fusion.5), channel_id=1, source_target_pairs={{0,6},{1,7},{2,4},{3,5},{4,2},{5,3},{6,0},{7,1},{8,14},{9,15},{10,... | collective-permute-start | bytes 196616 | tf_op jit(solution)/shard_map/ppermute | solution.py:159
  46.3 0.5 collective-permute-start.21
  46.8 1.5 %collective-permute-start.22 = (bf16[16,2048]{1,0:T(8,128)(2,1)S(1)}, bf16[16,2048]{1,0:T(8,128)(2,1)S(1)}, u32[]{:S(2)}, u32[]{:S(2)}) collective-permute-start(bf16[16,2048]{1,0:T(8,128)(2,1)S(1)} %get-tuple-element.31), channel_id=1, source_target_pairs={{0,2},{1,3},{2,0},{3,1},{4,6},{5,7},{6,4},{7,5},{8,10},{9,11},{10,... | collective-permute-start | bytes 196616 | tf_op jit(solution)/shard_map/ppermute | solution.py:159
  48.3 1.8 %collective-permute-done.20.refs_0_ = bf16[16,2048]{1,0:T(8,128)(2,1)S(1)} collective-permute-done((bf16[16,2048]{1,0:T(8,128)(2,1)S(1)}, bf16[16,2048]{1,0:T(8,128)(2,1)S(1)}, u32[]{:S(2)}, u32[]{:S(2)}) %collective-permute-start.20) | collective-permute-done | bytes 65568 | tf_op jit(solution)/shard_map/ppermute | solution.py:159
  50.1 1.3 %collective-permute-done.21.refs_1_ = bf16[16,2048]{1,0:T(8,128)(2,1)S(1)} collective-permute-done((bf16[16,2048]{1,0:T(8,128)(2,1)S(1)}, bf16[16,2048]{1,0:T(8,128)(2,1)S(1)}, u32[]{:S(2)}, u32[]{:S(2)}) %collective-permute-start.21) | collective-permute-done | bytes 65568 | tf_op jit(solution)/shard_map/ppermute | solution.py:159
  51.5 0.6 %select_bitcast_fusion = (bf16[1,8,2048]{2,1,0:T(8,128)(2,1)}, bf16[1,8,2048]{2,1,0:T(8,128)(2,1)}) fusion(pred[]{:T(512)S(6)} %eq.37, bf16[16,2048]{1,0:T(8,128)(2,1)S(1)} %shard_map.104), kind=kLoop, calls=%fused_computation.17 | loop fusion | flops 32768 | bytes 131073 | tf_op jit(solution)/shard_map/broadcast_in_dim | solution.py:230
  (65 shorter events, 3.6 us)
Async XLA Ops:
  0.6 0.8 %copy-start = (bf16[2,8,2048]{2,1,0:T(8,128)(2,1)S(1)}, bf16[2,8,2048]{2,1,0:T(8,128)(2,1)}, u32[]{:S(2)}) copy-start(bf16[2,8,2048]{2,1,0:T(8,128)(2,1)} %param.10) | copy-start | bytes 196612
  0.7 0.8 %copy-start.7 = (s32[2]{0:T(128)S(1)}, s32[2]{0:T(128)}, u32[]{:S(2)}) copy-start(s32[2]{0:T(128)} %param.11) | copy-start | bytes 28
  0.7 1.1 %copy-start.5 = (bf16[1,8,2048]{2,1,0:T(8,128)(2,1)S(1)}, bf16[1,8,2048]{2,1,0:T(8,128)(2,1)}, u32[]{:S(2)}) copy-start(bf16[1,8,2048]{2,1,0:T(8,128)(2,1)} %param.8) | copy-start | bytes 98308
  0.7 1.1 %copy-start.6 = (bf16[1,8,2048]{2,1,0:T(8,128)(2,1)S(1)}, bf16[1,8,2048]{2,1,0:T(8,128)(2,1)}, u32[]{:S(2)}) copy-start(bf16[1,8,2048]{2,1,0:T(8,128)(2,1)} %param.9) | copy-start | bytes 98308
  1.8 1.4 %collective-permute-start = (bf16[16,2048]{1,0:T(8,128)(2,1)S(1)}, bf16[16,2048]{1,0:T(8,128)(2,1)S(1)}, u32[]{:S(2)}, u32[]{:S(2)}) collective-permute-start(bf16[16,2048]{1,0:T(8,128)(2,1)S(1)} %pad_maximum_fusion), channel_id=1, source_target_pairs={{0,1},{1,0},{2,3},{3,2},{4,5},{5,4},{6,7},{7,6},{8,9},{9,8},{10,11... | collective-permute-start | bytes 196616 | tf_op jit(solution)/shard_map/ppermute | solution.py:155
  3.3 12.1 %copy-start.1 = (bf16[1,2,2048,512]{3,2,1,0:T(8,128)(2,1)S(1)}, bf16[1,2,2048,512]{3,2,1,0:T(8,128)(2,1)}, u32[]{:S(2)}) copy-start(bf16[1,2,2048,512]{3,2,1,0:T(8,128)(2,1)} %param.13) | copy-start | bytes 12582916
  3.3 12.1 %copy-start.2 = (bf16[1,2,2048,512]{3,2,1,0:T(8,128)(2,1)S(1)}, bf16[1,2,2048,512]{3,2,1,0:T(8,128)(2,1)}, u32[]{:S(2)}) copy-start(bf16[1,2,2048,512]{3,2,1,0:T(8,128)(2,1)} %param.14) | copy-start | bytes 12582916
  3.3 12.1 %copy-start.3 = (bf16[1,2,512,2048]{3,2,1,0:T(8,128)(2,1)S(1)}, bf16[1,2,512,2048]{3,2,1,0:T(8,128)(2,1)}, u32[]{:S(2)}) copy-start(bf16[1,2,512,2048]{3,2,1,0:T(8,128)(2,1)} %param.15) | copy-start | bytes 12582916
  3.3 12.1 %copy-start.4 = (f32[1,2,2048]{2,1,0:T(2,128)S(1)}, f32[1,2,2048]{2,1,0:T(2,128)}, u32[]{:S(2)}) copy-start(f32[1,2,2048]{2,1,0:T(2,128)} %param.12) | copy-start | bytes 49156
  3.3 6.8 %collective-permute-start.4 = (bf16[16,2048]{1,0:T(8,128)(2,1)S(1)}, bf16[16,2048]{1,0:T(8,128)(2,1)S(1)}, u32[]{:S(2)}, u32[]{:S(2)}) collective-permute-start(bf16[16,2048]{1,0:T(8,128)(2,1)S(1)} %pad_maximum_fusion.2.x_ref), channel_id=1, source_target_pairs={{0,6},{2,4},{4,2},{6,0},{1,15},{3,13},{5,11},{7,9},{8,22},{10,20},... | collective-permute-start | bytes 196616 | tf_op jit(solution)/shard_map/ppermute | solution.py:169
  7.2 4.5 %collective-permute-start.3 = (bf16[16,2048]{1,0:T(8,128)(2,1)S(1)}, bf16[16,2048]{1,0:T(8,128)(2,1)S(1)}, u32[]{:S(2)}, u32[]{:S(2)}) collective-permute-start(bf16[16,2048]{1,0:T(8,128)(2,1)S(1)} %pad_maximum_fusion.2.x_ref), channel_id=1, source_target_pairs={{0,4},{2,6},{4,0},{6,2},{1,13},{3,15},{5,9},{7,11},{8,20},{10,22},... | collective-permute-start | bytes 196616 | tf_op jit(solution)/shard_map/ppermute | solution.py:169
  7.7 5.0 %collective-permute-start.2 = (bf16[16,2048]{1,0:T(8,128)(2,1)S(1)}, bf16[16,2048]{1,0:T(8,128)(2,1)S(1)}, u32[]{:S(2)}, u32[]{:S(2)}) collective-permute-start(bf16[16,2048]{1,0:T(8,128)(2,1)S(1)} %pad_maximum_fusion.2.x_ref), channel_id=1, source_target_pairs={{0,2},{2,0},{4,6},{6,4},{1,11},{3,9},{5,15},{7,13},{8,18},{10,16},... | collective-permute-start | bytes 196616 | tf_op jit(solution)/shard_map/ppermute | solution.py:169
  7.8 4.8 %collective-permute-start.1 = (bf16[16,2048]{1,0:T(8,128)(2,1)S(1)}, bf16[16,2048]{1,0:T(8,128)(2,1)S(1)}, u32[]{:S(2)}, u32[]{:S(2)}) collective-permute-start(bf16[16,2048]{1,0:T(8,128)(2,1)S(1)} %pad_maximum_fusion.2.x_ref), channel_id=1, source_target_pairs={{0,0},{2,2},{4,4},{6,6},{1,9},{3,11},{5,13},{7,15},{8,16},{10,18},... | collective-permute-start | bytes 196616 | tf_op jit(solution)/shard_map/ppermute | solution.py:169
  10.2 4.3 %collective-permute-start.8 = (bf16[16,2048]{1,0:T(8,128)(2,1)S(1)}, bf16[16,2048]{1,0:T(8,128)(2,1)S(1)}, u32[]{:S(2)}, u32[]{:S(2)}) collective-permute-start(bf16[16,2048]{1,0:T(8,128)(2,1)S(1)} %collective-permute-done.4.refs_3_), channel_id=1, source_target_pairs={{0,1},{1,0},{2,3},{3,2},{4,5},{5,4},{6,7},{7,6},{8,9},{9,8},{10,11... | collective-permute-start | bytes 196616 | tf_op jit(solution)/shard_map/ppermute | solution.py:155
  11.8 2.7 %collective-permute-start.7 = (bf16[16,2048]{1,0:T(8,128)(2,1)S(1)}, bf16[16,2048]{1,0:T(8,128)(2,1)S(1)}, u32[]{:S(2)}, u32[]{:S(2)}) collective-permute-start(bf16[16,2048]{1,0:T(8,128)(2,1)S(1)} %collective-permute-done.3.refs_2_), channel_id=1, source_target_pairs={{0,1},{1,0},{2,3},{3,2},{4,5},{5,4},{6,7},{7,6},{8,9},{9,8},{10,11... | collective-permute-start | bytes 196616 | tf_op jit(solution)/shard_map/ppermute | solution.py:155
  12.7 1.8 %collective-permute-start.6 = (bf16[16,2048]{1,0:T(8,128)(2,1)S(1)}, bf16[16,2048]{1,0:T(8,128)(2,1)S(1)}, u32[]{:S(2)}, u32[]{:S(2)}) collective-permute-start(bf16[16,2048]{1,0:T(8,128)(2,1)S(1)} %collective-permute-done.2.refs_1_), channel_id=1, source_target_pairs={{0,1},{1,0},{2,3},{3,2},{4,5},{5,4},{6,7},{7,6},{8,9},{9,8},{10,11... | collective-permute-start | bytes 196616 | tf_op jit(solution)/shard_map/ppermute | solution.py:155
  12.7 2.7 %collective-permute-start.5 = (bf16[16,2048]{1,0:T(8,128)(2,1)S(1)}, bf16[16,2048]{1,0:T(8,128)(2,1)S(1)}, u32[]{:S(2)}, u32[]{:S(2)}) collective-permute-start(bf16[16,2048]{1,0:T(8,128)(2,1)S(1)} %collective-permute-done.1.refs_0_), channel_id=1, source_target_pairs={{0,1},{1,0},{2,3},{3,2},{4,5},{5,4},{6,7},{7,6},{8,9},{9,8},{10,11... | collective-permute-start | bytes 196616 | tf_op jit(solution)/shard_map/ppermute | solution.py:155
  16.8 1.8 %collective-permute-start.9 = (bf16[64,2048]{1,0:T(8,128)(2,1)S(1)}, bf16[64,2048]{1,0:T(8,128)(2,1)S(1)}, u32[]{:S(2)}, u32[]{:S(2)}) collective-permute-start(bf16[64,2048]{1,0:T(8,128)(2,1)S(1)} %shard_map.98), channel_id=1, source_target_pairs={{0,1},{1,0},{2,3},{3,2},{4,5},{5,4},{6,7},{7,6},{8,9},{9,8},{10,11... | collective-permute-start | bytes 786440 | tf_op jit(solution)/shard_map/ppermute | solution.py:155
  18.7 9.5 %collective-permute-start.10 = (bf16[16,2048]{1,0:T(8,128)(2,1)S(1)}, bf16[16,2048]{1,0:T(8,128)(2,1)S(1)}, u32[]{:S(2)}, u32[]{:S(2)}) collective-permute-start(bf16[16,2048]{1,0:T(8,128)(2,1)S(1)} %get-tuple-element.19), channel_id=1, source_target_pairs={{0,14},{2,12},{4,10},{6,8},{1,7},{3,5},{5,3},{7,1},{8,6},{10,4},{1... | collective-permute-start | bytes 196616 | tf_op jit(solution)/shard_map/ppermute | solution.py:169
  24.2 5.4 %collective-permute-start.11 = (bf16[16,2048]{1,0:T(8,128)(2,1)S(1)}, bf16[16,2048]{1,0:T(8,128)(2,1)S(1)}, u32[]{:S(2)}, u32[]{:S(2)}) collective-permute-start(bf16[16,2048]{1,0:T(8,128)(2,1)S(1)} %get-tuple-element.20), channel_id=1, source_target_pairs={{0,12},{2,14},{4,8},{6,10},{1,5},{3,7},{5,1},{7,3},{8,4},{10,6},{1... | collective-permute-start | bytes 196616 | tf_op jit(solution)/shard_map/ppermute | solution.py:169
  24.2 5.4 %collective-permute-start.12 = (bf16[16,2048]{1,0:T(8,128)(2,1)S(1)}, bf16[16,2048]{1,0:T(8,128)(2,1)S(1)}, u32[]{:S(2)}, u32[]{:S(2)}) collective-permute-start(bf16[16,2048]{1,0:T(8,128)(2,1)S(1)} %get-tuple-element.21), channel_id=1, source_target_pairs={{0,10},{2,8},{4,14},{6,12},{1,3},{3,1},{5,7},{7,5},{8,2},{10,0},{1... | collective-permute-start | bytes 196616 | tf_op jit(solution)/shard_map/ppermute | solution.py:169
  26.1 6.1 %collective-permute-start.13 = (bf16[16,2048]{1,0:T(8,128)(2,1)S(1)}, bf16[16,2048]{1,0:T(8,128)(2,1)S(1)}, u32[]{:S(2)}, u32[]{:S(2)}) collective-permute-start(bf16[16,2048]{1,0:T(8,128)(2,1)S(1)} %fusion), channel_id=1, source_target_pairs={{0,8},{2,10},{4,12},{6,14},{1,1},{3,3},{5,5},{7,7},{8,0},{10,2},{1... | collective-permute-start | bytes 196616 | tf_op jit(solution)/shard_map/ppermute | solution.py:169
  32.4 5.2 %collective-permute-start.16 = (bf16[16,2048]{1,0:T(8,128)(2,1)S(1)}, bf16[16,2048]{1,0:T(8,128)(2,1)S(1)}, u32[]{:S(2)}, u32[]{:S(2)}) collective-permute-start(bf16[16,2048]{1,0:T(8,128)(2,1)S(1)} %get-tuple-element.24.refs_0_), channel_id=1, source_target_pairs={{0,6},{1,7},{2,4},{3,5},{4,2},{5,3},{6,0},{7,1},{8,14},{9,15},{10,... | collective-permute-start | bytes 196616 | tf_op jit(solution)/shard_map/ppermute | solution.py:159
  35.0 4.3 %collective-permute-start.15 = (bf16[16,2048]{1,0:T(8,128)(2,1)S(1)}, bf16[16,2048]{1,0:T(8,128)(2,1)S(1)}, u32[]{:S(2)}, u32[]{:S(2)}) collective-permute-start(bf16[16,2048]{1,0:T(8,128)(2,1)S(1)} %get-tuple-element.24.refs_0_), channel_id=1, source_target_pairs={{0,4},{1,5},{2,6},{3,7},{4,0},{5,1},{6,2},{7,3},{8,12},{9,13},{10,... | collective-permute-start | bytes 196616 | tf_op jit(solution)/shard_map/ppermute | solution.py:159
  35.5 4.3 %collective-permute-start.14 = (bf16[16,2048]{1,0:T(8,128)(2,1)S(1)}, bf16[16,2048]{1,0:T(8,128)(2,1)S(1)}, u32[]{:S(2)}, u32[]{:S(2)}) collective-permute-start(bf16[16,2048]{1,0:T(8,128)(2,1)S(1)} %get-tuple-element.24.refs_0_), channel_id=1, source_target_pairs={{0,2},{1,3},{2,0},{3,1},{4,6},{5,7},{6,4},{7,5},{8,10},{9,11},{10,... | collective-permute-start | bytes 196616 | tf_op jit(solution)/shard_map/ppermute | solution.py:159
  39.8 2.0 %collective-permute-start.17 = (bf16[64,2048]{1,0:T(8,128)(2,1)S(1)}, bf16[64,2048]{1,0:T(8,128)(2,1)S(1)}, u32[]{:S(2)}, u32[]{:S(2)}) collective-permute-start(bf16[64,2048]{1,0:T(8,128)(2,1)S(1)} %shard_map.101.refs_0_), channel_id=1, source_target_pairs={{0,1},{1,0},{2,3},{3,2},{4,5},{5,4},{6,7},{7,6},{8,9},{9,8},{10,11... | collective-permute-start | bytes 786440 | tf_op jit(solution)/shard_map/ppermute | solution.py:155
  41.1 2.5 %collective-permute-start.19 = (bf16[32,2048]{1,0:T(8,128)(2,1)S(1)}, bf16[32,2048]{1,0:T(8,128)(2,1)S(1)}, u32[]{:S(2)}, u32[]{:S(2)}) collective-permute-start(bf16[32,2048]{1,0:T(8,128)(2,1)S(1)} %get-tuple-element.28), channel_id=1, source_target_pairs={{0,1},{1,0},{2,3},{3,2},{4,5},{5,4},{6,7},{7,6},{8,9},{9,8},{10,11... | collective-permute-start | bytes 393224 | tf_op jit(solution)/shard_map/ppermute | solution.py:155
  41.7 6.6 %collective-permute-start.23 = (bf16[8,2048]{1,0:T(8,128)(2,1)S(1)}, bf16[8,2048]{1,0:T(8,128)(2,1)S(1)}, u32[]{:S(2)}, u32[]{:S(2)}) collective-permute-start(bf16[8,2048]{1,0:T(8,128)(2,1)S(1)} %get-tuple-element.56), channel_id=1, source_target_pairs={{0,1},{1,0},{2,3},{3,2},{4,5},{5,4},{6,7},{7,6},{8,9},{9,8},{10,11... | collective-permute-start | bytes 98312 | tf_op jit(solution)/shard_map/ppermute | solution.py:155
  43.1 1.5 %collective-permute-start.18 = (bf16[32,2048]{1,0:T(8,128)(2,1)S(1)}, bf16[32,2048]{1,0:T(8,128)(2,1)S(1)}, u32[]{:S(2)}, u32[]{:S(2)}) collective-permute-start(bf16[32,2048]{1,0:T(8,128)(2,1)S(1)} %get-tuple-element.26), channel_id=1, source_target_pairs={{0,1},{1,0},{2,3},{3,2},{4,5},{5,4},{6,7},{7,6},{8,9},{9,8},{10,11... | collective-permute-start | bytes 393224 | tf_op jit(solution)/shard_map/ppermute | solution.py:155
  44.7 5.4 %collective-permute-start.20 = (bf16[16,2048]{1,0:T(8,128)(2,1)S(1)}, bf16[16,2048]{1,0:T(8,128)(2,1)S(1)}, u32[]{:S(2)}, u32[]{:S(2)}) collective-permute-start(bf16[16,2048]{1,0:T(8,128)(2,1)S(1)} %pad_maximum_fusion.5), channel_id=1, source_target_pairs={{0,6},{1,7},{2,4},{3,5},{4,2},{5,3},{6,0},{7,1},{8,14},{9,15},{10,... | collective-permute-start | bytes 196616 | tf_op jit(solution)/shard_map/ppermute | solution.py:159
  46.3 5.2 %collective-permute-start.21 = (bf16[16,2048]{1,0:T(8,128)(2,1)S(1)}, bf16[16,2048]{1,0:T(8,128)(2,1)S(1)}, u32[]{:S(2)}, u32[]{:S(2)}) collective-permute-start(bf16[16,2048]{1,0:T(8,128)(2,1)S(1)} %get-tuple-element.30), channel_id=1, source_target_pairs={{0,4},{1,5},{2,6},{3,7},{4,0},{5,1},{6,2},{7,3},{8,12},{9,13},{10,... | collective-permute-start | bytes 196616 | tf_op jit(solution)/shard_map/ppermute | solution.py:159
  46.8 4.7 %collective-permute-start.22 = (bf16[16,2048]{1,0:T(8,128)(2,1)S(1)}, bf16[16,2048]{1,0:T(8,128)(2,1)S(1)}, u32[]{:S(2)}, u32[]{:S(2)}) collective-permute-start(bf16[16,2048]{1,0:T(8,128)(2,1)S(1)} %get-tuple-element.31), channel_id=1, source_target_pairs={{0,2},{1,3},{2,0},{3,1},{4,6},{5,7},{6,4},{7,5},{8,10},{9,11},{10,... | collective-permute-start | bytes 196616 | tf_op jit(solution)/shard_map/ppermute | solution.py:159

commit v6 on v5

--- a/solution.py
+++ b/solution.py
@@ -9,6 +9,7 @@
 
 CORES = 2
 EPS = 1e-05
+BLOCK = 128
 LIMIT = 8 * 2**20
 BESIDE = 10**10
 
@@ -28,20 +29,26 @@
     normed = jnp.concatenate([ref[...] for ref in pieces], axis=0)
     if not ready:
         normed = normalize(normed, gains_ref[pl.ds(group, 1), :])
-    gate = jnp.dot(normed, gate_ref[group], preferred_element_type=jnp.float32)
-    up = jnp.dot(normed, up_ref[group], preferred_element_type=jnp.float32)
-    hidden = (gate / (1.0 + jnp.exp(-gate)) * up).astype(jnp.bfloat16)
-    part = jnp.dot(hidden, down_ref[group], preferred_element_type=jnp.float32)
-    if len(outs) == 1:
-        outs[0][...] = part.astype(outs[0].dtype)
-        return
+    hidden = []
+    for first in range(0, gate_ref.shape[2], BLOCK):
+        block = pl.ds(first, BLOCK)
+        gate = jnp.dot(normed, gate_ref[group, :, block], preferred_element_type=jnp.float32)
+        up = jnp.dot(normed, up_ref[group, :, block], preferred_element_type=jnp.float32)
+        hidden.append((gate / (1.0 + jnp.exp(-gate)) * up).astype(jnp.bfloat16))
+    hidden = jnp.concatenate(hidden, axis=1)
     first_core = lax.axis_index("zero") % CORES == 0
-    rows = part.shape[0] // (CORES * chips)
-    halves = [part[n * rows : (n + 1) * rows] for n in range(CORES * chips)]
-    keep = [jnp.where(first_core, a, b) for a, b in zip(halves[::2], halves[1::2])]
-    give = [jnp.where(first_core, b, a) for a, b in zip(halves[::2], halves[1::2])]
-    outs[0][...] = jnp.concatenate(keep, axis=0).astype(outs[0].dtype)
-    outs[1][...] = jnp.concatenate(give, axis=0).astype(outs[1].dtype)
+    for first in range(0, down_ref.shape[2], BLOCK):
+        block = pl.ds(first, BLOCK)
+        part = jnp.dot(hidden, down_ref[group, :, block], preferred_element_type=jnp.float32)
+        if len(outs) == 1:
+            outs[0][:, block] = part.astype(outs[0].dtype)
+            continue
+        rows = part.shape[0] // (CORES * chips)
+        halves = [part[n * rows : (n + 1) * rows] for n in range(CORES * chips)]
+        keep = [jnp.where(first_core, a, b) for a, b in zip(halves[::2], halves[1::2])]
+        give = [jnp.where(first_core, b, a) for a, b in zip(halves[::2], halves[1::2])]
+        outs[0][:, block] = jnp.concatenate(keep, axis=0).astype(outs[0].dtype)
+        outs[1][:, block] = jnp.concatenate(give, axis=0).astype(outs[1].dtype)
 
 
 def pass_kernel(x_ref, out):

time: 52.4 us -> 51.9 us (level)
  Pallas kernels: 5.51 us -> 4.94 us
    pallas_call x4, Pallas kernels: 5.31 us -> 4.74 us  [partial(): pl.pallas_call(functools.partial(group_kernel, tick, other, ready, len(pi...]
  transfers between devices with their start and end apart: 24 -> 24, of which waited for: 13 -> 13; matrix products, arithmetic and copies ran while one was open for 0% -> 0% of each run, Pallas kernels for 8% -> 7%
where the time goes in v6:
time: 51.9 us; the launch traced here: 51.7 us
  starting transfers between devices  27.9 us (54%)
  waiting for transfers between devices  15.9 us (31%)
  Pallas kernels  4.94 us (10%)
  between operations  1 us (2%)
  other arithmetic  0.89 us (2%)
  local copies, waits for them, and re-layouts  0.86 us (2%)
    ppermute x8, starting transfers between devices, to_next(): return lax.ppermute(value, both, pairs)  14.8 us
    ppermute x6, starting transfers between devices, to_chip(): return lax.ppermute(value, 'zero', pairs)  7.12 us
    ppermute x6, waiting for transfers between devices, to_chip(): return lax.ppermute(value, 'zero', pairs)  6.92 us
    ppermute x8, waiting for transfers between devices, to_next(): return lax.ppermute(value, both, pairs)  6.27 us
    ppermute x10, starting transfers between devices, to_sibling(): return lax.ppermute(value, 'zero', [(k, k ^ 1) for k in range(zero)])  5.93 us
    pallas_call x4, Pallas kernels, partial(): pl.pallas_call(functools.partial(group_kernel, tick, other, ready, len(pi...  4.74 us
    ppermute x10, waiting for transfers between devices, to_sibling(): return lax.ppermute(value, 'zero', [(k, k ^ 1) for k in range(zero)])  2.71 us
  transfers between devices with their start and end apart: 24, of which 13 were waited for; matrix products, arithmetic and copies ran while one was open for 0% of the time, Pallas kernels for 7%

profile of v6, /device:TPU:0, one launch (start us, length us, event | category | flops | bytes accessed | tf_op | source)
XLA Modules:
  0.0 51.7 jit_solution(11650665838109389342)
XLA Ops:
  0.7 0.7 %copy-done = bf16[2,8,2048]{2,1,0:T(8,128)(2,1)S(1)} copy-done((bf16[2,8,2048]{2,1,0:T(8,128)(2,1)S(1)}, bf16[2,8,2048]{2,1,0:T(8,128)(2,1)}, u32[]{:S(2)}) %copy-start) | copy-done | bytes 65560
  1.8 0.5 collective-permute-start
  2.4 0.9 %collective-permute-done = bf16[16,2048]{1,0:T(8,128)(2,1)S(1)} collective-permute-done((bf16[16,2048]{1,0:T(8,128)(2,1)S(1)}, bf16[16,2048]{1,0:T(8,128)(2,1)S(1)}, u32[]{:S(2)}, u32[]{:S(2)}) %collective-permute-start) | collective-permute-done | bytes 65568 | tf_op jit(solution)/shard_map/ppermute | solution.py:162
  3.3 3.9 %collective-permute-start.4 = (bf16[16,2048]{1,0:T(8,128)(2,1)S(1)}, bf16[16,2048]{1,0:T(8,128)(2,1)S(1)}, u32[]{:S(2)}, u32[]{:S(2)}) collective-permute-start(bf16[16,2048]{1,0:T(8,128)(2,1)S(1)} %pad_maximum_fusion.2.x_ref), channel_id=1, source_target_pairs={{0,6},{2,4},{4,2},{6,0},{1,15},{3,13},{5,11},{7,9},{8,22},{10,20},... | collective-permute-start | bytes 196616 | tf_op jit(solution)/shard_map/ppermute | solution.py:176
  7.8 0.7 %collective-permute-start.1 = (bf16[16,2048]{1,0:T(8,128)(2,1)S(1)}, bf16[16,2048]{1,0:T(8,128)(2,1)S(1)}, u32[]{:S(2)}, u32[]{:S(2)}) collective-permute-start(bf16[16,2048]{1,0:T(8,128)(2,1)S(1)} %pad_maximum_fusion.2.x_ref), channel_id=1, source_target_pairs={{0,0},{2,2},{4,4},{6,6},{1,9},{3,11},{5,13},{7,15},{8,16},{10,18},... | collective-permute-start | bytes 196616 | tf_op jit(solution)/shard_map/ppermute | solution.py:176
  8.5 1.6 %collective-permute-done.4.refs_3_ = bf16[16,2048]{1,0:T(8,128)(2,1)S(1)} collective-permute-done((bf16[16,2048]{1,0:T(8,128)(2,1)S(1)}, bf16[16,2048]{1,0:T(8,128)(2,1)S(1)}, u32[]{:S(2)}, u32[]{:S(2)}) %collective-permute-start.4) | collective-permute-done | bytes 65568 | tf_op jit(solution)/shard_map/ppermute | solution.py:176
  10.2 1.6 %collective-permute-start.8 = (bf16[16,2048]{1,0:T(8,128)(2,1)S(1)}, bf16[16,2048]{1,0:T(8,128)(2,1)S(1)}, u32[]{:S(2)}, u32[]{:S(2)}) collective-permute-start(bf16[16,2048]{1,0:T(8,128)(2,1)S(1)} %collective-permute-done.4.refs_3_), channel_id=1, source_target_pairs={{0,1},{1,0},{2,3},{3,2},{4,5},{5,4},{6,7},{7,6},{8,9},{9,8},{10,11... | collective-permute-start | bytes 196616 | tf_op jit(solution)/shard_map/ppermute | solution.py:162
  12.1 0.6 %collective-permute-done.2.refs_1_ = bf16[16,2048]{1,0:T(8,128)(2,1)S(1)} collective-permute-done((bf16[16,2048]{1,0:T(8,128)(2,1)S(1)}, bf16[16,2048]{1,0:T(8,128)(2,1)S(1)}, u32[]{:S(2)}, u32[]{:S(2)}) %collective-permute-start.2) | collective-permute-done | bytes 65568 | tf_op jit(solution)/shard_map/ppermute | solution.py:176
  12.7 1.8 %collective-permute-start.5 = (bf16[16,2048]{1,0:T(8,128)(2,1)S(1)}, bf16[16,2048]{1,0:T(8,128)(2,1)S(1)}, u32[]{:S(2)}, u32[]{:S(2)}) collective-permute-start(bf16[16,2048]{1,0:T(8,128)(2,1)S(1)} %collective-permute-done.1.refs_0_), channel_id=1, source_target_pairs={{0,1},{1,0},{2,3},{3,2},{4,5},{5,4},{6,7},{7,6},{8,9},{9,8},{10,11... | collective-permute-start | bytes 196616 | tf_op jit(solution)/shard_map/ppermute | solution.py:162
  14.5 0.9 %collective-permute-done.5.refs_0_ = bf16[16,2048]{1,0:T(8,128)(2,1)S(1)} collective-permute-done((bf16[16,2048]{1,0:T(8,128)(2,1)S(1)}, bf16[16,2048]{1,0:T(8,128)(2,1)S(1)}, u32[]{:S(2)}, u32[]{:S(2)}) %collective-permute-start.5) | collective-permute-done | bytes 65568 | tf_op jit(solution)/shard_map/ppermute | solution.py:162
  15.4 1.2 %shard_map.98 = bf16[64,2048]{1,0:T(8,128)(2,1)S(1)} custom-call(bf16[16,2048]{1,0:T(8,128)(2,1)S(1)} %shard_map.96.mark_ref, f32[2,2048]{1,0:T(2,128)S(1)} %bitcast.31, bf16[2,2048,512]{2,1,0:T(8,128)(2,1)S(1)} %bitcast.19, bf16[2,2048,512]{2,1,0:T(8,128)(2,1)S(1)} %bitcast.23, bf16[2,512,2048]{2,1,0:T(8,128)(2,1)S(1)} %bitcast.27, ...), custom_call_target="tpu_custom_call" | custom-call | flops 402653184 | bytes 6291456 | tf_op jit(solution)/shard_map/pallas_call | solution.py:137
  17.0 1.2 %shard_map.97 = f32[64,2048]{1,0:T(8,128)S(1)} custom-call(bf16[16,2048]{1,0:T(8,128)(2,1)S(1)} %shard_map.96.mark_ref, f32[2,2048]{1,0:T(2,128)S(1)} %bitcast.32, bf16[2,2048,512]{2,1,0:T(8,128)(2,1)S(1)} %bitcast.20, bf16[2,2048,512]{2,1,0:T(8,128)(2,1)S(1)} %bitcast.24, bf16[2,512,2048]{2,1,0:T(8,128)(2,1)S(1)} %bitcast.28, ...), custom_call_target="tpu_custom_call" | custom-call | flops 402653184 | bytes 6291456 | tf_op jit(solution)/shard_map/pallas_call | solution.py:137
  18.4 5.7 %collective-permute-start.10 = (bf16[16,2048]{1,0:T(8,128)(2,1)S(1)}, bf16[16,2048]{1,0:T(8,128)(2,1)S(1)}, u32[]{:S(2)}, u32[]{:S(2)}) collective-permute-start(bf16[16,2048]{1,0:T(8,128)(2,1)S(1)} %get-tuple-element.19), channel_id=1, source_target_pairs={{0,14},{2,12},{4,10},{6,8},{1,7},{3,5},{5,3},{7,1},{8,6},{10,4},{1... | collective-permute-start | bytes 196616 | tf_op jit(solution)/shard_map/ppermute | solution.py:176
  24.1 1.9 %collective-permute-start.12 = (bf16[16,2048]{1,0:T(8,128)(2,1)S(1)}, bf16[16,2048]{1,0:T(8,128)(2,1)S(1)}, u32[]{:S(2)}, u32[]{:S(2)}) collective-permute-start(bf16[16,2048]{1,0:T(8,128)(2,1)S(1)} %get-tuple-element.21), channel_id=1, source_target_pairs={{0,10},{2,8},{4,14},{6,12},{1,3},{3,1},{5,7},{7,5},{8,2},{10,0},{1... | collective-permute-start | bytes 196616 | tf_op jit(solution)/shard_map/ppermute | solution.py:176
  26.0 2.1 %collective-permute-start.13 = (bf16[16,2048]{1,0:T(8,128)(2,1)S(1)}, bf16[16,2048]{1,0:T(8,128)(2,1)S(1)}, u32[]{:S(2)}, u32[]{:S(2)}) collective-permute-start(bf16[16,2048]{1,0:T(8,128)(2,1)S(1)} %fusion), channel_id=1, source_target_pairs={{0,8},{2,10},{4,12},{6,14},{1,1},{3,3},{5,5},{7,7},{8,0},{10,2},{1... | collective-permute-start | bytes 196616 | tf_op jit(solution)/shard_map/ppermute | solution.py:176
  28.1 1.4 %collective-permute-done.11.refs_1_ = bf16[16,2048]{1,0:T(8,128)(2,1)S(1)} collective-permute-done((bf16[16,2048]{1,0:T(8,128)(2,1)S(1)}, bf16[16,2048]{1,0:T(8,128)(2,1)S(1)}, u32[]{:S(2)}, u32[]{:S(2)}) %collective-permute-start.11) | collective-permute-done | bytes 65568 | tf_op jit(solution)/shard_map/ppermute | solution.py:176
  29.5 2.6 %collective-permute-done.13.refs_3_ = bf16[16,2048]{1,0:T(8,128)(2,1)S(1)} collective-permute-done((bf16[16,2048]{1,0:T(8,128)(2,1)S(1)}, bf16[16,2048]{1,0:T(8,128)(2,1)S(1)}, u32[]{:S(2)}, u32[]{:S(2)}) %collective-permute-start.13) | collective-permute-done | bytes 65568 | tf_op jit(solution)/shard_map/ppermute | solution.py:176
  32.3 2.5 %collective-permute-start.16 = (bf16[16,2048]{1,0:T(8,128)(2,1)S(1)}, bf16[16,2048]{1,0:T(8,128)(2,1)S(1)}, u32[]{:S(2)}, u32[]{:S(2)}) collective-permute-start(bf16[16,2048]{1,0:T(8,128)(2,1)S(1)} %get-tuple-element.24.refs_0_), channel_id=1, source_target_pairs={{0,6},{1,7},{2,4},{3,5},{4,2},{5,3},{6,0},{7,1},{8,14},{9,15},{10,... | collective-permute-start | bytes 196616 | tf_op jit(solution)/shard_map/ppermute | solution.py:166
  34.8 0.5 collective-permute-start.15
  35.3 0.5 %collective-permute-start.14 = (bf16[16,2048]{1,0:T(8,128)(2,1)S(1)}, bf16[16,2048]{1,0:T(8,128)(2,1)S(1)}, u32[]{:S(2)}, u32[]{:S(2)}) collective-permute-start(bf16[16,2048]{1,0:T(8,128)(2,1)S(1)} %get-tuple-element.24.refs_0_), channel_id=1, source_target_pairs={{0,2},{1,3},{2,0},{3,1},{4,6},{5,7},{6,4},{7,5},{8,10},{9,11},{10,... | collective-permute-start | bytes 196616 | tf_op jit(solution)/shard_map/ppermute | solution.py:166
  35.9 1.7 %collective-permute-done.16.refs_3_ = bf16[16,2048]{1,0:T(8,128)(2,1)S(1)} collective-permute-done((bf16[16,2048]{1,0:T(8,128)(2,1)S(1)}, bf16[16,2048]{1,0:T(8,128)(2,1)S(1)}, u32[]{:S(2)}, u32[]{:S(2)}) %collective-permute-start.16) | collective-permute-done | bytes 65568 | tf_op jit(solution)/shard_map/ppermute | solution.py:166
  37.5 1.5 %collective-permute-done.15.refs_2_ = bf16[16,2048]{1,0:T(8,128)(2,1)S(1)} collective-permute-done((bf16[16,2048]{1,0:T(8,128)(2,1)S(1)}, bf16[16,2048]{1,0:T(8,128)(2,1)S(1)}, u32[]{:S(2)}, u32[]{:S(2)}) %collective-permute-start.15) | collective-permute-done | bytes 65568 | tf_op jit(solution)/shard_map/ppermute | solution.py:166
  39.7 1.2 %shard_map.102 = (f32[32,2048]{1,0:T(8,128)S(1)}, bf16[32,2048]{1,0:T(8,128)(2,1)S(1)}) custom-call(bf16[16,2048]{1,0:T(8,128)(2,1)S(1)} %shard_map.100.mark_ref, f32[2,2048]{1,0:T(2,128)S(1)} %bitcast.34, bf16[2,2048,512]{2,1,0:T(8,128)(2,1)S(1)} %bitcast.21, bf16[2,2048,512]{2,1,0:T(8,128)(2,1)S(1)} %bitcast.25, bf16[2,512,2048]{2,1,0:T(8,128)(2,1)S(1)} %bitcast.29, ...), custom_call_target="tpu_custom_call" | custom-call | flops 402653184 | bytes 6291456 | tf_op jit(solution)/shard_map/pallas_call | solution.py:137
  40.8 0.5 %collective-permute-start.19 = (bf16[32,2048]{1,0:T(8,128)(2,1)S(1)}, bf16[32,2048]{1,0:T(8,128)(2,1)S(1)}, u32[]{:S(2)}, u32[]{:S(2)}) collective-permute-start(bf16[32,2048]{1,0:T(8,128)(2,1)S(1)} %get-tuple-element.28), channel_id=1, source_target_pairs={{0,1},{1,0},{2,3},{3,2},{4,5},{5,4},{6,7},{7,6},{8,9},{9,8},{10,11... | collective-permute-start | bytes 393224 | tf_op jit(solution)/shard_map/ppermute | solution.py:162
  41.5 1.1 %shard_map.103 = (f32[32,2048]{1,0:T(8,128)S(1)}, bf16[32,2048]{1,0:T(8,128)(2,1)S(1)}) custom-call(bf16[16,2048]{1,0:T(8,128)(2,1)S(1)} %shard_map.100.mark_ref, f32[2,2048]{1,0:T(2,128)S(1)} %bitcast.35, bf16[2,2048,512]{2,1,0:T(8,128)(2,1)S(1)} %bitcast.22, bf16[2,2048,512]{2,1,0:T(8,128)(2,1)S(1)} %bitcast.26, bf16[2,512,2048]{2,1,0:T(8,128)(2,1)S(1)} %bitcast.30, ...), custom_call_target="tpu_custom_call" | custom-call | flops 402653184 | bytes 6291456 | tf_op jit(solution)/shard_map/pallas_call | solution.py:137
  42.6 0.5 %collective-permute-start.18 = (bf16[32,2048]{1,0:T(8,128)(2,1)S(1)}, bf16[32,2048]{1,0:T(8,128)(2,1)S(1)}, u32[]{:S(2)}, u32[]{:S(2)}) collective-permute-start(bf16[32,2048]{1,0:T(8,128)(2,1)S(1)} %get-tuple-element.26), channel_id=1, source_target_pairs={{0,1},{1,0},{2,3},{3,2},{4,5},{5,4},{6,7},{7,6},{8,9},{9,8},{10,11... | collective-permute-start | bytes 393224 | tf_op jit(solution)/shard_map/ppermute | solution.py:162
  43.3 0.9 %collective-permute-done.18 = bf16[32,2048]{1,0:T(8,128)(2,1)S(1)} collective-permute-done((bf16[32,2048]{1,0:T(8,128)(2,1)S(1)}, bf16[32,2048]{1,0:T(8,128)(2,1)S(1)}, u32[]{:S(2)}, u32[]{:S(2)}) %collective-permute-start.18) | collective-permute-done | bytes 131104 | tf_op jit(solution)/shard_map/ppermute | solution.py:162
  44.3 1.6 %collective-permute-start.20 = (bf16[16,2048]{1,0:T(8,128)(2,1)S(1)}, bf16[16,2048]{1,0:T(8,128)(2,1)S(1)}, u32[]{:S(2)}, u32[]{:S(2)}) collective-permute-start(bf16[16,2048]{1,0:T(8,128)(2,1)S(1)} %pad_maximum_fusion.5), channel_id=1, source_target_pairs={{0,6},{1,7},{2,4},{3,5},{4,2},{5,3},{6,0},{7,1},{8,14},{9,15},{10,... | collective-permute-start | bytes 196616 | tf_op jit(solution)/shard_map/ppermute | solution.py:166
  46.3 1.5 %collective-permute-start.22 = (bf16[16,2048]{1,0:T(8,128)(2,1)S(1)}, bf16[16,2048]{1,0:T(8,128)(2,1)S(1)}, u32[]{:S(2)}, u32[]{:S(2)}) collective-permute-start(bf16[16,2048]{1,0:T(8,128)(2,1)S(1)} %get-tuple-element.31), channel_id=1, source_target_pairs={{0,2},{1,3},{2,0},{3,1},{4,6},{5,7},{6,4},{7,5},{8,10},{9,11},{10,... | collective-permute-start | bytes 196616 | tf_op jit(solution)/shard_map/ppermute | solution.py:166
  47.9 1.8 %collective-permute-done.20.refs_0_ = bf16[16,2048]{1,0:T(8,128)(2,1)S(1)} collective-permute-done((bf16[16,2048]{1,0:T(8,128)(2,1)S(1)}, bf16[16,2048]{1,0:T(8,128)(2,1)S(1)}, u32[]{:S(2)}, u32[]{:S(2)}) %collective-permute-start.20) | collective-permute-done | bytes 65568 | tf_op jit(solution)/shard_map/ppermute | solution.py:166
  49.7 1.3 %collective-permute-done.21.refs_1_ = bf16[16,2048]{1,0:T(8,128)(2,1)S(1)} collective-permute-done((bf16[16,2048]{1,0:T(8,128)(2,1)S(1)}, bf16[16,2048]{1,0:T(8,128)(2,1)S(1)}, u32[]{:S(2)}, u32[]{:S(2)}) %collective-permute-start.21) | collective-permute-done | bytes 65568 | tf_op jit(solution)/shard_map/ppermute | solution.py:166
  51.1 0.6 %select_bitcast_fusion = (bf16[1,8,2048]{2,1,0:T(8,128)(2,1)}, bf16[1,8,2048]{2,1,0:T(8,128)(2,1)}) fusion(pred[]{:T(512)S(6)} %eq.37, bf16[16,2048]{1,0:T(8,128)(2,1)S(1)} %shard_map.104), kind=kLoop, calls=%fused_computation.17 | loop fusion | flops 32768 | bytes 131073 | tf_op jit(solution)/shard_map/broadcast_in_dim | solution.py:237
  (65 shorter events, 3.6 us)
Async XLA Ops:
  0.6 0.8 %copy-start = (bf16[2,8,2048]{2,1,0:T(8,128)(2,1)S(1)}, bf16[2,8,2048]{2,1,0:T(8,128)(2,1)}, u32[]{:S(2)}) copy-start(bf16[2,8,2048]{2,1,0:T(8,128)(2,1)} %param.10) | copy-start | bytes 196612
  0.7 0.8 %copy-start.7 = (s32[2]{0:T(128)S(1)}, s32[2]{0:T(128)}, u32[]{:S(2)}) copy-start(s32[2]{0:T(128)} %param.11) | copy-start | bytes 28
  0.7 1.1 %copy-start.5 = (bf16[1,8,2048]{2,1,0:T(8,128)(2,1)S(1)}, bf16[1,8,2048]{2,1,0:T(8,128)(2,1)}, u32[]{:S(2)}) copy-start(bf16[1,8,2048]{2,1,0:T(8,128)(2,1)} %param.8) | copy-start | bytes 98308
  0.7 1.1 %copy-start.6 = (bf16[1,8,2048]{2,1,0:T(8,128)(2,1)S(1)}, bf16[1,8,2048]{2,1,0:T(8,128)(2,1)}, u32[]{:S(2)}) copy-start(bf16[1,8,2048]{2,1,0:T(8,128)(2,1)} %param.9) | copy-start | bytes 98308
  1.8 1.4 %collective-permute-start = (bf16[16,2048]{1,0:T(8,128)(2,1)S(1)}, bf16[16,2048]{1,0:T(8,128)(2,1)S(1)}, u32[]{:S(2)}, u32[]{:S(2)}) collective-permute-start(bf16[16,2048]{1,0:T(8,128)(2,1)S(1)} %pad_maximum_fusion), channel_id=1, source_target_pairs={{0,1},{1,0},{2,3},{3,2},{4,5},{5,4},{6,7},{7,6},{8,9},{9,8},{10,11... | collective-permute-start | bytes 196616 | tf_op jit(solution)/shard_map/ppermute | solution.py:162
  3.3 12.1 %copy-start.1 = (bf16[1,2,2048,512]{3,2,1,0:T(8,128)(2,1)S(1)}, bf16[1,2,2048,512]{3,2,1,0:T(8,128)(2,1)}, u32[]{:S(2)}) copy-start(bf16[1,2,2048,512]{3,2,1,0:T(8,128)(2,1)} %param.13) | copy-start | bytes 12582916
  3.3 12.1 %copy-start.2 = (bf16[1,2,2048,512]{3,2,1,0:T(8,128)(2,1)S(1)}, bf16[1,2,2048,512]{3,2,1,0:T(8,128)(2,1)}, u32[]{:S(2)}) copy-start(bf16[1,2,2048,512]{3,2,1,0:T(8,128)(2,1)} %param.14) | copy-start | bytes 12582916
  3.3 12.1 %copy-start.3 = (bf16[1,2,512,2048]{3,2,1,0:T(8,128)(2,1)S(1)}, bf16[1,2,512,2048]{3,2,1,0:T(8,128)(2,1)}, u32[]{:S(2)}) copy-start(bf16[1,2,512,2048]{3,2,1,0:T(8,128)(2,1)} %param.15) | copy-start | bytes 12582916
  3.3 12.1 %copy-start.4 = (f32[1,2,2048]{2,1,0:T(2,128)S(1)}, f32[1,2,2048]{2,1,0:T(2,128)}, u32[]{:S(2)}) copy-start(f32[1,2,2048]{2,1,0:T(2,128)} %param.12) | copy-start | bytes 49156
  3.3 6.8 %collective-permute-start.4 = (bf16[16,2048]{1,0:T(8,128)(2,1)S(1)}, bf16[16,2048]{1,0:T(8,128)(2,1)S(1)}, u32[]{:S(2)}, u32[]{:S(2)}) collective-permute-start(bf16[16,2048]{1,0:T(8,128)(2,1)S(1)} %pad_maximum_fusion.2.x_ref), channel_id=1, source_target_pairs={{0,6},{2,4},{4,2},{6,0},{1,15},{3,13},{5,11},{7,9},{8,22},{10,20},... | collective-permute-start | bytes 196616 | tf_op jit(solution)/shard_map/ppermute | solution.py:176
  7.2 4.5 %collective-permute-start.3 = (bf16[16,2048]{1,0:T(8,128)(2,1)S(1)}, bf16[16,2048]{1,0:T(8,128)(2,1)S(1)}, u32[]{:S(2)}, u32[]{:S(2)}) collective-permute-start(bf16[16,2048]{1,0:T(8,128)(2,1)S(1)} %pad_maximum_fusion.2.x_ref), channel_id=1, source_target_pairs={{0,4},{2,6},{4,0},{6,2},{1,13},{3,15},{5,9},{7,11},{8,20},{10,22},... | collective-permute-start | bytes 196616 | tf_op jit(solution)/shard_map/ppermute | solution.py:176
  7.7 5.0 %collective-permute-start.2 = (bf16[16,2048]{1,0:T(8,128)(2,1)S(1)}, bf16[16,2048]{1,0:T(8,128)(2,1)S(1)}, u32[]{:S(2)}, u32[]{:S(2)}) collective-permute-start(bf16[16,2048]{1,0:T(8,128)(2,1)S(1)} %pad_maximum_fusion.2.x_ref), channel_id=1, source_target_pairs={{0,2},{2,0},{4,6},{6,4},{1,11},{3,9},{5,15},{7,13},{8,18},{10,16},... | collective-permute-start | bytes 196616 | tf_op jit(solution)/shard_map/ppermute | solution.py:176
  7.8 4.8 %collective-permute-start.1 = (bf16[16,2048]{1,0:T(8,128)(2,1)S(1)}, bf16[16,2048]{1,0:T(8,128)(2,1)S(1)}, u32[]{:S(2)}, u32[]{:S(2)}) collective-permute-start(bf16[16,2048]{1,0:T(8,128)(2,1)S(1)} %pad_maximum_fusion.2.x_ref), channel_id=1, source_target_pairs={{0,0},{2,2},{4,4},{6,6},{1,9},{3,11},{5,13},{7,15},{8,16},{10,18},... | collective-permute-start | bytes 196616 | tf_op jit(solution)/shard_map/ppermute | solution.py:176
  10.2 4.3 %collective-permute-start.8 = (bf16[16,2048]{1,0:T(8,128)(2,1)S(1)}, bf16[16,2048]{1,0:T(8,128)(2,1)S(1)}, u32[]{:S(2)}, u32[]{:S(2)}) collective-permute-start(bf16[16,2048]{1,0:T(8,128)(2,1)S(1)} %collective-permute-done.4.refs_3_), channel_id=1, source_target_pairs={{0,1},{1,0},{2,3},{3,2},{4,5},{5,4},{6,7},{7,6},{8,9},{9,8},{10,11... | collective-permute-start | bytes 196616 | tf_op jit(solution)/shard_map/ppermute | solution.py:162
  11.8 2.7 %collective-permute-start.7 = (bf16[16,2048]{1,0:T(8,128)(2,1)S(1)}, bf16[16,2048]{1,0:T(8,128)(2,1)S(1)}, u32[]{:S(2)}, u32[]{:S(2)}) collective-permute-start(bf16[16,2048]{1,0:T(8,128)(2,1)S(1)} %collective-permute-done.3.refs_2_), channel_id=1, source_target_pairs={{0,1},{1,0},{2,3},{3,2},{4,5},{5,4},{6,7},{7,6},{8,9},{9,8},{10,11... | collective-permute-start | bytes 196616 | tf_op jit(solution)/shard_map/ppermute | solution.py:162
  12.7 1.8 %collective-permute-start.6 = (bf16[16,2048]{1,0:T(8,128)(2,1)S(1)}, bf16[16,2048]{1,0:T(8,128)(2,1)S(1)}, u32[]{:S(2)}, u32[]{:S(2)}) collective-permute-start(bf16[16,2048]{1,0:T(8,128)(2,1)S(1)} %collective-permute-done.2.refs_1_), channel_id=1, source_target_pairs={{0,1},{1,0},{2,3},{3,2},{4,5},{5,4},{6,7},{7,6},{8,9},{9,8},{10,11... | collective-permute-start | bytes 196616 | tf_op jit(solution)/shard_map/ppermute | solution.py:162
  12.7 2.7 %collective-permute-start.5 = (bf16[16,2048]{1,0:T(8,128)(2,1)S(1)}, bf16[16,2048]{1,0:T(8,128)(2,1)S(1)}, u32[]{:S(2)}, u32[]{:S(2)}) collective-permute-start(bf16[16,2048]{1,0:T(8,128)(2,1)S(1)} %collective-permute-done.1.refs_0_), channel_id=1, source_target_pairs={{0,1},{1,0},{2,3},{3,2},{4,5},{5,4},{6,7},{7,6},{8,9},{9,8},{10,11... | collective-permute-start | bytes 196616 | tf_op jit(solution)/shard_map/ppermute | solution.py:162
  16.6 1.7 %collective-permute-start.9 = (bf16[64,2048]{1,0:T(8,128)(2,1)S(1)}, bf16[64,2048]{1,0:T(8,128)(2,1)S(1)}, u32[]{:S(2)}, u32[]{:S(2)}) collective-permute-start(bf16[64,2048]{1,0:T(8,128)(2,1)S(1)} %shard_map.98), channel_id=1, source_target_pairs={{0,1},{1,0},{2,3},{3,2},{4,5},{5,4},{6,7},{7,6},{8,9},{9,8},{10,11... | collective-permute-start | bytes 786440 | tf_op jit(solution)/shard_map/ppermute | solution.py:162
  18.4 9.7 %collective-permute-start.10 = (bf16[16,2048]{1,0:T(8,128)(2,1)S(1)}, bf16[16,2048]{1,0:T(8,128)(2,1)S(1)}, u32[]{:S(2)}, u32[]{:S(2)}) collective-permute-start(bf16[16,2048]{1,0:T(8,128)(2,1)S(1)} %get-tuple-element.19), channel_id=1, source_target_pairs={{0,14},{2,12},{4,10},{6,8},{1,7},{3,5},{5,3},{7,1},{8,6},{10,4},{1... | collective-permute-start | bytes 196616 | tf_op jit(solution)/shard_map/ppermute | solution.py:176
  24.1 5.4 %collective-permute-start.11 = (bf16[16,2048]{1,0:T(8,128)(2,1)S(1)}, bf16[16,2048]{1,0:T(8,128)(2,1)S(1)}, u32[]{:S(2)}, u32[]{:S(2)}) collective-permute-start(bf16[16,2048]{1,0:T(8,128)(2,1)S(1)} %get-tuple-element.20), channel_id=1, source_target_pairs={{0,12},{2,14},{4,8},{6,10},{1,5},{3,7},{5,1},{7,3},{8,4},{10,6},{1... | collective-permute-start | bytes 196616 | tf_op jit(solution)/shard_map/ppermute | solution.py:176
  24.1 5.4 %collective-permute-start.12 = (bf16[16,2048]{1,0:T(8,128)(2,1)S(1)}, bf16[16,2048]{1,0:T(8,128)(2,1)S(1)}, u32[]{:S(2)}, u32[]{:S(2)}) collective-permute-start(bf16[16,2048]{1,0:T(8,128)(2,1)S(1)} %get-tuple-element.21), channel_id=1, source_target_pairs={{0,10},{2,8},{4,14},{6,12},{1,3},{3,1},{5,7},{7,5},{8,2},{10,0},{1... | collective-permute-start | bytes 196616 | tf_op jit(solution)/shard_map/ppermute | solution.py:176
  26.0 6.1 %collective-permute-start.13 = (bf16[16,2048]{1,0:T(8,128)(2,1)S(1)}, bf16[16,2048]{1,0:T(8,128)(2,1)S(1)}, u32[]{:S(2)}, u32[]{:S(2)}) collective-permute-start(bf16[16,2048]{1,0:T(8,128)(2,1)S(1)} %fusion), channel_id=1, source_target_pairs={{0,8},{2,10},{4,12},{6,14},{1,1},{3,3},{5,5},{7,7},{8,0},{10,2},{1... | collective-permute-start | bytes 196616 | tf_op jit(solution)/shard_map/ppermute | solution.py:176
  32.3 5.2 %collective-permute-start.16 = (bf16[16,2048]{1,0:T(8,128)(2,1)S(1)}, bf16[16,2048]{1,0:T(8,128)(2,1)S(1)}, u32[]{:S(2)}, u32[]{:S(2)}) collective-permute-start(bf16[16,2048]{1,0:T(8,128)(2,1)S(1)} %get-tuple-element.24.refs_0_), channel_id=1, source_target_pairs={{0,6},{1,7},{2,4},{3,5},{4,2},{5,3},{6,0},{7,1},{8,14},{9,15},{10,... | collective-permute-start | bytes 196616 | tf_op jit(solution)/shard_map/ppermute | solution.py:166
  34.8 4.3 %collective-permute-start.15 = (bf16[16,2048]{1,0:T(8,128)(2,1)S(1)}, bf16[16,2048]{1,0:T(8,128)(2,1)S(1)}, u32[]{:S(2)}, u32[]{:S(2)}) collective-permute-start(bf16[16,2048]{1,0:T(8,128)(2,1)S(1)} %get-tuple-element.24.refs_0_), channel_id=1, source_target_pairs={{0,4},{1,5},{2,6},{3,7},{4,0},{5,1},{6,2},{7,3},{8,12},{9,13},{10,... | collective-permute-start | bytes 196616 | tf_op jit(solution)/shard_map/ppermute | solution.py:166
  35.3 4.3 %collective-permute-start.14 = (bf16[16,2048]{1,0:T(8,128)(2,1)S(1)}, bf16[16,2048]{1,0:T(8,128)(2,1)S(1)}, u32[]{:S(2)}, u32[]{:S(2)}) collective-permute-start(bf16[16,2048]{1,0:T(8,128)(2,1)S(1)} %get-tuple-element.24.refs_0_), channel_id=1, source_target_pairs={{0,2},{1,3},{2,0},{3,1},{4,6},{5,7},{6,4},{7,5},{8,10},{9,11},{10,... | collective-permute-start | bytes 196616 | tf_op jit(solution)/shard_map/ppermute | solution.py:166
  39.6 1.9 %collective-permute-start.17 = (bf16[64,2048]{1,0:T(8,128)(2,1)S(1)}, bf16[64,2048]{1,0:T(8,128)(2,1)S(1)}, u32[]{:S(2)}, u32[]{:S(2)}) collective-permute-start(bf16[64,2048]{1,0:T(8,128)(2,1)S(1)} %shard_map.101.refs_0_), channel_id=1, source_target_pairs={{0,1},{1,0},{2,3},{3,2},{4,5},{5,4},{6,7},{7,6},{8,9},{9,8},{10,11... | collective-permute-start | bytes 786440 | tf_op jit(solution)/shard_map/ppermute | solution.py:162
  40.8 2.3 %collective-permute-start.19 = (bf16[32,2048]{1,0:T(8,128)(2,1)S(1)}, bf16[32,2048]{1,0:T(8,128)(2,1)S(1)}, u32[]{:S(2)}, u32[]{:S(2)}) collective-permute-start(bf16[32,2048]{1,0:T(8,128)(2,1)S(1)} %get-tuple-element.28), channel_id=1, source_target_pairs={{0,1},{1,0},{2,3},{3,2},{4,5},{5,4},{6,7},{7,6},{8,9},{9,8},{10,11... | collective-permute-start | bytes 393224 | tf_op jit(solution)/shard_map/ppermute | solution.py:162
  41.4 6.4 %collective-permute-start.23 = (bf16[8,2048]{1,0:T(8,128)(2,1)S(1)}, bf16[8,2048]{1,0:T(8,128)(2,1)S(1)}, u32[]{:S(2)}, u32[]{:S(2)}) collective-permute-start(bf16[8,2048]{1,0:T(8,128)(2,1)S(1)} %get-tuple-element.56), channel_id=1, source_target_pairs={{0,1},{1,0},{2,3},{3,2},{4,5},{5,4},{6,7},{7,6},{8,9},{9,8},{10,11... | collective-permute-start | bytes 98312 | tf_op jit(solution)/shard_map/ppermute | solution.py:162
  42.6 1.5 %collective-permute-start.18 = (bf16[32,2048]{1,0:T(8,128)(2,1)S(1)}, bf16[32,2048]{1,0:T(8,128)(2,1)S(1)}, u32[]{:S(2)}, u32[]{:S(2)}) collective-permute-start(bf16[32,2048]{1,0:T(8,128)(2,1)S(1)} %get-tuple-element.26), channel_id=1, source_target_pairs={{0,1},{1,0},{2,3},{3,2},{4,5},{5,4},{6,7},{7,6},{8,9},{9,8},{10,11... | collective-permute-start | bytes 393224 | tf_op jit(solution)/shard_map/ppermute | solution.py:162
  44.3 5.4 %collective-permute-start.20 = (bf16[16,2048]{1,0:T(8,128)(2,1)S(1)}, bf16[16,2048]{1,0:T(8,128)(2,1)S(1)}, u32[]{:S(2)}, u32[]{:S(2)}) collective-permute-start(bf16[16,2048]{1,0:T(8,128)(2,1)S(1)} %pad_maximum_fusion.5), channel_id=1, source_target_pairs={{0,6},{1,7},{2,4},{3,5},{4,2},{5,3},{6,0},{7,1},{8,14},{9,15},{10,... | collective-permute-start | bytes 196616 | tf_op jit(solution)/shard_map/ppermute | solution.py:166
  45.8 5.2 %collective-permute-start.21 = (bf16[16,2048]{1,0:T(8,128)(2,1)S(1)}, bf16[16,2048]{1,0:T(8,128)(2,1)S(1)}, u32[]{:S(2)}, u32[]{:S(2)}) collective-permute-start(bf16[16,2048]{1,0:T(8,128)(2,1)S(1)} %get-tuple-element.30), channel_id=1, source_target_pairs={{0,4},{1,5},{2,6},{3,7},{4,0},{5,1},{6,2},{7,3},{8,12},{9,13},{10,... | collective-permute-start | bytes 196616 | tf_op jit(solution)/shard_map/ppermute | solution.py:166
  46.3 4.7 %collective-permute-start.22 = (bf16[16,2048]{1,0:T(8,128)(2,1)S(1)}, bf16[16,2048]{1,0:T(8,128)(2,1)S(1)}, u32[]{:S(2)}, u32[]{:S(2)}) collective-permute-start(bf16[16,2048]{1,0:T(8,128)(2,1)S(1)} %get-tuple-element.31), channel_id=1, source_target_pairs={{0,2},{1,3},{2,0},{3,1},{4,6},{5,7},{6,4},{7,5},{8,10},{9,11},{10,... | collective-permute-start | bytes 196616 | tf_op jit(solution)/shard_map/ppermute | solution.py:166

commit v7 on v6

--- a/solution.py
+++ b/solution.py
@@ -75,14 +75,61 @@
 
 def stacked(pieces, mark):
     vmem = pl.BlockSpec(memory_space=pltpu.VMEM)
-    rows, width = mark.shape
+    rows, width = pieces[0].shape
     return pl.pallas_call(
         stack_kernel,
-        out_shape=jax.ShapeDtypeStruct((len(pieces) * rows, width), mark.dtype),
+        out_shape=jax.ShapeDtypeStruct((len(pieces) * rows, width), pieces[0].dtype),
         in_specs=[vmem] * (1 + len(pieces)),
         out_specs=vmem,
         compiler_params=pltpu.CompilerParams(vmem_limit_bytes=LIMIT),
     )(mark, *pieces)
+
+
+def spread_kernel(slots, part_ref, got_ref, x_ref, *outs):
+    height = x_ref.shape[0]
+    for step, (slot, out) in enumerate(zip(slots, outs)):
+        place = slice(slot * height, (slot + 1) * height)
+        total = part_ref[place] + got_ref[place].astype(jnp.float32)
+        if step == 0:
+            total += x_ref[...].astype(jnp.float32)
+        out[...] = total.astype(out.dtype)
+
+
+def spread(slots, part, got, x):
+    vmem = pl.BlockSpec(memory_space=pltpu.VMEM)
+    return pl.pallas_call(
+        functools.partial(spread_kernel, slots),
+        out_shape=(jax.ShapeDtypeStruct(x.shape, x.dtype),) * len(slots),
+        in_specs=[vmem] * 3,
+        out_specs=(vmem,) * len(slots),
+        compiler_params=pltpu.CompilerParams(vmem_limit_bytes=LIMIT),
+    )(part, got, x)
+
+
+def spread_rows_kernel(slots, mine_ref, theirs_ref, to_mine_ref, to_theirs_ref, here_ref, there_ref, *outs):
+    rows = here_ref.shape[0]
+    groups = (mine_ref, to_mine_ref, here_ref), (theirs_ref, to_theirs_ref, there_ref)
+    for step, (slot, out) in enumerate(zip(slots, outs)):
+        place = slice(slot * rows, (slot + 1) * rows)
+        totals = [part[place] + got[place].astype(jnp.float32) for part, got, x in groups]
+        if step == 0:
+            totals = [total + x[...].astype(jnp.float32) for total, (part, got, x) in zip(totals, groups)]
+        out[...] = jnp.concatenate(totals, axis=0).astype(out.dtype)
+
+
+def spread_rows(slots, mine, theirs, to_mine, to_theirs, here, there):
+    vmem = pl.BlockSpec(memory_space=pltpu.VMEM)
+    rows, width = here.shape
+    return pl.pallas_call(
+        functools.partial(spread_rows_kernel, slots),
+        out_shape=tuple(
+            jax.ShapeDtypeStruct((2 * rows, width), jnp.float32 if step == 0 else here.dtype)
+            for step in range(len(slots))
+        ),
+        in_specs=[vmem] * 6,
+        out_specs=(vmem,) * len(slots),
+        compiler_params=pltpu.CompilerParams(vmem_limit_bytes=LIMIT),
+    )(mine, theirs, to_mine, to_theirs, here, there)
 
 
 def sum_kernel(*refs):
@@ -129,7 +176,7 @@
 
 def partial(tick, other, ready, split, chips, pieces, gains, weights, mark):
     vmem = pl.BlockSpec(memory_space=pltpu.VMEM)
-    rows, width = chips * mark.shape[0], mark.shape[1]
+    rows, width = sum(piece.shape[0] for piece in pieces), pieces[0].shape[1]
     size = sum(w.size // w.shape[0] for w in weights)
     out = jax.ShapeDtypeStruct((rows, width), jnp.bfloat16 if other else jnp.float32)
     if split:
@@ -204,31 +251,24 @@
         x = pieces[0] if tick == 0 else state
         height = x.shape[0]
         mark = passed(state)
+        pieces = pieces[::-1]
         slots = [step if chips & (chips - 1) == 0 else (chips - step) % chips for step in range(chips)]
+        slots = [chips - 1 - slot for slot in slots]
         if tick + 1 == ticks:
             break
         siblings = [to_sibling(piece) for piece in pieces]
         part = partial(tick, 0, tick > 0, False, chips, pieces, gains[0], weights, mark)
         given = partial(tick, 1, tick > 0, False, chips, siblings, gains[0], weights, mark)
-        part = part + to_sibling(given).astype(jnp.float32)
-        sums = [part[slot * height : (slot + 1) * height] for slot in slots]
-        sums[0] = sums[0] + x.astype(jnp.float32)
-        sums = lax.optimization_barrier([part.astype(jnp.bfloat16) for part in sums])
+        sums = spread(slots, part, to_sibling(given), x)
         sums = [to_next(part, tick + 1, step) for step, part in enumerate(sums)]
         state, normed = next_rows(tick + 1, gains[0], entering[tick], sums[::-1])
 
     rows_here = jnp.where(core == 0, x[:rows], x[rows:])
     rows_there = to_sibling(jnp.where(core == 0, x[rows:], x[:rows]))
-    stack = stacked(pieces, mark)
+    stack = stacked(pieces, rows_there)
     mine, given = partial(tick, 0, tick > 0, True, chips, [stack], gains[0], weights, mark)
     theirs, back = partial(tick, 1, tick > 0, True, chips, [to_sibling(stack)], gains[0], weights, mark)
-    theirs = theirs + to_sibling(given).astype(jnp.float32)
-    mine = mine + to_sibling(back).astype(jnp.float32)
-    sums = [
-        jnp.concatenate([part[slot * rows : (slot + 1) * rows] for part in (mine, theirs)], axis=0) for slot in slots
-    ]
-    sums[0] = sums[0] + jnp.concatenate([rows_here, rows_there], axis=0).astype(jnp.float32)
-    sums[1:] = lax.optimization_barrier([part.astype(jnp.bfloat16) for part in sums[1:]])
+    sums = list(spread_rows(slots, mine, theirs, to_sibling(back), to_sibling(given), rows_here, rows_there))
     sums[1:] = [to_chip(part, step) for step, part in enumerate(sums) if step > 0]
     state = summed(sums[::-1])
     role = role_at(ticks - 1)

time: 51.9 us -> 51.4 us (level)
    ppermute x10, waiting for transfers between devices: 2.71 us -> 4.29 us  [to_sibling(): return lax.ppermute(value, 'zero', [(k, k ^ 1) for k in range(zero)])]
    ppermute x6, waiting for transfers between devices: 6.92 us -> 5.46 us  [to_chip(): return lax.ppermute(value, 'zero', pairs)]
  transfers between devices with their start and end apart: 24 -> 24, of which waited for: 13 -> 14; matrix products, arithmetic and copies ran while one was open for 0% -> 0% of each run, Pallas kernels for 7% -> 7%
where the time goes in v7:
time: 51.4 us; the launch traced here: 51.2 us
  starting transfers between devices  27.4 us (53%)
  waiting for transfers between devices  16 us (31%)
  Pallas kernels  5.05 us (10%)
  between operations  0.94 us (2%)
  local copies, waits for them, and re-layouts  0.81 us (2%)
  other arithmetic  0.71 us (1%)
    ppermute x8, starting transfers between devices, to_next(): return lax.ppermute(value, both, pairs)  14.8 us
    ppermute x6, starting transfers between devices, to_chip(): return lax.ppermute(value, 'zero', pairs)  7.11 us
    ppermute x8, waiting for transfers between devices, to_next(): return lax.ppermute(value, both, pairs)  6.28 us
    ppermute x10, starting transfers between devices, to_sibling(): return lax.ppermute(value, 'zero', [(k, k ^ 1) for k in range(zero)])  5.48 us
    ppermute x6, waiting for transfers between devices, to_chip(): return lax.ppermute(value, 'zero', pairs)  5.46 us
    pallas_call x4, Pallas kernels, partial(): pl.pallas_call(functools.partial(group_kernel, tick, other, ready, len(pi...  4.73 us
    ppermute x10, waiting for transfers between devices, to_sibling(): return lax.ppermute(value, 'zero', [(k, k ^ 1) for k in range(zero)])  4.29 us
  transfers between devices with their start and end apart: 24, of which 14 were waited for; matrix products, arithmetic and copies ran while one was open for 0% of the time, Pallas kernels for 7%

profile of v7, /device:TPU:0, one launch (start us, length us, event | category | flops | bytes accessed | tf_op | source)
XLA Modules:
  0.0 51.2 jit_solution(6628503063077879283)
XLA Ops:
  0.7 0.7 %copy-done = bf16[2,8,2048]{2,1,0:T(8,128)(2,1)S(1)} copy-done((bf16[2,8,2048]{2,1,0:T(8,128)(2,1)S(1)}, bf16[2,8,2048]{2,1,0:T(8,128)(2,1)}, u32[]{:S(2)}) %copy-start) | copy-done | bytes 65560
  1.8 0.5 %collective-permute-start = (bf16[16,2048]{1,0:T(8,128)(2,1)S(1)}, bf16[16,2048]{1,0:T(8,128)(2,1)S(1)}, u32[]{:S(2)}, u32[]{:S(2)}) collective-permute-start(bf16[16,2048]{1,0:T(8,128)(2,1)S(1)} %pad_maximum_fusion), channel_id=1, source_target_pairs={{0,1},{1,0},{2,3},{3,2},{4,5},{5,4},{6,7},{7,6},{8,9},{9,8},{10,11... | collective-permute-start | bytes 196616 | tf_op jit(solution)/shard_map/ppermute | solution.py:209
  2.4 0.9 %collective-permute-done = bf16[16,2048]{1,0:T(8,128)(2,1)S(1)} collective-permute-done((bf16[16,2048]{1,0:T(8,128)(2,1)S(1)}, bf16[16,2048]{1,0:T(8,128)(2,1)S(1)}, u32[]{:S(2)}, u32[]{:S(2)}) %collective-permute-start) | collective-permute-done | bytes 65568 | tf_op jit(solution)/shard_map/ppermute | solution.py:209
  3.3 3.9 %collective-permute-start.1 = (bf16[16,2048]{1,0:T(8,128)(2,1)S(1)}, bf16[16,2048]{1,0:T(8,128)(2,1)S(1)}, u32[]{:S(2)}, u32[]{:S(2)}) collective-permute-start(bf16[16,2048]{1,0:T(8,128)(2,1)S(1)} %pad_maximum_fusion.2.x_ref), channel_id=1, source_target_pairs={{0,6},{2,4},{4,2},{6,0},{1,15},{3,13},{5,11},{7,9},{8,22},{10,20},... | collective-permute-start | bytes 196616 | tf_op jit(solution)/shard_map/ppermute | solution.py:223
  7.8 0.7 %collective-permute-start.4 = (bf16[16,2048]{1,0:T(8,128)(2,1)S(1)}, bf16[16,2048]{1,0:T(8,128)(2,1)S(1)}, u32[]{:S(2)}, u32[]{:S(2)}) collective-permute-start(bf16[16,2048]{1,0:T(8,128)(2,1)S(1)} %pad_maximum_fusion.2.x_ref), channel_id=1, source_target_pairs={{0,0},{2,2},{4,4},{6,6},{1,9},{3,11},{5,13},{7,15},{8,16},{10,18},... | collective-permute-start | bytes 196616 | tf_op jit(solution)/shard_map/ppermute | solution.py:223
  8.5 1.6 %collective-permute-done.1.refs_0_ = bf16[16,2048]{1,0:T(8,128)(2,1)S(1)} collective-permute-done((bf16[16,2048]{1,0:T(8,128)(2,1)S(1)}, bf16[16,2048]{1,0:T(8,128)(2,1)S(1)}, u32[]{:S(2)}, u32[]{:S(2)}) %collective-permute-start.1) | collective-permute-done | bytes 65568 | tf_op jit(solution)/shard_map/ppermute | solution.py:223
  10.2 1.6 %collective-permute-start.5 = (bf16[16,2048]{1,0:T(8,128)(2,1)S(1)}, bf16[16,2048]{1,0:T(8,128)(2,1)S(1)}, u32[]{:S(2)}, u32[]{:S(2)}) collective-permute-start(bf16[16,2048]{1,0:T(8,128)(2,1)S(1)} %collective-permute-done.1.refs_0_), channel_id=1, source_target_pairs={{0,1},{1,0},{2,3},{3,2},{4,5},{5,4},{6,7},{7,6},{8,9},{9,8},{10,11... | collective-permute-start | bytes 196616 | tf_op jit(solution)/shard_map/ppermute | solution.py:209
  12.1 0.6 %collective-permute-done.3.refs_2_ = bf16[16,2048]{1,0:T(8,128)(2,1)S(1)} collective-permute-done((bf16[16,2048]{1,0:T(8,128)(2,1)S(1)}, bf16[16,2048]{1,0:T(8,128)(2,1)S(1)}, u32[]{:S(2)}, u32[]{:S(2)}) %collective-permute-start.3) | collective-permute-done | bytes 65568 | tf_op jit(solution)/shard_map/ppermute | solution.py:223
  12.7 1.8 %collective-permute-start.8 = (bf16[16,2048]{1,0:T(8,128)(2,1)S(1)}, bf16[16,2048]{1,0:T(8,128)(2,1)S(1)}, u32[]{:S(2)}, u32[]{:S(2)}) collective-permute-start(bf16[16,2048]{1,0:T(8,128)(2,1)S(1)} %collective-permute-done.4.refs_3_.x_ref), channel_id=1, source_target_pairs={{0,1},{1,0},{2,3},{3,2},{4,5},{5,4},{6,7},{7,6},{8,9},{9,8},{10,11... | collective-permute-start | bytes 196616 | tf_op jit(solution)/shard_map/ppermute | solution.py:209
  14.5 0.9 %collective-permute-done.8.refs_3_ = bf16[16,2048]{1,0:T(8,128)(2,1)S(1)} collective-permute-done((bf16[16,2048]{1,0:T(8,128)(2,1)S(1)}, bf16[16,2048]{1,0:T(8,128)(2,1)S(1)}, u32[]{:S(2)}, u32[]{:S(2)}) %collective-permute-start.8) | collective-permute-done | bytes 65568 | tf_op jit(solution)/shard_map/ppermute | solution.py:209
  15.4 1.2 %shard_map.98 = bf16[64,2048]{1,0:T(8,128)(2,1)S(1)} custom-call(bf16[16,2048]{1,0:T(8,128)(2,1)S(1)} %shard_map.96.mark_ref, f32[2,2048]{1,0:T(2,128)S(1)} %bitcast.31, bf16[2,2048,512]{2,1,0:T(8,128)(2,1)S(1)} %bitcast.19, bf16[2,2048,512]{2,1,0:T(8,128)(2,1)S(1)} %bitcast.23, bf16[2,512,2048]{2,1,0:T(8,128)(2,1)S(1)} %bitcast.27, ...), custom_call_target="tpu_custom_call" | custom-call | flops 402653184 | bytes 6291456 | tf_op jit(solution)/shard_map/pallas_call | solution.py:184
  17.0 1.2 %shard_map.97.part_ref = f32[64,2048]{1,0:T(8,128)S(1)} custom-call(bf16[16,2048]{1,0:T(8,128)(2,1)S(1)} %shard_map.96.mark_ref, f32[2,2048]{1,0:T(2,128)S(1)} %bitcast.32, bf16[2,2048,512]{2,1,0:T(8,128)(2,1)S(1)} %bitcast.20, bf16[2,2048,512]{2,1,0:T(8,128)(2,1)S(1)} %bitcast.24, bf16[2,512,2048]{2,1,0:T(8,128)(2,1)S(1)} %bitcast.28, ...), custom_call_target="tpu_custom_call" | custom-call | flops 402653184 | bytes 6291456 | tf_op jit(solution)/shard_map/pallas_call | solution.py:184
  18.3 5.6 %collective-permute-start.10 = (bf16[16,2048]{1,0:T(8,128)(2,1)S(1)}, bf16[16,2048]{1,0:T(8,128)(2,1)S(1)}, u32[]{:S(2)}, u32[]{:S(2)}) collective-permute-start(bf16[16,2048]{1,0:T(8,128)(2,1)S(1)} %get-tuple-element.20), channel_id=1, source_target_pairs={{0,14},{2,12},{4,10},{6,8},{1,7},{3,5},{5,3},{7,1},{8,6},{10,4},{1... | collective-permute-start | bytes 196616 | tf_op jit(solution)/shard_map/ppermute | solution.py:223
  24.0 1.9 %collective-permute-start.12 = (bf16[16,2048]{1,0:T(8,128)(2,1)S(1)}, bf16[16,2048]{1,0:T(8,128)(2,1)S(1)}, u32[]{:S(2)}, u32[]{:S(2)}) collective-permute-start(bf16[16,2048]{1,0:T(8,128)(2,1)S(1)} %get-tuple-element.22), channel_id=1, source_target_pairs={{0,10},{2,8},{4,14},{6,12},{1,3},{3,1},{5,7},{7,5},{8,2},{10,0},{1... | collective-permute-start | bytes 196616 | tf_op jit(solution)/shard_map/ppermute | solution.py:223
  25.9 2.1 %collective-permute-start.13 = (bf16[16,2048]{1,0:T(8,128)(2,1)S(1)}, bf16[16,2048]{1,0:T(8,128)(2,1)S(1)}, u32[]{:S(2)}, u32[]{:S(2)}) collective-permute-start(bf16[16,2048]{1,0:T(8,128)(2,1)S(1)} %get-tuple-element.23), channel_id=1, source_target_pairs={{0,8},{2,10},{4,12},{6,14},{1,1},{3,3},{5,5},{7,7},{8,0},{10,2},{1... | collective-permute-start | bytes 196616 | tf_op jit(solution)/shard_map/ppermute | solution.py:223
  28.0 1.4 %collective-permute-done.11.refs_1_ = bf16[16,2048]{1,0:T(8,128)(2,1)S(1)} collective-permute-done((bf16[16,2048]{1,0:T(8,128)(2,1)S(1)}, bf16[16,2048]{1,0:T(8,128)(2,1)S(1)}, u32[]{:S(2)}, u32[]{:S(2)}) %collective-permute-start.11) | collective-permute-done | bytes 65568 | tf_op jit(solution)/shard_map/ppermute | solution.py:223
  29.4 2.6 %collective-permute-done.13.refs_3_ = bf16[16,2048]{1,0:T(8,128)(2,1)S(1)} collective-permute-done((bf16[16,2048]{1,0:T(8,128)(2,1)S(1)}, bf16[16,2048]{1,0:T(8,128)(2,1)S(1)}, u32[]{:S(2)}, u32[]{:S(2)}) %collective-permute-start.13) | collective-permute-done | bytes 65568 | tf_op jit(solution)/shard_map/ppermute | solution.py:223
  32.2 2.5 %collective-permute-start.15 = (bf16[16,2048]{1,0:T(8,128)(2,1)S(1)}, bf16[16,2048]{1,0:T(8,128)(2,1)S(1)}, u32[]{:S(2)}, u32[]{:S(2)}) collective-permute-start(bf16[16,2048]{1,0:T(8,128)(2,1)S(1)} %get-tuple-element.25.refs_3_), channel_id=1, source_target_pairs={{0,6},{1,7},{2,4},{3,5},{4,2},{5,3},{6,0},{7,1},{8,14},{9,15},{10,... | collective-permute-start | bytes 196616 | tf_op jit(solution)/shard_map/ppermute | solution.py:213
  34.7 0.5 collective-permute-start.16
  35.3 0.5 %collective-permute-start.17 = (bf16[16,2048]{1,0:T(8,128)(2,1)S(1)}, bf16[16,2048]{1,0:T(8,128)(2,1)S(1)}, u32[]{:S(2)}, u32[]{:S(2)}) collective-permute-start(bf16[16,2048]{1,0:T(8,128)(2,1)S(1)} %get-tuple-element.25.refs_3_), channel_id=1, source_target_pairs={{0,2},{1,3},{2,0},{3,1},{4,6},{5,7},{6,4},{7,5},{8,10},{9,11},{10,... | collective-permute-start | bytes 196616 | tf_op jit(solution)/shard_map/ppermute | solution.py:213
  35.9 1.2 %collective-permute-done.14.mark_ref.there_ref = bf16[8,2048]{1,0:T(8,128)(2,1)S(1)} collective-permute-done((bf16[8,2048]{1,0:T(8,128)(2,1)S(1)}, bf16[8,2048]{1,0:T(8,128)(2,1)S(1)}, u32[]{:S(2)}, u32[]{:S(2)}) %collective-permute-start.14) | collective-permute-done | bytes 32800 | tf_op jit(solution)/shard_map/ppermute | solution.py:209
  37.5 1.5 %collective-permute-done.16.refs_1_ = bf16[16,2048]{1,0:T(8,128)(2,1)S(1)} collective-permute-done((bf16[16,2048]{1,0:T(8,128)(2,1)S(1)}, bf16[16,2048]{1,0:T(8,128)(2,1)S(1)}, u32[]{:S(2)}, u32[]{:S(2)}) %collective-permute-start.16) | collective-permute-done | bytes 65568 | tf_op jit(solution)/shard_map/ppermute | solution.py:213
  39.0 0.5 collective-permute-done.17.refs_2_
  39.6 1.2 %shard_map.103 = (f32[32,2048]{1,0:T(8,128)S(1)}, bf16[32,2048]{1,0:T(8,128)(2,1)S(1)}) custom-call(bf16[16,2048]{1,0:T(8,128)(2,1)S(1)} %shard_map.101.mark_ref, f32[2,2048]{1,0:T(2,128)S(1)} %bitcast.34, bf16[2,2048,512]{2,1,0:T(8,128)(2,1)S(1)} %bitcast.21, bf16[2,2048,512]{2,1,0:T(8,128)(2,1)S(1)} %bitcast.25, bf16[2,512,2048]{2,1,0:T(8,128)(2,1)S(1)} %bitcast.29, ...), custom_call_target="tpu_custom_call" | custom-call | flops 402653184 | bytes 6291456 | tf_op jit(solution)/shard_map/pallas_call | solution.py:184
  40.8 0.5 %collective-permute-start.20 = (bf16[32,2048]{1,0:T(8,128)(2,1)S(1)}, bf16[32,2048]{1,0:T(8,128)(2,1)S(1)}, u32[]{:S(2)}, u32[]{:S(2)}) collective-permute-start(bf16[32,2048]{1,0:T(8,128)(2,1)S(1)} %get-tuple-element.29), channel_id=1, source_target_pairs={{0,1},{1,0},{2,3},{3,2},{4,5},{5,4},{6,7},{7,6},{8,9},{9,8},{10,11... | collective-permute-start | bytes 393224 | tf_op jit(solution)/shard_map/ppermute | solution.py:209
  41.3 1.1 %shard_map.104 = (f32[32,2048]{1,0:T(8,128)S(1)}, bf16[32,2048]{1,0:T(8,128)(2,1)S(1)}) custom-call(bf16[16,2048]{1,0:T(8,128)(2,1)S(1)} %shard_map.101.mark_ref, f32[2,2048]{1,0:T(2,128)S(1)} %bitcast.35, bf16[2,2048,512]{2,1,0:T(8,128)(2,1)S(1)} %bitcast.22, bf16[2,2048,512]{2,1,0:T(8,128)(2,1)S(1)} %bitcast.26, bf16[2,512,2048]{2,1,0:T(8,128)(2,1)S(1)} %bitcast.30, ...), custom_call_target="tpu_custom_call" | custom-call | flops 402653184 | bytes 6291456 | tf_op jit(solution)/shard_map/pallas_call | solution.py:184
  42.6 1.3 %collective-permute-done.19.to_mine_ref = bf16[32,2048]{1,0:T(8,128)(2,1)S(1)} collective-permute-done((bf16[32,2048]{1,0:T(8,128)(2,1)S(1)}, bf16[32,2048]{1,0:T(8,128)(2,1)S(1)}, u32[]{:S(2)}, u32[]{:S(2)}) %collective-permute-start.19) | collective-permute-done | bytes 131104 | tf_op jit(solution)/shard_map/ppermute | solution.py:209
  44.0 1.6 %collective-permute-start.21 = (bf16[16,2048]{1,0:T(8,128)(2,1)S(1)}, bf16[16,2048]{1,0:T(8,128)(2,1)S(1)}, u32[]{:S(2)}, u32[]{:S(2)}) collective-permute-start(bf16[16,2048]{1,0:T(8,128)(2,1)S(1)} %get-tuple-element.30), channel_id=1, source_target_pairs={{0,6},{1,7},{2,4},{3,5},{4,2},{5,3},{6,0},{7,1},{8,14},{9,15},{10,... | collective-permute-start | bytes 196616 | tf_op jit(solution)/shard_map/ppermute | solution.py:213
  46.0 1.5 %collective-permute-start.23 = (bf16[16,2048]{1,0:T(8,128)(2,1)S(1)}, bf16[16,2048]{1,0:T(8,128)(2,1)S(1)}, u32[]{:S(2)}, u32[]{:S(2)}) collective-permute-start(bf16[16,2048]{1,0:T(8,128)(2,1)S(1)} %get-tuple-element.32), channel_id=1, source_target_pairs={{0,2},{1,3},{2,0},{3,1},{4,6},{5,7},{6,4},{7,5},{8,10},{9,11},{10,... | collective-permute-start | bytes 196616 | tf_op jit(solution)/shard_map/ppermute | solution.py:213
  47.5 1.8 %collective-permute-done.21.refs_0_ = bf16[16,2048]{1,0:T(8,128)(2,1)S(1)} collective-permute-done((bf16[16,2048]{1,0:T(8,128)(2,1)S(1)}, bf16[16,2048]{1,0:T(8,128)(2,1)S(1)}, u32[]{:S(2)}, u32[]{:S(2)}) %collective-permute-start.21) | collective-permute-done | bytes 65568 | tf_op jit(solution)/shard_map/ppermute | solution.py:213
  49.3 1.2 %collective-permute-done.22.refs_1_ = bf16[16,2048]{1,0:T(8,128)(2,1)S(1)} collective-permute-done((bf16[16,2048]{1,0:T(8,128)(2,1)S(1)}, bf16[16,2048]{1,0:T(8,128)(2,1)S(1)}, u32[]{:S(2)}, u32[]{:S(2)}) %collective-permute-start.22) | collective-permute-done | bytes 65568 | tf_op jit(solution)/shard_map/ppermute | solution.py:213
  50.6 0.6 %select_bitcast_fusion = (bf16[1,8,2048]{2,1,0:T(8,128)(2,1)}, bf16[1,8,2048]{2,1,0:T(8,128)(2,1)}) fusion(pred[]{:T(512)S(6)} %eq.37, bf16[16,2048]{1,0:T(8,128)(2,1)S(1)} %shard_map.106), kind=kLoop, calls=%fused_computation.8 | loop fusion | flops 32768 | bytes 131073 | tf_op jit(solution)/shard_map/broadcast_in_dim | solution.py:277
  (55 shorter events, 3.4 us)
Async XLA Ops:
  0.6 0.8 %copy-start = (bf16[2,8,2048]{2,1,0:T(8,128)(2,1)S(1)}, bf16[2,8,2048]{2,1,0:T(8,128)(2,1)}, u32[]{:S(2)}) copy-start(bf16[2,8,2048]{2,1,0:T(8,128)(2,1)} %param.10) | copy-start | bytes 196612
  0.7 0.8 %copy-start.7 = (s32[2]{0:T(128)S(1)}, s32[2]{0:T(128)}, u32[]{:S(2)}) copy-start(s32[2]{0:T(128)} %param.11) | copy-start | bytes 28
  0.7 1.1 %copy-start.5 = (bf16[1,8,2048]{2,1,0:T(8,128)(2,1)S(1)}, bf16[1,8,2048]{2,1,0:T(8,128)(2,1)}, u32[]{:S(2)}) copy-start(bf16[1,8,2048]{2,1,0:T(8,128)(2,1)} %param.8) | copy-start | bytes 98308
  0.7 1.1 %copy-start.6 = (bf16[1,8,2048]{2,1,0:T(8,128)(2,1)S(1)}, bf16[1,8,2048]{2,1,0:T(8,128)(2,1)}, u32[]{:S(2)}) copy-start(bf16[1,8,2048]{2,1,0:T(8,128)(2,1)} %param.9) | copy-start | bytes 98308
  1.8 1.4 %collective-permute-start = (bf16[16,2048]{1,0:T(8,128)(2,1)S(1)}, bf16[16,2048]{1,0:T(8,128)(2,1)S(1)}, u32[]{:S(2)}, u32[]{:S(2)}) collective-permute-start(bf16[16,2048]{1,0:T(8,128)(2,1)S(1)} %pad_maximum_fusion), channel_id=1, source_target_pairs={{0,1},{1,0},{2,3},{3,2},{4,5},{5,4},{6,7},{7,6},{8,9},{9,8},{10,11... | collective-permute-start | bytes 196616 | tf_op jit(solution)/shard_map/ppermute | solution.py:209
  3.3 12.1 %copy-start.1 = (bf16[1,2,2048,512]{3,2,1,0:T(8,128)(2,1)S(1)}, bf16[1,2,2048,512]{3,2,1,0:T(8,128)(2,1)}, u32[]{:S(2)}) copy-start(bf16[1,2,2048,512]{3,2,1,0:T(8,128)(2,1)} %param.13) | copy-start | bytes 12582916
  3.3 12.1 %copy-start.2 = (bf16[1,2,2048,512]{3,2,1,0:T(8,128)(2,1)S(1)}, bf16[1,2,2048,512]{3,2,1,0:T(8,128)(2,1)}, u32[]{:S(2)}) copy-start(bf16[1,2,2048,512]{3,2,1,0:T(8,128)(2,1)} %param.14) | copy-start | bytes 12582916
  3.3 12.1 %copy-start.3 = (bf16[1,2,512,2048]{3,2,1,0:T(8,128)(2,1)S(1)}, bf16[1,2,512,2048]{3,2,1,0:T(8,128)(2,1)}, u32[]{:S(2)}) copy-start(bf16[1,2,512,2048]{3,2,1,0:T(8,128)(2,1)} %param.15) | copy-start | bytes 12582916
  3.3 12.1 %copy-start.4 = (f32[1,2,2048]{2,1,0:T(2,128)S(1)}, f32[1,2,2048]{2,1,0:T(2,128)}, u32[]{:S(2)}) copy-start(f32[1,2,2048]{2,1,0:T(2,128)} %param.12) | copy-start | bytes 49156
  3.3 6.8 %collective-permute-start.1 = (bf16[16,2048]{1,0:T(8,128)(2,1)S(1)}, bf16[16,2048]{1,0:T(8,128)(2,1)S(1)}, u32[]{:S(2)}, u32[]{:S(2)}) collective-permute-start(bf16[16,2048]{1,0:T(8,128)(2,1)S(1)} %pad_maximum_fusion.2.x_ref), channel_id=1, source_target_pairs={{0,6},{2,4},{4,2},{6,0},{1,15},{3,13},{5,11},{7,9},{8,22},{10,20},... | collective-permute-start | bytes 196616 | tf_op jit(solution)/shard_map/ppermute | solution.py:223
  7.2 4.5 %collective-permute-start.2 = (bf16[16,2048]{1,0:T(8,128)(2,1)S(1)}, bf16[16,2048]{1,0:T(8,128)(2,1)S(1)}, u32[]{:S(2)}, u32[]{:S(2)}) collective-permute-start(bf16[16,2048]{1,0:T(8,128)(2,1)S(1)} %pad_maximum_fusion.2.x_ref), channel_id=1, source_target_pairs={{0,4},{2,6},{4,0},{6,2},{1,13},{3,15},{5,9},{7,11},{8,20},{10,22},... | collective-permute-start | bytes 196616 | tf_op jit(solution)/shard_map/ppermute | solution.py:223
  7.7 5.0 %collective-permute-start.3 = (bf16[16,2048]{1,0:T(8,128)(2,1)S(1)}, bf16[16,2048]{1,0:T(8,128)(2,1)S(1)}, u32[]{:S(2)}, u32[]{:S(2)}) collective-permute-start(bf16[16,2048]{1,0:T(8,128)(2,1)S(1)} %pad_maximum_fusion.2.x_ref), channel_id=1, source_target_pairs={{0,2},{2,0},{4,6},{6,4},{1,11},{3,9},{5,15},{7,13},{8,18},{10,16},... | collective-permute-start | bytes 196616 | tf_op jit(solution)/shard_map/ppermute | solution.py:223
  7.8 4.8 %collective-permute-start.4 = (bf16[16,2048]{1,0:T(8,128)(2,1)S(1)}, bf16[16,2048]{1,0:T(8,128)(2,1)S(1)}, u32[]{:S(2)}, u32[]{:S(2)}) collective-permute-start(bf16[16,2048]{1,0:T(8,128)(2,1)S(1)} %pad_maximum_fusion.2.x_ref), channel_id=1, source_target_pairs={{0,0},{2,2},{4,4},{6,6},{1,9},{3,11},{5,13},{7,15},{8,16},{10,18},... | collective-permute-start | bytes 196616 | tf_op jit(solution)/shard_map/ppermute | solution.py:223
  10.2 4.3 %collective-permute-start.5 = (bf16[16,2048]{1,0:T(8,128)(2,1)S(1)}, bf16[16,2048]{1,0:T(8,128)(2,1)S(1)}, u32[]{:S(2)}, u32[]{:S(2)}) collective-permute-start(bf16[16,2048]{1,0:T(8,128)(2,1)S(1)} %collective-permute-done.1.refs_0_), channel_id=1, source_target_pairs={{0,1},{1,0},{2,3},{3,2},{4,5},{5,4},{6,7},{7,6},{8,9},{9,8},{10,11... | collective-permute-start | bytes 196616 | tf_op jit(solution)/shard_map/ppermute | solution.py:209
  11.8 2.7 %collective-permute-start.6 = (bf16[16,2048]{1,0:T(8,128)(2,1)S(1)}, bf16[16,2048]{1,0:T(8,128)(2,1)S(1)}, u32[]{:S(2)}, u32[]{:S(2)}) collective-permute-start(bf16[16,2048]{1,0:T(8,128)(2,1)S(1)} %collective-permute-done.2.refs_1_), channel_id=1, source_target_pairs={{0,1},{1,0},{2,3},{3,2},{4,5},{5,4},{6,7},{7,6},{8,9},{9,8},{10,11... | collective-permute-start | bytes 196616 | tf_op jit(solution)/shard_map/ppermute | solution.py:209
  12.7 1.8 %collective-permute-start.7 = (bf16[16,2048]{1,0:T(8,128)(2,1)S(1)}, bf16[16,2048]{1,0:T(8,128)(2,1)S(1)}, u32[]{:S(2)}, u32[]{:S(2)}) collective-permute-start(bf16[16,2048]{1,0:T(8,128)(2,1)S(1)} %collective-permute-done.3.refs_2_), channel_id=1, source_target_pairs={{0,1},{1,0},{2,3},{3,2},{4,5},{5,4},{6,7},{7,6},{8,9},{9,8},{10,11... | collective-permute-start | bytes 196616 | tf_op jit(solution)/shard_map/ppermute | solution.py:209
  12.7 2.7 %collective-permute-start.8 = (bf16[16,2048]{1,0:T(8,128)(2,1)S(1)}, bf16[16,2048]{1,0:T(8,128)(2,1)S(1)}, u32[]{:S(2)}, u32[]{:S(2)}) collective-permute-start(bf16[16,2048]{1,0:T(8,128)(2,1)S(1)} %collective-permute-done.4.refs_3_.x_ref), channel_id=1, source_target_pairs={{0,1},{1,0},{2,3},{3,2},{4,5},{5,4},{6,7},{7,6},{8,9},{9,8},{10,11... | collective-permute-start | bytes 196616 | tf_op jit(solution)/shard_map/ppermute | solution.py:209
  16.6 1.7 %collective-permute-start.9 = (bf16[64,2048]{1,0:T(8,128)(2,1)S(1)}, bf16[64,2048]{1,0:T(8,128)(2,1)S(1)}, u32[]{:S(2)}, u32[]{:S(2)}) collective-permute-start(bf16[64,2048]{1,0:T(8,128)(2,1)S(1)} %shard_map.98), channel_id=1, source_target_pairs={{0,1},{1,0},{2,3},{3,2},{4,5},{5,4},{6,7},{7,6},{8,9},{9,8},{10,11... | collective-permute-start | bytes 786440 | tf_op jit(solution)/shard_map/ppermute | solution.py:209
  18.3 9.7 %collective-permute-start.10 = (bf16[16,2048]{1,0:T(8,128)(2,1)S(1)}, bf16[16,2048]{1,0:T(8,128)(2,1)S(1)}, u32[]{:S(2)}, u32[]{:S(2)}) collective-permute-start(bf16[16,2048]{1,0:T(8,128)(2,1)S(1)} %get-tuple-element.20), channel_id=1, source_target_pairs={{0,14},{2,12},{4,10},{6,8},{1,7},{3,5},{5,3},{7,1},{8,6},{10,4},{1... | collective-permute-start | bytes 196616 | tf_op jit(solution)/shard_map/ppermute | solution.py:223
  24.0 5.4 %collective-permute-start.11 = (bf16[16,2048]{1,0:T(8,128)(2,1)S(1)}, bf16[16,2048]{1,0:T(8,128)(2,1)S(1)}, u32[]{:S(2)}, u32[]{:S(2)}) collective-permute-start(bf16[16,2048]{1,0:T(8,128)(2,1)S(1)} %get-tuple-element.21), channel_id=1, source_target_pairs={{0,12},{2,14},{4,8},{6,10},{1,5},{3,7},{5,1},{7,3},{8,4},{10,6},{1... | collective-permute-start | bytes 196616 | tf_op jit(solution)/shard_map/ppermute | solution.py:223
  24.0 5.4 %collective-permute-start.12 = (bf16[16,2048]{1,0:T(8,128)(2,1)S(1)}, bf16[16,2048]{1,0:T(8,128)(2,1)S(1)}, u32[]{:S(2)}, u32[]{:S(2)}) collective-permute-start(bf16[16,2048]{1,0:T(8,128)(2,1)S(1)} %get-tuple-element.22), channel_id=1, source_target_pairs={{0,10},{2,8},{4,14},{6,12},{1,3},{3,1},{5,7},{7,5},{8,2},{10,0},{1... | collective-permute-start | bytes 196616 | tf_op jit(solution)/shard_map/ppermute | solution.py:223
  25.9 6.1 %collective-permute-start.13 = (bf16[16,2048]{1,0:T(8,128)(2,1)S(1)}, bf16[16,2048]{1,0:T(8,128)(2,1)S(1)}, u32[]{:S(2)}, u32[]{:S(2)}) collective-permute-start(bf16[16,2048]{1,0:T(8,128)(2,1)S(1)} %get-tuple-element.23), channel_id=1, source_target_pairs={{0,8},{2,10},{4,12},{6,14},{1,1},{3,3},{5,5},{7,7},{8,0},{10,2},{1... | collective-permute-start | bytes 196616 | tf_op jit(solution)/shard_map/ppermute | solution.py:223
  32.2 5.2 %collective-permute-start.15 = (bf16[16,2048]{1,0:T(8,128)(2,1)S(1)}, bf16[16,2048]{1,0:T(8,128)(2,1)S(1)}, u32[]{:S(2)}, u32[]{:S(2)}) collective-permute-start(bf16[16,2048]{1,0:T(8,128)(2,1)S(1)} %get-tuple-element.25.refs_3_), channel_id=1, source_target_pairs={{0,6},{1,7},{2,4},{3,5},{4,2},{5,3},{6,0},{7,1},{8,14},{9,15},{10,... | collective-permute-start | bytes 196616 | tf_op jit(solution)/shard_map/ppermute | solution.py:213
  34.7 4.3 %collective-permute-start.16 = (bf16[16,2048]{1,0:T(8,128)(2,1)S(1)}, bf16[16,2048]{1,0:T(8,128)(2,1)S(1)}, u32[]{:S(2)}, u32[]{:S(2)}) collective-permute-start(bf16[16,2048]{1,0:T(8,128)(2,1)S(1)} %get-tuple-element.25.refs_3_), channel_id=1, source_target_pairs={{0,4},{1,5},{2,6},{3,7},{4,0},{5,1},{6,2},{7,3},{8,12},{9,13},{10,... | collective-permute-start | bytes 196616 | tf_op jit(solution)/shard_map/ppermute | solution.py:213
  35.3 4.3 %collective-permute-start.17 = (bf16[16,2048]{1,0:T(8,128)(2,1)S(1)}, bf16[16,2048]{1,0:T(8,128)(2,1)S(1)}, u32[]{:S(2)}, u32[]{:S(2)}) collective-permute-start(bf16[16,2048]{1,0:T(8,128)(2,1)S(1)} %get-tuple-element.25.refs_3_), channel_id=1, source_target_pairs={{0,2},{1,3},{2,0},{3,1},{4,6},{5,7},{6,4},{7,5},{8,10},{9,11},{10,... | collective-permute-start | bytes 196616 | tf_op jit(solution)/shard_map/ppermute | solution.py:213
  35.8 1.3 %collective-permute-start.14 = (bf16[8,2048]{1,0:T(8,128)(2,1)S(1)}, bf16[8,2048]{1,0:T(8,128)(2,1)S(1)}, u32[]{:S(2)}, u32[]{:S(2)}) collective-permute-start(bf16[8,2048]{1,0:T(8,128)(2,1)S(1)} %get-tuple-element.43), channel_id=1, source_target_pairs={{0,1},{1,0},{2,3},{3,2},{4,5},{5,4},{6,7},{7,6},{8,9},{9,8},{10,11... | collective-permute-start | bytes 98312 | tf_op jit(solution)/shard_map/ppermute | solution.py:209
  39.5 1.8 %collective-permute-start.18 = (bf16[64,2048]{1,0:T(8,128)(2,1)S(1)}, bf16[64,2048]{1,0:T(8,128)(2,1)S(1)}, u32[]{:S(2)}, u32[]{:S(2)}) collective-permute-start(bf16[64,2048]{1,0:T(8,128)(2,1)S(1)} %shard_map.102.refs_0_), channel_id=1, source_target_pairs={{0,1},{1,0},{2,3},{3,2},{4,5},{5,4},{6,7},{7,6},{8,9},{9,8},{10,11... | collective-permute-start | bytes 786440 | tf_op jit(solution)/shard_map/ppermute | solution.py:209
  40.8 1.8 %collective-permute-start.20 = (bf16[32,2048]{1,0:T(8,128)(2,1)S(1)}, bf16[32,2048]{1,0:T(8,128)(2,1)S(1)}, u32[]{:S(2)}, u32[]{:S(2)}) collective-permute-start(bf16[32,2048]{1,0:T(8,128)(2,1)S(1)} %get-tuple-element.29), channel_id=1, source_target_pairs={{0,1},{1,0},{2,3},{3,2},{4,5},{5,4},{6,7},{7,6},{8,9},{9,8},{10,11... | collective-permute-start | bytes 393224 | tf_op jit(solution)/shard_map/ppermute | solution.py:209
  42.5 1.4 %collective-permute-start.19 = (bf16[32,2048]{1,0:T(8,128)(2,1)S(1)}, bf16[32,2048]{1,0:T(8,128)(2,1)S(1)}, u32[]{:S(2)}, u32[]{:S(2)}) collective-permute-start(bf16[32,2048]{1,0:T(8,128)(2,1)S(1)} %get-tuple-element.28), channel_id=1, source_target_pairs={{0,1},{1,0},{2,3},{3,2},{4,5},{5,4},{6,7},{7,6},{8,9},{9,8},{10,11... | collective-permute-start | bytes 393224 | tf_op jit(solution)/shard_map/ppermute | solution.py:209
  44.0 5.3 %collective-permute-start.21 = (bf16[16,2048]{1,0:T(8,128)(2,1)S(1)}, bf16[16,2048]{1,0:T(8,128)(2,1)S(1)}, u32[]{:S(2)}, u32[]{:S(2)}) collective-permute-start(bf16[16,2048]{1,0:T(8,128)(2,1)S(1)} %get-tuple-element.30), channel_id=1, source_target_pairs={{0,6},{1,7},{2,4},{3,5},{4,2},{5,3},{6,0},{7,1},{8,14},{9,15},{10,... | collective-permute-start | bytes 196616 | tf_op jit(solution)/shard_map/ppermute | solution.py:213
  45.5 5.0 %collective-permute-start.22 = (bf16[16,2048]{1,0:T(8,128)(2,1)S(1)}, bf16[16,2048]{1,0:T(8,128)(2,1)S(1)}, u32[]{:S(2)}, u32[]{:S(2)}) collective-permute-start(bf16[16,2048]{1,0:T(8,128)(2,1)S(1)} %get-tuple-element.31), channel_id=1, source_target_pairs={{0,4},{1,5},{2,6},{3,7},{4,0},{5,1},{6,2},{7,3},{8,12},{9,13},{10,... | collective-permute-start | bytes 196616 | tf_op jit(solution)/shard_map/ppermute | solution.py:213
  46.0 4.5 %collective-permute-start.23 = (bf16[16,2048]{1,0:T(8,128)(2,1)S(1)}, bf16[16,2048]{1,0:T(8,128)(2,1)S(1)}, u32[]{:S(2)}, u32[]{:S(2)}) collective-permute-start(bf16[16,2048]{1,0:T(8,128)(2,1)S(1)} %get-tuple-element.32), channel_id=1, source_target_pairs={{0,2},{1,3},{2,0},{3,1},{4,6},{5,7},{6,4},{7,5},{8,10},{9,11},{10,... | collective-permute-start | bytes 196616 | tf_op jit(solution)/shard_map/ppermute | solution.py:213

commit v8 on v7

--- a/solution.py
+++ b/solution.py
@@ -20,7 +20,7 @@
 
 
 def role_at(tick):
-    return (lax.axis_index("pipe") + lax.axis_index("zero") % CORES + tick) % 2
+    return (lax.axis_index("pipe") + lax.axis_index("zero") % CORES + tick + 1) % 2
 
 
 def group_kernel(tick, other, ready, count, chips, mark_ref, gains_ref, gate_ref, up_ref, down_ref, *refs):
@@ -216,7 +216,7 @@
         pairs = []
         for s in range(sections):
             for r in range(CORES):
-                other = s - 1 if (s + r + tick) % 2 == 0 else s + 1
+                other = s - 1 if (s + r + tick + 1) % 2 == 0 else s + 1
                 other = other if 0 <= other < sections else s
                 for a, b in chip_pairs(chips, step):
                     pairs.append((s * zero + a * CORES + r, other * zero + b * CORES + r))

time: 51.4 us -> 50 us (0.973)
  the two profiles are of different devices: /device:TPU:0 before, /device:TPU:9 now
where the time goes in v8:
time: 50 us; the launch traced here: 49.8 us
  starting transfers between devices  31.3 us (63%)
  waiting for transfers between devices  10.7 us (21%)
  Pallas kernels  5.05 us (10%)
  between operations  0.93 us (2%)
  local copies, waits for them, and re-layouts  0.81 us (2%)
  other arithmetic  0.71 us (1%)
    ppermute x8, starting transfers between devices, to_next(): return lax.ppermute(value, both, pairs)  13.8 us
    ppermute x10, starting transfers between devices, to_sibling(): return lax.ppermute(value, 'zero', [(k, k ^ 1) for k in range(zero)])  12.1 us
    ppermute x6, starting transfers between devices, to_chip(): return lax.ppermute(value, 'zero', pairs)  5.43 us
    pallas_call x4, Pallas kernels, partial(): pl.pallas_call(functools.partial(group_kernel, tick, other, ready, len(pi...  4.74 us
    ppermute x10, waiting for transfers between devices, to_sibling(): return lax.ppermute(value, 'zero', [(k, k ^ 1) for k in range(zero)])  3.63 us
    ppermute x6, waiting for transfers between devices, to_chip(): return lax.ppermute(value, 'zero', pairs)  3.61 us
    ppermute x8, waiting for transfers between devices, to_next(): return lax.ppermute(value, both, pairs)  3.49 us
  transfers between devices with their start and end apart: 24, of which 10 were waited for; matrix products, arithmetic and copies ran while one was open for 0% of the time, Pallas kernels for 7%

profile of v8, /device:TPU:9, one launch (start us, length us, event | category | flops | bytes accessed | tf_op | source)
XLA Modules:
  0.0 49.8 jit_solution(7244733431565399149)
XLA Ops:
  0.7 0.7 %copy-done = bf16[2,8,2048]{2,1,0:T(8,128)(2,1)S(1)} copy-done((bf16[2,8,2048]{2,1,0:T(8,128)(2,1)S(1)}, bf16[2,8,2048]{2,1,0:T(8,128)(2,1)}, u32[]{:S(2)}) %copy-start) | copy-done | bytes 65560
  1.8 0.7 %collective-permute-start = (bf16[16,2048]{1,0:T(8,128)(2,1)S(1)}, bf16[16,2048]{1,0:T(8,128)(2,1)S(1)}, u32[]{:S(2)}, u32[]{:S(2)}) collective-permute-start(bf16[16,2048]{1,0:T(8,128)(2,1)S(1)} %pad_maximum_fusion), channel_id=1, source_target_pairs={{0,1},{1,0},{2,3},{3,2},{4,5},{5,4},{6,7},{7,6},{8,9},{9,8},{10,11... | collective-permute-start | bytes 196616 | tf_op jit(solution)/shard_map/ppermute | solution.py:209
  2.6 0.9 %collective-permute-done = bf16[16,2048]{1,0:T(8,128)(2,1)S(1)} collective-permute-done((bf16[16,2048]{1,0:T(8,128)(2,1)S(1)}, bf16[16,2048]{1,0:T(8,128)(2,1)S(1)}, u32[]{:S(2)}, u32[]{:S(2)}) %collective-permute-start) | collective-permute-done | bytes 65568 | tf_op jit(solution)/shard_map/ppermute | solution.py:209
  3.6 3.2 %collective-permute-start.1 = (bf16[16,2048]{1,0:T(8,128)(2,1)S(1)}, bf16[16,2048]{1,0:T(8,128)(2,1)S(1)}, u32[]{:S(2)}, u32[]{:S(2)}) collective-permute-start(bf16[16,2048]{1,0:T(8,128)(2,1)S(1)} %pad_maximum_fusion.2.x_ref), channel_id=1, source_target_pairs={{0,14},{2,12},{4,10},{6,8},{1,7},{3,5},{5,3},{7,1},{8,6},{10,4},{1... | collective-permute-start | bytes 196616 | tf_op jit(solution)/shard_map/ppermute | solution.py:223
  6.9 1.3 %collective-permute-start.3 = (bf16[16,2048]{1,0:T(8,128)(2,1)S(1)}, bf16[16,2048]{1,0:T(8,128)(2,1)S(1)}, u32[]{:S(2)}, u32[]{:S(2)}) collective-permute-start(bf16[16,2048]{1,0:T(8,128)(2,1)S(1)} %pad_maximum_fusion.2.x_ref), channel_id=1, source_target_pairs={{0,10},{2,8},{4,14},{6,12},{1,3},{3,1},{5,7},{7,5},{8,2},{10,0},{1... | collective-permute-start | bytes 196616 | tf_op jit(solution)/shard_map/ppermute | solution.py:223
  8.2 2.2 %collective-permute-start.4 = (bf16[16,2048]{1,0:T(8,128)(2,1)S(1)}, bf16[16,2048]{1,0:T(8,128)(2,1)S(1)}, u32[]{:S(2)}, u32[]{:S(2)}) collective-permute-start(bf16[16,2048]{1,0:T(8,128)(2,1)S(1)} %pad_maximum_fusion.2.x_ref), channel_id=1, source_target_pairs={{0,8},{2,10},{4,12},{6,14},{1,1},{3,3},{5,5},{7,7},{8,0},{10,2},{1... | collective-permute-start | bytes 196616 | tf_op jit(solution)/shard_map/ppermute | solution.py:223
  10.4 1.4 %collective-permute-start.5 = (bf16[16,2048]{1,0:T(8,128)(2,1)S(1)}, bf16[16,2048]{1,0:T(8,128)(2,1)S(1)}, u32[]{:S(2)}, u32[]{:S(2)}) collective-permute-start(bf16[16,2048]{1,0:T(8,128)(2,1)S(1)} %collective-permute-done.1.refs_0_), channel_id=1, source_target_pairs={{0,1},{1,0},{2,3},{3,2},{4,5},{5,4},{6,7},{7,6},{8,9},{9,8},{10,11... | collective-permute-start | bytes 196616 | tf_op jit(solution)/shard_map/ppermute | solution.py:209
  12.2 0.9 %collective-permute-start.7 = (bf16[16,2048]{1,0:T(8,128)(2,1)S(1)}, bf16[16,2048]{1,0:T(8,128)(2,1)S(1)}, u32[]{:S(2)}, u32[]{:S(2)}) collective-permute-start(bf16[16,2048]{1,0:T(8,128)(2,1)S(1)} %collective-permute-done.3.refs_2_), channel_id=1, source_target_pairs={{0,1},{1,0},{2,3},{3,2},{4,5},{5,4},{6,7},{7,6},{8,9},{9,8},{10,11... | collective-permute-start | bytes 196616 | tf_op jit(solution)/shard_map/ppermute | solution.py:209
  13.0 0.5 collective-permute-done.4.refs_3_.x_ref
  13.5 0.6 %collective-permute-start.8 = (bf16[16,2048]{1,0:T(8,128)(2,1)S(1)}, bf16[16,2048]{1,0:T(8,128)(2,1)S(1)}, u32[]{:S(2)}, u32[]{:S(2)}) collective-permute-start(bf16[16,2048]{1,0:T(8,128)(2,1)S(1)} %collective-permute-done.4.refs_3_.x_ref), channel_id=1, source_target_pairs={{0,1},{1,0},{2,3},{3,2},{4,5},{5,4},{6,7},{7,6},{8,9},{9,8},{10,11... | collective-permute-start | bytes 196616 | tf_op jit(solution)/shard_map/ppermute | solution.py:209
  14.2 0.9 %collective-permute-done.8.refs_3_ = bf16[16,2048]{1,0:T(8,128)(2,1)S(1)} collective-permute-done((bf16[16,2048]{1,0:T(8,128)(2,1)S(1)}, bf16[16,2048]{1,0:T(8,128)(2,1)S(1)}, u32[]{:S(2)}, u32[]{:S(2)}) %collective-permute-start.8) | collective-permute-done | bytes 65568 | tf_op jit(solution)/shard_map/ppermute | solution.py:209
  15.0 1.2 %shard_map.98 = bf16[64,2048]{1,0:T(8,128)(2,1)S(1)} custom-call(bf16[16,2048]{1,0:T(8,128)(2,1)S(1)} %shard_map.96.mark_ref, f32[2,2048]{1,0:T(2,128)S(1)} %bitcast.31, bf16[2,2048,512]{2,1,0:T(8,128)(2,1)S(1)} %bitcast.19, bf16[2,2048,512]{2,1,0:T(8,128)(2,1)S(1)} %bitcast.23, bf16[2,512,2048]{2,1,0:T(8,128)(2,1)S(1)} %bitcast.27, ...), custom_call_target="tpu_custom_call" | custom-call | flops 402653184 | bytes 6291456 | tf_op jit(solution)/shard_map/pallas_call | solution.py:184
  16.3 0.4 collective-permute-start.9
  16.7 1.2 %shard_map.97.part_ref = f32[64,2048]{1,0:T(8,128)S(1)} custom-call(bf16[16,2048]{1,0:T(8,128)(2,1)S(1)} %shard_map.96.mark_ref, f32[2,2048]{1,0:T(2,128)S(1)} %bitcast.32, bf16[2,2048,512]{2,1,0:T(8,128)(2,1)S(1)} %bitcast.20, bf16[2,2048,512]{2,1,0:T(8,128)(2,1)S(1)} %bitcast.24, bf16[2,512,2048]{2,1,0:T(8,128)(2,1)S(1)} %bitcast.28, ...), custom_call_target="tpu_custom_call" | custom-call | flops 402653184 | bytes 6291456 | tf_op jit(solution)/shard_map/pallas_call | solution.py:184
  18.0 3.5 %collective-permute-start.10 = (bf16[16,2048]{1,0:T(8,128)(2,1)S(1)}, bf16[16,2048]{1,0:T(8,128)(2,1)S(1)}, u32[]{:S(2)}, u32[]{:S(2)}) collective-permute-start(bf16[16,2048]{1,0:T(8,128)(2,1)S(1)} %get-tuple-element.20), channel_id=1, source_target_pairs={{0,6},{2,4},{4,2},{6,0},{1,15},{3,13},{5,11},{7,9},{8,22},{10,20},... | collective-permute-start | bytes 196616 | tf_op jit(solution)/shard_map/ppermute | solution.py:223
  21.6 1.3 %collective-permute-start.12 = (bf16[16,2048]{1,0:T(8,128)(2,1)S(1)}, bf16[16,2048]{1,0:T(8,128)(2,1)S(1)}, u32[]{:S(2)}, u32[]{:S(2)}) collective-permute-start(bf16[16,2048]{1,0:T(8,128)(2,1)S(1)} %get-tuple-element.22), channel_id=1, source_target_pairs={{0,2},{2,0},{4,6},{6,4},{1,11},{3,9},{5,15},{7,13},{8,18},{10,16},... | collective-permute-start | bytes 196616 | tf_op jit(solution)/shard_map/ppermute | solution.py:223
  22.9 2.1 %collective-permute-start.13 = (bf16[16,2048]{1,0:T(8,128)(2,1)S(1)}, bf16[16,2048]{1,0:T(8,128)(2,1)S(1)}, u32[]{:S(2)}, u32[]{:S(2)}) collective-permute-start(bf16[16,2048]{1,0:T(8,128)(2,1)S(1)} %get-tuple-element.23), channel_id=1, source_target_pairs={{0,0},{2,2},{4,4},{6,6},{1,9},{3,11},{5,13},{7,15},{8,16},{10,18},... | collective-permute-start | bytes 196616 | tf_op jit(solution)/shard_map/ppermute | solution.py:223
  25.0 0.5 %collective-permute-done.11.refs_1_ = bf16[16,2048]{1,0:T(8,128)(2,1)S(1)} collective-permute-done((bf16[16,2048]{1,0:T(8,128)(2,1)S(1)}, bf16[16,2048]{1,0:T(8,128)(2,1)S(1)}, u32[]{:S(2)}, u32[]{:S(2)}) %collective-permute-start.11) | collective-permute-done | bytes 65568 | tf_op jit(solution)/shard_map/ppermute | solution.py:223
  25.7 2.3 %collective-permute-done.13.refs_3_ = bf16[16,2048]{1,0:T(8,128)(2,1)S(1)} collective-permute-done((bf16[16,2048]{1,0:T(8,128)(2,1)S(1)}, bf16[16,2048]{1,0:T(8,128)(2,1)S(1)}, u32[]{:S(2)}, u32[]{:S(2)}) %collective-permute-start.13) | collective-permute-done | bytes 65568 | tf_op jit(solution)/shard_map/ppermute | solution.py:223
  28.1 2.1 %collective-permute-start.15 = (bf16[16,2048]{1,0:T(8,128)(2,1)S(1)}, bf16[16,2048]{1,0:T(8,128)(2,1)S(1)}, u32[]{:S(2)}, u32[]{:S(2)}) collective-permute-start(bf16[16,2048]{1,0:T(8,128)(2,1)S(1)} %get-tuple-element.25.refs_3_), channel_id=1, source_target_pairs={{0,6},{1,7},{2,4},{3,5},{4,2},{5,3},{6,0},{7,1},{8,14},{9,15},{10,... | collective-permute-start | bytes 196616 | tf_op jit(solution)/shard_map/ppermute | solution.py:213
  30.9 4.2 %collective-permute-start.14 = (bf16[8,2048]{1,0:T(8,128)(2,1)S(1)}, bf16[8,2048]{1,0:T(8,128)(2,1)S(1)}, u32[]{:S(2)}, u32[]{:S(2)}) collective-permute-start(bf16[8,2048]{1,0:T(8,128)(2,1)S(1)} %get-tuple-element.43), channel_id=1, source_target_pairs={{0,1},{1,0},{2,3},{3,2},{4,5},{5,4},{6,7},{7,6},{8,9},{9,8},{10,11... | collective-permute-start | bytes 98312 | tf_op jit(solution)/shard_map/ppermute | solution.py:209
  35.1 0.9 %collective-permute-done.14.mark_ref.there_ref = bf16[8,2048]{1,0:T(8,128)(2,1)S(1)} collective-permute-done((bf16[8,2048]{1,0:T(8,128)(2,1)S(1)}, bf16[8,2048]{1,0:T(8,128)(2,1)S(1)}, u32[]{:S(2)}, u32[]{:S(2)}) %collective-permute-start.14) | collective-permute-done | bytes 32800 | tf_op jit(solution)/shard_map/ppermute | solution.py:209
  36.0 2.8 %collective-permute-start.18 = (bf16[64,2048]{1,0:T(8,128)(2,1)S(1)}, bf16[64,2048]{1,0:T(8,128)(2,1)S(1)}, u32[]{:S(2)}, u32[]{:S(2)}) collective-permute-start(bf16[64,2048]{1,0:T(8,128)(2,1)S(1)} %shard_map.102.refs_0_), channel_id=1, source_target_pairs={{0,1},{1,0},{2,3},{3,2},{4,5},{5,4},{6,7},{7,6},{8,9},{9,8},{10,11... | collective-permute-start | bytes 786440 | tf_op jit(solution)/shard_map/ppermute | solution.py:209
  38.8 1.1 %shard_map.103 = (f32[32,2048]{1,0:T(8,128)S(1)}, bf16[32,2048]{1,0:T(8,128)(2,1)S(1)}) custom-call(bf16[16,2048]{1,0:T(8,128)(2,1)S(1)} %shard_map.101.mark_ref, f32[2,2048]{1,0:T(2,128)S(1)} %bitcast.34, bf16[2,2048,512]{2,1,0:T(8,128)(2,1)S(1)} %bitcast.21, bf16[2,2048,512]{2,1,0:T(8,128)(2,1)S(1)} %bitcast.25, bf16[2,512,2048]{2,1,0:T(8,128)(2,1)S(1)} %bitcast.29, ...), custom_call_target="tpu_custom_call" | custom-call | flops 402653184 | bytes 6291456 | tf_op jit(solution)/shard_map/pallas_call | solution.py:184
  40.1 1.1 %shard_map.104 = (f32[32,2048]{1,0:T(8,128)S(1)}, bf16[32,2048]{1,0:T(8,128)(2,1)S(1)}) custom-call(bf16[16,2048]{1,0:T(8,128)(2,1)S(1)} %shard_map.101.mark_ref, f32[2,2048]{1,0:T(2,128)S(1)} %bitcast.35, bf16[2,2048,512]{2,1,0:T(8,128)(2,1)S(1)} %bitcast.22, bf16[2,2048,512]{2,1,0:T(8,128)(2,1)S(1)} %bitcast.26, bf16[2,512,2048]{2,1,0:T(8,128)(2,1)S(1)} %bitcast.30, ...), custom_call_target="tpu_custom_call" | custom-call | flops 402653184 | bytes 6291456 | tf_op jit(solution)/shard_map/pallas_call | solution.py:184
  41.2 0.5 %collective-permute-start.19 = (bf16[32,2048]{1,0:T(8,128)(2,1)S(1)}, bf16[32,2048]{1,0:T(8,128)(2,1)S(1)}, u32[]{:S(2)}, u32[]{:S(2)}) collective-permute-start(bf16[32,2048]{1,0:T(8,128)(2,1)S(1)} %get-tuple-element.28), channel_id=1, source_target_pairs={{0,1},{1,0},{2,3},{3,2},{4,5},{5,4},{6,7},{7,6},{8,9},{9,8},{10,11... | collective-permute-start | bytes 393224 | tf_op jit(solution)/shard_map/ppermute | solution.py:209
  41.8 1.0 %collective-permute-done.19.to_mine_ref = bf16[32,2048]{1,0:T(8,128)(2,1)S(1)} collective-permute-done((bf16[32,2048]{1,0:T(8,128)(2,1)S(1)}, bf16[32,2048]{1,0:T(8,128)(2,1)S(1)}, u32[]{:S(2)}, u32[]{:S(2)}) %collective-permute-start.19) | collective-permute-done | bytes 131104 | tf_op jit(solution)/shard_map/ppermute | solution.py:209
  42.8 1.3 %collective-permute-start.21 = (bf16[16,2048]{1,0:T(8,128)(2,1)S(1)}, bf16[16,2048]{1,0:T(8,128)(2,1)S(1)}, u32[]{:S(2)}, u32[]{:S(2)}) collective-permute-start(bf16[16,2048]{1,0:T(8,128)(2,1)S(1)} %get-tuple-element.30), channel_id=1, source_target_pairs={{0,6},{1,7},{2,4},{3,5},{4,2},{5,3},{6,0},{7,1},{8,14},{9,15},{10,... | collective-permute-start | bytes 196616 | tf_op jit(solution)/shard_map/ppermute | solution.py:213
  44.3 1.2 %collective-permute-start.23 = (bf16[16,2048]{1,0:T(8,128)(2,1)S(1)}, bf16[16,2048]{1,0:T(8,128)(2,1)S(1)}, u32[]{:S(2)}, u32[]{:S(2)}) collective-permute-start(bf16[16,2048]{1,0:T(8,128)(2,1)S(1)} %get-tuple-element.32), channel_id=1, source_target_pairs={{0,2},{1,3},{2,0},{3,1},{4,6},{5,7},{6,4},{7,5},{8,10},{9,11},{10,... | collective-permute-start | bytes 196616 | tf_op jit(solution)/shard_map/ppermute | solution.py:213
  45.5 1.4 %collective-permute-done.21.refs_0_ = bf16[16,2048]{1,0:T(8,128)(2,1)S(1)} collective-permute-done((bf16[16,2048]{1,0:T(8,128)(2,1)S(1)}, bf16[16,2048]{1,0:T(8,128)(2,1)S(1)}, u32[]{:S(2)}, u32[]{:S(2)}) %collective-permute-start.21) | collective-permute-done | bytes 65568 | tf_op jit(solution)/shard_map/ppermute | solution.py:213
  46.9 2.2 %collective-permute-done.22.refs_1_ = bf16[16,2048]{1,0:T(8,128)(2,1)S(1)} collective-permute-done((bf16[16,2048]{1,0:T(8,128)(2,1)S(1)}, bf16[16,2048]{1,0:T(8,128)(2,1)S(1)}, u32[]{:S(2)}, u32[]{:S(2)}) %collective-permute-start.22) | collective-permute-done | bytes 65568 | tf_op jit(solution)/shard_map/ppermute | solution.py:213
  49.2 0.6 %select_bitcast_fusion = (bf16[1,8,2048]{2,1,0:T(8,128)(2,1)}, bf16[1,8,2048]{2,1,0:T(8,128)(2,1)}) fusion(pred[]{:T(512)S(6)} %eq.37, bf16[16,2048]{1,0:T(8,128)(2,1)S(1)} %shard_map.106), kind=kLoop, calls=%fused_computation.8 | loop fusion | flops 32768 | bytes 131073 | tf_op jit(solution)/shard_map/broadcast_in_dim | solution.py:277
  (55 shorter events, 2.3 us)
Async XLA Ops:
  0.6 0.8 %copy-start = (bf16[2,8,2048]{2,1,0:T(8,128)(2,1)S(1)}, bf16[2,8,2048]{2,1,0:T(8,128)(2,1)}, u32[]{:S(2)}) copy-start(bf16[2,8,2048]{2,1,0:T(8,128)(2,1)} %param.10) | copy-start | bytes 196612
  0.7 0.8 %copy-start.7 = (s32[2]{0:T(128)S(1)}, s32[2]{0:T(128)}, u32[]{:S(2)}) copy-start(s32[2]{0:T(128)} %param.11) | copy-start | bytes 28
  0.7 1.1 %copy-start.5 = (bf16[1,8,2048]{2,1,0:T(8,128)(2,1)S(1)}, bf16[1,8,2048]{2,1,0:T(8,128)(2,1)}, u32[]{:S(2)}) copy-start(bf16[1,8,2048]{2,1,0:T(8,128)(2,1)} %param.8) | copy-start | bytes 98308
  0.7 1.1 %copy-start.6 = (bf16[1,8,2048]{2,1,0:T(8,128)(2,1)S(1)}, bf16[1,8,2048]{2,1,0:T(8,128)(2,1)}, u32[]{:S(2)}) copy-start(bf16[1,8,2048]{2,1,0:T(8,128)(2,1)} %param.9) | copy-start | bytes 98308
  1.8 1.6 %collective-permute-start = (bf16[16,2048]{1,0:T(8,128)(2,1)S(1)}, bf16[16,2048]{1,0:T(8,128)(2,1)S(1)}, u32[]{:S(2)}, u32[]{:S(2)}) collective-permute-start(bf16[16,2048]{1,0:T(8,128)(2,1)S(1)} %pad_maximum_fusion), channel_id=1, source_target_pairs={{0,1},{1,0},{2,3},{3,2},{4,5},{5,4},{6,7},{7,6},{8,9},{9,8},{10,11... | collective-permute-start | bytes 196616 | tf_op jit(solution)/shard_map/ppermute | solution.py:209
  3.5 11.5 %copy-start.1 = (bf16[1,2,2048,512]{3,2,1,0:T(8,128)(2,1)S(1)}, bf16[1,2,2048,512]{3,2,1,0:T(8,128)(2,1)}, u32[]{:S(2)}) copy-start(bf16[1,2,2048,512]{3,2,1,0:T(8,128)(2,1)} %param.13) | copy-start | bytes 12582916
  3.5 11.5 %copy-start.2 = (bf16[1,2,2048,512]{3,2,1,0:T(8,128)(2,1)S(1)}, bf16[1,2,2048,512]{3,2,1,0:T(8,128)(2,1)}, u32[]{:S(2)}) copy-start(bf16[1,2,2048,512]{3,2,1,0:T(8,128)(2,1)} %param.14) | copy-start | bytes 12582916
  3.5 11.5 %copy-start.3 = (bf16[1,2,512,2048]{3,2,1,0:T(8,128)(2,1)S(1)}, bf16[1,2,512,2048]{3,2,1,0:T(8,128)(2,1)}, u32[]{:S(2)}) copy-start(bf16[1,2,512,2048]{3,2,1,0:T(8,128)(2,1)} %param.15) | copy-start | bytes 12582916
  3.6 11.5 %copy-start.4 = (f32[1,2,2048]{2,1,0:T(2,128)S(1)}, f32[1,2,2048]{2,1,0:T(2,128)}, u32[]{:S(2)}) copy-start(f32[1,2,2048]{2,1,0:T(2,128)} %param.12) | copy-start | bytes 49156
  3.6 6.8 %collective-permute-start.1 = (bf16[16,2048]{1,0:T(8,128)(2,1)S(1)}, bf16[16,2048]{1,0:T(8,128)(2,1)S(1)}, u32[]{:S(2)}, u32[]{:S(2)}) collective-permute-start(bf16[16,2048]{1,0:T(8,128)(2,1)S(1)} %pad_maximum_fusion.2.x_ref), channel_id=1, source_target_pairs={{0,14},{2,12},{4,10},{6,8},{1,7},{3,5},{5,3},{7,1},{8,6},{10,4},{1... | collective-permute-start | bytes 196616 | tf_op jit(solution)/shard_map/ppermute | solution.py:223
  6.8 5.0 %collective-permute-start.2 = (bf16[16,2048]{1,0:T(8,128)(2,1)S(1)}, bf16[16,2048]{1,0:T(8,128)(2,1)S(1)}, u32[]{:S(2)}, u32[]{:S(2)}) collective-permute-start(bf16[16,2048]{1,0:T(8,128)(2,1)S(1)} %pad_maximum_fusion.2.x_ref), channel_id=1, source_target_pairs={{0,12},{2,14},{4,8},{6,10},{1,5},{3,7},{5,1},{7,3},{8,4},{10,6},{1... | collective-permute-start | bytes 196616 | tf_op jit(solution)/shard_map/ppermute | solution.py:223
  6.9 5.2 %collective-permute-start.3 = (bf16[16,2048]{1,0:T(8,128)(2,1)S(1)}, bf16[16,2048]{1,0:T(8,128)(2,1)S(1)}, u32[]{:S(2)}, u32[]{:S(2)}) collective-permute-start(bf16[16,2048]{1,0:T(8,128)(2,1)S(1)} %pad_maximum_fusion.2.x_ref), channel_id=1, source_target_pairs={{0,10},{2,8},{4,14},{6,12},{1,3},{3,1},{5,7},{7,5},{8,2},{10,0},{1... | collective-permute-start | bytes 196616 | tf_op jit(solution)/shard_map/ppermute | solution.py:223
  8.2 5.3 %collective-permute-start.4 = (bf16[16,2048]{1,0:T(8,128)(2,1)S(1)}, bf16[16,2048]{1,0:T(8,128)(2,1)S(1)}, u32[]{:S(2)}, u32[]{:S(2)}) collective-permute-start(bf16[16,2048]{1,0:T(8,128)(2,1)S(1)} %pad_maximum_fusion.2.x_ref), channel_id=1, source_target_pairs={{0,8},{2,10},{4,12},{6,14},{1,1},{3,3},{5,5},{7,7},{8,0},{10,2},{1... | collective-permute-start | bytes 196616 | tf_op jit(solution)/shard_map/ppermute | solution.py:223
  10.4 3.7 %collective-permute-start.5 = (bf16[16,2048]{1,0:T(8,128)(2,1)S(1)}, bf16[16,2048]{1,0:T(8,128)(2,1)S(1)}, u32[]{:S(2)}, u32[]{:S(2)}) collective-permute-start(bf16[16,2048]{1,0:T(8,128)(2,1)S(1)} %collective-permute-done.1.refs_0_), channel_id=1, source_target_pairs={{0,1},{1,0},{2,3},{3,2},{4,5},{5,4},{6,7},{7,6},{8,9},{9,8},{10,11... | collective-permute-start | bytes 196616 | tf_op jit(solution)/shard_map/ppermute | solution.py:209
  11.8 2.3 %collective-permute-start.6 = (bf16[16,2048]{1,0:T(8,128)(2,1)S(1)}, bf16[16,2048]{1,0:T(8,128)(2,1)S(1)}, u32[]{:S(2)}, u32[]{:S(2)}) collective-permute-start(bf16[16,2048]{1,0:T(8,128)(2,1)S(1)} %collective-permute-done.2.refs_1_), channel_id=1, source_target_pairs={{0,1},{1,0},{2,3},{3,2},{4,5},{5,4},{6,7},{7,6},{8,9},{9,8},{10,11... | collective-permute-start | bytes 196616 | tf_op jit(solution)/shard_map/ppermute | solution.py:209
  12.2 2.0 %collective-permute-start.7 = (bf16[16,2048]{1,0:T(8,128)(2,1)S(1)}, bf16[16,2048]{1,0:T(8,128)(2,1)S(1)}, u32[]{:S(2)}, u32[]{:S(2)}) collective-permute-start(bf16[16,2048]{1,0:T(8,128)(2,1)S(1)} %collective-permute-done.3.refs_2_), channel_id=1, source_target_pairs={{0,1},{1,0},{2,3},{3,2},{4,5},{5,4},{6,7},{7,6},{8,9},{9,8},{10,11... | collective-permute-start | bytes 196616 | tf_op jit(solution)/shard_map/ppermute | solution.py:209
  13.5 1.5 %collective-permute-start.8 = (bf16[16,2048]{1,0:T(8,128)(2,1)S(1)}, bf16[16,2048]{1,0:T(8,128)(2,1)S(1)}, u32[]{:S(2)}, u32[]{:S(2)}) collective-permute-start(bf16[16,2048]{1,0:T(8,128)(2,1)S(1)} %collective-permute-done.4.refs_3_.x_ref), channel_id=1, source_target_pairs={{0,1},{1,0},{2,3},{3,2},{4,5},{5,4},{6,7},{7,6},{8,9},{9,8},{10,11... | collective-permute-start | bytes 196616 | tf_op jit(solution)/shard_map/ppermute | solution.py:209
  16.3 1.7 %collective-permute-start.9 = (bf16[64,2048]{1,0:T(8,128)(2,1)S(1)}, bf16[64,2048]{1,0:T(8,128)(2,1)S(1)}, u32[]{:S(2)}, u32[]{:S(2)}) collective-permute-start(bf16[64,2048]{1,0:T(8,128)(2,1)S(1)} %shard_map.98), channel_id=1, source_target_pairs={{0,1},{1,0},{2,3},{3,2},{4,5},{5,4},{6,7},{7,6},{8,9},{9,8},{10,11... | collective-permute-start | bytes 786440 | tf_op jit(solution)/shard_map/ppermute | solution.py:209
  18.0 7.0 %collective-permute-start.10 = (bf16[16,2048]{1,0:T(8,128)(2,1)S(1)}, bf16[16,2048]{1,0:T(8,128)(2,1)S(1)}, u32[]{:S(2)}, u32[]{:S(2)}) collective-permute-start(bf16[16,2048]{1,0:T(8,128)(2,1)S(1)} %get-tuple-element.20), channel_id=1, source_target_pairs={{0,6},{2,4},{4,2},{6,0},{1,15},{3,13},{5,11},{7,9},{8,22},{10,20},... | collective-permute-start | bytes 196616 | tf_op jit(solution)/shard_map/ppermute | solution.py:223
  21.5 4.0 %collective-permute-start.11 = (bf16[16,2048]{1,0:T(8,128)(2,1)S(1)}, bf16[16,2048]{1,0:T(8,128)(2,1)S(1)}, u32[]{:S(2)}, u32[]{:S(2)}) collective-permute-start(bf16[16,2048]{1,0:T(8,128)(2,1)S(1)} %get-tuple-element.21), channel_id=1, source_target_pairs={{0,4},{2,6},{4,0},{6,2},{1,13},{3,15},{5,9},{7,11},{8,20},{10,22},... | collective-permute-start | bytes 196616 | tf_op jit(solution)/shard_map/ppermute | solution.py:223
  21.6 4.0 %collective-permute-start.12 = (bf16[16,2048]{1,0:T(8,128)(2,1)S(1)}, bf16[16,2048]{1,0:T(8,128)(2,1)S(1)}, u32[]{:S(2)}, u32[]{:S(2)}) collective-permute-start(bf16[16,2048]{1,0:T(8,128)(2,1)S(1)} %get-tuple-element.22), channel_id=1, source_target_pairs={{0,2},{2,0},{4,6},{6,4},{1,11},{3,9},{5,15},{7,13},{8,18},{10,16},... | collective-permute-start | bytes 196616 | tf_op jit(solution)/shard_map/ppermute | solution.py:223
  22.9 5.1 %collective-permute-start.13 = (bf16[16,2048]{1,0:T(8,128)(2,1)S(1)}, bf16[16,2048]{1,0:T(8,128)(2,1)S(1)}, u32[]{:S(2)}, u32[]{:S(2)}) collective-permute-start(bf16[16,2048]{1,0:T(8,128)(2,1)S(1)} %get-tuple-element.23), channel_id=1, source_target_pairs={{0,0},{2,2},{4,4},{6,6},{1,9},{3,11},{5,13},{7,15},{8,16},{10,18},... | collective-permute-start | bytes 196616 | tf_op jit(solution)/shard_map/ppermute | solution.py:223
  28.1 7.8 %collective-permute-start.15 = (bf16[16,2048]{1,0:T(8,128)(2,1)S(1)}, bf16[16,2048]{1,0:T(8,128)(2,1)S(1)}, u32[]{:S(2)}, u32[]{:S(2)}) collective-permute-start(bf16[16,2048]{1,0:T(8,128)(2,1)S(1)} %get-tuple-element.25.refs_3_), channel_id=1, source_target_pairs={{0,6},{1,7},{2,4},{3,5},{4,2},{5,3},{6,0},{7,1},{8,14},{9,15},{10,... | collective-permute-start | bytes 196616 | tf_op jit(solution)/shard_map/ppermute | solution.py:213
  30.3 5.7 %collective-permute-start.16 = (bf16[16,2048]{1,0:T(8,128)(2,1)S(1)}, bf16[16,2048]{1,0:T(8,128)(2,1)S(1)}, u32[]{:S(2)}, u32[]{:S(2)}) collective-permute-start(bf16[16,2048]{1,0:T(8,128)(2,1)S(1)} %get-tuple-element.25.refs_3_), channel_id=1, source_target_pairs={{0,4},{1,5},{2,6},{3,7},{4,0},{5,1},{6,2},{7,3},{8,12},{9,13},{10,... | collective-permute-start | bytes 196616 | tf_op jit(solution)/shard_map/ppermute | solution.py:213
  30.5 5.5 %collective-permute-start.17 = (bf16[16,2048]{1,0:T(8,128)(2,1)S(1)}, bf16[16,2048]{1,0:T(8,128)(2,1)S(1)}, u32[]{:S(2)}, u32[]{:S(2)}) collective-permute-start(bf16[16,2048]{1,0:T(8,128)(2,1)S(1)} %get-tuple-element.25.refs_3_), channel_id=1, source_target_pairs={{0,2},{1,3},{2,0},{3,1},{4,6},{5,7},{6,4},{7,5},{8,10},{9,11},{10,... | collective-permute-start | bytes 196616 | tf_op jit(solution)/shard_map/ppermute | solution.py:213
  30.9 5.1 %collective-permute-start.14 = (bf16[8,2048]{1,0:T(8,128)(2,1)S(1)}, bf16[8,2048]{1,0:T(8,128)(2,1)S(1)}, u32[]{:S(2)}, u32[]{:S(2)}) collective-permute-start(bf16[8,2048]{1,0:T(8,128)(2,1)S(1)} %get-tuple-element.43), channel_id=1, source_target_pairs={{0,1},{1,0},{2,3},{3,2},{4,5},{5,4},{6,7},{7,6},{8,9},{9,8},{10,11... | collective-permute-start | bytes 98312 | tf_op jit(solution)/shard_map/ppermute | solution.py:209
  36.0 4.1 %collective-permute-start.18 = (bf16[64,2048]{1,0:T(8,128)(2,1)S(1)}, bf16[64,2048]{1,0:T(8,128)(2,1)S(1)}, u32[]{:S(2)}, u32[]{:S(2)}) collective-permute-start(bf16[64,2048]{1,0:T(8,128)(2,1)S(1)} %shard_map.102.refs_0_), channel_id=1, source_target_pairs={{0,1},{1,0},{2,3},{3,2},{4,5},{5,4},{6,7},{7,6},{8,9},{9,8},{10,11... | collective-permute-start | bytes 786440 | tf_op jit(solution)/shard_map/ppermute | solution.py:209
  40.0 1.8 %collective-permute-start.20 = (bf16[32,2048]{1,0:T(8,128)(2,1)S(1)}, bf16[32,2048]{1,0:T(8,128)(2,1)S(1)}, u32[]{:S(2)}, u32[]{:S(2)}) collective-permute-start(bf16[32,2048]{1,0:T(8,128)(2,1)S(1)} %get-tuple-element.29), channel_id=1, source_target_pairs={{0,1},{1,0},{2,3},{3,2},{4,5},{5,4},{6,7},{7,6},{8,9},{9,8},{10,11... | collective-permute-start | bytes 393224 | tf_op jit(solution)/shard_map/ppermute | solution.py:209
  41.2 1.5 %collective-permute-start.19 = (bf16[32,2048]{1,0:T(8,128)(2,1)S(1)}, bf16[32,2048]{1,0:T(8,128)(2,1)S(1)}, u32[]{:S(2)}, u32[]{:S(2)}) collective-permute-start(bf16[32,2048]{1,0:T(8,128)(2,1)S(1)} %get-tuple-element.28), channel_id=1, source_target_pairs={{0,1},{1,0},{2,3},{3,2},{4,5},{5,4},{6,7},{7,6},{8,9},{9,8},{10,11... | collective-permute-start | bytes 393224 | tf_op jit(solution)/shard_map/ppermute | solution.py:209
  42.8 4.1 %collective-permute-start.21 = (bf16[16,2048]{1,0:T(8,128)(2,1)S(1)}, bf16[16,2048]{1,0:T(8,128)(2,1)S(1)}, u32[]{:S(2)}, u32[]{:S(2)}) collective-permute-start(bf16[16,2048]{1,0:T(8,128)(2,1)S(1)} %get-tuple-element.30), channel_id=1, source_target_pairs={{0,6},{1,7},{2,4},{3,5},{4,2},{5,3},{6,0},{7,1},{8,14},{9,15},{10,... | collective-permute-start | bytes 196616 | tf_op jit(solution)/shard_map/ppermute | solution.py:213
  44.1 5.0 %collective-permute-start.22 = (bf16[16,2048]{1,0:T(8,128)(2,1)S(1)}, bf16[16,2048]{1,0:T(8,128)(2,1)S(1)}, u32[]{:S(2)}, u32[]{:S(2)}) collective-permute-start(bf16[16,2048]{1,0:T(8,128)(2,1)S(1)} %get-tuple-element.31), channel_id=1, source_target_pairs={{0,4},{1,5},{2,6},{3,7},{4,0},{5,1},{6,2},{7,3},{8,12},{9,13},{10,... | collective-permute-start | bytes 196616 | tf_op jit(solution)/shard_map/ppermute | solution.py:213
  44.3 4.8 %collective-permute-start.23 = (bf16[16,2048]{1,0:T(8,128)(2,1)S(1)}, bf16[16,2048]{1,0:T(8,128)(2,1)S(1)}, u32[]{:S(2)}, u32[]{:S(2)}) collective-permute-start(bf16[16,2048]{1,0:T(8,128)(2,1)S(1)} %get-tuple-element.32), channel_id=1, source_target_pairs={{0,2},{1,3},{2,0},{3,1},{4,6},{5,7},{6,4},{7,5},{8,10},{9,11},{10,... | collective-permute-start | bytes 196616 | tf_op jit(solution)/shard_map/ppermute | solution.py:213

commit v9 on v8

--- a/solution.py
+++ b/solution.py
@@ -237,11 +237,9 @@
     given = jnp.where(was_down, ascended, down_out[0])
     own = jnp.where(was_down, down_out[0], ascended)
     rows = own.shape[0]
-    given = jnp.concatenate([given] + [fed[tick] for tick in range(1, ticks)], axis=0)
-    own, given = lax.optimization_barrier((own, given))
-    taken = to_sibling(given)
-    state = joined(own, taken[:rows])
-    entering = [joined(given[rows * tick : rows * (tick + 1)], taken[rows * tick : rows * (tick + 1)]) for tick in range(1, ticks)]
+    own, given, later = lax.optimization_barrier((own, given, [fed[tick] for tick in range(1, ticks)]))
+    state = joined(own, to_sibling(given))
+    entering = [joined(feed, to_sibling(feed)) for feed in later]
 
     for tick in range(ticks):
         if tick == 0:

time: 50 us -> 49.9 us (level)
    ppermute x10 -> x11, waiting for transfers between devices: 3.63 us -> 3.59 us  [to_sibling(): return lax.ppermute(value, 'zero', [(k, k ^ 1) for k in range(zero)])]
    ppermute x10 -> x11, starting transfers between devices: 12.1 us -> 12.1 us  [to_sibling(): return lax.ppermute(value, 'zero', [(k, k ^ 1) for k in range(zero)])]
  transfers between devices with their start and end apart: 24 -> 25, of which waited for: 10 -> 10; matrix products, arithmetic and copies ran while one was open for 0% -> 0% of each run, Pallas kernels for 7% -> 10%
where the time goes in v9:
time: 49.9 us; the launch traced here: 49.7 us
  starting transfers between devices  31.3 us (63%)
  waiting for transfers between devices  10.7 us (21%)
  Pallas kernels  5.07 us (10%)
  between operations  0.92 us (2%)
  local copies, waits for them, and re-layouts  0.81 us (2%)
  other arithmetic  0.7 us (1%)
    ppermute x8, starting transfers between devices, to_next(): return lax.ppermute(value, both, pairs)  13.8 us
    ppermute x11, starting transfers between devices, to_sibling(): return lax.ppermute(value, 'zero', [(k, k ^ 1) for k in range(zero)])  12.1 us
    ppermute x6, starting transfers between devices, to_chip(): return lax.ppermute(value, 'zero', pairs)  5.43 us
    pallas_call x4, Pallas kernels, partial(): pl.pallas_call(functools.partial(group_kernel, tick, other, ready, len(pi...  4.75 us
    ppermute x6, waiting for transfers between devices, to_chip(): return lax.ppermute(value, 'zero', pairs)  3.61 us
    ppermute x11, waiting for transfers between devices, to_sibling(): return lax.ppermute(value, 'zero', [(k, k ^ 1) for k in range(zero)])  3.59 us
    ppermute x8, waiting for transfers between devices, to_next(): return lax.ppermute(value, both, pairs)  3.48 us
  transfers between devices with their start and end apart: 25, of which 10 were waited for; matrix products, arithmetic and copies ran while one was open for 0% of the time, Pallas kernels for 10%

profile of v9, /device:TPU:9, one launch (start us, length us, event | category | flops | bytes accessed | tf_op | source)
XLA Modules:
  0.0 49.7 jit_solution(14111873697066282757)
XLA Ops:
  0.7 0.7 %copy-done = bf16[2,8,2048]{2,1,0:T(8,128)(2,1)S(1)} copy-done((bf16[2,8,2048]{2,1,0:T(8,128)(2,1)S(1)}, bf16[2,8,2048]{2,1,0:T(8,128)(2,1)}, u32[]{:S(2)}) %copy-start) | copy-done | bytes 65560
  1.8 0.7 %collective-permute-start.1 = (bf16[8,2048]{1,0:T(8,128)(2,1)S(1)}, bf16[8,2048]{1,0:T(8,128)(2,1)S(1)}, u32[]{:S(2)}, u32[]{:S(2)}) collective-permute-start(bf16[8,2048]{1,0:T(8,128)(2,1)S(1)} %get-tuple-element.21), channel_id=1, source_target_pairs={{0,1},{1,0},{2,3},{3,2},{4,5},{5,4},{6,7},{7,6},{8,9},{9,8},{10,11... | collective-permute-start | bytes 98312 | tf_op jit(solution)/shard_map/ppermute | solution.py:209
  2.6 0.9 %collective-permute-done.1 = bf16[8,2048]{1,0:T(8,128)(2,1)S(1)} collective-permute-done((bf16[8,2048]{1,0:T(8,128)(2,1)S(1)}, bf16[8,2048]{1,0:T(8,128)(2,1)S(1)}, u32[]{:S(2)}, u32[]{:S(2)}) %collective-permute-start.1) | collective-permute-done | bytes 32800 | tf_op jit(solution)/shard_map/ppermute | solution.py:209
  3.5 3.2 %collective-permute-start.2 = (bf16[16,2048]{1,0:T(8,128)(2,1)S(1)}, bf16[16,2048]{1,0:T(8,128)(2,1)S(1)}, u32[]{:S(2)}, u32[]{:S(2)}) collective-permute-start(bf16[16,2048]{1,0:T(8,128)(2,1)S(1)} %pad_maximum_fusion.1.x_ref), channel_id=1, source_target_pairs={{0,14},{2,12},{4,10},{6,8},{1,7},{3,5},{5,3},{7,1},{8,6},{10,4},{1... | collective-permute-start | bytes 196616 | tf_op jit(solution)/shard_map/ppermute | solution.py:223
  6.9 1.3 %collective-permute-start.4 = (bf16[16,2048]{1,0:T(8,128)(2,1)S(1)}, bf16[16,2048]{1,0:T(8,128)(2,1)S(1)}, u32[]{:S(2)}, u32[]{:S(2)}) collective-permute-start(bf16[16,2048]{1,0:T(8,128)(2,1)S(1)} %pad_maximum_fusion.1.x_ref), channel_id=1, source_target_pairs={{0,10},{2,8},{4,14},{6,12},{1,3},{3,1},{5,7},{7,5},{8,2},{10,0},{1... | collective-permute-start | bytes 196616 | tf_op jit(solution)/shard_map/ppermute | solution.py:223
  8.1 2.2 %collective-permute-start.5 = (bf16[16,2048]{1,0:T(8,128)(2,1)S(1)}, bf16[16,2048]{1,0:T(8,128)(2,1)S(1)}, u32[]{:S(2)}, u32[]{:S(2)}) collective-permute-start(bf16[16,2048]{1,0:T(8,128)(2,1)S(1)} %pad_maximum_fusion.1.x_ref), channel_id=1, source_target_pairs={{0,8},{2,10},{4,12},{6,14},{1,1},{3,3},{5,5},{7,7},{8,0},{10,2},{1... | collective-permute-start | bytes 196616 | tf_op jit(solution)/shard_map/ppermute | solution.py:223
  10.3 1.4 %collective-permute-start = (bf16[8,2048]{1,0:T(8,128)(2,1)S(1)}, bf16[8,2048]{1,0:T(8,128)(2,1)S(1)}, u32[]{:S(2)}, u32[]{:S(2)}) collective-permute-start(bf16[8,2048]{1,0:T(8,128)(2,1)S(1)} %get-tuple-element.19), channel_id=1, source_target_pairs={{0,1},{1,0},{2,3},{3,2},{4,5},{5,4},{6,7},{7,6},{8,9},{9,8},{10,11... | collective-permute-start | bytes 98312 | tf_op jit(solution)/shard_map/ppermute | solution.py:209
  11.8 0.4 collective-permute-start.7
  12.3 0.7 %collective-permute-start.8 = (bf16[16,2048]{1,0:T(8,128)(2,1)S(1)}, bf16[16,2048]{1,0:T(8,128)(2,1)S(1)}, u32[]{:S(2)}, u32[]{:S(2)}) collective-permute-start(bf16[16,2048]{1,0:T(8,128)(2,1)S(1)} %collective-permute-done.4.refs_2_), channel_id=1, source_target_pairs={{0,1},{1,0},{2,3},{3,2},{4,5},{5,4},{6,7},{7,6},{8,9},{9,8},{10,11... | collective-permute-start | bytes 196616 | tf_op jit(solution)/shard_map/ppermute | solution.py:209
  12.9 0.5 collective-permute-done.5.refs_3_.x_ref
  13.4 0.6 %collective-permute-start.9 = (bf16[16,2048]{1,0:T(8,128)(2,1)S(1)}, bf16[16,2048]{1,0:T(8,128)(2,1)S(1)}, u32[]{:S(2)}, u32[]{:S(2)}) collective-permute-start(bf16[16,2048]{1,0:T(8,128)(2,1)S(1)} %collective-permute-done.5.refs_3_.x_ref), channel_id=1, source_target_pairs={{0,1},{1,0},{2,3},{3,2},{4,5},{5,4},{6,7},{7,6},{8,9},{9,8},{10,11... | collective-permute-start | bytes 196616 | tf_op jit(solution)/shard_map/ppermute | solution.py:209
  14.1 0.9 %collective-permute-done.9.refs_3_ = bf16[16,2048]{1,0:T(8,128)(2,1)S(1)} collective-permute-done((bf16[16,2048]{1,0:T(8,128)(2,1)S(1)}, bf16[16,2048]{1,0:T(8,128)(2,1)S(1)}, u32[]{:S(2)}, u32[]{:S(2)}) %collective-permute-start.9) | collective-permute-done | bytes 65568 | tf_op jit(solution)/shard_map/ppermute | solution.py:209
  15.0 1.2 %shard_map.98 = bf16[64,2048]{1,0:T(8,128)(2,1)S(1)} custom-call(bf16[16,2048]{1,0:T(8,128)(2,1)S(1)} %shard_map.96.mark_ref, f32[2,2048]{1,0:T(2,128)S(1)} %bitcast.31, bf16[2,2048,512]{2,1,0:T(8,128)(2,1)S(1)} %bitcast.19, bf16[2,2048,512]{2,1,0:T(8,128)(2,1)S(1)} %bitcast.23, bf16[2,512,2048]{2,1,0:T(8,128)(2,1)S(1)} %bitcast.27, ...), custom_call_target="tpu_custom_call" | custom-call | flops 402653184 | bytes 6291456 | tf_op jit(solution)/shard_map/pallas_call | solution.py:184
  16.6 1.2 %shard_map.97.part_ref = f32[64,2048]{1,0:T(8,128)S(1)} custom-call(bf16[16,2048]{1,0:T(8,128)(2,1)S(1)} %shard_map.96.mark_ref, f32[2,2048]{1,0:T(2,128)S(1)} %bitcast.32, bf16[2,2048,512]{2,1,0:T(8,128)(2,1)S(1)} %bitcast.20, bf16[2,2048,512]{2,1,0:T(8,128)(2,1)S(1)} %bitcast.24, bf16[2,512,2048]{2,1,0:T(8,128)(2,1)S(1)} %bitcast.28, ...), custom_call_target="tpu_custom_call" | custom-call | flops 402653184 | bytes 6291456 | tf_op jit(solution)/shard_map/pallas_call | solution.py:184
  17.9 3.5 %collective-permute-start.11 = (bf16[16,2048]{1,0:T(8,128)(2,1)S(1)}, bf16[16,2048]{1,0:T(8,128)(2,1)S(1)}, u32[]{:S(2)}, u32[]{:S(2)}) collective-permute-start(bf16[16,2048]{1,0:T(8,128)(2,1)S(1)} %get-tuple-element.22), channel_id=1, source_target_pairs={{0,6},{2,4},{4,2},{6,0},{1,15},{3,13},{5,11},{7,9},{8,22},{10,20},... | collective-permute-start | bytes 196616 | tf_op jit(solution)/shard_map/ppermute | solution.py:223
  21.6 1.3 %collective-permute-start.13 = (bf16[16,2048]{1,0:T(8,128)(2,1)S(1)}, bf16[16,2048]{1,0:T(8,128)(2,1)S(1)}, u32[]{:S(2)}, u32[]{:S(2)}) collective-permute-start(bf16[16,2048]{1,0:T(8,128)(2,1)S(1)} %get-tuple-element.24), channel_id=1, source_target_pairs={{0,2},{2,0},{4,6},{6,4},{1,11},{3,9},{5,15},{7,13},{8,18},{10,16},... | collective-permute-start | bytes 196616 | tf_op jit(solution)/shard_map/ppermute | solution.py:223
  22.9 2.1 %collective-permute-start.14 = (bf16[16,2048]{1,0:T(8,128)(2,1)S(1)}, bf16[16,2048]{1,0:T(8,128)(2,1)S(1)}, u32[]{:S(2)}, u32[]{:S(2)}) collective-permute-start(bf16[16,2048]{1,0:T(8,128)(2,1)S(1)} %get-tuple-element.25), channel_id=1, source_target_pairs={{0,0},{2,2},{4,4},{6,6},{1,9},{3,11},{5,13},{7,15},{8,16},{10,18},... | collective-permute-start | bytes 196616 | tf_op jit(solution)/shard_map/ppermute | solution.py:223
  25.0 0.5 %collective-permute-done.12.refs_1_ = bf16[16,2048]{1,0:T(8,128)(2,1)S(1)} collective-permute-done((bf16[16,2048]{1,0:T(8,128)(2,1)S(1)}, bf16[16,2048]{1,0:T(8,128)(2,1)S(1)}, u32[]{:S(2)}, u32[]{:S(2)}) %collective-permute-start.12) | collective-permute-done | bytes 65568 | tf_op jit(solution)/shard_map/ppermute | solution.py:223
  25.6 2.3 %collective-permute-done.14.refs_3_ = bf16[16,2048]{1,0:T(8,128)(2,1)S(1)} collective-permute-done((bf16[16,2048]{1,0:T(8,128)(2,1)S(1)}, bf16[16,2048]{1,0:T(8,128)(2,1)S(1)}, u32[]{:S(2)}, u32[]{:S(2)}) %collective-permute-start.14) | collective-permute-done | bytes 65568 | tf_op jit(solution)/shard_map/ppermute | solution.py:223
  28.1 2.2 %collective-permute-start.16 = (bf16[16,2048]{1,0:T(8,128)(2,1)S(1)}, bf16[16,2048]{1,0:T(8,128)(2,1)S(1)}, u32[]{:S(2)}, u32[]{:S(2)}) collective-permute-start(bf16[16,2048]{1,0:T(8,128)(2,1)S(1)} %get-tuple-element.27.refs_3_), channel_id=1, source_target_pairs={{0,6},{1,7},{2,4},{3,5},{4,2},{5,3},{6,0},{7,1},{8,14},{9,15},{10,... | collective-permute-start | bytes 196616 | tf_op jit(solution)/shard_map/ppermute | solution.py:213
  30.8 4.2 %collective-permute-start.15 = (bf16[8,2048]{1,0:T(8,128)(2,1)S(1)}, bf16[8,2048]{1,0:T(8,128)(2,1)S(1)}, u32[]{:S(2)}, u32[]{:S(2)}) collective-permute-start(bf16[8,2048]{1,0:T(8,128)(2,1)S(1)} %get-tuple-element.41), channel_id=1, source_target_pairs={{0,1},{1,0},{2,3},{3,2},{4,5},{5,4},{6,7},{7,6},{8,9},{9,8},{10,11... | collective-permute-start | bytes 98312 | tf_op jit(solution)/shard_map/ppermute | solution.py:209
  35.0 0.9 %collective-permute-done.15.mark_ref.there_ref = bf16[8,2048]{1,0:T(8,128)(2,1)S(1)} collective-permute-done((bf16[8,2048]{1,0:T(8,128)(2,1)S(1)}, bf16[8,2048]{1,0:T(8,128)(2,1)S(1)}, u32[]{:S(2)}, u32[]{:S(2)}) %collective-permute-start.15) | collective-permute-done | bytes 32800 | tf_op jit(solution)/shard_map/ppermute | solution.py:209
  35.9 2.8 %collective-permute-start.19 = (bf16[64,2048]{1,0:T(8,128)(2,1)S(1)}, bf16[64,2048]{1,0:T(8,128)(2,1)S(1)}, u32[]{:S(2)}, u32[]{:S(2)}) collective-permute-start(bf16[64,2048]{1,0:T(8,128)(2,1)S(1)} %shard_map.102.refs_0_), channel_id=1, source_target_pairs={{0,1},{1,0},{2,3},{3,2},{4,5},{5,4},{6,7},{7,6},{8,9},{9,8},{10,11... | collective-permute-start | bytes 786440 | tf_op jit(solution)/shard_map/ppermute | solution.py:209
  38.8 1.1 %shard_map.103 = (f32[32,2048]{1,0:T(8,128)S(1)}, bf16[32,2048]{1,0:T(8,128)(2,1)S(1)}) custom-call(bf16[16,2048]{1,0:T(8,128)(2,1)S(1)} %shard_map.101.mark_ref, f32[2,2048]{1,0:T(2,128)S(1)} %bitcast.34, bf16[2,2048,512]{2,1,0:T(8,128)(2,1)S(1)} %bitcast.21, bf16[2,2048,512]{2,1,0:T(8,128)(2,1)S(1)} %bitcast.25, bf16[2,512,2048]{2,1,0:T(8,128)(2,1)S(1)} %bitcast.29, ...), custom_call_target="tpu_custom_call" | custom-call | flops 402653184 | bytes 6291456 | tf_op jit(solution)/shard_map/pallas_call | solution.py:184
  40.0 1.1 %shard_map.104 = (f32[32,2048]{1,0:T(8,128)S(1)}, bf16[32,2048]{1,0:T(8,128)(2,1)S(1)}) custom-call(bf16[16,2048]{1,0:T(8,128)(2,1)S(1)} %shard_map.101.mark_ref, f32[2,2048]{1,0:T(2,128)S(1)} %bitcast.35, bf16[2,2048,512]{2,1,0:T(8,128)(2,1)S(1)} %bitcast.22, bf16[2,2048,512]{2,1,0:T(8,128)(2,1)S(1)} %bitcast.26, bf16[2,512,2048]{2,1,0:T(8,128)(2,1)S(1)} %bitcast.30, ...), custom_call_target="tpu_custom_call" | custom-call | flops 402653184 | bytes 6291456 | tf_op jit(solution)/shard_map/pallas_call | solution.py:184
  41.2 0.5 %collective-permute-start.20 = (bf16[32,2048]{1,0:T(8,128)(2,1)S(1)}, bf16[32,2048]{1,0:T(8,128)(2,1)S(1)}, u32[]{:S(2)}, u32[]{:S(2)}) collective-permute-start(bf16[32,2048]{1,0:T(8,128)(2,1)S(1)} %get-tuple-element.30), channel_id=1, source_target_pairs={{0,1},{1,0},{2,3},{3,2},{4,5},{5,4},{6,7},{7,6},{8,9},{9,8},{10,11... | collective-permute-start | bytes 393224 | tf_op jit(solution)/shard_map/ppermute | solution.py:209
  41.7 1.0 %collective-permute-done.20.to_mine_ref = bf16[32,2048]{1,0:T(8,128)(2,1)S(1)} collective-permute-done((bf16[32,2048]{1,0:T(8,128)(2,1)S(1)}, bf16[32,2048]{1,0:T(8,128)(2,1)S(1)}, u32[]{:S(2)}, u32[]{:S(2)}) %collective-permute-start.20) | collective-permute-done | bytes 131104 | tf_op jit(solution)/shard_map/ppermute | solution.py:209
  42.8 1.3 %collective-permute-start.22 = (bf16[16,2048]{1,0:T(8,128)(2,1)S(1)}, bf16[16,2048]{1,0:T(8,128)(2,1)S(1)}, u32[]{:S(2)}, u32[]{:S(2)}) collective-permute-start(bf16[16,2048]{1,0:T(8,128)(2,1)S(1)} %get-tuple-element.32), channel_id=1, source_target_pairs={{0,6},{1,7},{2,4},{3,5},{4,2},{5,3},{6,0},{7,1},{8,14},{9,15},{10,... | collective-permute-start | bytes 196616 | tf_op jit(solution)/shard_map/ppermute | solution.py:213
  44.3 1.2 %collective-permute-start.24 = (bf16[16,2048]{1,0:T(8,128)(2,1)S(1)}, bf16[16,2048]{1,0:T(8,128)(2,1)S(1)}, u32[]{:S(2)}, u32[]{:S(2)}) collective-permute-start(bf16[16,2048]{1,0:T(8,128)(2,1)S(1)} %get-tuple-element.34), channel_id=1, source_target_pairs={{0,2},{1,3},{2,0},{3,1},{4,6},{5,7},{6,4},{7,5},{8,10},{9,11},{10,... | collective-permute-start | bytes 196616 | tf_op jit(solution)/shard_map/ppermute | solution.py:213
  45.5 1.4 %collective-permute-done.22.refs_0_ = bf16[16,2048]{1,0:T(8,128)(2,1)S(1)} collective-permute-done((bf16[16,2048]{1,0:T(8,128)(2,1)S(1)}, bf16[16,2048]{1,0:T(8,128)(2,1)S(1)}, u32[]{:S(2)}, u32[]{:S(2)}) %collective-permute-start.22) | collective-permute-done | bytes 65568 | tf_op jit(solution)/shard_map/ppermute | solution.py:213
  46.9 2.2 %collective-permute-done.23.refs_1_ = bf16[16,2048]{1,0:T(8,128)(2,1)S(1)} collective-permute-done((bf16[16,2048]{1,0:T(8,128)(2,1)S(1)}, bf16[16,2048]{1,0:T(8,128)(2,1)S(1)}, u32[]{:S(2)}, u32[]{:S(2)}) %collective-permute-start.23) | collective-permute-done | bytes 65568 | tf_op jit(solution)/shard_map/ppermute | solution.py:213
  49.1 0.6 %select_bitcast_fusion = (bf16[1,8,2048]{2,1,0:T(8,128)(2,1)}, bf16[1,8,2048]{2,1,0:T(8,128)(2,1)}) fusion(pred[]{:T(512)S(6)} %eq.37, bf16[16,2048]{1,0:T(8,128)(2,1)S(1)} %shard_map.106), kind=kLoop, calls=%fused_computation.7 | loop fusion | flops 32768 | bytes 131073 | tf_op jit(solution)/shard_map/broadcast_in_dim | solution.py:275
  (57 shorter events, 2.5 us)
Async XLA Ops:
  0.6 0.8 %copy-start = (bf16[2,8,2048]{2,1,0:T(8,128)(2,1)S(1)}, bf16[2,8,2048]{2,1,0:T(8,128)(2,1)}, u32[]{:S(2)}) copy-start(bf16[2,8,2048]{2,1,0:T(8,128)(2,1)} %param.10) | copy-start | bytes 196612
  0.7 1.1 %copy-start.5 = (bf16[1,8,2048]{2,1,0:T(8,128)(2,1)S(1)}, bf16[1,8,2048]{2,1,0:T(8,128)(2,1)}, u32[]{:S(2)}) copy-start(bf16[1,8,2048]{2,1,0:T(8,128)(2,1)} %param.8) | copy-start | bytes 98308
  0.7 1.1 %copy-start.6 = (bf16[1,8,2048]{2,1,0:T(8,128)(2,1)S(1)}, bf16[1,8,2048]{2,1,0:T(8,128)(2,1)}, u32[]{:S(2)}) copy-start(bf16[1,8,2048]{2,1,0:T(8,128)(2,1)} %param.9) | copy-start | bytes 98308
  1.8 1.6 %collective-permute-start.1 = (bf16[8,2048]{1,0:T(8,128)(2,1)S(1)}, bf16[8,2048]{1,0:T(8,128)(2,1)S(1)}, u32[]{:S(2)}, u32[]{:S(2)}) collective-permute-start(bf16[8,2048]{1,0:T(8,128)(2,1)S(1)} %get-tuple-element.21), channel_id=1, source_target_pairs={{0,1},{1,0},{2,3},{3,2},{4,5},{5,4},{6,7},{7,6},{8,9},{9,8},{10,11... | collective-permute-start | bytes 98312 | tf_op jit(solution)/shard_map/ppermute | solution.py:209
  3.5 11.5 %copy-start.1 = (bf16[1,2,2048,512]{3,2,1,0:T(8,128)(2,1)S(1)}, bf16[1,2,2048,512]{3,2,1,0:T(8,128)(2,1)}, u32[]{:S(2)}) copy-start(bf16[1,2,2048,512]{3,2,1,0:T(8,128)(2,1)} %param.13) | copy-start | bytes 12582916
  3.5 11.5 %copy-start.2 = (bf16[1,2,2048,512]{3,2,1,0:T(8,128)(2,1)S(1)}, bf16[1,2,2048,512]{3,2,1,0:T(8,128)(2,1)}, u32[]{:S(2)}) copy-start(bf16[1,2,2048,512]{3,2,1,0:T(8,128)(2,1)} %param.14) | copy-start | bytes 12582916
  3.5 11.5 %copy-start.3 = (bf16[1,2,512,2048]{3,2,1,0:T(8,128)(2,1)S(1)}, bf16[1,2,512,2048]{3,2,1,0:T(8,128)(2,1)}, u32[]{:S(2)}) copy-start(bf16[1,2,512,2048]{3,2,1,0:T(8,128)(2,1)} %param.15) | copy-start | bytes 12582916
  3.5 11.5 %copy-start.4 = (f32[1,2,2048]{2,1,0:T(2,128)S(1)}, f32[1,2,2048]{2,1,0:T(2,128)}, u32[]{:S(2)}) copy-start(f32[1,2,2048]{2,1,0:T(2,128)} %param.12) | copy-start | bytes 49156
  3.5 8.2 %collective-permute-start.2 = (bf16[16,2048]{1,0:T(8,128)(2,1)S(1)}, bf16[16,2048]{1,0:T(8,128)(2,1)S(1)}, u32[]{:S(2)}, u32[]{:S(2)}) collective-permute-start(bf16[16,2048]{1,0:T(8,128)(2,1)S(1)} %pad_maximum_fusion.1.x_ref), channel_id=1, source_target_pairs={{0,14},{2,12},{4,10},{6,8},{1,7},{3,5},{5,3},{7,1},{8,6},{10,4},{1... | collective-permute-start | bytes 196616 | tf_op jit(solution)/shard_map/ppermute | solution.py:223
  6.8 5.1 %collective-permute-start.3 = (bf16[16,2048]{1,0:T(8,128)(2,1)S(1)}, bf16[16,2048]{1,0:T(8,128)(2,1)S(1)}, u32[]{:S(2)}, u32[]{:S(2)}) collective-permute-start(bf16[16,2048]{1,0:T(8,128)(2,1)S(1)} %pad_maximum_fusion.1.x_ref), channel_id=1, source_target_pairs={{0,12},{2,14},{4,8},{6,10},{1,5},{3,7},{5,1},{7,3},{8,4},{10,6},{1... | collective-permute-start | bytes 196616 | tf_op jit(solution)/shard_map/ppermute | solution.py:223
  6.9 5.4 %collective-permute-start.4 = (bf16[16,2048]{1,0:T(8,128)(2,1)S(1)}, bf16[16,2048]{1,0:T(8,128)(2,1)S(1)}, u32[]{:S(2)}, u32[]{:S(2)}) collective-permute-start(bf16[16,2048]{1,0:T(8,128)(2,1)S(1)} %pad_maximum_fusion.1.x_ref), channel_id=1, source_target_pairs={{0,10},{2,8},{4,14},{6,12},{1,3},{3,1},{5,7},{7,5},{8,2},{10,0},{1... | collective-permute-start | bytes 196616 | tf_op jit(solution)/shard_map/ppermute | solution.py:223
  8.1 5.3 %collective-permute-start.5 = (bf16[16,2048]{1,0:T(8,128)(2,1)S(1)}, bf16[16,2048]{1,0:T(8,128)(2,1)S(1)}, u32[]{:S(2)}, u32[]{:S(2)}) collective-permute-start(bf16[16,2048]{1,0:T(8,128)(2,1)S(1)} %pad_maximum_fusion.1.x_ref), channel_id=1, source_target_pairs={{0,8},{2,10},{4,12},{6,14},{1,1},{3,3},{5,5},{7,7},{8,0},{10,2},{1... | collective-permute-start | bytes 196616 | tf_op jit(solution)/shard_map/ppermute | solution.py:223
  10.3 6.3 %collective-permute-start = (bf16[8,2048]{1,0:T(8,128)(2,1)S(1)}, bf16[8,2048]{1,0:T(8,128)(2,1)S(1)}, u32[]{:S(2)}, u32[]{:S(2)}) collective-permute-start(bf16[8,2048]{1,0:T(8,128)(2,1)S(1)} %get-tuple-element.19), channel_id=1, source_target_pairs={{0,1},{1,0},{2,3},{3,2},{4,5},{5,4},{6,7},{7,6},{8,9},{9,8},{10,11... | collective-permute-start | bytes 98312 | tf_op jit(solution)/shard_map/ppermute | solution.py:209
  11.7 2.3 %collective-permute-start.6 = (bf16[16,2048]{1,0:T(8,128)(2,1)S(1)}, bf16[16,2048]{1,0:T(8,128)(2,1)S(1)}, u32[]{:S(2)}, u32[]{:S(2)}) collective-permute-start(bf16[16,2048]{1,0:T(8,128)(2,1)S(1)} %collective-permute-done.2.refs_0_), channel_id=1, source_target_pairs={{0,1},{1,0},{2,3},{3,2},{4,5},{5,4},{6,7},{7,6},{8,9},{9,8},{10,11... | collective-permute-start | bytes 196616 | tf_op jit(solution)/shard_map/ppermute | solution.py:209
  11.8 2.2 %collective-permute-start.7 = (bf16[16,2048]{1,0:T(8,128)(2,1)S(1)}, bf16[16,2048]{1,0:T(8,128)(2,1)S(1)}, u32[]{:S(2)}, u32[]{:S(2)}) collective-permute-start(bf16[16,2048]{1,0:T(8,128)(2,1)S(1)} %collective-permute-done.3.refs_1_), channel_id=1, source_target_pairs={{0,1},{1,0},{2,3},{3,2},{4,5},{5,4},{6,7},{7,6},{8,9},{9,8},{10,11... | collective-permute-start | bytes 196616 | tf_op jit(solution)/shard_map/ppermute | solution.py:209
  12.3 1.8 %collective-permute-start.8 = (bf16[16,2048]{1,0:T(8,128)(2,1)S(1)}, bf16[16,2048]{1,0:T(8,128)(2,1)S(1)}, u32[]{:S(2)}, u32[]{:S(2)}) collective-permute-start(bf16[16,2048]{1,0:T(8,128)(2,1)S(1)} %collective-permute-done.4.refs_2_), channel_id=1, source_target_pairs={{0,1},{1,0},{2,3},{3,2},{4,5},{5,4},{6,7},{7,6},{8,9},{9,8},{10,11... | collective-permute-start | bytes 196616 | tf_op jit(solution)/shard_map/ppermute | solution.py:209
  13.4 1.5 %collective-permute-start.9 = (bf16[16,2048]{1,0:T(8,128)(2,1)S(1)}, bf16[16,2048]{1,0:T(8,128)(2,1)S(1)}, u32[]{:S(2)}, u32[]{:S(2)}) collective-permute-start(bf16[16,2048]{1,0:T(8,128)(2,1)S(1)} %collective-permute-done.5.refs_3_.x_ref), channel_id=1, source_target_pairs={{0,1},{1,0},{2,3},{3,2},{4,5},{5,4},{6,7},{7,6},{8,9},{9,8},{10,11... | collective-permute-start | bytes 196616 | tf_op jit(solution)/shard_map/ppermute | solution.py:209
  16.2 1.7 %collective-permute-start.10 = (bf16[64,2048]{1,0:T(8,128)(2,1)S(1)}, bf16[64,2048]{1,0:T(8,128)(2,1)S(1)}, u32[]{:S(2)}, u32[]{:S(2)}) collective-permute-start(bf16[64,2048]{1,0:T(8,128)(2,1)S(1)} %shard_map.98), channel_id=1, source_target_pairs={{0,1},{1,0},{2,3},{3,2},{4,5},{5,4},{6,7},{7,6},{8,9},{9,8},{10,11... | collective-permute-start | bytes 786440 | tf_op jit(solution)/shard_map/ppermute | solution.py:209
  17.9 7.0 %collective-permute-start.11 = (bf16[16,2048]{1,0:T(8,128)(2,1)S(1)}, bf16[16,2048]{1,0:T(8,128)(2,1)S(1)}, u32[]{:S(2)}, u32[]{:S(2)}) collective-permute-start(bf16[16,2048]{1,0:T(8,128)(2,1)S(1)} %get-tuple-element.22), channel_id=1, source_target_pairs={{0,6},{2,4},{4,2},{6,0},{1,15},{3,13},{5,11},{7,9},{8,22},{10,20},... | collective-permute-start | bytes 196616 | tf_op jit(solution)/shard_map/ppermute | solution.py:223
  21.5 4.0 %collective-permute-start.12 = (bf16[16,2048]{1,0:T(8,128)(2,1)S(1)}, bf16[16,2048]{1,0:T(8,128)(2,1)S(1)}, u32[]{:S(2)}, u32[]{:S(2)}) collective-permute-start(bf16[16,2048]{1,0:T(8,128)(2,1)S(1)} %get-tuple-element.23), channel_id=1, source_target_pairs={{0,4},{2,6},{4,0},{6,2},{1,13},{3,15},{5,9},{7,11},{8,20},{10,22},... | collective-permute-start | bytes 196616 | tf_op jit(solution)/shard_map/ppermute | solution.py:223
  21.6 4.0 %collective-permute-start.13 = (bf16[16,2048]{1,0:T(8,128)(2,1)S(1)}, bf16[16,2048]{1,0:T(8,128)(2,1)S(1)}, u32[]{:S(2)}, u32[]{:S(2)}) collective-permute-start(bf16[16,2048]{1,0:T(8,128)(2,1)S(1)} %get-tuple-element.24), channel_id=1, source_target_pairs={{0,2},{2,0},{4,6},{6,4},{1,11},{3,9},{5,15},{7,13},{8,18},{10,16},... | collective-permute-start | bytes 196616 | tf_op jit(solution)/shard_map/ppermute | solution.py:223
  22.9 5.1 %collective-permute-start.14 = (bf16[16,2048]{1,0:T(8,128)(2,1)S(1)}, bf16[16,2048]{1,0:T(8,128)(2,1)S(1)}, u32[]{:S(2)}, u32[]{:S(2)}) collective-permute-start(bf16[16,2048]{1,0:T(8,128)(2,1)S(1)} %get-tuple-element.25), channel_id=1, source_target_pairs={{0,0},{2,2},{4,4},{6,6},{1,9},{3,11},{5,13},{7,15},{8,16},{10,18},... | collective-permute-start | bytes 196616 | tf_op jit(solution)/shard_map/ppermute | solution.py:223
  28.1 7.8 %collective-permute-start.16 = (bf16[16,2048]{1,0:T(8,128)(2,1)S(1)}, bf16[16,2048]{1,0:T(8,128)(2,1)S(1)}, u32[]{:S(2)}, u32[]{:S(2)}) collective-permute-start(bf16[16,2048]{1,0:T(8,128)(2,1)S(1)} %get-tuple-element.27.refs_3_), channel_id=1, source_target_pairs={{0,6},{1,7},{2,4},{3,5},{4,2},{5,3},{6,0},{7,1},{8,14},{9,15},{10,... | collective-permute-start | bytes 196616 | tf_op jit(solution)/shard_map/ppermute | solution.py:213
  30.2 5.7 %collective-permute-start.17 = (bf16[16,2048]{1,0:T(8,128)(2,1)S(1)}, bf16[16,2048]{1,0:T(8,128)(2,1)S(1)}, u32[]{:S(2)}, u32[]{:S(2)}) collective-permute-start(bf16[16,2048]{1,0:T(8,128)(2,1)S(1)} %get-tuple-element.27.refs_3_), channel_id=1, source_target_pairs={{0,4},{1,5},{2,6},{3,7},{4,0},{5,1},{6,2},{7,3},{8,12},{9,13},{10,... | collective-permute-start | bytes 196616 | tf_op jit(solution)/shard_map/ppermute | solution.py:213
  30.5 5.4 %collective-permute-start.18 = (bf16[16,2048]{1,0:T(8,128)(2,1)S(1)}, bf16[16,2048]{1,0:T(8,128)(2,1)S(1)}, u32[]{:S(2)}, u32[]{:S(2)}) collective-permute-start(bf16[16,2048]{1,0:T(8,128)(2,1)S(1)} %get-tuple-element.27.refs_3_), channel_id=1, source_target_pairs={{0,2},{1,3},{2,0},{3,1},{4,6},{5,7},{6,4},{7,5},{8,10},{9,11},{10,... | collective-permute-start | bytes 196616 | tf_op jit(solution)/shard_map/ppermute | solution.py:213
  30.8 5.1 %collective-permute-start.15 = (bf16[8,2048]{1,0:T(8,128)(2,1)S(1)}, bf16[8,2048]{1,0:T(8,128)(2,1)S(1)}, u32[]{:S(2)}, u32[]{:S(2)}) collective-permute-start(bf16[8,2048]{1,0:T(8,128)(2,1)S(1)} %get-tuple-element.41), channel_id=1, source_target_pairs={{0,1},{1,0},{2,3},{3,2},{4,5},{5,4},{6,7},{7,6},{8,9},{9,8},{10,11... | collective-permute-start | bytes 98312 | tf_op jit(solution)/shard_map/ppermute | solution.py:209
  35.9 4.1 %collective-permute-start.19 = (bf16[64,2048]{1,0:T(8,128)(2,1)S(1)}, bf16[64,2048]{1,0:T(8,128)(2,1)S(1)}, u32[]{:S(2)}, u32[]{:S(2)}) collective-permute-start(bf16[64,2048]{1,0:T(8,128)(2,1)S(1)} %shard_map.102.refs_0_), channel_id=1, source_target_pairs={{0,1},{1,0},{2,3},{3,2},{4,5},{5,4},{6,7},{7,6},{8,9},{9,8},{10,11... | collective-permute-start | bytes 786440 | tf_op jit(solution)/shard_map/ppermute | solution.py:209
  39.9 1.8 %collective-permute-start.21 = (bf16[32,2048]{1,0:T(8,128)(2,1)S(1)}, bf16[32,2048]{1,0:T(8,128)(2,1)S(1)}, u32[]{:S(2)}, u32[]{:S(2)}) collective-permute-start(bf16[32,2048]{1,0:T(8,128)(2,1)S(1)} %get-tuple-element.31), channel_id=1, source_target_pairs={{0,1},{1,0},{2,3},{3,2},{4,5},{5,4},{6,7},{7,6},{8,9},{9,8},{10,11... | collective-permute-start | bytes 393224 | tf_op jit(solution)/shard_map/ppermute | solution.py:209
  41.2 1.5 %collective-permute-start.20 = (bf16[32,2048]{1,0:T(8,128)(2,1)S(1)}, bf16[32,2048]{1,0:T(8,128)(2,1)S(1)}, u32[]{:S(2)}, u32[]{:S(2)}) collective-permute-start(bf16[32,2048]{1,0:T(8,128)(2,1)S(1)} %get-tuple-element.30), channel_id=1, source_target_pairs={{0,1},{1,0},{2,3},{3,2},{4,5},{5,4},{6,7},{7,6},{8,9},{9,8},{10,11... | collective-permute-start | bytes 393224 | tf_op jit(solution)/shard_map/ppermute | solution.py:209
  42.8 4.1 %collective-permute-start.22 = (bf16[16,2048]{1,0:T(8,128)(2,1)S(1)}, bf16[16,2048]{1,0:T(8,128)(2,1)S(1)}, u32[]{:S(2)}, u32[]{:S(2)}) collective-permute-start(bf16[16,2048]{1,0:T(8,128)(2,1)S(1)} %get-tuple-element.32), channel_id=1, source_target_pairs={{0,6},{1,7},{2,4},{3,5},{4,2},{5,3},{6,0},{7,1},{8,14},{9,15},{10,... | collective-permute-start | bytes 196616 | tf_op jit(solution)/shard_map/ppermute | solution.py:213
  44.0 5.0 %collective-permute-start.23 = (bf16[16,2048]{1,0:T(8,128)(2,1)S(1)}, bf16[16,2048]{1,0:T(8,128)(2,1)S(1)}, u32[]{:S(2)}, u32[]{:S(2)}) collective-permute-start(bf16[16,2048]{1,0:T(8,128)(2,1)S(1)} %get-tuple-element.33), channel_id=1, source_target_pairs={{0,4},{1,5},{2,6},{3,7},{4,0},{5,1},{6,2},{7,3},{8,12},{9,13},{10,... | collective-permute-start | bytes 196616 | tf_op jit(solution)/shard_map/ppermute | solution.py:213
  44.3 4.8 %collective-permute-start.24 = (bf16[16,2048]{1,0:T(8,128)(2,1)S(1)}, bf16[16,2048]{1,0:T(8,128)(2,1)S(1)}, u32[]{:S(2)}, u32[]{:S(2)}) collective-permute-start(bf16[16,2048]{1,0:T(8,128)(2,1)S(1)} %get-tuple-element.34), channel_id=1, source_target_pairs={{0,2},{1,3},{2,0},{3,1},{4,6},{5,7},{6,4},{7,5},{8,10},{9,11},{10,... | collective-permute-start | bytes 196616 | tf_op jit(solution)/shard_map/ppermute | solution.py:213
  (1 other events, 0.8 us)

commit v10 on v9

--- a/solution.py
+++ b/solution.py
@@ -248,7 +248,7 @@
             pieces = [normed] + [to_chip(normed, step) for step in range(1, chips)]
         x = pieces[0] if tick == 0 else state
         height = x.shape[0]
-        mark = passed(state)
+        mark = passed(state) if tick + 1 < ticks else gains[0]
         pieces = pieces[::-1]
         slots = [step if chips & (chips - 1) == 0 else (chips - step) % chips for step in range(chips)]
         slots = [chips - 1 - slot for slot in slots]

time: 49.9 us -> 49.9 us (level)
  no operation moved by 1% of the time
where the time goes in v10:
time: 49.9 us; the launch traced here: 49.7 us
  starting transfers between devices  31.3 us (63%)
  waiting for transfers between devices  10.7 us (21%)
  Pallas kernels  5.06 us (10%)
  between operations  0.92 us (2%)
  local copies, waits for them, and re-layouts  0.81 us (2%)
  other arithmetic  0.7 us (1%)
    ppermute x8, starting transfers between devices, to_next(): return lax.ppermute(value, both, pairs)  13.8 us
    ppermute x11, starting transfers between devices, to_sibling(): return lax.ppermute(value, 'zero', [(k, k ^ 1) for k in range(zero)])  12.1 us
    ppermute x6, starting transfers between devices, to_chip(): return lax.ppermute(value, 'zero', pairs)  5.43 us
    pallas_call x4, Pallas kernels, partial(): pl.pallas_call(functools.partial(group_kernel, tick, other, ready, len(pi...  4.73 us
    ppermute x6, waiting for transfers between devices, to_chip(): return lax.ppermute(value, 'zero', pairs)  3.61 us
    ppermute x11, waiting for transfers between devices, to_sibling(): return lax.ppermute(value, 'zero', [(k, k ^ 1) for k in range(zero)])  3.59 us
    ppermute x8, waiting for transfers between devices, to_next(): return lax.ppermute(value, both, pairs)  3.48 us
  transfers between devices with their start and end apart: 25, of which 10 were waited for; matrix products, arithmetic and copies ran while one was open for 0% of the time, Pallas kernels for 10%

profile of v10, /device:TPU:9, one launch (start us, length us, event | category | flops | bytes accessed | tf_op | source)
XLA Modules:
  0.0 49.7 jit_solution(14021558791651032018)
XLA Ops:
  0.7 0.7 %copy-done = bf16[2,8,2048]{2,1,0:T(8,128)(2,1)S(1)} copy-done((bf16[2,8,2048]{2,1,0:T(8,128)(2,1)S(1)}, bf16[2,8,2048]{2,1,0:T(8,128)(2,1)}, u32[]{:S(2)}) %copy-start) | copy-done | bytes 65560
  1.8 0.7 %collective-permute-start.1 = (bf16[8,2048]{1,0:T(8,128)(2,1)S(1)}, bf16[8,2048]{1,0:T(8,128)(2,1)S(1)}, u32[]{:S(2)}, u32[]{:S(2)}) collective-permute-start(bf16[8,2048]{1,0:T(8,128)(2,1)S(1)} %get-tuple-element.21), channel_id=1, source_target_pairs={{0,1},{1,0},{2,3},{3,2},{4,5},{5,4},{6,7},{7,6},{8,9},{9,8},{10,11... | collective-permute-start | bytes 98312 | tf_op jit(solution)/shard_map/ppermute | solution.py:209
  2.6 0.9 %collective-permute-done.1 = bf16[8,2048]{1,0:T(8,128)(2,1)S(1)} collective-permute-done((bf16[8,2048]{1,0:T(8,128)(2,1)S(1)}, bf16[8,2048]{1,0:T(8,128)(2,1)S(1)}, u32[]{:S(2)}, u32[]{:S(2)}) %collective-permute-start.1) | collective-permute-done | bytes 32800 | tf_op jit(solution)/shard_map/ppermute | solution.py:209
  3.5 3.2 %collective-permute-start.2 = (bf16[16,2048]{1,0:T(8,128)(2,1)S(1)}, bf16[16,2048]{1,0:T(8,128)(2,1)S(1)}, u32[]{:S(2)}, u32[]{:S(2)}) collective-permute-start(bf16[16,2048]{1,0:T(8,128)(2,1)S(1)} %pad_maximum_fusion.1.x_ref), channel_id=1, source_target_pairs={{0,14},{2,12},{4,10},{6,8},{1,7},{3,5},{5,3},{7,1},{8,6},{10,4},{1... | collective-permute-start | bytes 196616 | tf_op jit(solution)/shard_map/ppermute | solution.py:223
  6.9 1.3 %collective-permute-start.4 = (bf16[16,2048]{1,0:T(8,128)(2,1)S(1)}, bf16[16,2048]{1,0:T(8,128)(2,1)S(1)}, u32[]{:S(2)}, u32[]{:S(2)}) collective-permute-start(bf16[16,2048]{1,0:T(8,128)(2,1)S(1)} %pad_maximum_fusion.1.x_ref), channel_id=1, source_target_pairs={{0,10},{2,8},{4,14},{6,12},{1,3},{3,1},{5,7},{7,5},{8,2},{10,0},{1... | collective-permute-start | bytes 196616 | tf_op jit(solution)/shard_map/ppermute | solution.py:223
  8.1 2.2 %collective-permute-start.5 = (bf16[16,2048]{1,0:T(8,128)(2,1)S(1)}, bf16[16,2048]{1,0:T(8,128)(2,1)S(1)}, u32[]{:S(2)}, u32[]{:S(2)}) collective-permute-start(bf16[16,2048]{1,0:T(8,128)(2,1)S(1)} %pad_maximum_fusion.1.x_ref), channel_id=1, source_target_pairs={{0,8},{2,10},{4,12},{6,14},{1,1},{3,3},{5,5},{7,7},{8,0},{10,2},{1... | collective-permute-start | bytes 196616 | tf_op jit(solution)/shard_map/ppermute | solution.py:223
  10.3 1.4 %collective-permute-start = (bf16[8,2048]{1,0:T(8,128)(2,1)S(1)}, bf16[8,2048]{1,0:T(8,128)(2,1)S(1)}, u32[]{:S(2)}, u32[]{:S(2)}) collective-permute-start(bf16[8,2048]{1,0:T(8,128)(2,1)S(1)} %get-tuple-element.19), channel_id=1, source_target_pairs={{0,1},{1,0},{2,3},{3,2},{4,5},{5,4},{6,7},{7,6},{8,9},{9,8},{10,11... | collective-permute-start | bytes 98312 | tf_op jit(solution)/shard_map/ppermute | solution.py:209
  11.8 0.4 collective-permute-start.7
  12.3 0.7 %collective-permute-start.8 = (bf16[16,2048]{1,0:T(8,128)(2,1)S(1)}, bf16[16,2048]{1,0:T(8,128)(2,1)S(1)}, u32[]{:S(2)}, u32[]{:S(2)}) collective-permute-start(bf16[16,2048]{1,0:T(8,128)(2,1)S(1)} %collective-permute-done.4.refs_2_), channel_id=1, source_target_pairs={{0,1},{1,0},{2,3},{3,2},{4,5},{5,4},{6,7},{7,6},{8,9},{9,8},{10,11... | collective-permute-start | bytes 196616 | tf_op jit(solution)/shard_map/ppermute | solution.py:209
  12.9 0.5 collective-permute-done.5.refs_3_.x_ref
  13.4 0.6 %collective-permute-start.9 = (bf16[16,2048]{1,0:T(8,128)(2,1)S(1)}, bf16[16,2048]{1,0:T(8,128)(2,1)S(1)}, u32[]{:S(2)}, u32[]{:S(2)}) collective-permute-start(bf16[16,2048]{1,0:T(8,128)(2,1)S(1)} %collective-permute-done.5.refs_3_.x_ref), channel_id=1, source_target_pairs={{0,1},{1,0},{2,3},{3,2},{4,5},{5,4},{6,7},{7,6},{8,9},{9,8},{10,11... | collective-permute-start | bytes 196616 | tf_op jit(solution)/shard_map/ppermute | solution.py:209
  14.1 0.9 %collective-permute-done.9.refs_3_ = bf16[16,2048]{1,0:T(8,128)(2,1)S(1)} collective-permute-done((bf16[16,2048]{1,0:T(8,128)(2,1)S(1)}, bf16[16,2048]{1,0:T(8,128)(2,1)S(1)}, u32[]{:S(2)}, u32[]{:S(2)}) %collective-permute-start.9) | collective-permute-done | bytes 65568 | tf_op jit(solution)/shard_map/ppermute | solution.py:209
  15.0 1.2 %shard_map.98 = bf16[64,2048]{1,0:T(8,128)(2,1)S(1)} custom-call(bf16[16,2048]{1,0:T(8,128)(2,1)S(1)} %shard_map.96.mark_ref, f32[2,2048]{1,0:T(2,128)S(1)} %bitcast.31, bf16[2,2048,512]{2,1,0:T(8,128)(2,1)S(1)} %bitcast.19, bf16[2,2048,512]{2,1,0:T(8,128)(2,1)S(1)} %bitcast.23, bf16[2,512,2048]{2,1,0:T(8,128)(2,1)S(1)} %bitcast.27, ...), custom_call_target="tpu_custom_call" | custom-call | flops 402653184 | bytes 6291456 | tf_op jit(solution)/shard_map/pallas_call | solution.py:184
  16.6 1.2 %shard_map.97.part_ref = f32[64,2048]{1,0:T(8,128)S(1)} custom-call(bf16[16,2048]{1,0:T(8,128)(2,1)S(1)} %shard_map.96.mark_ref, f32[2,2048]{1,0:T(2,128)S(1)} %bitcast.32, bf16[2,2048,512]{2,1,0:T(8,128)(2,1)S(1)} %bitcast.20, bf16[2,2048,512]{2,1,0:T(8,128)(2,1)S(1)} %bitcast.24, bf16[2,512,2048]{2,1,0:T(8,128)(2,1)S(1)} %bitcast.28, ...), custom_call_target="tpu_custom_call" | custom-call | flops 402653184 | bytes 6291456 | tf_op jit(solution)/shard_map/pallas_call | solution.py:184
  17.9 3.5 %collective-permute-start.11 = (bf16[16,2048]{1,0:T(8,128)(2,1)S(1)}, bf16[16,2048]{1,0:T(8,128)(2,1)S(1)}, u32[]{:S(2)}, u32[]{:S(2)}) collective-permute-start(bf16[16,2048]{1,0:T(8,128)(2,1)S(1)} %get-tuple-element.22), channel_id=1, source_target_pairs={{0,6},{2,4},{4,2},{6,0},{1,15},{3,13},{5,11},{7,9},{8,22},{10,20},... | collective-permute-start | bytes 196616 | tf_op jit(solution)/shard_map/ppermute | solution.py:223
  21.6 1.3 %collective-permute-start.13 = (bf16[16,2048]{1,0:T(8,128)(2,1)S(1)}, bf16[16,2048]{1,0:T(8,128)(2,1)S(1)}, u32[]{:S(2)}, u32[]{:S(2)}) collective-permute-start(bf16[16,2048]{1,0:T(8,128)(2,1)S(1)} %get-tuple-element.24), channel_id=1, source_target_pairs={{0,2},{2,0},{4,6},{6,4},{1,11},{3,9},{5,15},{7,13},{8,18},{10,16},... | collective-permute-start | bytes 196616 | tf_op jit(solution)/shard_map/ppermute | solution.py:223
  22.9 2.1 %collective-permute-start.14 = (bf16[16,2048]{1,0:T(8,128)(2,1)S(1)}, bf16[16,2048]{1,0:T(8,128)(2,1)S(1)}, u32[]{:S(2)}, u32[]{:S(2)}) collective-permute-start(bf16[16,2048]{1,0:T(8,128)(2,1)S(1)} %get-tuple-element.25), channel_id=1, source_target_pairs={{0,0},{2,2},{4,4},{6,6},{1,9},{3,11},{5,13},{7,15},{8,16},{10,18},... | collective-permute-start | bytes 196616 | tf_op jit(solution)/shard_map/ppermute | solution.py:223
  25.0 0.5 %collective-permute-done.12.refs_1_ = bf16[16,2048]{1,0:T(8,128)(2,1)S(1)} collective-permute-done((bf16[16,2048]{1,0:T(8,128)(2,1)S(1)}, bf16[16,2048]{1,0:T(8,128)(2,1)S(1)}, u32[]{:S(2)}, u32[]{:S(2)}) %collective-permute-start.12) | collective-permute-done | bytes 65568 | tf_op jit(solution)/shard_map/ppermute | solution.py:223
  25.6 2.3 %collective-permute-done.14.refs_3_ = bf16[16,2048]{1,0:T(8,128)(2,1)S(1)} collective-permute-done((bf16[16,2048]{1,0:T(8,128)(2,1)S(1)}, bf16[16,2048]{1,0:T(8,128)(2,1)S(1)}, u32[]{:S(2)}, u32[]{:S(2)}) %collective-permute-start.14) | collective-permute-done | bytes 65568 | tf_op jit(solution)/shard_map/ppermute | solution.py:223
  28.1 2.2 %collective-permute-start.16 = (bf16[16,2048]{1,0:T(8,128)(2,1)S(1)}, bf16[16,2048]{1,0:T(8,128)(2,1)S(1)}, u32[]{:S(2)}, u32[]{:S(2)}) collective-permute-start(bf16[16,2048]{1,0:T(8,128)(2,1)S(1)} %get-tuple-element.27.refs_3_), channel_id=1, source_target_pairs={{0,6},{1,7},{2,4},{3,5},{4,2},{5,3},{6,0},{7,1},{8,14},{9,15},{10,... | collective-permute-start | bytes 196616 | tf_op jit(solution)/shard_map/ppermute | solution.py:213
  30.8 4.2 %collective-permute-start.15 = (bf16[8,2048]{1,0:T(8,128)(2,1)S(1)}, bf16[8,2048]{1,0:T(8,128)(2,1)S(1)}, u32[]{:S(2)}, u32[]{:S(2)}) collective-permute-start(bf16[8,2048]{1,0:T(8,128)(2,1)S(1)} %get-tuple-element.41), channel_id=1, source_target_pairs={{0,1},{1,0},{2,3},{3,2},{4,5},{5,4},{6,7},{7,6},{8,9},{9,8},{10,11... | collective-permute-start | bytes 98312 | tf_op jit(solution)/shard_map/ppermute | solution.py:209
  35.0 0.9 %collective-permute-done.15.mark_ref.there_ref = bf16[8,2048]{1,0:T(8,128)(2,1)S(1)} collective-permute-done((bf16[8,2048]{1,0:T(8,128)(2,1)S(1)}, bf16[8,2048]{1,0:T(8,128)(2,1)S(1)}, u32[]{:S(2)}, u32[]{:S(2)}) %collective-permute-start.15) | collective-permute-done | bytes 32800 | tf_op jit(solution)/shard_map/ppermute | solution.py:209
  35.9 2.8 %collective-permute-start.19 = (bf16[64,2048]{1,0:T(8,128)(2,1)S(1)}, bf16[64,2048]{1,0:T(8,128)(2,1)S(1)}, u32[]{:S(2)}, u32[]{:S(2)}) collective-permute-start(bf16[64,2048]{1,0:T(8,128)(2,1)S(1)} %shard_map.101.refs_0_), channel_id=1, source_target_pairs={{0,1},{1,0},{2,3},{3,2},{4,5},{5,4},{6,7},{7,6},{8,9},{9,8},{10,11... | collective-permute-start | bytes 786440 | tf_op jit(solution)/shard_map/ppermute | solution.py:209
  38.8 1.1 %shard_map.102 = (f32[32,2048]{1,0:T(8,128)S(1)}, bf16[32,2048]{1,0:T(8,128)(2,1)S(1)}) custom-call(f32[2,2048]{1,0:T(2,128)S(1)} %bitcast.34, f32[2,2048]{1,0:T(2,128)S(1)} %bitcast.35, bf16[2,2048,512]{2,1,0:T(8,128)(2,1)S(1)} %bitcast.21, bf16[2,2048,512]{2,1,0:T(8,128)(2,1)S(1)} %bitcast.25, bf16[2,512,2048]{2,1,0:T(8,128)(2,1)S(1)} %bitcast.29, ...), custom_call_target="tpu_custom_call" | custom-call | flops 402653184 | bytes 6291456 | tf_op jit(solution)/shard_map/pallas_call | solution.py:184
  40.0 1.1 %shard_map.103 = (f32[32,2048]{1,0:T(8,128)S(1)}, bf16[32,2048]{1,0:T(8,128)(2,1)S(1)}) custom-call(f32[2,2048]{1,0:T(2,128)S(1)} %bitcast.36, f32[2,2048]{1,0:T(2,128)S(1)} %bitcast.37, bf16[2,2048,512]{2,1,0:T(8,128)(2,1)S(1)} %bitcast.22, bf16[2,2048,512]{2,1,0:T(8,128)(2,1)S(1)} %bitcast.26, bf16[2,512,2048]{2,1,0:T(8,128)(2,1)S(1)} %bitcast.30, ...), custom_call_target="tpu_custom_call" | custom-call | flops 402653184 | bytes 6291456 | tf_op jit(solution)/shard_map/pallas_call | solution.py:184
  41.2 0.5 %collective-permute-start.20 = (bf16[32,2048]{1,0:T(8,128)(2,1)S(1)}, bf16[32,2048]{1,0:T(8,128)(2,1)S(1)}, u32[]{:S(2)}, u32[]{:S(2)}) collective-permute-start(bf16[32,2048]{1,0:T(8,128)(2,1)S(1)} %get-tuple-element.30), channel_id=1, source_target_pairs={{0,1},{1,0},{2,3},{3,2},{4,5},{5,4},{6,7},{7,6},{8,9},{9,8},{10,11... | collective-permute-start | bytes 393224 | tf_op jit(solution)/shard_map/ppermute | solution.py:209
  41.7 1.0 %collective-permute-done.20.to_mine_ref = bf16[32,2048]{1,0:T(8,128)(2,1)S(1)} collective-permute-done((bf16[32,2048]{1,0:T(8,128)(2,1)S(1)}, bf16[32,2048]{1,0:T(8,128)(2,1)S(1)}, u32[]{:S(2)}, u32[]{:S(2)}) %collective-permute-start.20) | collective-permute-done | bytes 131104 | tf_op jit(solution)/shard_map/ppermute | solution.py:209
  42.7 1.3 %collective-permute-start.22 = (bf16[16,2048]{1,0:T(8,128)(2,1)S(1)}, bf16[16,2048]{1,0:T(8,128)(2,1)S(1)}, u32[]{:S(2)}, u32[]{:S(2)}) collective-permute-start(bf16[16,2048]{1,0:T(8,128)(2,1)S(1)} %get-tuple-element.32), channel_id=1, source_target_pairs={{0,6},{1,7},{2,4},{3,5},{4,2},{5,3},{6,0},{7,1},{8,14},{9,15},{10,... | collective-permute-start | bytes 196616 | tf_op jit(solution)/shard_map/ppermute | solution.py:213
  44.2 1.2 %collective-permute-start.24 = (bf16[16,2048]{1,0:T(8,128)(2,1)S(1)}, bf16[16,2048]{1,0:T(8,128)(2,1)S(1)}, u32[]{:S(2)}, u32[]{:S(2)}) collective-permute-start(bf16[16,2048]{1,0:T(8,128)(2,1)S(1)} %get-tuple-element.34), channel_id=1, source_target_pairs={{0,2},{1,3},{2,0},{3,1},{4,6},{5,7},{6,4},{7,5},{8,10},{9,11},{10,... | collective-permute-start | bytes 196616 | tf_op jit(solution)/shard_map/ppermute | solution.py:213
  45.5 1.4 %collective-permute-done.22.refs_0_ = bf16[16,2048]{1,0:T(8,128)(2,1)S(1)} collective-permute-done((bf16[16,2048]{1,0:T(8,128)(2,1)S(1)}, bf16[16,2048]{1,0:T(8,128)(2,1)S(1)}, u32[]{:S(2)}, u32[]{:S(2)}) %collective-permute-start.22) | collective-permute-done | bytes 65568 | tf_op jit(solution)/shard_map/ppermute | solution.py:213
  46.9 2.2 %collective-permute-done.23.refs_1_ = bf16[16,2048]{1,0:T(8,128)(2,1)S(1)} collective-permute-done((bf16[16,2048]{1,0:T(8,128)(2,1)S(1)}, bf16[16,2048]{1,0:T(8,128)(2,1)S(1)}, u32[]{:S(2)}, u32[]{:S(2)}) %collective-permute-start.23) | collective-permute-done | bytes 65568 | tf_op jit(solution)/shard_map/ppermute | solution.py:213
  49.1 0.6 %select_bitcast_fusion = (bf16[1,8,2048]{2,1,0:T(8,128)(2,1)}, bf16[1,8,2048]{2,1,0:T(8,128)(2,1)}) fusion(pred[]{:T(512)S(6)} %eq.37, bf16[16,2048]{1,0:T(8,128)(2,1)S(1)} %shard_map.105), kind=kLoop, calls=%fused_computation.7 | loop fusion | flops 32768 | bytes 131073 | tf_op jit(solution)/shard_map/broadcast_in_dim | solution.py:275
  (56 shorter events, 2.5 us)
Async XLA Ops:
  0.6 0.8 %copy-start = (bf16[2,8,2048]{2,1,0:T(8,128)(2,1)S(1)}, bf16[2,8,2048]{2,1,0:T(8,128)(2,1)}, u32[]{:S(2)}) copy-start(bf16[2,8,2048]{2,1,0:T(8,128)(2,1)} %param.10) | copy-start | bytes 196612
  0.7 1.1 %copy-start.5 = (bf16[1,8,2048]{2,1,0:T(8,128)(2,1)S(1)}, bf16[1,8,2048]{2,1,0:T(8,128)(2,1)}, u32[]{:S(2)}) copy-start(bf16[1,8,2048]{2,1,0:T(8,128)(2,1)} %param.8) | copy-start | bytes 98308
  0.7 1.1 %copy-start.6 = (bf16[1,8,2048]{2,1,0:T(8,128)(2,1)S(1)}, bf16[1,8,2048]{2,1,0:T(8,128)(2,1)}, u32[]{:S(2)}) copy-start(bf16[1,8,2048]{2,1,0:T(8,128)(2,1)} %param.9) | copy-start | bytes 98308
  1.8 1.6 %collective-permute-start.1 = (bf16[8,2048]{1,0:T(8,128)(2,1)S(1)}, bf16[8,2048]{1,0:T(8,128)(2,1)S(1)}, u32[]{:S(2)}, u32[]{:S(2)}) collective-permute-start(bf16[8,2048]{1,0:T(8,128)(2,1)S(1)} %get-tuple-element.21), channel_id=1, source_target_pairs={{0,1},{1,0},{2,3},{3,2},{4,5},{5,4},{6,7},{7,6},{8,9},{9,8},{10,11... | collective-permute-start | bytes 98312 | tf_op jit(solution)/shard_map/ppermute | solution.py:209
  3.5 11.5 %copy-start.1 = (bf16[1,2,2048,512]{3,2,1,0:T(8,128)(2,1)S(1)}, bf16[1,2,2048,512]{3,2,1,0:T(8,128)(2,1)}, u32[]{:S(2)}) copy-start(bf16[1,2,2048,512]{3,2,1,0:T(8,128)(2,1)} %param.13) | copy-start | bytes 12582916
  3.5 11.5 %copy-start.2 = (bf16[1,2,2048,512]{3,2,1,0:T(8,128)(2,1)S(1)}, bf16[1,2,2048,512]{3,2,1,0:T(8,128)(2,1)}, u32[]{:S(2)}) copy-start(bf16[1,2,2048,512]{3,2,1,0:T(8,128)(2,1)} %param.14) | copy-start | bytes 12582916
  3.5 11.5 %copy-start.3 = (bf16[1,2,512,2048]{3,2,1,0:T(8,128)(2,1)S(1)}, bf16[1,2,512,2048]{3,2,1,0:T(8,128)(2,1)}, u32[]{:S(2)}) copy-start(bf16[1,2,512,2048]{3,2,1,0:T(8,128)(2,1)} %param.15) | copy-start | bytes 12582916
  3.5 11.5 %copy-start.4 = (f32[1,2,2048]{2,1,0:T(2,128)S(1)}, f32[1,2,2048]{2,1,0:T(2,128)}, u32[]{:S(2)}) copy-start(f32[1,2,2048]{2,1,0:T(2,128)} %param.12) | copy-start | bytes 49156
  3.5 8.2 %collective-permute-start.2 = (bf16[16,2048]{1,0:T(8,128)(2,1)S(1)}, bf16[16,2048]{1,0:T(8,128)(2,1)S(1)}, u32[]{:S(2)}, u32[]{:S(2)}) collective-permute-start(bf16[16,2048]{1,0:T(8,128)(2,1)S(1)} %pad_maximum_fusion.1.x_ref), channel_id=1, source_target_pairs={{0,14},{2,12},{4,10},{6,8},{1,7},{3,5},{5,3},{7,1},{8,6},{10,4},{1... | collective-permute-start | bytes 196616 | tf_op jit(solution)/shard_map/ppermute | solution.py:223
  6.8 5.1 %collective-permute-start.3 = (bf16[16,2048]{1,0:T(8,128)(2,1)S(1)}, bf16[16,2048]{1,0:T(8,128)(2,1)S(1)}, u32[]{:S(2)}, u32[]{:S(2)}) collective-permute-start(bf16[16,2048]{1,0:T(8,128)(2,1)S(1)} %pad_maximum_fusion.1.x_ref), channel_id=1, source_target_pairs={{0,12},{2,14},{4,8},{6,10},{1,5},{3,7},{5,1},{7,3},{8,4},{10,6},{1... | collective-permute-start | bytes 196616 | tf_op jit(solution)/shard_map/ppermute | solution.py:223
  6.9 5.4 %collective-permute-start.4 = (bf16[16,2048]{1,0:T(8,128)(2,1)S(1)}, bf16[16,2048]{1,0:T(8,128)(2,1)S(1)}, u32[]{:S(2)}, u32[]{:S(2)}) collective-permute-start(bf16[16,2048]{1,0:T(8,128)(2,1)S(1)} %pad_maximum_fusion.1.x_ref), channel_id=1, source_target_pairs={{0,10},{2,8},{4,14},{6,12},{1,3},{3,1},{5,7},{7,5},{8,2},{10,0},{1... | collective-permute-start | bytes 196616 | tf_op jit(solution)/shard_map/ppermute | solution.py:223
  8.1 5.3 %collective-permute-start.5 = (bf16[16,2048]{1,0:T(8,128)(2,1)S(1)}, bf16[16,2048]{1,0:T(8,128)(2,1)S(1)}, u32[]{:S(2)}, u32[]{:S(2)}) collective-permute-start(bf16[16,2048]{1,0:T(8,128)(2,1)S(1)} %pad_maximum_fusion.1.x_ref), channel_id=1, source_target_pairs={{0,8},{2,10},{4,12},{6,14},{1,1},{3,3},{5,5},{7,7},{8,0},{10,2},{1... | collective-permute-start | bytes 196616 | tf_op jit(solution)/shard_map/ppermute | solution.py:223
  10.3 6.3 %collective-permute-start = (bf16[8,2048]{1,0:T(8,128)(2,1)S(1)}, bf16[8,2048]{1,0:T(8,128)(2,1)S(1)}, u32[]{:S(2)}, u32[]{:S(2)}) collective-permute-start(bf16[8,2048]{1,0:T(8,128)(2,1)S(1)} %get-tuple-element.19), channel_id=1, source_target_pairs={{0,1},{1,0},{2,3},{3,2},{4,5},{5,4},{6,7},{7,6},{8,9},{9,8},{10,11... | collective-permute-start | bytes 98312 | tf_op jit(solution)/shard_map/ppermute | solution.py:209
  11.7 2.3 %collective-permute-start.6 = (bf16[16,2048]{1,0:T(8,128)(2,1)S(1)}, bf16[16,2048]{1,0:T(8,128)(2,1)S(1)}, u32[]{:S(2)}, u32[]{:S(2)}) collective-permute-start(bf16[16,2048]{1,0:T(8,128)(2,1)S(1)} %collective-permute-done.2.refs_0_), channel_id=1, source_target_pairs={{0,1},{1,0},{2,3},{3,2},{4,5},{5,4},{6,7},{7,6},{8,9},{9,8},{10,11... | collective-permute-start | bytes 196616 | tf_op jit(solution)/shard_map/ppermute | solution.py:209
  11.8 2.2 %collective-permute-start.7 = (bf16[16,2048]{1,0:T(8,128)(2,1)S(1)}, bf16[16,2048]{1,0:T(8,128)(2,1)S(1)}, u32[]{:S(2)}, u32[]{:S(2)}) collective-permute-start(bf16[16,2048]{1,0:T(8,128)(2,1)S(1)} %collective-permute-done.3.refs_1_), channel_id=1, source_target_pairs={{0,1},{1,0},{2,3},{3,2},{4,5},{5,4},{6,7},{7,6},{8,9},{9,8},{10,11... | collective-permute-start | bytes 196616 | tf_op jit(solution)/shard_map/ppermute | solution.py:209
  12.3 1.8 %collective-permute-start.8 = (bf16[16,2048]{1,0:T(8,128)(2,1)S(1)}, bf16[16,2048]{1,0:T(8,128)(2,1)S(1)}, u32[]{:S(2)}, u32[]{:S(2)}) collective-permute-start(bf16[16,2048]{1,0:T(8,128)(2,1)S(1)} %collective-permute-done.4.refs_2_), channel_id=1, source_target_pairs={{0,1},{1,0},{2,3},{3,2},{4,5},{5,4},{6,7},{7,6},{8,9},{9,8},{10,11... | collective-permute-start | bytes 196616 | tf_op jit(solution)/shard_map/ppermute | solution.py:209
  13.4 1.5 %collective-permute-start.9 = (bf16[16,2048]{1,0:T(8,128)(2,1)S(1)}, bf16[16,2048]{1,0:T(8,128)(2,1)S(1)}, u32[]{:S(2)}, u32[]{:S(2)}) collective-permute-start(bf16[16,2048]{1,0:T(8,128)(2,1)S(1)} %collective-permute-done.5.refs_3_.x_ref), channel_id=1, source_target_pairs={{0,1},{1,0},{2,3},{3,2},{4,5},{5,4},{6,7},{7,6},{8,9},{9,8},{10,11... | collective-permute-start | bytes 196616 | tf_op jit(solution)/shard_map/ppermute | solution.py:209
  16.2 1.7 %collective-permute-start.10 = (bf16[64,2048]{1,0:T(8,128)(2,1)S(1)}, bf16[64,2048]{1,0:T(8,128)(2,1)S(1)}, u32[]{:S(2)}, u32[]{:S(2)}) collective-permute-start(bf16[64,2048]{1,0:T(8,128)(2,1)S(1)} %shard_map.98), channel_id=1, source_target_pairs={{0,1},{1,0},{2,3},{3,2},{4,5},{5,4},{6,7},{7,6},{8,9},{9,8},{10,11... | collective-permute-start | bytes 786440 | tf_op jit(solution)/shard_map/ppermute | solution.py:209
  17.9 7.0 %collective-permute-start.11 = (bf16[16,2048]{1,0:T(8,128)(2,1)S(1)}, bf16[16,2048]{1,0:T(8,128)(2,1)S(1)}, u32[]{:S(2)}, u32[]{:S(2)}) collective-permute-start(bf16[16,2048]{1,0:T(8,128)(2,1)S(1)} %get-tuple-element.22), channel_id=1, source_target_pairs={{0,6},{2,4},{4,2},{6,0},{1,15},{3,13},{5,11},{7,9},{8,22},{10,20},... | collective-permute-start | bytes 196616 | tf_op jit(solution)/shard_map/ppermute | solution.py:223
  21.5 4.0 %collective-permute-start.12 = (bf16[16,2048]{1,0:T(8,128)(2,1)S(1)}, bf16[16,2048]{1,0:T(8,128)(2,1)S(1)}, u32[]{:S(2)}, u32[]{:S(2)}) collective-permute-start(bf16[16,2048]{1,0:T(8,128)(2,1)S(1)} %get-tuple-element.23), channel_id=1, source_target_pairs={{0,4},{2,6},{4,0},{6,2},{1,13},{3,15},{5,9},{7,11},{8,20},{10,22},... | collective-permute-start | bytes 196616 | tf_op jit(solution)/shard_map/ppermute | solution.py:223
  21.6 4.0 %collective-permute-start.13 = (bf16[16,2048]{1,0:T(8,128)(2,1)S(1)}, bf16[16,2048]{1,0:T(8,128)(2,1)S(1)}, u32[]{:S(2)}, u32[]{:S(2)}) collective-permute-start(bf16[16,2048]{1,0:T(8,128)(2,1)S(1)} %get-tuple-element.24), channel_id=1, source_target_pairs={{0,2},{2,0},{4,6},{6,4},{1,11},{3,9},{5,15},{7,13},{8,18},{10,16},... | collective-permute-start | bytes 196616 | tf_op jit(solution)/shard_map/ppermute | solution.py:223
  22.9 5.1 %collective-permute-start.14 = (bf16[16,2048]{1,0:T(8,128)(2,1)S(1)}, bf16[16,2048]{1,0:T(8,128)(2,1)S(1)}, u32[]{:S(2)}, u32[]{:S(2)}) collective-permute-start(bf16[16,2048]{1,0:T(8,128)(2,1)S(1)} %get-tuple-element.25), channel_id=1, source_target_pairs={{0,0},{2,2},{4,4},{6,6},{1,9},{3,11},{5,13},{7,15},{8,16},{10,18},... | collective-permute-start | bytes 196616 | tf_op jit(solution)/shard_map/ppermute | solution.py:223
  28.1 7.8 %collective-permute-start.16 = (bf16[16,2048]{1,0:T(8,128)(2,1)S(1)}, bf16[16,2048]{1,0:T(8,128)(2,1)S(1)}, u32[]{:S(2)}, u32[]{:S(2)}) collective-permute-start(bf16[16,2048]{1,0:T(8,128)(2,1)S(1)} %get-tuple-element.27.refs_3_), channel_id=1, source_target_pairs={{0,6},{1,7},{2,4},{3,5},{4,2},{5,3},{6,0},{7,1},{8,14},{9,15},{10,... | collective-permute-start | bytes 196616 | tf_op jit(solution)/shard_map/ppermute | solution.py:213
  30.2 5.7 %collective-permute-start.17 = (bf16[16,2048]{1,0:T(8,128)(2,1)S(1)}, bf16[16,2048]{1,0:T(8,128)(2,1)S(1)}, u32[]{:S(2)}, u32[]{:S(2)}) collective-permute-start(bf16[16,2048]{1,0:T(8,128)(2,1)S(1)} %get-tuple-element.27.refs_3_), channel_id=1, source_target_pairs={{0,4},{1,5},{2,6},{3,7},{4,0},{5,1},{6,2},{7,3},{8,12},{9,13},{10,... | collective-permute-start | bytes 196616 | tf_op jit(solution)/shard_map/ppermute | solution.py:213
  30.5 5.4 %collective-permute-start.18 = (bf16[16,2048]{1,0:T(8,128)(2,1)S(1)}, bf16[16,2048]{1,0:T(8,128)(2,1)S(1)}, u32[]{:S(2)}, u32[]{:S(2)}) collective-permute-start(bf16[16,2048]{1,0:T(8,128)(2,1)S(1)} %get-tuple-element.27.refs_3_), channel_id=1, source_target_pairs={{0,2},{1,3},{2,0},{3,1},{4,6},{5,7},{6,4},{7,5},{8,10},{9,11},{10,... | collective-permute-start | bytes 196616 | tf_op jit(solution)/shard_map/ppermute | solution.py:213
  30.8 5.1 %collective-permute-start.15 = (bf16[8,2048]{1,0:T(8,128)(2,1)S(1)}, bf16[8,2048]{1,0:T(8,128)(2,1)S(1)}, u32[]{:S(2)}, u32[]{:S(2)}) collective-permute-start(bf16[8,2048]{1,0:T(8,128)(2,1)S(1)} %get-tuple-element.41), channel_id=1, source_target_pairs={{0,1},{1,0},{2,3},{3,2},{4,5},{5,4},{6,7},{7,6},{8,9},{9,8},{10,11... | collective-permute-start | bytes 98312 | tf_op jit(solution)/shard_map/ppermute | solution.py:209
  35.9 4.1 %collective-permute-start.19 = (bf16[64,2048]{1,0:T(8,128)(2,1)S(1)}, bf16[64,2048]{1,0:T(8,128)(2,1)S(1)}, u32[]{:S(2)}, u32[]{:S(2)}) collective-permute-start(bf16[64,2048]{1,0:T(8,128)(2,1)S(1)} %shard_map.101.refs_0_), channel_id=1, source_target_pairs={{0,1},{1,0},{2,3},{3,2},{4,5},{5,4},{6,7},{7,6},{8,9},{9,8},{10,11... | collective-permute-start | bytes 786440 | tf_op jit(solution)/shard_map/ppermute | solution.py:209
  39.9 1.8 %collective-permute-start.21 = (bf16[32,2048]{1,0:T(8,128)(2,1)S(1)}, bf16[32,2048]{1,0:T(8,128)(2,1)S(1)}, u32[]{:S(2)}, u32[]{:S(2)}) collective-permute-start(bf16[32,2048]{1,0:T(8,128)(2,1)S(1)} %get-tuple-element.31), channel_id=1, source_target_pairs={{0,1},{1,0},{2,3},{3,2},{4,5},{5,4},{6,7},{7,6},{8,9},{9,8},{10,11... | collective-permute-start | bytes 393224 | tf_op jit(solution)/shard_map/ppermute | solution.py:209
  41.2 1.5 %collective-permute-start.20 = (bf16[32,2048]{1,0:T(8,128)(2,1)S(1)}, bf16[32,2048]{1,0:T(8,128)(2,1)S(1)}, u32[]{:S(2)}, u32[]{:S(2)}) collective-permute-start(bf16[32,2048]{1,0:T(8,128)(2,1)S(1)} %get-tuple-element.30), channel_id=1, source_target_pairs={{0,1},{1,0},{2,3},{3,2},{4,5},{5,4},{6,7},{7,6},{8,9},{9,8},{10,11... | collective-permute-start | bytes 393224 | tf_op jit(solution)/shard_map/ppermute | solution.py:209
  42.7 4.1 %collective-permute-start.22 = (bf16[16,2048]{1,0:T(8,128)(2,1)S(1)}, bf16[16,2048]{1,0:T(8,128)(2,1)S(1)}, u32[]{:S(2)}, u32[]{:S(2)}) collective-permute-start(bf16[16,2048]{1,0:T(8,128)(2,1)S(1)} %get-tuple-element.32), channel_id=1, source_target_pairs={{0,6},{1,7},{2,4},{3,5},{4,2},{5,3},{6,0},{7,1},{8,14},{9,15},{10,... | collective-permute-start | bytes 196616 | tf_op jit(solution)/shard_map/ppermute | solution.py:213
  44.0 5.0 %collective-permute-start.23 = (bf16[16,2048]{1,0:T(8,128)(2,1)S(1)}, bf16[16,2048]{1,0:T(8,128)(2,1)S(1)}, u32[]{:S(2)}, u32[]{:S(2)}) collective-permute-start(bf16[16,2048]{1,0:T(8,128)(2,1)S(1)} %get-tuple-element.33), channel_id=1, source_target_pairs={{0,4},{1,5},{2,6},{3,7},{4,0},{5,1},{6,2},{7,3},{8,12},{9,13},{10,... | collective-permute-start | bytes 196616 | tf_op jit(solution)/shard_map/ppermute | solution.py:213
  44.2 4.8 %collective-permute-start.24 = (bf16[16,2048]{1,0:T(8,128)(2,1)S(1)}, bf16[16,2048]{1,0:T(8,128)(2,1)S(1)}, u32[]{:S(2)}, u32[]{:S(2)}) collective-permute-start(bf16[16,2048]{1,0:T(8,128)(2,1)S(1)} %get-tuple-element.34), channel_id=1, source_target_pairs={{0,2},{1,3},{2,0},{3,1},{4,6},{5,7},{6,4},{7,5},{8,10},{9,11},{10,... | collective-permute-start | bytes 196616 | tf_op jit(solution)/shard_map/ppermute | solution.py:213
  (1 other events, 0.8 us)
